TPU v7x, 32 devices: a whole 2x2x4 slice. The times are simulated.
32 devices in a mesh: parts: 2 (over y), group: 8 (over z, x), tensor: 2 (over core).
Axes of the slice: x: 2, y: 2, z: 4, core: 2. Of those that a mesh axis runs over, the one named last changes fastest.
Arguments:
- normed_hidden_states: bfloat16 [1024, 2, 8192], P(('parts', 'group'), None, 'tensor'), parts along dimension 0, may hold values from -6 to 6
- query_matrix: bfloat16 [8192, 512], P('tensor', 'group'), may hold values from -0.0625 to 0.0625
- factor_down: bfloat16 [8, 8192, 64], P('group', None, 'tensor'), may hold values from -0.0625 to 0.0625
- factor_up: bfloat16 [8, 64, 512], P('group', None, 'tensor'), may hold values from -0.75 to 0.75
- kv_cache: bfloat16 [1024, 32, 256], P(('parts', 'group'), 'tensor'), parts along dimension 0, may hold values from -500 to 500
- incoming_key_value: bfloat16 [1024, 2, 256], P(('parts', 'group')), parts along dimension 0, may hold values from -6 to 6
- kv_lengths: int32 [1024], P(('parts', 'group')), parts along dimension 0, may hold values from 1 to 32, 8192 in all
- request_adapter: int32 [1024], P(('parts', 'group')), parts along dimension 0, may hold values from 0 to 7, as said below
- adapter_owner: int32 [16], P('parts'), parts along dimension 0, may hold values from 0 to 7, as said below
Outputs:
- queries: bfloat16 [1024, 2, 512], P(('parts', 'group')), parts along dimension 0
- attended: bfloat16 [1024, 2, 512], P(('parts', 'group')), parts along dimension 0
There are 2 independent parts, one for each index of `parts`. A program takes and returns all parts, laid end to end along the dimension named above; an argument that names none is the same for every part. Nothing has to cross between parts.
Inputs may be any that keep to these rules, and one draw needn't show every extreme that they name: `adapter_owner`: each owner holds exactly one adapter. `request_adapter`: within each aligned block of 64 requests (the requests of one device), at most 8 requests name adapters of one owner, and in every block some owner is named by exactly 8.
All inputs are finite; a program needn't handle non-finite values. No bound on the sum of `kv_lengths` on one device may be relied on, other than what follows from the above.
Results may differ from a plain program's by a relative error of at most 0.01695.
Values may be sent and summed in bfloat16 or wider, within the bound.
No kernel may reach another device: no remote copies, remote signals or barrier semaphores. Data moves between devices by JAX's collectives and lax.ppermute only.
A program may use at most 64 MiB of HBM per device.

v0:
```python
import math

import jax
import jax.numpy as jnp
from jax import lax
from jax.sharding import PartitionSpec as P


def merged(x, axis, combine):
    everything = jax.tree.map(
        lambda part, kind: lax.all_gather(part.astype(kind), axis),
        x,
        (jnp.bfloat16, jnp.bfloat16, jnp.bfloat16),
    )

    def take(k):
        return jax.tree.map(lambda part, own: part[k].astype(own.dtype), everything, x)

    return lax.fori_loop(
        1, lax.axis_size(axis), lambda k, so_far: combine(so_far, take(k)), take(0)
    )


def combine(first, second):
    highest = jnp.maximum(first[0], second[0])
    first_factor = jnp.exp(first[0] - highest)
    second_factor = jnp.exp(second[0] - highest)
    totals = first[1] * first_factor + second[1] * second_factor
    sums = first[2] * first_factor[..., None] + second[2] * second_factor[..., None]
    return (highest, totals, sums)


def body(
    normed_hidden_states,
    query_matrix,
    factor_down,
    factor_up,
    kv_cache,
    incoming_key_value,
    kv_lengths,
    request_adapter,
    adapter_owner,
):
    owners_count = lax.axis_size("group")
    requests_here = normed_hidden_states.shape[0]
    step_count = normed_hidden_states.shape[1]
    capacity = max(2, requests_here // owners_count)
    adapter_ids = jnp.arange(adapter_owner.shape[0], dtype=jnp.int32)
    lookup = request_adapter[:, None] == adapter_ids[None, :]
    holder = jnp.sum(jnp.where(lookup, adapter_owner[None, :], 0), axis=1)
    same_owner = holder[:, None] == holder[None, :]
    request_ids = jnp.arange(requests_here, dtype=jnp.int32)
    earlier = request_ids[None, :] < request_ids[:, None]
    before = jnp.sum(jnp.logical_and(same_owner, earlier).astype(jnp.int32), axis=1)
    slot_index = holder * capacity + before
    slots_all = owners_count * capacity
    select = (jnp.arange(slots_all, dtype=jnp.int32)[:, None] == slot_index[None, :]).astype(
        jnp.bfloat16
    )
    up_factor = factor_up[0]
    partial_value = jnp.einsum(
        "cah,hj->caj",
        normed_hidden_states,
        lax.all_gather(query_matrix, "group", axis=1, tiled=True),
        preferred_element_type=jnp.float32,
    )
    base_sum = lax.psum(partial_value, "tensor")
    whole_rows = lax.all_gather(normed_hidden_states, "tensor", axis=2, tiled=True)
    outgoing = jnp.einsum("kr,rsd->ksd", select, whole_rows, preferred_element_type=jnp.bfloat16)
    down_factor = factor_down[0]
    shrink_part = jnp.einsum(
        "ksd,dc->ksc",
        lax.all_to_all(outgoing, "group", split_axis=0, concat_axis=0, tiled=True),
        down_factor,
        preferred_element_type=jnp.float32,
    ).astype(jnp.bfloat16)
    shrink = lax.all_gather(shrink_part, "tensor", axis=2, tiled=True)
    adapted = jnp.einsum("ksc,cq->ksq", shrink, up_factor, preferred_element_type=jnp.float32)
    returned = lax.all_to_all(adapted, "group", split_axis=0, concat_axis=0, tiled=True)
    adapted_rows = jnp.take(returned, slot_index, axis=0)
    core_index = lax.axis_index("tensor")
    adapted_full = lax.all_gather(adapted_rows, "tensor", axis=2, tiled=True)
    query_sum = base_sum + adapted_full
    queries = query_sum.astype(jnp.bfloat16)
    head_size = kv_cache.shape[2] // 2
    head_rows = queries.reshape(requests_here, step_count, -1, head_size)
    scaling = 1.0 / math.sqrt(head_size)
    key_rows = kv_cache[:, :, :head_size]
    value_rows = kv_cache[:, :, head_size:]
    local_count = kv_cache.shape[1]
    position = core_index * local_count + jnp.arange(local_count, dtype=jnp.int32)
    usable = position[None, :] < kv_lengths[:, None]
    scores = (
        jnp.einsum("rshd,rpd->rshp", head_rows, key_rows, preferred_element_type=jnp.float32)
        * scaling
    )
    scores = jnp.where(usable[:, None, None, :], scores, -1e30)
    incoming_key_rows = incoming_key_value[:, :, :head_size]
    fresh_values = incoming_key_value[:, :, head_size:]
    fresh = (
        jnp.einsum(
            "rshd,rjd->rshj", head_rows, incoming_key_rows, preferred_element_type=jnp.float32
        )
        * scaling
    )
    step_ids = jnp.arange(step_count, dtype=jnp.int32)
    allowed = jnp.logical_and(step_ids[None, :] <= step_ids[:, None], core_index == 0)
    fresh = jnp.where(allowed[None, :, None, :], fresh, -1e30)
    highest = jnp.maximum(jnp.max(scores, axis=3), jnp.max(fresh, axis=3))
    attention_weights = jnp.where(
        usable[:, None, None, :], jnp.exp(scores - highest[..., None]), 0.0
    )
    fresh_weights = jnp.where(allowed[None, :, None, :], jnp.exp(fresh - highest[..., None]), 0.0)
    totals = jnp.sum(attention_weights, axis=3) + jnp.sum(fresh_weights, axis=3)
    sums = jnp.einsum(
        "rshp,rpd->rshd",
        attention_weights.astype(jnp.bfloat16),
        value_rows,
        preferred_element_type=jnp.float32,
    )
    sums = sums + jnp.einsum(
        "rshj,rjd->rshd",
        fresh_weights.astype(jnp.bfloat16),
        fresh_values,
        preferred_element_type=jnp.float32,
    )
    highest, totals, sums = merged((highest, totals, sums), "tensor", combine)
    attended = (
        (sums / totals[..., None]).reshape(requests_here, step_count, -1).astype(jnp.bfloat16)
    )
    return (queries, attended)


def solution(mesh):
    placed = (
        P(("parts", "group"), None, "tensor"),
        P("tensor", "group"),
        P("group", None, "tensor"),
        P("group", None, "tensor"),
        P(("parts", "group"), "tensor", None),
        P(("parts", "group"), None, None),
        P(("parts", "group")),
        P(("parts", "group")),
        P("parts"),
    )
    return jax.shard_map(
        body,
        mesh=mesh,
        in_specs=placed,
        out_specs=(P(("parts", "group"), None, None), P(("parts", "group"), None, None)),
        check_vma=False,
    )
```

profile of v0, /device:TPU:0, one launch (start us, length us, event | category | flops | bytes accessed | tf_op | source)
XLA Modules:
  0.0 183.4 jit_solution(8652877171737877941)
XLA Ops:
  7.2 0.0 copy-start
  7.2 0.0 all-gather.8.cloned.1.call-start
  7.2 2.8 %copy.46 = bf16[64,2,4096]{2,0,1:T(8,128)(2,1)} copy(bf16[64,2,4096]{2,1,0:T(2,128)(2,1)} %param.9) | data formatting | bytes 2097152 | tf_op args[0]
  10.1 0.0 all-gather.8.cloned.1.call-update
  10.1 0.0 all-gather.6.cloned.1.call-start
  10.2 0.7 all-gather.6.cloned.1.call-update
  10.9 0.1 select_reduce_fusion
  11.0 0.2 convert_reduce_fusion
  11.2 12.4 %all-gather.8.cloned.1.call-done = bf16[64,2,8192]{2,0,1:T(8,128)(2,1)} async-done(((bf16[64,2,4096]{2,0,1:T(8,128)(2,1)}), bf16[64,2,8192]{2,0,1:T(8,128)(2,1)}) %all-gather.8.cloned.1.call-update) | async-done | bytes 2097168 | tf_op jit(solution)/shard_map/all_gather | solution.py:68
  23.6 2.3 %fusion.32 = bf16[64,2,8192]{2,0,1:T(8,128)(2,1)S(1)} fusion(bf16[64,2,8192]{2,0,1:T(8,128)(2,1)} %all-gather.8.cloned.1.call-done, s32[64]{0:T(128)S(1)} %get-tuple-element.41), kind=kOutput, calls=%fused_computation.43 | convolution fusion | flops 134221824 | bytes 4194560 | tf_op jit(solution)/shard_map/kr,rsd->ksd/dot_general | solution.py:69
  25.8 3.5 %copy.48 = bf16[64,2,8192]{2,1,0:T(2,128)(2,1)} copy(bf16[64,2,8192]{2,0,1:T(8,128)(2,1)S(1)} %fusion.32) | data formatting | bytes 4194304 | tf_op jit(solution)/shard_map/kr,rsd->ksd/dot_general | solution.py:69
  29.4 5.8 %all-to-all-start = ((bf16[64,2,8192]{2,1,0:T(2,128)(2,1)}), bf16[64,2,8192]{2,1,0:T(2,128)(2,1)}, u32[]{:S(2)}, u32[]{:S(2)}) async-start(bf16[64,2,8192]{2,1,0:T(2,128)(2,1)} %copy.48), calls=%async_computation | async-start | bytes 4194304 | tf_op jit(solution)/shard_map/all_to_all | solution.py:73
  35.2 89.4 %all-to-all-done = bf16[64,2,8192]{2,1,0:T(2,128)(2,1)} async-done(((bf16[64,2,8192]{2,1,0:T(2,128)(2,1)}), bf16[64,2,8192]{2,1,0:T(2,128)(2,1)}, u32[]{:S(2)}, u32[]{:S(2)}) %all-to-all-start) | async-done | bytes 2097184 | tf_op jit(solution)/shard_map/all_to_all | solution.py:73
  124.6 3.9 %fusion.7 = bf16[64,2,32]{0,2,1:T(8,128)(2,1)S(1)} fusion(bf16[64,2,8192]{2,1,0:T(2,128)(2,1)} %all-to-all-done, bf16[1,8192,32]{1,2,0:T(8,128)(2,1)S(1)} %copy-done), kind=kOutput, calls=%fused_computation.11 | convolution fusion | flops 67112960 | bytes 2629632 | tf_op jit(solution)/shard_map/ksd,dc->ksc/dot_general | solution.py:71
  128.6 1.8 all_gather.28
  130.4 0.2 fusion.27
  130.6 0.8 copy.50
  131.4 3.4 %all-to-all-start.1 = ((f32[64,2,256]{2,1,0:T(2,128)}), f32[64,2,256]{2,1,0:T(2,128)S(1)}, u32[]{:S(2)}, u32[]{:S(2)}) async-start(f32[64,2,256]{2,1,0:T(2,128)} %copy.50), calls=%async_computation.1 | async-start | bytes 262144 | tf_op jit(solution)/shard_map/all_to_all | solution.py:79
  134.8 0.0 all-reduce.2.cloned.1.call-start
  134.8 0.1 broadcast_compare_fusion
  134.9 7.4 %all-to-all-done.1 = f32[64,2,256]{2,1,0:T(2,128)S(1)} async-done(((f32[64,2,256]{2,1,0:T(2,128)}), f32[64,2,256]{2,1,0:T(2,128)S(1)}, u32[]{:S(2)}, u32[]{:S(2)}) %all-to-all-start.1) | async-done | bytes 131104 | tf_op jit(solution)/shard_map/all_to_all | solution.py:79
  142.3 0.7 gather_fusion
  143.0 0.0 all-gather.6.cloned.1.call-done
  143.1 4.4 %fusion = f32[64,2,512]{2,0,1:T(8,128)} fusion(bf16[4096,512]{0,1:T(8,128)(2,1)} %all-gather.6.cloned.1.call-done, bf16[64,2,4096]{2,1,0:T(2,128)(2,1)S(1)} %copy-done.1), kind=kOutput, calls=%fused_computation.1 | convolution fusion | flops 536870912 | bytes 5505024 | tf_op jit(solution)/shard_map/cah,hj->caj/dot_general | solution.py:61
  147.5 0.0 all-reduce.2.cloned.1.call-update
  147.5 0.1 copy_select_fusion
  147.6 2.1 %all_gather.29 = f32[64,2,512]{2,0,1:T(8,128)S(1)} all-gather(f32[64,2,256]{2,0,1:T(8,128)S(1)} %copy_select_fusion), channel_id=1, replica_groups=mesh['parts'=2,'group'=8,'tensor'=2] {'tensor'}, dimensions={2}, use_global_device_ids=true | all-gather | bytes 393216 | tf_op jit(solution)/shard_map/all_gather | solution.py:82
  149.7 14.3 %all-reduce.2.cloned.1.call-done = f32[64,2,512]{2,0,1:T(8,128)} async-done(((f32[64,2,512]{2,0,1:T(8,128)}), f32[64,2,512]{2,0,1:T(8,128)}) %all-reduce.2.cloned.1.call-update) | async-done | bytes 262160 | tf_op jit(solution)/shard_map/psum | solution.py:67
  164.0 1.0 add_convert_fusion
  165.0 0.8 copy.61
  165.8 1.3 fusion.47
  167.1 0.4 fusion.46
  167.6 0.4 fusion.24
  167.9 0.3 fusion.35
  168.2 0.4 fusion.16
  168.7 0.4 fusion.5
  169.1 2.0 %all-gather = bf16[128,2,4,128]{3,2,1,0:T(4,128)(2,1)S(1)} all-gather(bf16[64,2,4,128]{3,2,1,0:T(4,128)(2,1)S(1)} %fusion.5), channel_id=2, replica_groups=mesh['parts'=2,'group'=8,'tensor'=2] {'tensor'}, dimensions={0}, use_global_device_ids=true | all-gather | bytes 393216 | tf_op jit(solution)/shard_map/all_gather | solution.py:11
  171.0 1.8 %all-gather.1 = bf16[128,2,4]{2,1,0:T(2,128)(2,1)S(1)} all-gather(bf16[64,2,4]{2,1,0:T(2,128)(2,1)S(1)} %get-tuple-element.38), channel_id=3, replica_groups=mesh['parts'=2,'group'=8,'tensor'=2] {'tensor'}, dimensions={0}, use_global_device_ids=true | all-gather | bytes 3072 | tf_op jit(solution)/shard_map/all_gather | solution.py:11
  172.9 0.1 copy.67
  173.0 0.1 copy.66
  173.2 1.9 %all-gather.2 = bf16[128,2,4]{2,1,0:T(2,128)(2,1)S(1)} all-gather(bf16[64,2,4]{2,1,0:T(2,128)(2,1)S(1)} %add_convert_fusion.1), channel_id=4, replica_groups=mesh['parts'=2,'group'=8,'tensor'=2] {'tensor'}, dimensions={0}, use_global_device_ids=true | all-gather | bytes 3072 | tf_op jit(solution)/shard_map/all_gather | solution.py:11
  175.1 0.1 copy.69
  175.2 0.1 copy.68
  175.3 0.1 copy.60
  175.4 0.1 copy.57
  175.6 0.1 copy.56
  175.7 0.5 fusion.15
  176.2 0.7 reshape.224
  (26 shorter events, 0.3 us)
Async XLA Ops:
  7.2 117.5 %copy-start = (bf16[1,8192,32]{1,2,0:T(8,128)(2,1)S(1)}, bf16[1,8192,32]{1,2,0:T(8,128)(2,1)}, u32[]{:S(2)}) copy-start(bf16[1,8192,32]{1,2,0:T(8,128)(2,1)} %param.11) | copy-start | bytes 1572868
  7.2 3.7 %copy-start.6 = (s32[8]{0:T(128)S(1)}, s32[8]{0:T(128)}, u32[]{:S(2)}) copy-start(s32[8]{0:T(128)} %param.17) | copy-start | bytes 100
  7.2 3.7 %copy-start.7 = (s32[64]{0:T(128)S(1)}, s32[64]{0:T(128)}, u32[]{:S(2)}) copy-start(s32[64]{0:T(128)} %param.16) | copy-start | bytes 772
  7.2 16.4 %all-gather.8.cloned.1.call-start = ((), (), s32[]{:S(2)}) async-start(), calls=%async_computation.4 | async-start | bytes 3145728 | tf_op jit(solution)/shard_map/all_gather | solution.py:68
  10.1 132.9 %all-gather.6.cloned.1.call-start = ((), (), s32[]{:S(2)}) async-start(), calls=%async_computation.2 | async-start | bytes 4718592 | tf_op jit(solution)/shard_map/all_gather | solution.py:64
  29.4 95.3 %all-to-all-start = ((bf16[64,2,8192]{2,1,0:T(2,128)(2,1)}), bf16[64,2,8192]{2,1,0:T(2,128)(2,1)}, u32[]{:S(2)}, u32[]{:S(2)}) async-start(bf16[64,2,8192]{2,1,0:T(2,128)(2,1)} %copy.48), calls=%async_computation | async-start | bytes 4194304 | tf_op jit(solution)/shard_map/all_to_all | solution.py:73
  35.1 95.3 %copy-start.2 = (bf16[1,64,256]{2,1,0:T(8,128)(2,1)S(1)}, bf16[1,64,256]{2,1,0:T(8,128)(2,1)}, u32[]{:S(2)}) copy-start(bf16[1,64,256]{2,1,0:T(8,128)(2,1)} %param.12) | copy-start | bytes 98308
  35.2 99.7 %copy-start.3 = (s32[64]{0:T(128)S(1)}, s32[64]{0:T(128)}, u32[]{:S(2)}) copy-start(s32[64]{0:T(128)} %param.15) | copy-start | bytes 772
  35.2 107.8 %copy-start.1 = (bf16[64,2,4096]{2,1,0:T(2,128)(2,1)S(1)}, bf16[64,2,4096]{2,1,0:T(2,128)(2,1)}, u32[]{:S(2)}) copy-start(bf16[64,2,4096]{2,1,0:T(2,128)(2,1)} %param.9) | copy-start | bytes 3145732
  131.4 10.9 %all-to-all-start.1 = ((f32[64,2,256]{2,1,0:T(2,128)}), f32[64,2,256]{2,1,0:T(2,128)S(1)}, u32[]{:S(2)}, u32[]{:S(2)}) async-start(f32[64,2,256]{2,1,0:T(2,128)} %copy.50), calls=%async_computation.1 | async-start | bytes 262144 | tf_op jit(solution)/shard_map/all_to_all | solution.py:79
  134.8 29.2 %all-reduce.2.cloned.1.call-start = ((), (), s32[]{:S(2)}) async-start(), calls=%async_computation.3 | async-start | bytes 524288 | tf_op jit(solution)/shard_map/psum | solution.py:67
  147.5 18.3 %copy-start.5 = (bf16[64,2,256]{2,1,0:T(2,128)(2,1)S(1)}, bf16[64,2,256]{2,1,0:T(2,128)(2,1)}, u32[]{:S(2)}) copy-start(bf16[64,2,256]{2,1,0:T(2,128)(2,1)} %param.14) | copy-start | bytes 196612
  147.5 19.6 %copy-start.4 = (bf16[64,16,256]{2,1,0:T(8,128)(2,1)S(1)}, bf16[64,16,256]{2,1,0:T(8,128)(2,1)}, u32[]{:S(2)}) copy-start(bf16[64,16,256]{2,1,0:T(8,128)(2,1)} %param.13) | copy-start | bytes 1572868
Sparse Core Ops, SparseCore 0:
  10.2 13.2 all-gather.7
  25.7 110.8 all-gather.5
  147.6 16.3 all-reduce.1
where the time goes:
time: 184 us; the launch traced here: 183 us
  waiting for transfers between devices  124 us (67%)
  between operations  14 us (8%)
  matrix products  13.2 us (7%)
  local copies, waits for them, and re-layouts  10.3 us (6%)
  blocking collectives  9.64 us (5%)
  starting transfers between devices  9.27 us (5%)
  other arithmetic  2.75 us (1%)
    all_to_all x1, waiting for transfers between devices, body(): lax.all_to_all(outgoing, 'group', split_axis=0, concat_axis=0, tiled=True)  89.4 us
    psum x1, waiting for transfers between devices, body(): base_sum = lax.psum(partial_value, 'tensor')  14.3 us
    all_gather x1, waiting for transfers between devices, body(): lax.all_gather(normed_hidden_states, 'tensor', axis=2, tiled=True)  12.4 us
    all_to_all x1, waiting for transfers between devices, body(): lax.all_to_all(adapted, 'group', split_axis=0, concat_axis=0, tiled=True)  7.39 us
    all_to_all x1, starting transfers between devices, body(): lax.all_to_all(outgoing, 'group', split_axis=0, concat_axis=0, tiled=True)  5.77 us
    all_gather x3, blocking collectives, merged(): lax.all_gather(part.astype(kind), axis)  5.69 us
    dot_general x1, matrix products, body(): jnp.einsum('cah,hj->caj', normed_hidden_states, lax.all_gather(query_matr...  4.43 us
    unnamed x22, local copies, waits for them, and re-layouts  4.07 us
  transfers between devices with their start and end apart: 5, of which 4 were waited for; matrix products, arithmetic and copies ran while one was open for 6% of the time, Pallas kernels for 0%

commit v1 on v0

v1 whole, which is shorter than its diff:
```python
import functools
import math

import jax
import jax.numpy as jnp
from jax import lax
from jax.experimental import pallas as pl
from jax.experimental.pallas import tpu as pltpu
from jax.sharding import PartitionSpec as P

SWAP = [(0, 1), (1, 0)]
FAR = -1e30


def nt_dot(a, b):
    return lax.dot_general(a, b, (((1,), (1,)), ((), ())), preferred_element_type=jnp.float32)


def pair_product_kernel(own_ref, near_ref, first_ref, second_ref, out_ref):
    rows, half = own_ref.shape[0], first_ref.shape[0]
    weights = jnp.concatenate([first_ref[...], second_ref[...]], axis=0)
    out_ref[:rows, :] = nt_dot(own_ref[...], weights)
    out_ref[rows:, :] = nt_dot(near_ref[...], weights)


def pair_product(own, near, first, second):
    return pl.pallas_call(
        pair_product_kernel,
        out_shape=jax.ShapeDtypeStruct((2 * own.shape[0], 2 * first.shape[0]), jnp.float32),
        compiler_params=pltpu.CompilerParams(vmem_limit_bytes=24 << 20),
    )(own, near, first, second)


def last_product_kernel(
    where_ref, own_ref, near_ref, first_ref, second_ref, t0_ref, t1_ref, t2_ref, holder_ref, out_ref, t3_ref
):
    z, x, y = where_ref[0], where_ref[1], where_ref[2]
    pair_product_kernel(own_ref, near_ref, first_ref, second_ref, t3_ref)
    low_pair = z < 2
    places = (z, z + 1 - 2 * lax.rem(z, 2), jnp.where(low_pair, 2, 1), jnp.where(low_pair, 3, 0))
    rows, width = t3_ref.shape
    half = width // 2
    low_lanes = lax.broadcasted_iota(jnp.int32, (rows, width), 1) < half
    holder = holder_ref[...]
    columns = [jnp.zeros((rows, width), jnp.float32) for _ in range(4)]
    shrink = jnp.zeros((rows, width), jnp.float32)
    for j, ref in enumerate((t0_ref, t1_ref, t2_ref, t3_ref)):
        t = ref[...]
        if j > 0:
            t = jnp.where(y == 0, t, pltpu.roll(t, half, 1))
        shrink = shrink + jnp.where(holder == places[j] * 2 + x, t, 0.0)
        columns = [jnp.where(places[j] == k, t, columns[k]) for k in range(4)]
    out_ref[:, :width] = jnp.where(low_lanes, columns[0], pltpu.roll(columns[1], half, 1))
    out_ref[:, width : 2 * width] = jnp.where(low_lanes, columns[2], pltpu.roll(columns[3], half, 1))
    out_ref[:, 2 * width :] = jnp.where(low_lanes, 0.0, shrink)


def last_product(where, own, near, first, second, t0, t1, t2, holder):
    rows, width = t0.shape
    vmem = pl.BlockSpec(memory_space=pltpu.VMEM)
    return pl.pallas_call(
        last_product_kernel,
        out_shape=jax.ShapeDtypeStruct((rows, 3 * width), jnp.float32),
        in_specs=[pl.BlockSpec(memory_space=pltpu.SMEM)] + [vmem] * 8,
        out_specs=vmem,
        scratch_shapes=[pltpu.VMEM((rows, width), jnp.float32)],
        compiler_params=pltpu.CompilerParams(vmem_limit_bytes=24 << 20),
    )(where, own, near, first, second, t0, t1, t2, holder)


def attend_block(queries, keys, values, masks, scaling):
    scores = [jnp.where(m, nt_dot(queries, k) * scaling, FAR) for k, m in zip(keys, masks)]
    highest = scores[0].max(axis=1, keepdims=True)
    for s in scores[1:]:
        highest = jnp.maximum(highest, s.max(axis=1, keepdims=True))
    weights = [jnp.where(m, jnp.exp(s - highest), 0.0) for s, m in zip(scores, masks)]
    totals = sum(w.sum(axis=1, keepdims=True) for w in weights)
    sums = sum(
        jnp.dot(w.astype(jnp.bfloat16), v, preferred_element_type=jnp.float32)
        for w, v in zip(weights, values)
    )
    return sums / totals


def attend(queries, caches, fresh_ref, lengths_ref, out_ref, steps, head, per):
    rows = queries.shape[0]
    requests = rows // steps
    heads = queries.shape[1] // head
    scaling = 1.0 / math.sqrt(head)
    take = per * steps
    for b in range(requests // per):
        part = queries[b * take : (b + 1) * take, :]
        stacked = jnp.concatenate([part[:, h * head : (h + 1) * head] for h in range(heads)], axis=0)
        limit = jnp.concatenate([lengths_ref[b * take : (b + 1) * take, :]] * heads, axis=0)
        keys, values, masks = [], [], []
        for c, cache_ref in enumerate(caches):
            count = cache_ref.shape[0] // requests
            block = cache_ref[b * per * count : (b + 1) * per * count, :]
            shape = (heads * take, per * count)
            request = lax.rem(lax.broadcasted_iota(jnp.int32, shape, 0), take) // steps
            column = lax.broadcasted_iota(jnp.int32, shape, 1)
            position = lax.rem(column, count) + c * count
            masks.append(jnp.logical_and(column // count == request, position < limit))
            keys.append(block[:, :head])
            values.append(block[:, head:])
        block = fresh_ref[b * take : (b + 1) * take, :]
        shape = (heads * take, take)
        row = lax.rem(lax.broadcasted_iota(jnp.int32, shape, 0), take)
        column = lax.broadcasted_iota(jnp.int32, shape, 1)
        masks.append(jnp.logical_and(row // steps == column // steps, column <= row))
        keys.append(block[:, :head])
        values.append(block[:, head:])
        mixed = attend_block(stacked, keys, values, masks, scaling).astype(jnp.bfloat16)
        for h in range(heads):
            out_ref[b * take : (b + 1) * take, h * head : (h + 1) * head] = mixed[
                h * take : (h + 1) * take, :
            ]


def finish_kernel(
    steps, per, where_ref, mine_ref, other_ref, got_ref, holder_ref, up_ref,
    low_ref, high_ref, fresh_ref, lengths_ref, queries_ref, out_ref,
):
    x = where_ref[1]
    rows = got_ref.shape[0]
    width = got_ref.shape[1] // 3
    half = width // 2
    here = mine_ref[...] + other_ref[...]
    there = got_ref[...]
    even = jnp.where(x == 0, here, there)
    odd = jnp.where(x == 0, there, here)
    low_lanes = lax.broadcasted_iota(jnp.int32, (rows, width), 1) < half
    groups = []
    for k in range(4):
        g = (k // 2) * width
        left, right = even[:, g : g + width], odd[:, g : g + width]
        if k % 2 == 0:
            groups.append(jnp.where(low_lanes, left, pltpu.roll(right, half, 1)))
        else:
            groups.append(jnp.where(low_lanes, pltpu.roll(left, half, 1), right))
    base = jnp.concatenate(groups, axis=1)
    shrink = here[:, 2 * width :] + there[:, 2 * width :]
    shrink = jnp.where(low_lanes, pltpu.roll(shrink, half, 1), shrink)
    holder = holder_ref[...]
    owners = up_ref.shape[0] // half
    lane_owner = (lax.broadcasted_iota(jnp.int32, (rows, width), 1) >= half).astype(jnp.int32)
    spread = jnp.concatenate(
        [jnp.where(holder == lane_owner + 2 * k, shrink, 0.0) for k in range(owners // 2)], axis=1
    ).astype(jnp.bfloat16)
    adapted = jnp.dot(spread, up_ref[...], preferred_element_type=jnp.float32)
    queries = (base + adapted).astype(jnp.bfloat16)
    queries_ref[...] = queries
    head = fresh_ref.shape[1] // 2
    attend(queries, (low_ref, high_ref), fresh_ref, lengths_ref, out_ref, steps, head, per)


def finish(steps, where, mine, other, got, holder, up, low, high, fresh, lengths):
    rows = got.shape[0]
    vmem = pl.BlockSpec(memory_space=pltpu.VMEM)
    shape = jax.ShapeDtypeStruct((rows, up.shape[1]), jnp.bfloat16)
    return pl.pallas_call(
        functools.partial(finish_kernel, steps, 8),
        out_shape=(shape, shape),
        in_specs=[pl.BlockSpec(memory_space=pltpu.SMEM)] + [vmem] * 9,
        out_specs=(vmem, vmem),
        compiler_params=pltpu.CompilerParams(vmem_limit_bytes=24 << 20),
    )(where, mine, other, got, holder, up, low, high, fresh, lengths)


def attend_kernel(steps, per, q_ref, low_ref, high_ref, fresh_ref, lengths_ref, out_ref):
    head = fresh_ref.shape[1] // 2
    attend(q_ref[...], (low_ref, high_ref), fresh_ref, lengths_ref, out_ref, steps, head, per)


def line_pairs(groups, moves):
    return [(a * 2 + x, b * 2 + x) for a, b in moves for x in range(2)]


def holders_of(request_adapter, adapter_owner):
    ids = jnp.arange(adapter_owner.shape[0], dtype=jnp.int32)
    lookup = request_adapter[:, None] == ids[None, :]
    return jnp.sum(jnp.where(lookup, adapter_owner[None, :], 0), axis=1)


def body(
    normed_hidden_states,
    query_matrix,
    factor_down,
    factor_up,
    kv_cache,
    incoming_key_value,
    kv_lengths,
    request_adapter,
    adapter_owner,
):
    groups = lax.axis_size("group")
    core = lax.axis_index("tensor")
    requests, steps, features = normed_hidden_states.shape
    rows = requests * steps
    holder = holders_of(request_adapter, adapter_owner)
    holder_rows = jnp.repeat(holder, steps)[:, None]
    lengths_rows = jnp.repeat(kv_lengths, steps)[:, None]

    down = factor_down[0].T
    kept = lax.dynamic_slice_in_dim(down, core * features, features, 1)
    given = lax.dynamic_slice_in_dim(down, (1 - core) * features, features, 1)
    taken = lax.ppermute(given, "tensor", SWAP)
    down_block = jnp.where(
        core == 0, jnp.concatenate([kept, taken], 0), jnp.concatenate([taken, kept], 0)
    )
    query_block = query_matrix.T

    other_cache = lax.ppermute(kv_cache, "tensor", SWAP)
    low = jnp.where(core == 0, kv_cache, other_cache).reshape(-1, kv_cache.shape[2])
    high = jnp.where(core == 0, other_cache, kv_cache).reshape(-1, kv_cache.shape[2])
    fresh = incoming_key_value.reshape(rows, -1)

    up = lax.all_gather(factor_up[0], "group", axis=0, tiled=True)
    up_other = lax.ppermute(up, "tensor", SWAP)
    up_full = jnp.where(
        core == 0, jnp.concatenate([up, up_other], 1), jnp.concatenate([up_other, up], 1)
    )
    own = normed_hidden_states.reshape(rows, features)
    width = query_matrix.shape[1] * groups
    out_shape = (requests, steps, width)

    if groups == 8 and lax.axis_size("parts") == 2 and query_block.shape == down_block.shape:
        place = lax.axis_index("group")
        z, x, y = place // 2, lax.rem(place, 2), lax.axis_index("parts")
        where = jnp.stack([z, x, y]).astype(jnp.int32)
        middle = jnp.logical_or(z == 1, z == 2)
        along = lambda a, moves: lax.ppermute(a, "group", line_pairs(groups, moves))
        ends, inner = ((0, 1), (1, 0), (2, 3), (3, 2)), ((1, 2), (2, 1))
        outward = ((1, 0), (2, 3))
        beside = [(i, i ^ 1) for i in range(groups)]
        mine = jnp.where(y == 0, query_block, down_block)
        near = lax.ppermute(normed_hidden_states, "group", beside).reshape(rows, features)
        near_holder = lax.ppermute(holder_rows, "group", beside)
        both_holders = jnp.concatenate([holder_rows, near_holder], axis=0)
        e1 = along(mine, ends)
        m1 = along(mine, inner)
        m2 = along(e1, inner)
        p1 = along(m1, outward)
        p2 = along(m2, outward)
        r1, r2, r3 = e1, jnp.where(middle, m1, p1), jnp.where(middle, m2, p2)
        s1, s2, s3 = (lax.ppermute(r, "parts", SWAP) for r in (r1, r2, r3))
        t0 = pair_product(own, near, query_block, down_block)
        t1 = pair_product(own, near, r1, s1)
        t2 = pair_product(own, near, r2, s2)
        total = last_product(where, own, near, r3, s3, t0, t1, t2, both_holders)
        total_other = lax.ppermute(total, "tensor", SWAP)
        got = lax.ppermute(total[rows:] + total_other[rows:], "group", beside)
        queries, attended = finish(
            steps, where, total[:rows], total_other[:rows], got,
            holder_rows, up_full, low, high, fresh, lengths_rows,
        )
        return queries.reshape(out_shape), attended.reshape(out_shape)

    place = lax.axis_index("group")
    ring = [(i, (i + 1) % groups) for i in range(groups)]

    def step(k, carry):
        q_part, d_part, base, shrink = carry
        at = lax.rem(place - k + groups, groups)
        base = lax.dynamic_update_slice_in_dim(base, nt_dot(own, q_part), at * q_part.shape[0], 1)
        shrink = shrink + jnp.where(holder_rows == at, nt_dot(own, d_part), 0.0)
        q_part, d_part = (lax.ppermute(w, "group", ring) for w in (q_part, d_part))
        return q_part, d_part, base, shrink

    start = (
        query_block,
        down_block,
        jnp.zeros((rows, width), jnp.float32),
        jnp.zeros((rows, down_block.shape[0]), jnp.float32),
    )
    _, _, base, shrink = lax.fori_loop(0, groups, step, start)
    base = base + lax.ppermute(base, "tensor", SWAP)
    shrink = (shrink + lax.ppermute(shrink, "tensor", SWAP)).astype(jnp.bfloat16)
    named = holder_rows == jnp.arange(groups, dtype=jnp.int32)[None, :]
    spread = jnp.where(named[:, :, None], shrink[:, None, :], 0).reshape(rows, -1)
    adapted = jnp.dot(spread, up_full, preferred_element_type=jnp.float32)
    queries = (base + adapted).astype(jnp.bfloat16)
    attended = pl.pallas_call(
        functools.partial(attend_kernel, steps, 8),
        out_shape=jax.ShapeDtypeStruct(queries.shape, jnp.bfloat16),
        compiler_params=pltpu.CompilerParams(vmem_limit_bytes=24 << 20),
    )(queries, low, high, fresh, lengths_rows)
    return queries.reshape(out_shape), attended.reshape(out_shape)


def solution(mesh):
    placed = (
        P(("parts", "group"), None, "tensor"),
        P("tensor", "group"),
        P("group", None, "tensor"),
        P("group", None, "tensor"),
        P(("parts", "group"), "tensor", None),
        P(("parts", "group"), None, None),
        P(("parts", "group")),
        P(("parts", "group")),
        P("parts"),
    )
    return jax.shard_map(
        body,
        mesh=mesh,
        in_specs=placed,
        out_specs=(P(("parts", "group"), None, None), P(("parts", "group"), None, None)),
        check_vma=False,
    )
```

time: 184 us -> 109 us (0.59)
  waiting for transfers between devices: 124 us -> 40.7 us
  blocking collectives: 9.64 us -> 30.9 us
  matrix products: 13.2 us -> 0 us
  between operations: 14 us -> 0.89 us
  Pallas kernels: 0 us -> 9.41 us
  starting transfers between devices: 9.27 us -> 16.4 us
  local copies, waits for them, and re-layouts: 10.3 us -> 7.91 us
    all_to_all x2 -> x0, waiting for transfers between devices: 96.8 us -> none  [the longest x1 89.4 us: body(): lax.all_to_all(outgoing, 'group', split_axis=0, concat_axis=0, tiled=True)]
    ppermute x0 -> x15, waiting for transfers between devices: none -> 40.7 us  [the longest x5 32.3 us: body(): along = lambda a, moves: lax.ppermute(a, 'group', line_pairs(groups, moves))]
    all_gather x5 -> x1, blocking collectives: 9.64 us -> 30.9 us  [body(): up = lax.all_gather(factor_up[0], 'group', axis=0, tiled=True)]
    ppermute x0 -> x15, starting transfers between devices: none -> 16.4 us  [the longest x5 6.88 us: body(): along = lambda a, moves: lax.ppermute(a, 'group', line_pairs(groups, moves))]
    psum x1 -> x0, waiting for transfers between devices: 14.3 us -> none  [body(): base_sum = lax.psum(partial_value, 'tensor')]
    dot_general x8 -> x0, matrix products: 13.2 us -> none  [the longest x1 4.43 us: body(): jnp.einsum('cah,hj->caj', normed_hidden_states, lax.all_gather(query_matr...]
    all_gather x2 -> x0, waiting for transfers between devices: 12.4 us -> none  [the longest x1 12.4 us: body(): lax.all_gather(normed_hidden_states, 'tensor', axis=2, tiled=True)]
    pallas_call x0 -> x5, Pallas kernels: none -> 9.41 us  [the longest x3 4.35 us: pair_product(): pl.pallas_call(pair_product_kernel, out_shape=jax.ShapeDtypeStruct((2 * o...]
  transfers between devices with their start and end apart: 5 -> 15, of which waited for: 4 -> 8; matrix products, arithmetic and copies ran while one was open for 6% -> 4% of each run, Pallas kernels for 0% -> 4%
where the time goes in v1:
time: 109 us
  waiting for transfers between devices  40.7 us (37%)
  blocking collectives  30.9 us (28%)
  starting transfers between devices  16.4 us (15%)
  Pallas kernels  9.41 us (9%)
  local copies, waits for them, and re-layouts  7.91 us (7%)
  other arithmetic  2.55 us (2%)
    ppermute x5, waiting for transfers between devices, body(): along = lambda a, moves: lax.ppermute(a, 'group', line_pairs(groups, moves))  32.3 us
    all_gather x1, blocking collectives, body(): up = lax.all_gather(factor_up[0], 'group', axis=0, tiled=True)  30.9 us
    ppermute x5, starting transfers between devices, body(): along = lambda a, moves: lax.ppermute(a, 'group', line_pairs(groups, moves))  6.88 us
    ppermute x1, waiting for transfers between devices, body(): got = lax.ppermute(total[rows:] + total_other[rows:], 'group', beside)  5.32 us
    ppermute x3, starting transfers between devices, body(): s1, s2, s3 = (lax.ppermute(r, 'parts', SWAP) for r in (r1, r2, r3))  4.69 us
    pallas_call x3, Pallas kernels, pair_product(): pl.pallas_call(pair_product_kernel, out_shape=jax.ShapeDtypeStruct((2 * o...  4.35 us
    pallas_call x1, Pallas kernels, finish(): pl.pallas_call(functools.partial(finish_kernel, steps, 8), out_shape=(sha...  3.11 us
    unnamed x18, local copies, waits for them, and re-layouts  2.83 us
  transfers between devices with their start and end apart: 15, of which 8 were waited for; matrix products, arithmetic and copies ran while one was open for 4% of the time, Pallas kernels for 4%

profile of v1, /device:TPU:0, one launch (start us, length us, event | category | flops | bytes accessed | tf_op | source)
XLA Modules:
  0.0 108.7 jit_solution(8567925487271944119)
XLA Ops:
  0.6 1.1 %dynamic-slice_bitcast_fusion = (bf16[32,4096]{1,0:T(8,128)(2,1)S(1)}, bf16[32,4096]{1,0:T(8,128)(2,1)S(1)}) fusion(bf16[1,8192,32]{1,2,0:T(8,128)(2,1)} %param.11, s32[]{:T(128)S(6)} %select_n.64, s32[]{:T(128)S(6)} %select_n.63), kind=kLoop, calls=%fused_computation.7 | loop fusion | bytes 1048584 | tf_op jit(solution)/shard_map/dynamic_slice | solution.py:206
  1.8 0.5 collective-permute-start.1
  2.3 1.2 %collective-permute-done.1 = bf16[32,4096]{1,0:T(8,128)(2,1)S(1)} collective-permute-done((bf16[32,4096]{1,0:T(8,128)(2,1)S(1)}, bf16[32,4096]{1,0:T(8,128)(2,1)S(1)}, u32[]{:S(2)}, u32[]{:S(2)}) %collective-permute-start.1) | collective-permute-done | bytes 262176 | tf_op jit(solution)/shard_map/ppermute | solution.py:207
  3.5 1.0 broadcast_select_fusion.2
  4.5 2.9 %collective-permute-start.2 = (bf16[64,4096]{1,0:T(8,128)(2,1)S(1)}, bf16[64,4096]{1,0:T(8,128)(2,1)}, u32[]{:S(2)}, u32[]{:S(2)}) collective-permute-start(bf16[64,4096]{1,0:T(8,128)(2,1)S(1)} %get-tuple-element.6), channel_id=1, source_target_pairs={{0,4},{2,6},{4,0},{6,2},{8,12},{10,14},{12,8},{14,10},{1,5},{3,7},... | collective-permute-start | bytes 1572872 | tf_op jit(solution)/shard_map/ppermute | solution.py:232
  7.4 0.7 collective-permute-start.7
  8.1 11.6 %collective-permute-done.2.first_ref = bf16[64,4096]{1,0:T(8,128)(2,1)} collective-permute-done((bf16[64,4096]{1,0:T(8,128)(2,1)S(1)}, bf16[64,4096]{1,0:T(8,128)(2,1)}, u32[]{:S(2)}, u32[]{:S(2)}) %collective-permute-start.2) | collective-permute-done | bytes 524320 | tf_op jit(solution)/shard_map/ppermute | solution.py:232
  19.7 0.7 collective-permute-start.3
  20.4 1.3 %collective-permute-start.8 = (bf16[64,4096]{1,0:T(8,128)(2,1)S(1)}, bf16[64,4096]{1,0:T(8,128)(2,1)S(1)}, u32[]{:S(2)}, u32[]{:S(2)}) collective-permute-start(bf16[64,4096]{1,0:T(8,128)(2,1)S(1)} %collective-permute-done.7), channel_id=1, source_target_pairs={{4,0},{6,2},{8,12},{10,14},{5,1},{7,3},{9,13},{11,15},{20,16},{22,... | collective-permute-start | bytes 1572872 | tf_op jit(solution)/shard_map/ppermute | solution.py:232
  21.7 1.7 %collective-permute-start = (bf16[64,2,4096]{2,1,0:T(2,128)(2,1)S(1)}, bf16[64,2,4096]{2,1,0:T(2,128)(2,1)}, u32[]{:S(2)}, u32[]{:S(2)}) collective-permute-start(bf16[64,2,4096]{2,1,0:T(2,128)(2,1)S(1)} %copy-done.3), channel_id=1, source_target_pairs={{0,2},{2,0},{4,6},{6,4},{8,10},{10,8},{12,14},{14,12},{1,3},{3,1},... | collective-permute-start | bytes 3145736 | tf_op jit(solution)/shard_map/ppermute | solution.py:237
  23.5 1.5 %collective-permute-start.6 = (bf16[64,4096]{1,0:T(8,128)(2,1)}, bf16[64,4096]{1,0:T(8,128)(2,1)}, u32[]{:S(2)}, u32[]{:S(2)}) collective-permute-start(bf16[64,4096]{1,0:T(8,128)(2,1)} %collective-permute-done.2.first_ref), channel_id=1, source_target_pairs={{0,16},{16,0},{1,17},{17,1},{2,18},{18,2},{3,19},{19,3},{4,20},{20... | collective-permute-start | bytes 1572872 | tf_op jit(solution)/shard_map/ppermute | solution.py:246
  25.0 1.3 %collective-permute-start.4 = (bf16[64,4096]{1,0:T(8,128)(2,1)S(1)}, bf16[64,4096]{1,0:T(8,128)(2,1)S(1)}, u32[]{:S(2)}, u32[]{:S(2)}) collective-permute-start(bf16[64,4096]{1,0:T(8,128)(2,1)S(1)} %collective-permute-done.3), channel_id=1, source_target_pairs={{4,0},{6,2},{8,12},{10,14},{5,1},{7,3},{9,13},{11,15},{20,16},{22,... | collective-permute-start | bytes 1572872 | tf_op jit(solution)/shard_map/ppermute | solution.py:232
  26.3 11.1 %collective-permute-done.8 = bf16[64,4096]{1,0:T(8,128)(2,1)S(1)} collective-permute-done((bf16[64,4096]{1,0:T(8,128)(2,1)S(1)}, bf16[64,4096]{1,0:T(8,128)(2,1)S(1)}, u32[]{:S(2)}, u32[]{:S(2)}) %collective-permute-start.8) | collective-permute-done | bytes 524320 | tf_op jit(solution)/shard_map/ppermute | solution.py:232
  37.4 0.1 broadcast_select_fusion.3.first_ref
  37.4 1.6 %collective-permute-start.9 = (bf16[64,4096]{1,0:T(8,128)(2,1)S(1)}, bf16[64,4096]{1,0:T(8,128)(2,1)}, u32[]{:S(2)}, u32[]{:S(2)}) collective-permute-start(bf16[64,4096]{1,0:T(8,128)(2,1)S(1)} %broadcast_select_fusion.3.first_ref), channel_id=1, source_target_pairs={{0,16},{16,0},{1,17},{17,1},{2,18},{18,2},{3,19},{19,3},{4,20},{20... | collective-permute-start | bytes 1572872 | tf_op jit(solution)/shard_map/ppermute | solution.py:246
  39.0 9.6 %collective-permute-done.4 = bf16[64,4096]{1,0:T(8,128)(2,1)S(1)} collective-permute-done((bf16[64,4096]{1,0:T(8,128)(2,1)S(1)}, bf16[64,4096]{1,0:T(8,128)(2,1)S(1)}, u32[]{:S(2)}, u32[]{:S(2)}) %collective-permute-start.4) | collective-permute-done | bytes 524320 | tf_op jit(solution)/shard_map/ppermute | solution.py:232
  48.6 1.6 %collective-permute-start.5 = (bf16[64,4096]{1,0:T(8,128)(2,1)S(1)}, bf16[64,4096]{1,0:T(8,128)(2,1)}, u32[]{:S(2)}, u32[]{:S(2)}) collective-permute-start(bf16[64,4096]{1,0:T(8,128)(2,1)S(1)} %broadcast_select_fusion.4.first_ref), channel_id=1, source_target_pairs={{0,16},{16,0},{1,17},{17,1},{2,18},{18,2},{3,19},{19,3},{4,20},{20... | collective-permute-start | bytes 1572872 | tf_op jit(solution)/shard_map/ppermute | solution.py:246
  50.2 0.1 select_reduce_fusion
  50.3 0.1 broadcast_in_dim.23
  50.4 0.1 broadcast_in_dim_reshape.6
  50.5 1.6 %collective-permute-start.10 = (s32[128,1]{0,1:T(1,128)S(1)}, s32[128,1]{0,1:T(1,128)S(1)}, u32[]{:S(2)}, u32[]{:S(2)}) collective-permute-start(s32[128,1]{0,1:T(1,128)S(1)} %broadcast_in_dim_reshape.6), channel_id=1, source_target_pairs={{0,2},{2,0},{4,6},{6,4},{8,10},{10,8},{12,14},{14,12},{1,3},{3,1},... | collective-permute-start | bytes 1544 | tf_op jit(solution)/shard_map/ppermute | solution.py:238
  52.1 0.1 pad_add_fusion.1.where_ref
  52.2 0.4 reshape.33.own_ref
  52.6 1.5 %collective-permute-done.10 = s32[128,1]{0,1:T(1,128)S(1)} collective-permute-done((s32[128,1]{0,1:T(1,128)S(1)}, s32[128,1]{0,1:T(1,128)S(1)}, u32[]{:S(2)}, u32[]{:S(2)}) %collective-permute-start.10) | collective-permute-done | bytes 544 | tf_op jit(solution)/shard_map/ppermute | solution.py:238
  54.2 0.1 copy.22.holder_ref
  54.3 1.5 %reshape.34.near_ref = bf16[128,4096]{1,0:T(8,128)(2,1)S(1)} reshape(bf16[64,2,4096]{2,1,0:T(2,128)(2,1)} %collective-permute-done) | data formatting | bytes 2097152 | tf_op jit(solution)/shard_map/reshape | solution.py:237
  55.8 1.0 copy-done.1
  56.8 1.0 copy-done.2
  57.9 0.7 shard_map.104.t0_ref
  58.6 1.9 %shard_map.105.t1_ref = f32[256,128]{1,0:T(8,128)S(1)} custom-call(bf16[128,4096]{1,0:T(8,128)(2,1)S(1)} %reshape.33.own_ref, bf16[128,4096]{1,0:T(8,128)(2,1)S(1)} %reshape.34.near_ref, bf16[64,4096]{1,0:T(8,128)(2,1)} %collective-permute-done.2.first_ref, bf16[64,4096]{1,0:T(8,128)(2,1)} %collective-permute-done.6.second_ref), custom_call_target="tpu_custom_call" | custom-call | tf_op jit(solution)/shard_map/pallas_call | solution.py:27
  60.5 1.7 %shard_map.106.t2_ref = f32[256,128]{1,0:T(8,128)S(1)} custom-call(bf16[128,4096]{1,0:T(8,128)(2,1)S(1)} %reshape.33.own_ref, bf16[128,4096]{1,0:T(8,128)(2,1)S(1)} %reshape.34.near_ref, bf16[64,4096]{1,0:T(8,128)(2,1)S(1)} %broadcast_select_fusion.3.first_ref, bf16[64,4096]{1,0:T(8,128)(2,1)} %collective-permute-done.9.second_ref), custom_call_target="tpu_custom_call" | custom-call | tf_op jit(solution)/shard_map/pallas_call | solution.py:27
  62.3 1.9 %shard_map.107 = f32[256,384]{1,0:T(8,128)S(1)} custom-call(s32[3]{0:T(128)S(1)} %pad_add_fusion.1.where_ref, bf16[128,4096]{1,0:T(8,128)(2,1)S(1)} %reshape.33.own_ref, bf16[128,4096]{1,0:T(8,128)(2,1)S(1)} %reshape.34.near_ref, bf16[64,4096]{1,0:T(8,128)(2,1)S(1)} %broadcast_select_fusion.4.first_ref, bf16[64,4096]{1,0:T(8,128)(2,1)} %collective-permute-done.5.second_ref, ...), custom_call_target="tpu_custom_call" | custom-call | tf_op jit(solution)/shard_map/pallas_call | solution.py:61
  64.2 0.1 collective-permute-start.11
  64.3 30.9 %all-gather = bf16[1,512,256]{2,1,0:T(8,128)(2,1)S(1)} all-gather(bf16[1,64,256]{2,1,0:T(8,128)(2,1)S(1)} %copy-done.5), channel_id=2, replica_groups=mesh['parts'=2,'group'=8,'tensor'=2] {'group'}, dimensions={1}, use_global_device_ids=true | all-gather | bytes 294912 | tf_op jit(solution)/shard_map/all_gather | solution.py:218
  95.2 0.5 collective-permute-start.14
  95.7 0.1 copy.23.holder_ref
  95.8 0.1 broadcast_in_dim.24
  95.9 0.1 broadcast_in_dim_reshape.8.lengths_ref
  96.0 0.7 copy-done.4
  96.7 0.2 collective-permute-done.13
  96.9 0.1 maximum_select_fusion.1.up_ref
  97.1 0.5 collective-permute-start.12
  97.6 0.1 collective-permute-done.14
  97.7 1.1 %broadcast_select_fusion = (bf16[64,16,256]{2,1,0:T(8,128)(2,1)S(1)}, bf16[64,16,256]{2,1,0:T(8,128)(2,1)S(1)}) fusion(bf16[64,16,256]{2,1,0:T(8,128)(2,1)S(1)} %collective-permute-done.14, bf16[64,16,256]{2,1,0:T(8,128)(2,1)} %param.13, pred[]{:T(512)S(6)} %eq.31), kind=kLoop, calls=%fused_computation.2 | loop fusion | flops 524288 | bytes 2097153 | tf_op jit(solution)/shard_map/jit(_where)/select_n | solution.py:215
  98.8 5.3 %collective-permute-done.12.got_ref = f32[128,384]{1,0:T(8,128)S(1)} collective-permute-done((f32[128,384]{1,0:T(8,128)S(1)}, f32[128,384]{1,0:T(8,128)S(1)}, u32[]{:S(2)}, u32[]{:S(2)}) %collective-permute-start.12) | collective-permute-done | bytes 196640 | tf_op jit(solution)/shard_map/ppermute | solution.py:252
  104.1 3.1 %shard_map.108 = (bf16[128,512]{1,0:T(8,128)(2,1)S(1)}, bf16[128,512]{1,0:T(8,128)(2,1)S(1)}) custom-call(s32[3]{0:T(128)S(1)} %pad_add_fusion.1.where_ref, f32[128,384]{1,0:T(8,128)S(1)} %get-tuple-element.13.mine_ref, f32[128,384]{1,0:T(8,128)S(1)} %get-tuple-element.14.other_ref, f32[128,384]{1,0:T(8,128)S(1)} %collective-permute-done.12.got_ref, ...), custom_call_target="tpu_custom_call" | custom-call | tf_op jit(solution)/shard_map/pallas_call | solution.py:161
  107.2 0.7 reshape.40
  107.9 0.7 reshape.41
  (27 shorter events, 0.2 us)
Async XLA Ops:
  0.6 2.8 %copy-start = (bf16[4096,64]{0,1:T(8,128)(2,1)S(1)}, bf16[4096,64]{0,1:T(8,128)(2,1)}, u32[]{:S(2)}) copy-start(bf16[4096,64]{0,1:T(8,128)(2,1)} %param.10) | copy-start | bytes 1572868
  1.8 1.7 %collective-permute-start.1 = (bf16[32,4096]{1,0:T(8,128)(2,1)S(1)}, bf16[32,4096]{1,0:T(8,128)(2,1)S(1)}, u32[]{:S(2)}, u32[]{:S(2)}) collective-permute-start(bf16[32,4096]{1,0:T(8,128)(2,1)S(1)} %get-tuple-element.10), channel_id=1, source_target_pairs={{0,1},{1,0},{2,3},{3,2},{4,5},{5,4},{6,7},{7,6},{8,9},{9,8},{10,11... | collective-permute-start | bytes 786440 | tf_op jit(solution)/shard_map/ppermute | solution.py:207
  3.5 18.3 %copy-start.3 = (bf16[64,2,4096]{2,1,0:T(2,128)(2,1)S(1)}, bf16[64,2,4096]{2,1,0:T(2,128)(2,1)}, u32[]{:S(2)}) copy-start(bf16[64,2,4096]{2,1,0:T(2,128)(2,1)} %param.9) | copy-start | bytes 3145732
  4.5 15.3 %collective-permute-start.2 = (bf16[64,4096]{1,0:T(8,128)(2,1)S(1)}, bf16[64,4096]{1,0:T(8,128)(2,1)}, u32[]{:S(2)}, u32[]{:S(2)}) collective-permute-start(bf16[64,4096]{1,0:T(8,128)(2,1)S(1)} %get-tuple-element.6), channel_id=1, source_target_pairs={{0,4},{2,6},{4,0},{6,2},{8,12},{10,14},{12,8},{14,10},{1,5},{3,7},... | collective-permute-start | bytes 1572872 | tf_op jit(solution)/shard_map/ppermute | solution.py:232
  7.4 13.0 %collective-permute-start.7 = (bf16[64,4096]{1,0:T(8,128)(2,1)S(1)}, bf16[64,4096]{1,0:T(8,128)(2,1)S(1)}, u32[]{:S(2)}, u32[]{:S(2)}) collective-permute-start(bf16[64,4096]{1,0:T(8,128)(2,1)S(1)} %get-tuple-element.6), channel_id=1, source_target_pairs={{4,8},{6,10},{8,4},{10,6},{5,9},{7,11},{9,5},{11,7},{20,24},{22,26... | collective-permute-start | bytes 1572872 | tf_op jit(solution)/shard_map/ppermute | solution.py:232
  19.7 5.3 %collective-permute-start.3 = (bf16[64,4096]{1,0:T(8,128)(2,1)}, bf16[64,4096]{1,0:T(8,128)(2,1)S(1)}, u32[]{:S(2)}, u32[]{:S(2)}) collective-permute-start(bf16[64,4096]{1,0:T(8,128)(2,1)} %collective-permute-done.2.first_ref), channel_id=1, source_target_pairs={{4,8},{6,10},{8,4},{10,6},{5,9},{7,11},{9,5},{11,7},{20,24},{22,26... | collective-permute-start | bytes 1572872 | tf_op jit(solution)/shard_map/ppermute | solution.py:232
  20.4 16.9 %collective-permute-start.8 = (bf16[64,4096]{1,0:T(8,128)(2,1)S(1)}, bf16[64,4096]{1,0:T(8,128)(2,1)S(1)}, u32[]{:S(2)}, u32[]{:S(2)}) collective-permute-start(bf16[64,4096]{1,0:T(8,128)(2,1)S(1)} %collective-permute-done.7), channel_id=1, source_target_pairs={{4,0},{6,2},{8,12},{10,14},{5,1},{7,3},{9,13},{11,15},{20,16},{22,... | collective-permute-start | bytes 1572872 | tf_op jit(solution)/shard_map/ppermute | solution.py:232
  21.7 32.6 %collective-permute-start = (bf16[64,2,4096]{2,1,0:T(2,128)(2,1)S(1)}, bf16[64,2,4096]{2,1,0:T(2,128)(2,1)}, u32[]{:S(2)}, u32[]{:S(2)}) collective-permute-start(bf16[64,2,4096]{2,1,0:T(2,128)(2,1)S(1)} %copy-done.3), channel_id=1, source_target_pairs={{0,2},{2,0},{4,6},{6,4},{8,10},{10,8},{12,14},{14,12},{1,3},{3,1},... | collective-permute-start | bytes 3145736 | tf_op jit(solution)/shard_map/ppermute | solution.py:237
  23.5 35.1 %collective-permute-start.6 = (bf16[64,4096]{1,0:T(8,128)(2,1)}, bf16[64,4096]{1,0:T(8,128)(2,1)}, u32[]{:S(2)}, u32[]{:S(2)}) collective-permute-start(bf16[64,4096]{1,0:T(8,128)(2,1)} %collective-permute-done.2.first_ref), channel_id=1, source_target_pairs={{0,16},{16,0},{1,17},{17,1},{2,18},{18,2},{3,19},{19,3},{4,20},{20... | collective-permute-start | bytes 1572872 | tf_op jit(solution)/shard_map/ppermute | solution.py:246
  25.0 23.6 %collective-permute-start.4 = (bf16[64,4096]{1,0:T(8,128)(2,1)S(1)}, bf16[64,4096]{1,0:T(8,128)(2,1)S(1)}, u32[]{:S(2)}, u32[]{:S(2)}) collective-permute-start(bf16[64,4096]{1,0:T(8,128)(2,1)S(1)} %collective-permute-done.3), channel_id=1, source_target_pairs={{4,0},{6,2},{8,12},{10,14},{5,1},{7,3},{9,13},{11,15},{20,16},{22,... | collective-permute-start | bytes 1572872 | tf_op jit(solution)/shard_map/ppermute | solution.py:232
  37.4 12.8 %copy-start.7 = (s32[8]{0:T(128)S(1)}, s32[8]{0:T(128)}, u32[]{:S(2)}) copy-start(s32[8]{0:T(128)} %param.17) | copy-start | bytes 100
  37.4 12.8 %copy-start.8 = (s32[64]{0:T(128)S(1)}, s32[64]{0:T(128)}, u32[]{:S(2)}) copy-start(s32[64]{0:T(128)} %param.16) | copy-start | bytes 772
  37.4 23.1 %collective-permute-start.9 = (bf16[64,4096]{1,0:T(8,128)(2,1)S(1)}, bf16[64,4096]{1,0:T(8,128)(2,1)}, u32[]{:S(2)}, u32[]{:S(2)}) collective-permute-start(bf16[64,4096]{1,0:T(8,128)(2,1)S(1)} %broadcast_select_fusion.3.first_ref), channel_id=1, source_target_pairs={{0,16},{16,0},{1,17},{17,1},{2,18},{18,2},{3,19},{19,3},{4,20},{20... | collective-permute-start | bytes 1572872 | tf_op jit(solution)/shard_map/ppermute | solution.py:246
  48.6 13.6 %collective-permute-start.5 = (bf16[64,4096]{1,0:T(8,128)(2,1)S(1)}, bf16[64,4096]{1,0:T(8,128)(2,1)}, u32[]{:S(2)}, u32[]{:S(2)}) collective-permute-start(bf16[64,4096]{1,0:T(8,128)(2,1)S(1)} %broadcast_select_fusion.4.first_ref), channel_id=1, source_target_pairs={{0,16},{16,0},{1,17},{17,1},{2,18},{18,2},{3,19},{19,3},{4,20},{20... | collective-permute-start | bytes 1572872 | tf_op jit(solution)/shard_map/ppermute | solution.py:246
  50.5 3.6 %collective-permute-start.10 = (s32[128,1]{0,1:T(1,128)S(1)}, s32[128,1]{0,1:T(1,128)S(1)}, u32[]{:S(2)}, u32[]{:S(2)}) collective-permute-start(s32[128,1]{0,1:T(1,128)S(1)} %broadcast_in_dim_reshape.6), channel_id=1, source_target_pairs={{0,2},{2,0},{4,6},{6,4},{8,10},{10,8},{12,14},{14,12},{1,3},{3,1},... | collective-permute-start | bytes 1544 | tf_op jit(solution)/shard_map/ppermute | solution.py:238
  55.8 1.0 copy-start.1
  56.8 1.0 copy-start.2
  62.3 2.1 %copy-start.5 = (bf16[1,64,256]{2,1,0:T(8,128)(2,1)S(1)}, bf16[1,64,256]{2,1,0:T(8,128)(2,1)}, u32[]{:S(2)}) copy-start(bf16[1,64,256]{2,1,0:T(8,128)(2,1)} %param.12) | copy-start | bytes 98308
  64.2 32.8 %collective-permute-start.11 = (f32[256,384]{1,0:T(8,128)S(1)}, f32[256,384]{1,0:T(8,128)S(1)}, u32[]{:S(2)}, u32[]{:S(2)}) collective-permute-start(f32[256,384]{1,0:T(8,128)S(1)} %shard_map.107), channel_id=1, source_target_pairs={{0,1},{1,0},{2,3},{3,2},{4,5},{5,4},{6,7},{7,6},{8,9},{9,8},{10,11... | collective-permute-start | bytes 1179656 | tf_op jit(solution)/shard_map/ppermute | solution.py:251
  95.2 0.7 copy-start.6
  95.2 1.7 %collective-permute-start.13 = (bf16[512,256]{1,0:T(8,128)(2,1)S(1)}, bf16[512,256]{1,0:T(8,128)(2,1)S(1)}, u32[]{:S(2)}, u32[]{:S(2)}) collective-permute-start(bf16[512,256]{1,0:T(8,128)(2,1)S(1)} %bitcast.19), channel_id=1, source_target_pairs={{0,1},{1,0},{2,3},{3,2},{4,5},{5,4},{6,7},{7,6},{8,9},{9,8},{10,11... | collective-permute-start | bytes 786440 | tf_op jit(solution)/shard_map/ppermute | solution.py:219
  95.2 2.5 %collective-permute-start.14 = (bf16[64,16,256]{2,1,0:T(8,128)(2,1)}, bf16[64,16,256]{2,1,0:T(8,128)(2,1)S(1)}, u32[]{:S(2)}, u32[]{:S(2)}) collective-permute-start(bf16[64,16,256]{2,1,0:T(8,128)(2,1)} %param.13), channel_id=1, source_target_pairs={{0,1},{1,0},{2,3},{3,2},{4,5},{5,4},{6,7},{7,6},{8,9},{9,8},{10,11... | collective-permute-start | bytes 1572872 | tf_op jit(solution)/shard_map/ppermute | solution.py:213
  95.8 0.8 copy-start.4
  97.1 7.0 %collective-permute-start.12 = (f32[128,384]{1,0:T(8,128)S(1)}, f32[128,384]{1,0:T(8,128)S(1)}, u32[]{:S(2)}, u32[]{:S(2)}) collective-permute-start(f32[128,384]{1,0:T(8,128)S(1)} %get-tuple-element.12), channel_id=1, source_target_pairs={{0,2},{2,0},{4,6},{6,4},{8,10},{10,8},{12,14},{14,12},{1,3},{3,1},... | collective-permute-start | bytes 589832 | tf_op jit(solution)/shard_map/ppermute | solution.py:252

commit v2 on v1

v2 whole, which is shorter than its diff:
```python
import functools
import math

import jax
import jax.numpy as jnp
from jax import lax
from jax.experimental import pallas as pl
from jax.experimental.pallas import tpu as pltpu
from jax.sharding import PartitionSpec as P

SWAP = [(0, 1), (1, 0)]
FAR = -1e30


def nt_dot(a, b):
    return lax.dot_general(a, b, (((1,), (1,)), ((), ())), preferred_element_type=jnp.float32)


def first_kernel(*refs):
    *halves, w0_ref, w1_ref, w2_ref, out_ref = refs
    weights = jnp.concatenate([w[...] for w in (w0_ref, w1_ref, w2_ref)], axis=0)
    known = jnp.concatenate([h[...] for h in halves], axis=0)
    out_ref[:, : weights.shape[0]] = nt_dot(known, weights)


def last_kernel(core_ref, *refs):
    *known, late0_ref, late1_ref, w0_ref, w1_ref, w2_ref, w3_ref, t_ref, kept_ref, given_ref = refs
    half, count = known[0].shape[0], w3_ref.shape[0]
    weights = jnp.concatenate([w[...] for w in (w0_ref, w1_ref, w2_ref, w3_ref)], axis=0)
    late = nt_dot(jnp.concatenate([late0_ref[...], late1_ref[...]], axis=0), weights)
    fresh = nt_dot(jnp.concatenate([h[...] for h in known], axis=0), w3_ref[...])
    first = core_ref[0] == 0

    def value(k):
        at = slice(k * half, (k + 1) * half)
        return jnp.concatenate([t_ref[at, : 3 * count], fresh[at]], axis=1)

    halves = (
        (value(0), value(1)), (late[:half], value(2)), (value(3), late[half:]), (value(4), value(5)),
    )
    for k, (low, high) in enumerate(halves):
        kept_ref[k] = jnp.where(first, low, high)
        given_ref[k] = jnp.where(first, high, low)


def first_products(known, *weights):
    rows, count = known[0].shape[0], weights[0].shape[0]
    return pl.pallas_call(
        first_kernel,
        out_shape=jax.ShapeDtypeStruct((len(known) * rows, 4 * count), jnp.float32),
        cost_estimate=pl.CostEstimate(
            flops=36 * rows * count * known[0].shape[1], bytes_accessed=5 << 20, transcendentals=0
        ),
        compiler_params=pltpu.CompilerParams(vmem_limit_bytes=12 << 20),
    )(*known, *weights)


def last_products(core, known, late, weights, t):
    rows, count = known[0].shape[0], weights[0].shape[0]
    vmem = pl.BlockSpec(memory_space=pltpu.VMEM)
    shape = jax.ShapeDtypeStruct((4, rows, 4 * count), jnp.float32)
    return pl.pallas_call(
        last_kernel,
        out_shape=(shape, shape),
        in_specs=[pl.BlockSpec(memory_space=pltpu.SMEM)] + [vmem] * (len(known) + len(late) + 5),
        out_specs=(vmem, vmem),
        compiler_params=pltpu.CompilerParams(vmem_limit_bytes=12 << 20),
    )(core, *known, *late, *weights, t)


def add_kernel(a_ref, b_ref, *outs):
    for k, out in enumerate(outs):
        out[...] = a_ref[k + 1] + b_ref[k + 1]


def add_halves(a, b):
    shape = jax.ShapeDtypeStruct(a.shape[1:], a.dtype)
    return pl.pallas_call(
        add_kernel,
        out_shape=(shape,) * (a.shape[0] - 1),
        compiler_params=pltpu.CompilerParams(vmem_limit_bytes=2 << 20),
    )(a, b)


def attend_block(queries, keys, values, masks, scaling):
    scores = [jnp.where(m, nt_dot(queries, k) * scaling, FAR) for k, m in zip(keys, masks)]
    highest = scores[0].max(axis=1, keepdims=True)
    for s in scores[1:]:
        highest = jnp.maximum(highest, s.max(axis=1, keepdims=True))
    weights = [jnp.where(m, jnp.exp(s - highest), 0.0) for s, m in zip(scores, masks)]
    totals = sum(w.sum(axis=1, keepdims=True) for w in weights)
    sums = sum(
        jnp.dot(w.astype(jnp.bfloat16), v, preferred_element_type=jnp.float32)
        for w, v in zip(weights, values)
    )
    return sums / totals


def attend(queries, caches, fresh_ref, lengths_ref, out_ref, steps, head, per):
    rows = queries.shape[0]
    requests = rows // steps
    heads = queries.shape[1] // head
    scaling = 1.0 / math.sqrt(head)
    take = per * steps
    for b in range(requests // per):
        part = queries[b * take : (b + 1) * take, :]
        stacked = jnp.concatenate([part[:, h * head : (h + 1) * head] for h in range(heads)], axis=0)
        limit = jnp.concatenate([lengths_ref[b * take : (b + 1) * take, :]] * heads, axis=0)
        keys, values, masks = [], [], []
        for c, cache_ref in enumerate(caches):
            count = cache_ref.shape[0] // requests
            block = cache_ref[b * per * count : (b + 1) * per * count, :]
            shape = (heads * take, per * count)
            request = lax.rem(lax.broadcasted_iota(jnp.int32, shape, 0), take) // steps
            column = lax.broadcasted_iota(jnp.int32, shape, 1)
            position = lax.rem(column, count) + c * count
            masks.append(jnp.logical_and(column // count == request, position < limit))
            keys.append(block[:, :head])
            values.append(block[:, head:])
        block = fresh_ref[b * take : (b + 1) * take, :]
        shape = (heads * take, take)
        row = lax.rem(lax.broadcasted_iota(jnp.int32, shape, 0), take)
        column = lax.broadcasted_iota(jnp.int32, shape, 1)
        masks.append(jnp.logical_and(row // steps == column // steps, column <= row))
        keys.append(block[:, :head])
        values.append(block[:, head:])
        mixed = attend_block(stacked, keys, values, masks, scaling).astype(jnp.bfloat16)
        for h in range(heads):
            out_ref[b * take : (b + 1) * take, h * head : (h + 1) * head] = mixed[
                h * take : (h + 1) * take, :
            ]


def finish_kernel(
    steps, per, where_ref, own_ref, other_ref, beside_ref, across_ref, both_ref,
    holder_ref, up_ref, low_ref, high_ref, fresh_ref, lengths_ref, out_ref,
):
    rows = own_ref.shape[1]
    x, part = where_ref[0], where_ref[1]
    width = 128
    half = width // 2
    own = own_ref[0] + other_ref[0]
    beside, across, both = beside_ref[...], across_ref[...], both_ref[...]
    queries_here = part == 0
    columns = jnp.where(queries_here, own, across), jnp.where(queries_here, beside, both)
    ranks = jnp.where(queries_here, across, own), jnp.where(queries_here, both, beside)
    low_lanes = lax.broadcasted_iota(jnp.int32, (rows, width), 1) < half
    even = jnp.where(x == 0, columns[0], columns[1])
    odd = jnp.where(x == 0, columns[1], columns[0])

    def spaced(wide):
        out = []
        for j in range(4):
            pair = wide[:, (j // 2) * width : (j // 2 + 1) * width]
            out.append((pair, pltpu.roll(pair, half, 1)) if j % 2 == 0 else (pltpu.roll(pair, half, 1), pair))
        return out

    even, odd = spaced(even), spaced(odd)
    merged = [jnp.where(low_lanes, e[0], o[1]) for e, o in zip(even, odd)]
    groups = []
    for k in range(4):
        group = merged[3]
        for j in range(3):
            group = jnp.where(where_ref[2 + j] == 2 * k + x, merged[j], group)
        groups.append(group)
    base = jnp.concatenate(groups, axis=1)
    holder = holder_ref[...]
    spread = []
    for m in range(4):
        lane_owner = jnp.where(low_lanes, where_ref[2 + 2 * m], where_ref[3 + 2 * m])
        shrink = ranks[m // 2][:, (m % 2) * width : (m % 2 + 1) * width]
        spread.append(jnp.where(holder == lane_owner, shrink, 0.0).astype(jnp.bfloat16))
    adapted = jnp.dot(
        jnp.concatenate(spread, axis=1), up_ref[...], preferred_element_type=jnp.float32
    )
    queries = (base + adapted).astype(jnp.bfloat16)
    out_ref[0] = queries
    head = fresh_ref.shape[1] // 2
    attend(
        queries, (low_ref, high_ref), fresh_ref, lengths_ref, out_ref.at[1], steps, head, per
    )


def finish(steps, where, *arrays):
    rows, up = arrays[0].shape[1], arrays[6]
    vmem = pl.BlockSpec(memory_space=pltpu.VMEM)
    return pl.pallas_call(
        functools.partial(finish_kernel, steps, 8),
        out_shape=jax.ShapeDtypeStruct((2, rows, up.shape[1]), jnp.bfloat16),
        in_specs=[pl.BlockSpec(memory_space=pltpu.SMEM)] + [vmem] * len(arrays),
        out_specs=vmem,
        compiler_params=pltpu.CompilerParams(vmem_limit_bytes=16 << 20),
    )(where, *arrays)


def attend_kernel(steps, per, q_ref, low_ref, high_ref, fresh_ref, lengths_ref, out_ref):
    head = fresh_ref.shape[1] // 2
    attend(q_ref[...], (low_ref, high_ref), fresh_ref, lengths_ref, out_ref, steps, head, per)


def line_pairs(groups, moves):
    return [(a * 2 + x, b * 2 + x) for a, b in moves for x in range(2)]


def holders_of(request_adapter, adapter_owner):
    ids = jnp.arange(adapter_owner.shape[0], dtype=jnp.int32)
    lookup = request_adapter[:, None] == ids[None, :]
    return jnp.sum(jnp.where(lookup, adapter_owner[None, :], 0), axis=1)


def body(
    normed_hidden_states,
    query_matrix,
    factor_down,
    factor_up,
    kv_cache,
    incoming_key_value,
    kv_lengths,
    request_adapter,
    adapter_owner,
):
    groups = lax.axis_size("group")
    core = lax.axis_index("tensor")
    requests, steps, features = normed_hidden_states.shape
    rows = requests * steps
    holder = holders_of(request_adapter, adapter_owner)

    down = factor_down[0].T
    down_other = lax.ppermute(factor_down, "tensor", SWAP)[0].T
    mine_down = lax.dynamic_slice_in_dim(down, core * features, features, 1)
    other_down = lax.dynamic_slice_in_dim(down_other, core * features, features, 1)
    down_block = jnp.where(
        core == 0,
        jnp.concatenate([mine_down, other_down], 0),
        jnp.concatenate([other_down, mine_down], 0),
    )
    query_block = query_matrix.T
    width = query_matrix.shape[1] * groups
    out_shape = (requests, steps, width)

    if groups == 8 and lax.axis_size("parts") == 2 and query_block.shape == down_block.shape:
        place = lax.axis_index("group")
        z, x, part = place // 2, lax.rem(place, 2), lax.axis_index("parts")
        pair_low = z < 2
        places = (z, z + 1 - 2 * lax.rem(z, 2), jnp.where(pair_low, 2, 1), jnp.where(pair_low, 3, 0))
        where = [x, part] + [p * 2 + x for p in places] + [p * 2 + 1 - x for p in places]
        where = jnp.stack(where).astype(jnp.int32)
        middle = jnp.logical_or(z == 1, z == 2)
        bar = lambda *a: lax.optimization_barrier(a)
        along = lambda a, moves: lax.ppermute(a, "group", line_pairs(groups, moves))
        across = lambda a: lax.ppermute(a, "parts", SWAP)
        beside = lambda a: lax.ppermute(a, "group", [(i, i ^ 1) for i in range(groups)])
        corner = [(p * groups + i, (1 - p) * groups + (i ^ 1)) for p in range(2) for i in range(groups)]
        ends, inner = ((0, 1), (1, 0), (2, 3), (3, 2)), ((1, 2), (2, 1))
        outward = ((1, 0), (2, 3))
        mid, at = requests // 2, rows // 2

        w0 = jnp.where(part == 0, query_block, down_block)
        hidden = normed_hidden_states.reshape(rows, features)
        h0, h1 = hidden[:at], hidden[at:]
        w1, m1 = along(w0, ends), along(w0, inner)
        b1, a0 = beside(h1), across(h0)
        up_pair = along(factor_up[0], ends)
        w1, m1, b1, a0 = bar(w1, m1, b1, a0)
        m2, p1 = along(w1, inner), along(m1, outward)
        c0, c1 = beside(a0), across(b1)
        b0, a1 = beside(h0), across(h1)
        up_two = jnp.concatenate([factor_up[0], up_pair], axis=0)
        up_far = along(up_two, inner)
        w2 = jnp.where(middle, m1, p1)
        m2, p1, c0, c1, up_far = bar(m2, p1, c0, c1, up_far)
        p2 = along(m2, outward)
        up_far = jnp.where(middle, up_far, along(up_far, outward))
        w3 = jnp.where(middle, m2, p2)
        up_four = jnp.concatenate([up_two, up_far], axis=0)
        up_all = jnp.concatenate([up_four, beside(up_four)], axis=0)
        up_other = lax.ppermute(up_all, "tensor", SWAP)
        up_full = jnp.where(
            core == 0,
            jnp.concatenate([up_all, up_other], 1),
            jnp.concatenate([up_other, up_all], 1),
        )
        known = h0, h1, b1, a0, c0, c1
        t = first_products(known, w0, w1, w2)

        half = lambda a, k: lax.dynamic_slice_in_dim(a, k * mid, mid, 0)
        cache, given = half(kv_cache, core), half(kv_cache, 1 - core)
        got_cache = lax.ppermute(given, "tensor", SWAP)
        low = jnp.where(core == 0, cache, got_cache).reshape(-1, kv_cache.shape[2])
        high = jnp.where(core == 0, got_cache, cache).reshape(-1, kv_cache.shape[2])
        spread_rows = lambda a: jnp.repeat(half(a, core), steps)[:, None]
        fresh = half(incoming_key_value, core).reshape(rows // 2, -1)
        holder_rows, lengths_rows = spread_rows(holder), spread_rows(kv_lengths)
        p2, b0, a1, t, low, high, fresh, holder_rows, lengths_rows = bar(
            p2, b0, a1, t, low, high, fresh, holder_rows, lengths_rows
        )
        w3 = jnp.where(middle, m2, p2)
        core_at = jnp.reshape(core, (1,)).astype(jnp.int32)
        kept, given = last_products(core_at, known, (b0, a1), (w0, w1, w2, w3), t)
        got = lax.ppermute(given, "tensor", SWAP)
        t_beside, t_across, t_both = add_halves(kept, got)
        t_beside, t_across = beside(t_beside), across(t_across)
        t_both = lax.ppermute(t_both, ("parts", "group"), corner)
        done = finish(
            steps, where, kept, got, t_beside, t_across, t_both,
            holder_rows, up_full, low, high, fresh, lengths_rows,
        )
        done_other = lax.ppermute(done, "tensor", SWAP)
        outs = jnp.where(
            core == 0,
            jnp.concatenate([done, done_other], 1),
            jnp.concatenate([done_other, done], 1),
        )
        return outs[0].reshape(out_shape), outs[1].reshape(out_shape)

    holder_rows = jnp.repeat(holder, steps)[:, None]
    lengths_rows = jnp.repeat(kv_lengths, steps)[:, None]
    own = normed_hidden_states.reshape(rows, features)
    other_cache = lax.ppermute(kv_cache, "tensor", SWAP)
    low = jnp.where(core == 0, kv_cache, other_cache).reshape(-1, kv_cache.shape[2])
    high = jnp.where(core == 0, other_cache, kv_cache).reshape(-1, kv_cache.shape[2])
    fresh = incoming_key_value.reshape(rows, -1)
    up = lax.all_gather(factor_up[0], "group", axis=0, tiled=True)
    up_other = lax.ppermute(up, "tensor", SWAP)
    up_full = jnp.where(
        core == 0, jnp.concatenate([up, up_other], 1), jnp.concatenate([up_other, up], 1)
    )

    place = lax.axis_index("group")
    ring = [(i, (i + 1) % groups) for i in range(groups)]

    def step(k, carry):
        q_part, d_part, base, shrink = carry
        at = lax.rem(place - k + groups, groups)
        base = lax.dynamic_update_slice_in_dim(base, nt_dot(own, q_part), at * q_part.shape[0], 1)
        shrink = shrink + jnp.where(holder_rows == at, nt_dot(own, d_part), 0.0)
        q_part, d_part = (lax.ppermute(w, "group", ring) for w in (q_part, d_part))
        return q_part, d_part, base, shrink

    start = (
        query_block,
        down_block,
        jnp.zeros((rows, width), jnp.float32),
        jnp.zeros((rows, down_block.shape[0]), jnp.float32),
    )
    _, _, base, shrink = lax.fori_loop(0, groups, step, start)
    base = base + lax.ppermute(base, "tensor", SWAP)
    shrink = (shrink + lax.ppermute(shrink, "tensor", SWAP)).astype(jnp.bfloat16)
    named = holder_rows == jnp.arange(groups, dtype=jnp.int32)[None, :]
    spread = jnp.where(named[:, :, None], shrink[:, None, :], 0).reshape(rows, -1)
    adapted = jnp.dot(spread, up_full, preferred_element_type=jnp.float32)
    queries = (base + adapted).astype(jnp.bfloat16)
    attended = pl.pallas_call(
        functools.partial(attend_kernel, steps, 8),
        out_shape=jax.ShapeDtypeStruct(queries.shape, jnp.bfloat16),
        compiler_params=pltpu.CompilerParams(vmem_limit_bytes=24 << 20),
    )(queries, low, high, fresh, lengths_rows)
    return queries.reshape(out_shape), attended.reshape(out_shape)


def solution(mesh):
    placed = (
        P(("parts", "group"), None, "tensor"),
        P("tensor", "group"),
        P("group", None, "tensor"),
        P("group", None, "tensor"),
        P(("parts", "group"), "tensor", None),
        P(("parts", "group"), None, None),
        P(("parts", "group")),
        P(("parts", "group")),
        P("parts"),
    )
    return jax.shard_map(
        body,
        mesh=mesh,
        in_specs=placed,
        out_specs=(P(("parts", "group"), None, None), P(("parts", "group"), None, None)),
        check_vma=False,
    )
```

time: 109 us -> 79.5 us (0.73)
  blocking collectives: 30.9 us -> 0 us
  waiting for transfers between devices: 40.7 us -> 29.2 us
  starting transfers between devices: 16.4 us -> 27.1 us
  local copies, waits for them, and re-layouts: 7.91 us -> 10.4 us
  Pallas kernels: 9.41 us -> 7.71 us
    all_gather x1 -> x0, blocking collectives: 30.9 us -> none  [body(): up = lax.all_gather(factor_up[0], 'group', axis=0, tiled=True)]
    ppermute x5 -> x8, waiting for transfers between devices: 32.3 us -> 21.2 us  [body(): along = lambda a, moves: lax.ppermute(a, 'group', line_pairs(groups, moves))]
    ppermute x5 -> x8, starting transfers between devices: 6.88 us -> 12.7 us  [body(): along = lambda a, moves: lax.ppermute(a, 'group', line_pairs(groups, moves))]
    ppermute x10 -> x15, starting transfers between devices: 9.52 us -> 14.4 us  [the longest x5 6.82 us: body(): lax.ppermute(a, 'group', [(i, i ^ 1) for i in range(groups)])]
    reshape x5 -> x1, local copies, waits for them, and re-layouts: 3.34 us -> 0.02 us  [body(): fresh = half(incoming_key_value, core).reshape(rows // 2, -1)]
    slice x0 -> x4, local copies, waits for them, and re-layouts: none -> 2.58 us  [the longest x3 2.56 us: body(): h0, h1 = (hidden[:at], hidden[at:])]
    pallas_call x5 -> x4, Pallas kernels: 9.41 us -> 7.71 us  [the longest x1 3.51 us: last_products(): pl.pallas_call(last_kernel, out_shape=(shape, shape), in_specs=[pl.BlockS...]
    another operation x3 -> x5, local copies, waits for them, and re-layouts: 0.33 us -> 1.72 us  [the longest x2 1.42 us: body(): return (outs[0].reshape(out_shape), outs[1].reshape(out_shape))]
  transfers between devices with their start and end apart: 15 -> 23, of which waited for: 8 -> 10; matrix products, arithmetic and copies ran while one was open for 4% -> 11% of each run, Pallas kernels for 4% -> 7%
where the time goes in v2:
time: 79.5 us; the launch traced here: 78.9 us
  waiting for transfers between devices  29.2 us (37%)
  starting transfers between devices  27.1 us (34%)
  local copies, waits for them, and re-layouts  10.4 us (13%)
  Pallas kernels  7.71 us (10%)
  other arithmetic  3.45 us (4%)
  between operations  0.95 us (1%)
    ppermute x8, waiting for transfers between devices, body(): along = lambda a, moves: lax.ppermute(a, 'group', line_pairs(groups, moves))  21.2 us
    ppermute x8, starting transfers between devices, body(): along = lambda a, moves: lax.ppermute(a, 'group', line_pairs(groups, moves))  12.7 us
    ppermute x5, starting transfers between devices, body(): lax.ppermute(a, 'group', [(i, i ^ 1) for i in range(groups)])  6.82 us
    ppermute x4, starting transfers between devices, body(): across = lambda a: lax.ppermute(a, 'parts', SWAP)  5.15 us
    unnamed x36, local copies, waits for them, and re-layouts  3.84 us
    pallas_call x1, Pallas kernels, last_products(): pl.pallas_call(last_kernel, out_shape=(shape, shape), in_specs=[pl.BlockS...  3.51 us
    slice x3, local copies, waits for them, and re-layouts, body(): h0, h1 = (hidden[:at], hidden[at:])  2.56 us
    ppermute x1, waiting for transfers between devices, body(): t_both = lax.ppermute(t_both, ('parts', 'group'), corner)  2.44 us
  transfers between devices with their start and end apart: 23, of which 10 were waited for; matrix products, arithmetic and copies ran while one was open for 11% of the time, Pallas kernels for 7%

profile of v2, /device:TPU:0, one launch (start us, length us, event | category | flops | bytes accessed | tf_op | source)
XLA Modules:
  0.0 78.9 jit_solution(7579276761703560355)
XLA Ops:
  0.6 0.5 collective-permute-start
  1.2 2.2 %fusion.1 = (bf16[32,2,4096]{2,1,0:T(2,128)(2,1)S(1)}, bf16[32,2,4096]{2,1,0:T(2,128)(2,1)S(1)}) fusion(bf16[64,2,4096]{2,1,0:T(2,128)(2,1)} %param.9), kind=kLoop, calls=%fused_computation.18 | loop fusion | bytes 2097152 | tf_op jit(solution)/shard_map/slice | solution.py:260
  3.3 0.2 slice.21.refs_1_
  3.5 2.6 %collective-permute-start.3 = (bf16[64,4096]{1,0:T(8,128)(2,1)S(1)}, bf16[64,4096]{1,0:T(8,128)(2,1)S(1)}, u32[]{:S(2)}, u32[]{:S(2)}) collective-permute-start(bf16[64,4096]{1,0:T(8,128)(2,1)S(1)} %slice.21.refs_1_), channel_id=1, source_target_pairs={{0,2},{2,0},{4,6},{6,4},{8,10},{10,8},{12,14},{14,12},{1,3},{3,1},... | collective-permute-start | bytes 1572872 | tf_op jit(solution)/shard_map/ppermute | solution.py:252
  6.1 0.2 slice.19.refs_0_
  6.3 1.6 %collective-permute-start.4 = (bf16[64,4096]{1,0:T(8,128)(2,1)S(1)}, bf16[64,4096]{1,0:T(8,128)(2,1)S(1)}, u32[]{:S(2)}, u32[]{:S(2)}) collective-permute-start(bf16[64,4096]{1,0:T(8,128)(2,1)S(1)} %slice.19.refs_0_), channel_id=1, source_target_pairs={{0,16},{16,0},{1,17},{17,1},{2,18},{18,2},{3,19},{19,3},{4,20},{20... | collective-permute-start | bytes 1572872 | tf_op jit(solution)/shard_map/ppermute | solution.py:251
  8.0 1.0 %copy-done.7 = bf16[4096,64]{0,1:T(8,128)(2,1)S(1)} copy-done((bf16[4096,64]{0,1:T(8,128)(2,1)S(1)}, bf16[4096,64]{0,1:T(8,128)(2,1)}, u32[]{:S(2)}) %copy-start.7) | copy-done | bytes 524312
  8.9 0.2 fusion.refs_6_.refs_8_
  9.1 1.6 %collective-permute-start.1 = (bf16[64,4096]{1,0:T(8,128)(2,1)S(1)}, bf16[64,4096]{1,0:T(8,128)(2,1)S(1)}, u32[]{:S(2)}, u32[]{:S(2)}) collective-permute-start(bf16[64,4096]{1,0:T(8,128)(2,1)S(1)} %fusion.refs_6_.refs_8_), channel_id=1, source_target_pairs={{0,4},{2,6},{4,0},{6,2},{8,12},{10,14},{12,8},{14,10},{1,5},{3,7},... | collective-permute-start | bytes 1572872 | tf_op jit(solution)/shard_map/ppermute | solution.py:250
  10.7 1.4 %collective-permute-start.2 = (bf16[64,4096]{1,0:T(8,128)(2,1)S(1)}, bf16[64,4096]{1,0:T(8,128)(2,1)}, u32[]{:S(2)}, u32[]{:S(2)}) collective-permute-start(bf16[64,4096]{1,0:T(8,128)(2,1)S(1)} %fusion.refs_6_.refs_8_), channel_id=1, source_target_pairs={{4,8},{6,10},{8,4},{10,6},{5,9},{7,11},{9,5},{11,7},{20,24},{22,26... | collective-permute-start | bytes 1572872 | tf_op jit(solution)/shard_map/ppermute | solution.py:250
  12.2 3.7 %collective-permute-start.9 = (bf16[64,256]{1,0:T(8,128)(2,1)S(1)}, bf16[64,256]{1,0:T(8,128)(2,1)S(1)}, u32[]{:S(2)}, u32[]{:S(2)}) collective-permute-start(bf16[64,256]{1,0:T(8,128)(2,1)S(1)} %bitcast.26), channel_id=1, source_target_pairs={{0,4},{2,6},{4,0},{6,2},{8,12},{10,14},{12,8},{14,10},{1,5},{3,7},... | collective-permute-start | bytes 98312 | tf_op jit(solution)/shard_map/ppermute | solution.py:250
  15.9 1.7 %constant_dynamic-slice_fusion.1 = bf16[32,16,256]{2,1,0:T(8,128)(2,1)} fusion(bf16[64,16,256]{2,1,0:T(8,128)(2,1)} %param.13, s32[]{:T(128)S(6)} %select_n.102), kind=kLoop, calls=%fused_computation.17 | loop fusion | bytes 524292 | tf_op jit(solution)/shard_map/dynamic_slice | solution.py:286
  17.6 1.1 %collective-permute-done.3.refs_2_ = bf16[64,4096]{1,0:T(8,128)(2,1)S(1)} collective-permute-done((bf16[64,4096]{1,0:T(8,128)(2,1)S(1)}, bf16[64,4096]{1,0:T(8,128)(2,1)S(1)}, u32[]{:S(2)}, u32[]{:S(2)}) %collective-permute-start.3) | collective-permute-done | bytes 524320 | tf_op jit(solution)/shard_map/ppermute | solution.py:252
  18.7 1.7 %collective-permute-done.4.refs_3_ = bf16[64,4096]{1,0:T(8,128)(2,1)S(1)} collective-permute-done((bf16[64,4096]{1,0:T(8,128)(2,1)S(1)}, bf16[64,4096]{1,0:T(8,128)(2,1)S(1)}, u32[]{:S(2)}, u32[]{:S(2)}) %collective-permute-start.4) | collective-permute-done | bytes 524320 | tf_op jit(solution)/shard_map/ppermute | solution.py:251
  20.4 2.9 %collective-permute-done.1.refs_7_.refs_9_ = bf16[64,4096]{1,0:T(8,128)(2,1)S(1)} collective-permute-done((bf16[64,4096]{1,0:T(8,128)(2,1)S(1)}, bf16[64,4096]{1,0:T(8,128)(2,1)S(1)}, u32[]{:S(2)}, u32[]{:S(2)}) %collective-permute-start.1) | collective-permute-done | bytes 524320 | tf_op jit(solution)/shard_map/ppermute | solution.py:250
  23.3 1.5 %collective-permute-start.5 = (bf16[64,4096]{1,0:T(8,128)(2,1)S(1)}, bf16[64,4096]{1,0:T(8,128)(2,1)}, u32[]{:S(2)}, u32[]{:S(2)}) collective-permute-start(bf16[64,4096]{1,0:T(8,128)(2,1)S(1)} %collective-permute-done.1.refs_7_.refs_9_), channel_id=1, source_target_pairs={{4,8},{6,10},{8,4},{10,6},{5,9},{7,11},{9,5},{11,7},{20,24},{22,26... | collective-permute-start | bytes 1572872 | tf_op jit(solution)/shard_map/ppermute | solution.py:250
  24.7 1.3 %collective-permute-start.6 = (bf16[64,4096]{1,0:T(8,128)(2,1)}, bf16[64,4096]{1,0:T(8,128)(2,1)}, u32[]{:S(2)}, u32[]{:S(2)}) collective-permute-start(bf16[64,4096]{1,0:T(8,128)(2,1)} %collective-permute-done.2), channel_id=1, source_target_pairs={{4,0},{6,2},{8,12},{10,14},{5,1},{7,3},{9,13},{11,15},{20,16},{22,... | collective-permute-start | bytes 1572872 | tf_op jit(solution)/shard_map/ppermute | solution.py:250
  26.0 0.6 collective-permute-start.7
  26.6 1.1 %collective-permute-start.8 = (bf16[64,4096]{1,0:T(8,128)(2,1)S(1)}, bf16[64,4096]{1,0:T(8,128)(2,1)}, u32[]{:S(2)}, u32[]{:S(2)}) collective-permute-start(bf16[64,4096]{1,0:T(8,128)(2,1)S(1)} %collective-permute-done.3.refs_2_), channel_id=1, source_target_pairs={{0,16},{16,0},{1,17},{17,1},{2,18},{18,2},{3,19},{19,3},{4,20},{20... | collective-permute-start | bytes 1572872 | tf_op jit(solution)/shard_map/ppermute | solution.py:251
  27.8 0.6 copy-done.15
  28.8 0.5 copy-done.17
  29.6 0.7 collective-permute-start.10
  30.3 1.8 %broadcast_select_fusion.2 = (bf16[32,16,256]{2,1,0:T(8,128)(2,1)S(1)}, bf16[32,16,256]{2,1,0:T(8,128)(2,1)}) fusion(bf16[32,16,256]{2,1,0:T(8,128)(2,1)} %collective-permute-done.14, pred[]{:T(512)S(6)} %eq.14, bf16[64,16,256]{2,1,0:T(8,128)(2,1)} %param.13, s32[]{:T(128)S(6)} %select_n.101), kind=kLoop, calls=%fused_computation.9 | loop fusion | flops 262144 | bytes 1048581 | tf_op jit(solution)/shard_map/jit(_where)/select_n | solution.py:290
  32.1 1.5 %collective-permute-start.12 = (bf16[64,4096]{1,0:T(8,128)(2,1)S(1)}, bf16[64,4096]{1,0:T(8,128)(2,1)S(1)}, u32[]{:S(2)}, u32[]{:S(2)}) collective-permute-start(bf16[64,4096]{1,0:T(8,128)(2,1)S(1)} %slice.19.refs_0_), channel_id=1, source_target_pairs={{0,2},{2,0},{4,6},{6,4},{8,10},{10,8},{12,14},{14,12},{1,3},{3,1},... | collective-permute-start | bytes 1572872 | tf_op jit(solution)/shard_map/ppermute | solution.py:252
  33.6 1.0 %collective-permute-start.13 = (bf16[64,4096]{1,0:T(8,128)(2,1)S(1)}, bf16[64,4096]{1,0:T(8,128)(2,1)S(1)}, u32[]{:S(2)}, u32[]{:S(2)}) collective-permute-start(bf16[64,4096]{1,0:T(8,128)(2,1)S(1)} %slice.21.refs_1_), channel_id=1, source_target_pairs={{0,16},{16,0},{1,17},{17,1},{2,18},{18,2},{3,19},{19,3},{4,20},{20... | collective-permute-start | bytes 1572872 | tf_op jit(solution)/shard_map/ppermute | solution.py:251
  34.5 8.9 %collective-permute-done.6 = bf16[64,4096]{1,0:T(8,128)(2,1)} collective-permute-done((bf16[64,4096]{1,0:T(8,128)(2,1)}, bf16[64,4096]{1,0:T(8,128)(2,1)}, u32[]{:S(2)}, u32[]{:S(2)}) %collective-permute-start.6) | collective-permute-done | bytes 524320 | tf_op jit(solution)/shard_map/ppermute | solution.py:250
  43.4 1.3 %collective-permute-start.11 = (bf16[64,4096]{1,0:T(8,128)(2,1)}, bf16[64,4096]{1,0:T(8,128)(2,1)S(1)}, u32[]{:S(2)}, u32[]{:S(2)}) collective-permute-start(bf16[64,4096]{1,0:T(8,128)(2,1)} %collective-permute-done.5), channel_id=1, source_target_pairs={{4,0},{6,2},{8,12},{10,14},{5,1},{7,3},{9,13},{11,15},{20,16},{22,... | collective-permute-start | bytes 1572872 | tf_op jit(solution)/shard_map/ppermute | solution.py:250
  44.7 1.3 %collective-permute-start.19 = (bf16[128,256]{1,0:T(8,128)(2,1)S(1)}, bf16[128,256]{1,0:T(8,128)(2,1)S(1)}, u32[]{:S(2)}, u32[]{:S(2)}) collective-permute-start(bf16[128,256]{1,0:T(8,128)(2,1)S(1)} %collective-permute-done.10), channel_id=1, source_target_pairs={{4,0},{6,2},{8,12},{10,14},{5,1},{7,3},{9,13},{11,15},{20,16},{22,... | collective-permute-start | bytes 196616 | tf_op jit(solution)/shard_map/ppermute | solution.py:250
  46.0 1.1 %broadcast_select_fusion.1.refs_8_.refs_10_ = bf16[64,4096]{1,0:T(8,128)(2,1)S(1)} fusion(bf16[64,4096]{1,0:T(8,128)(2,1)} %collective-permute-done.2, bf16[64,4096]{1,0:T(8,128)(2,1)} %collective-permute-done.6, pred[]{:T(512)S(6)} %or.3), kind=kLoop, calls=%fused_computation.4 | loop fusion | flops 262144 | bytes 1572865 | tf_op jit(solution)/shard_map/jit(_where)/select_n | solution.py:270
  47.1 2.2 %shard_map.104.refs_12_ = f32[384,256]{1,0:T(8,128)S(1)} custom-call(bf16[64,4096]{1,0:T(8,128)(2,1)S(1)} %slice.19.refs_0_, bf16[64,4096]{1,0:T(8,128)(2,1)S(1)} %slice.21.refs_1_, bf16[64,4096]{1,0:T(8,128)(2,1)S(1)} %collective-permute-done.3.refs_2_, bf16[64,4096]{1,0:T(8,128)(2,1)S(1)} %collective-permute-done.4.refs_3_, ...), custom_call_target="tpu_custom_call" | custom-call | flops 603979776 | bytes 5242880 | tf_op jit(solution)/shard_map/pallas_call | solution.py:48
  49.3 9.4 %collective-permute-done.19 = bf16[128,256]{1,0:T(8,128)(2,1)S(1)} collective-permute-done((bf16[128,256]{1,0:T(8,128)(2,1)S(1)}, bf16[128,256]{1,0:T(8,128)(2,1)S(1)}, u32[]{:S(2)}, u32[]{:S(2)}) %collective-permute-start.19) | collective-permute-done | bytes 65568 | tf_op jit(solution)/shard_map/ppermute | solution.py:250
  58.8 1.6 %collective-permute-start.20 = (bf16[256,256]{1,0:T(8,128)(2,1)S(1)}, bf16[256,256]{1,0:T(8,128)(2,1)S(1)}, u32[]{:S(2)}, u32[]{:S(2)}) collective-permute-start(bf16[256,256]{1,0:T(8,128)(2,1)S(1)} %pad_maximum_fusion.1), channel_id=1, source_target_pairs={{0,2},{2,0},{4,6},{6,4},{8,10},{10,8},{12,14},{14,12},{1,3},{3,1},... | collective-permute-start | bytes 393224 | tf_op jit(solution)/shard_map/ppermute | solution.py:252
  60.4 3.5 %shard_map.105 = (f32[4,64,256]{2,1,0:T(8,128)S(1)}, f32[4,64,256]{2,1,0:T(8,128)}) custom-call(s32[1]{0:T(128)} %bitcast.10.core_ref, bf16[64,4096]{1,0:T(8,128)(2,1)S(1)} %slice.19.refs_0_, bf16[64,4096]{1,0:T(8,128)(2,1)S(1)} %slice.21.refs_1_, bf16[64,4096]{1,0:T(8,128)(2,1)S(1)} %collective-permute-done.3.refs_2_, ...), custom_call_target="tpu_custom_call" | custom-call | tf_op jit(solution)/shard_map/pallas_call | solution.py:62
  64.0 0.6 copy-done.2
  64.7 0.4 collective-permute-start.21
  65.2 0.5 collective-permute-done.15.b_ref.other_ref
  65.7 0.9 %copy-done.3 = f32[4,64,256]{2,1,0:T(8,128)S(1)} copy-done((f32[4,64,256]{2,1,0:T(8,128)S(1)}, f32[4,64,256]{2,1,0:T(8,128)}, u32[]{:S(2)}) %copy-start.3) | copy-done | bytes 262168
  66.7 0.6 collective-permute-start.16
  67.3 1.5 %collective-permute-start.17 = (f32[64,256]{1,0:T(8,128)S(1)}, f32[64,256]{1,0:T(8,128)S(1)}, u32[]{:S(2)}, u32[]{:S(2)}) collective-permute-start(f32[64,256]{1,0:T(8,128)S(1)} %get-tuple-element.38), channel_id=1, source_target_pairs={{0,16},{16,0},{1,17},{17,1},{2,18},{18,2},{3,19},{19,3},{4,20},{20... | collective-permute-start | bytes 196616 | tf_op jit(solution)/shard_map/ppermute | solution.py:251
  68.8 1.4 %collective-permute-start.18 = (f32[64,256]{1,0:T(8,128)S(1)}, f32[64,256]{1,0:T(8,128)S(1)}, u32[]{:S(2)}, u32[]{:S(2)}) collective-permute-start(f32[64,256]{1,0:T(8,128)S(1)} %get-tuple-element.39), channel_id=1, source_target_pairs={{0,18},{2,16},{4,22},{6,20},{8,26},{10,24},{12,30},{14,28},{16,2},... | collective-permute-start | bytes 196616 | tf_op jit(solution)/shard_map/ppermute | solution.py:303
  70.3 0.1 maximum_select_fusion.1.up_ref
  70.6 0.4 collective-permute-done.16.beside_ref
  71.0 0.5 collective-permute-done.17.across_ref
  71.5 2.4 %collective-permute-done.18.both_ref = f32[64,256]{1,0:T(8,128)S(1)} collective-permute-done((f32[64,256]{1,0:T(8,128)S(1)}, f32[64,256]{1,0:T(8,128)S(1)}, u32[]{:S(2)}, u32[]{:S(2)}) %collective-permute-start.18) | collective-permute-done | bytes 65568 | tf_op jit(solution)/shard_map/ppermute | solution.py:303
  74.0 2.0 %shard_map.107 = bf16[2,64,512]{2,1,0:T(8,128)(2,1)S(1)} custom-call(s32[10]{0:T(128)S(1)} %stack.43.where_ref, f32[4,64,256]{2,1,0:T(8,128)S(1)} %copy-done.4, f32[4,64,256]{2,1,0:T(8,128)S(1)} %collective-permute-done.15.b_ref.other_ref, f32[64,256]{1,0:T(8,128)S(1)} %collective-permute-done.16.beside_ref, ...), custom_call_target="tpu_custom_call" | custom-call | tf_op jit(solution)/shard_map/pallas_call | solution.py:187
  76.0 1.3 %collective-permute-done.22 = bf16[2,64,512]{2,1,0:T(8,128)(2,1)S(1)} collective-permute-done((bf16[2,64,512]{2,1,0:T(8,128)(2,1)S(1)}, bf16[2,64,512]{2,1,0:T(8,128)(2,1)S(1)}, u32[]{:S(2)}, u32[]{:S(2)}) %collective-permute-start.22) | collective-permute-done | bytes 131104 | tf_op jit(solution)/shard_map/ppermute | solution.py:308
  77.5 0.7 reshape_squeeze.6
  78.2 0.7 reshape_squeeze.7
  (69 shorter events, 1.4 us)
Async XLA Ops:
  0.6 27.1 %copy-start = (bf16[64,2,256]{2,1,0:T(2,128)(2,1)S(1)}, bf16[64,2,256]{2,1,0:T(2,128)(2,1)}, u32[]{:S(2)}) copy-start(bf16[64,2,256]{2,1,0:T(2,128)(2,1)} %param.14) | copy-start | bytes 196612
  0.6 7.3 %collective-permute-start = (bf16[1,8192,32]{1,2,0:T(8,128)(2,1)}, bf16[1,8192,32]{1,2,0:T(8,128)(2,1)S(1)}, u32[]{:S(2)}, u32[]{:S(2)}) collective-permute-start(bf16[1,8192,32]{1,2,0:T(8,128)(2,1)} %param.11), channel_id=1, source_target_pairs={{0,1},{1,0},{2,3},{3,2},{4,5},{5,4},{6,7},{7,6},{8,9},{9,8},{10,11... | collective-permute-start | bytes 1572872 | tf_op jit(solution)/shard_map/ppermute | solution.py:229
  3.5 15.2 %collective-permute-start.3 = (bf16[64,4096]{1,0:T(8,128)(2,1)S(1)}, bf16[64,4096]{1,0:T(8,128)(2,1)S(1)}, u32[]{:S(2)}, u32[]{:S(2)}) collective-permute-start(bf16[64,4096]{1,0:T(8,128)(2,1)S(1)} %slice.21.refs_1_), channel_id=1, source_target_pairs={{0,2},{2,0},{4,6},{6,4},{8,10},{10,8},{12,14},{14,12},{1,3},{3,1},... | collective-permute-start | bytes 1572872 | tf_op jit(solution)/shard_map/ppermute | solution.py:252
  6.1 1.8 %copy-start.14 = (bf16[1,8192,32]{1,2,0:T(8,128)(2,1)S(1)}, bf16[1,8192,32]{1,2,0:T(8,128)(2,1)}, u32[]{:S(2)}) copy-start(bf16[1,8192,32]{1,2,0:T(8,128)(2,1)} %param.11) | copy-start | bytes 1572868
  6.3 14.1 %collective-permute-start.4 = (bf16[64,4096]{1,0:T(8,128)(2,1)S(1)}, bf16[64,4096]{1,0:T(8,128)(2,1)S(1)}, u32[]{:S(2)}, u32[]{:S(2)}) collective-permute-start(bf16[64,4096]{1,0:T(8,128)(2,1)S(1)} %slice.19.refs_0_), channel_id=1, source_target_pairs={{0,16},{16,0},{1,17},{17,1},{2,18},{18,2},{3,19},{19,3},{4,20},{20... | collective-permute-start | bytes 1572872 | tf_op jit(solution)/shard_map/ppermute | solution.py:251
  7.9 1.0 %copy-start.7 = (bf16[4096,64]{0,1:T(8,128)(2,1)S(1)}, bf16[4096,64]{0,1:T(8,128)(2,1)}, u32[]{:S(2)}) copy-start(bf16[4096,64]{0,1:T(8,128)(2,1)} %param.10) | copy-start | bytes 1572868
  8.9 3.2 %copy-start.10 = (bf16[1,64,256]{2,1,0:T(8,128)(2,1)S(1)}, bf16[1,64,256]{2,1,0:T(8,128)(2,1)}, u32[]{:S(2)}) copy-start(bf16[1,64,256]{2,1,0:T(8,128)(2,1)} %param.12) | copy-start | bytes 98308
  9.1 14.2 %collective-permute-start.1 = (bf16[64,4096]{1,0:T(8,128)(2,1)S(1)}, bf16[64,4096]{1,0:T(8,128)(2,1)S(1)}, u32[]{:S(2)}, u32[]{:S(2)}) collective-permute-start(bf16[64,4096]{1,0:T(8,128)(2,1)S(1)} %fusion.refs_6_.refs_8_), channel_id=1, source_target_pairs={{0,4},{2,6},{4,0},{6,2},{8,12},{10,14},{12,8},{14,10},{1,5},{3,7},... | collective-permute-start | bytes 1572872 | tf_op jit(solution)/shard_map/ppermute | solution.py:250
  10.7 12.5 %collective-permute-start.2 = (bf16[64,4096]{1,0:T(8,128)(2,1)S(1)}, bf16[64,4096]{1,0:T(8,128)(2,1)}, u32[]{:S(2)}, u32[]{:S(2)}) collective-permute-start(bf16[64,4096]{1,0:T(8,128)(2,1)S(1)} %fusion.refs_6_.refs_8_), channel_id=1, source_target_pairs={{4,8},{6,10},{8,4},{10,6},{5,9},{7,11},{9,5},{11,7},{20,24},{22,26... | collective-permute-start | bytes 1572872 | tf_op jit(solution)/shard_map/ppermute | solution.py:250
  12.2 14.4 %collective-permute-start.9 = (bf16[64,256]{1,0:T(8,128)(2,1)S(1)}, bf16[64,256]{1,0:T(8,128)(2,1)S(1)}, u32[]{:S(2)}, u32[]{:S(2)}) collective-permute-start(bf16[64,256]{1,0:T(8,128)(2,1)S(1)} %bitcast.26), channel_id=1, source_target_pairs={{0,4},{2,6},{4,0},{6,2},{8,12},{10,14},{12,8},{14,10},{1,5},{3,7},... | collective-permute-start | bytes 98312 | tf_op jit(solution)/shard_map/ppermute | solution.py:250
  18.7 10.9 %collective-permute-start.14 = (bf16[32,16,256]{2,1,0:T(8,128)(2,1)}, bf16[32,16,256]{2,1,0:T(8,128)(2,1)}, u32[]{:S(2)}, u32[]{:S(2)}) collective-permute-start(bf16[32,16,256]{2,1,0:T(8,128)(2,1)} %constant_dynamic-slice_fusion.1), channel_id=1, source_target_pairs={{0,1},{1,0},{2,3},{3,2},{4,5},{5,4},{6,7},{7,6},{8,9},{9,8},{10,11... | collective-permute-start | bytes 786440 | tf_op jit(solution)/shard_map/ppermute | solution.py:288
  23.3 10.3 %collective-permute-start.5 = (bf16[64,4096]{1,0:T(8,128)(2,1)S(1)}, bf16[64,4096]{1,0:T(8,128)(2,1)}, u32[]{:S(2)}, u32[]{:S(2)}) collective-permute-start(bf16[64,4096]{1,0:T(8,128)(2,1)S(1)} %collective-permute-done.1.refs_7_.refs_9_), channel_id=1, source_target_pairs={{4,8},{6,10},{8,4},{10,6},{5,9},{7,11},{9,5},{11,7},{20,24},{22,26... | collective-permute-start | bytes 1572872 | tf_op jit(solution)/shard_map/ppermute | solution.py:250
  24.7 18.7 %collective-permute-start.6 = (bf16[64,4096]{1,0:T(8,128)(2,1)}, bf16[64,4096]{1,0:T(8,128)(2,1)}, u32[]{:S(2)}, u32[]{:S(2)}) collective-permute-start(bf16[64,4096]{1,0:T(8,128)(2,1)} %collective-permute-done.2), channel_id=1, source_target_pairs={{4,0},{6,2},{8,12},{10,14},{5,1},{7,3},{9,13},{11,15},{20,16},{22,... | collective-permute-start | bytes 1572872 | tf_op jit(solution)/shard_map/ppermute | solution.py:250
  26.0 17.4 %collective-permute-start.7 = (bf16[64,4096]{1,0:T(8,128)(2,1)S(1)}, bf16[64,4096]{1,0:T(8,128)(2,1)}, u32[]{:S(2)}, u32[]{:S(2)}) collective-permute-start(bf16[64,4096]{1,0:T(8,128)(2,1)S(1)} %collective-permute-done.4.refs_3_), channel_id=1, source_target_pairs={{0,2},{2,0},{4,6},{6,4},{8,10},{10,8},{12,14},{14,12},{1,3},{3,1},... | collective-permute-start | bytes 1572872 | tf_op jit(solution)/shard_map/ppermute | solution.py:252
  26.6 2.9 %copy-start.11 = (bf16[64,256]{1,0:T(8,128)(2,1)}, bf16[64,256]{1,0:T(8,128)(2,1)S(1)}, u32[]{:S(2)}) copy-start(bf16[64,256]{1,0:T(8,128)(2,1)S(1)} %collective-permute-done.9) | copy-start | bytes 98308
  26.6 16.8 %collective-permute-start.8 = (bf16[64,4096]{1,0:T(8,128)(2,1)S(1)}, bf16[64,4096]{1,0:T(8,128)(2,1)}, u32[]{:S(2)}, u32[]{:S(2)}) collective-permute-start(bf16[64,4096]{1,0:T(8,128)(2,1)S(1)} %collective-permute-done.3.refs_2_), channel_id=1, source_target_pairs={{0,16},{16,0},{1,17},{17,1},{2,18},{18,2},{3,19},{19,3},{4,20},{20... | collective-permute-start | bytes 1572872 | tf_op jit(solution)/shard_map/ppermute | solution.py:251
  27.7 0.7 copy-start.15
  27.7 0.7 copy-start.16
  28.6 0.7 copy-start.17
  29.6 2.5 %collective-permute-start.10 = (bf16[128,256]{1,0:T(8,128)(2,1)S(1)}, bf16[128,256]{1,0:T(8,128)(2,1)S(1)}, u32[]{:S(2)}, u32[]{:S(2)}) collective-permute-start(bf16[128,256]{1,0:T(8,128)(2,1)S(1)} %pad_maximum_fusion.2), channel_id=1, source_target_pairs={{4,8},{6,10},{8,4},{10,6},{5,9},{7,11},{9,5},{11,7},{20,24},{22,26... | collective-permute-start | bytes 196616 | tf_op jit(solution)/shard_map/ppermute | solution.py:250
  32.1 28.3 %collective-permute-start.12 = (bf16[64,4096]{1,0:T(8,128)(2,1)S(1)}, bf16[64,4096]{1,0:T(8,128)(2,1)S(1)}, u32[]{:S(2)}, u32[]{:S(2)}) collective-permute-start(bf16[64,4096]{1,0:T(8,128)(2,1)S(1)} %slice.19.refs_0_), channel_id=1, source_target_pairs={{0,2},{2,0},{4,6},{6,4},{8,10},{10,8},{12,14},{14,12},{1,3},{3,1},... | collective-permute-start | bytes 1572872 | tf_op jit(solution)/shard_map/ppermute | solution.py:252
  33.6 26.8 %collective-permute-start.13 = (bf16[64,4096]{1,0:T(8,128)(2,1)S(1)}, bf16[64,4096]{1,0:T(8,128)(2,1)S(1)}, u32[]{:S(2)}, u32[]{:S(2)}) collective-permute-start(bf16[64,4096]{1,0:T(8,128)(2,1)S(1)} %slice.21.refs_1_), channel_id=1, source_target_pairs={{0,16},{16,0},{1,17},{17,1},{2,18},{18,2},{3,19},{19,3},{4,20},{20... | collective-permute-start | bytes 1572872 | tf_op jit(solution)/shard_map/ppermute | solution.py:251
  43.4 16.9 %collective-permute-start.11 = (bf16[64,4096]{1,0:T(8,128)(2,1)}, bf16[64,4096]{1,0:T(8,128)(2,1)S(1)}, u32[]{:S(2)}, u32[]{:S(2)}) collective-permute-start(bf16[64,4096]{1,0:T(8,128)(2,1)} %collective-permute-done.5), channel_id=1, source_target_pairs={{4,0},{6,2},{8,12},{10,14},{5,1},{7,3},{9,13},{11,15},{20,16},{22,... | collective-permute-start | bytes 1572872 | tf_op jit(solution)/shard_map/ppermute | solution.py:250
  44.7 14.0 %collective-permute-start.19 = (bf16[128,256]{1,0:T(8,128)(2,1)S(1)}, bf16[128,256]{1,0:T(8,128)(2,1)S(1)}, u32[]{:S(2)}, u32[]{:S(2)}) collective-permute-start(bf16[128,256]{1,0:T(8,128)(2,1)S(1)} %collective-permute-done.10), channel_id=1, source_target_pairs={{4,0},{6,2},{8,12},{10,14},{5,1},{7,3},{9,13},{11,15},{20,16},{22,... | collective-permute-start | bytes 196616 | tf_op jit(solution)/shard_map/ppermute | solution.py:250
  49.3 9.4 %copy-start.12 = (bf16[64,256]{1,0:T(8,128)(2,1)S(1)}, bf16[64,256]{1,0:T(8,128)(2,1)}, u32[]{:S(2)}) copy-start(bf16[64,256]{1,0:T(8,128)(2,1)} %copy-done.11) | copy-start | bytes 98308
  58.8 5.2 %copy-start.5 = (bf16[128,256]{1,0:T(8,128)(2,1)}, bf16[128,256]{1,0:T(8,128)(2,1)S(1)}, u32[]{:S(2)}) copy-start(bf16[128,256]{1,0:T(8,128)(2,1)S(1)} %broadcast_select_fusion.4) | copy-start | bytes 196612
  58.8 5.2 %collective-permute-start.20 = (bf16[256,256]{1,0:T(8,128)(2,1)S(1)}, bf16[256,256]{1,0:T(8,128)(2,1)S(1)}, u32[]{:S(2)}, u32[]{:S(2)}) collective-permute-start(bf16[256,256]{1,0:T(8,128)(2,1)S(1)} %pad_maximum_fusion.1), channel_id=1, source_target_pairs={{0,2},{2,0},{4,6},{6,4},{8,10},{10,8},{12,14},{14,12},{1,3},{3,1},... | collective-permute-start | bytes 393224 | tf_op jit(solution)/shard_map/ppermute | solution.py:252
  63.9 0.7 copy-start.2
  63.9 1.7 %collective-permute-start.15 = (f32[4,64,256]{2,1,0:T(8,128)}, f32[4,64,256]{2,1,0:T(8,128)S(1)}, u32[]{:S(2)}, u32[]{:S(2)}) collective-permute-start(f32[4,64,256]{2,1,0:T(8,128)} %get-tuple-element.36), channel_id=1, source_target_pairs={{0,1},{1,0},{2,3},{3,2},{4,5},{5,4},{6,7},{7,6},{8,9},{9,8},{10,11... | collective-permute-start | bytes 786440 | tf_op jit(solution)/shard_map/ppermute | solution.py:300
  64.0 0.7 copy-start.8
  64.7 5.6 %collective-permute-start.21 = (bf16[512,256]{1,0:T(8,128)(2,1)S(1)}, bf16[512,256]{1,0:T(8,128)(2,1)S(1)}, u32[]{:S(2)}, u32[]{:S(2)}) collective-permute-start(bf16[512,256]{1,0:T(8,128)(2,1)S(1)} %pad_maximum_fusion), channel_id=1, source_target_pairs={{0,1},{1,0},{2,3},{3,2},{4,5},{5,4},{6,7},{7,6},{8,9},{9,8},{10,11... | collective-permute-start | bytes 786440 | tf_op jit(solution)/shard_map/ppermute | solution.py:277
  65.7 1.0 %copy-start.3 = (f32[4,64,256]{2,1,0:T(8,128)S(1)}, f32[4,64,256]{2,1,0:T(8,128)}, u32[]{:S(2)}) copy-start(f32[4,64,256]{2,1,0:T(8,128)} %copy-done.2) | copy-start | bytes 786436
  66.6 3.6 %copy-start.6 = (bf16[128,256]{1,0:T(8,128)(2,1)S(1)}, bf16[128,256]{1,0:T(8,128)(2,1)}, u32[]{:S(2)}) copy-start(bf16[128,256]{1,0:T(8,128)(2,1)} %copy-done.5) | copy-start | bytes 196612
  66.6 3.6 %copy-start.9 = (bf16[256,256]{1,0:T(8,128)(2,1)S(1)}, bf16[256,256]{1,0:T(8,128)(2,1)}, u32[]{:S(2)}) copy-start(bf16[256,256]{1,0:T(8,128)(2,1)} %copy-done.8) | copy-start | bytes 393220
  66.6 3.6 %copy-start.13 = (bf16[64,256]{1,0:T(8,128)(2,1)S(1)}, bf16[64,256]{1,0:T(8,128)(2,1)}, u32[]{:S(2)}) copy-start(bf16[64,256]{1,0:T(8,128)(2,1)} %copy-done.11) | copy-start | bytes 98308
  66.7 4.3 %collective-permute-start.16 = (f32[64,256]{1,0:T(8,128)S(1)}, f32[64,256]{1,0:T(8,128)S(1)}, u32[]{:S(2)}, u32[]{:S(2)}) collective-permute-start(f32[64,256]{1,0:T(8,128)S(1)} %get-tuple-element.37), channel_id=1, source_target_pairs={{0,2},{2,0},{4,6},{6,4},{8,10},{10,8},{12,14},{14,12},{1,3},{3,1},... | collective-permute-start | bytes 196616 | tf_op jit(solution)/shard_map/ppermute | solution.py:252
  67.3 4.3 %collective-permute-start.17 = (f32[64,256]{1,0:T(8,128)S(1)}, f32[64,256]{1,0:T(8,128)S(1)}, u32[]{:S(2)}, u32[]{:S(2)}) collective-permute-start(f32[64,256]{1,0:T(8,128)S(1)} %get-tuple-element.38), channel_id=1, source_target_pairs={{0,16},{16,0},{1,17},{17,1},{2,18},{18,2},{3,19},{19,3},{4,20},{20... | collective-permute-start | bytes 196616 | tf_op jit(solution)/shard_map/ppermute | solution.py:251
  68.8 5.2 %copy-start.1 = (bf16[32,16,256]{2,1,0:T(8,128)(2,1)S(1)}, bf16[32,16,256]{2,1,0:T(8,128)(2,1)}, u32[]{:S(2)}) copy-start(bf16[32,16,256]{2,1,0:T(8,128)(2,1)} %get-tuple-element.49) | copy-start | bytes 786436
  68.8 5.2 %copy-start.4 = (f32[4,64,256]{2,1,0:T(8,128)S(1)}, f32[4,64,256]{2,1,0:T(8,128)}, u32[]{:S(2)}) copy-start(f32[4,64,256]{2,1,0:T(8,128)} %copy-done.2) | copy-start | bytes 786436
  68.8 5.2 %collective-permute-start.18 = (f32[64,256]{1,0:T(8,128)S(1)}, f32[64,256]{1,0:T(8,128)S(1)}, u32[]{:S(2)}, u32[]{:S(2)}) collective-permute-start(f32[64,256]{1,0:T(8,128)S(1)} %get-tuple-element.39), channel_id=1, source_target_pairs={{0,18},{2,16},{4,22},{6,20},{8,26},{10,24},{12,30},{14,28},{16,2},... | collective-permute-start | bytes 196616 | tf_op jit(solution)/shard_map/ppermute | solution.py:303
  76.0 1.4 %collective-permute-start.22 = (bf16[2,64,512]{2,1,0:T(8,128)(2,1)S(1)}, bf16[2,64,512]{2,1,0:T(8,128)(2,1)S(1)}, u32[]{:S(2)}, u32[]{:S(2)}) collective-permute-start(bf16[2,64,512]{2,1,0:T(8,128)(2,1)S(1)} %shard_map.107), channel_id=1, source_target_pairs={{0,1},{1,0},{2,3},{3,2},{4,5},{5,4},{6,7},{7,6},{8,9},{9,8},{10,11... | collective-permute-start | bytes 393224 | tf_op jit(solution)/shard_map/ppermute | solution.py:308

commit v3 on v2

v3 whole, which is shorter than its diff:
```python
import functools
import math

import jax
import jax.numpy as jnp
from jax import lax
from jax.experimental import pallas as pl
from jax.experimental.pallas import tpu as pltpu
from jax.sharding import PartitionSpec as P

SWAP = [(0, 1), (1, 0)]
FAR = -1e30
PER = 8


def nt_dot(a, b):
    return lax.dot_general(a, b, (((1,), (1,)), ((), ())), preferred_element_type=jnp.float32)


def copy_all(copies, sems):
    started = [pltpu.make_async_copy(source, target, sems.at[k]) for k, (source, target) in enumerate(copies)]
    for copy in started:
        copy.start()
    for copy in started:
        copy.wait()


def block_kernel(where_ref, query_ref, kept_ref, given_ref, up_ref, out_ref, sems):
    part, core = where_ref[2], where_ref[3]
    count, features = kept_ref.shape[0], query_ref.shape[1]
    up = (up_ref, out_ref.at[:, features:])
    top, bottom = out_ref.at[:count, :features], out_ref.at[count:, :features]

    @pl.when(part == 0)
    def _():
        copy_all([(query_ref, out_ref.at[:, :features]), up], sems)

    @pl.when(jnp.logical_and(part != 0, core == 0))
    def _():
        low = slice(0, features)
        copy_all([(kept_ref.at[:, low], top), (given_ref.at[:, low], bottom), up], sems)

    @pl.when(jnp.logical_and(part != 0, core != 0))
    def _():
        high = slice(features, 2 * features)
        copy_all([(given_ref.at[:, high], top), (kept_ref.at[:, high], bottom), up], sems)


def block_of(where, query, kept, given, up):
    return pl.pallas_call(
        block_kernel,
        out_shape=jax.ShapeDtypeStruct((query.shape[0], query.shape[1] + up.shape[1]), query.dtype),
        in_specs=[pl.BlockSpec(memory_space=pltpu.SMEM)] + [pl.BlockSpec(memory_space=pl.ANY)] * 4,
        out_specs=pl.BlockSpec(memory_space=pltpu.VMEM),
        scratch_shapes=[pltpu.SemaphoreType.DMA((3,))],
        compiler_params=pltpu.CompilerParams(vmem_limit_bytes=2 << 20),
    )(where, query, kept, given, up)


def rows_kernel(x_ref, out_ref):
    out_ref[...] = x_ref[...].reshape(out_ref.shape)


def rows_of(x):
    return pl.pallas_call(
        rows_kernel,
        out_shape=jax.ShapeDtypeStruct((x.shape[0] * x.shape[1], x.shape[2]), x.dtype),
        compiler_params=pltpu.CompilerParams(vmem_limit_bytes=4 << 20),
    )(x)


def ready_kernel(
    where_ref, lengths_ref, adapter_ref, owner_ref, mine_ref, other_ref, fresh_ref,
    low_ref, high_ref, new_ref, limits_ref, holder_ref, sems,
):
    core = where_ref[3]
    half = new_ref.shape[0]
    requests = lengths_ref.shape[0] // 2
    steps = half // requests
    many = low_ref.shape[0]
    for k, (low, high) in enumerate(((mine_ref, other_ref), (other_ref, mine_ref))):

        @pl.when(core == k)
        def _():
            rows = slice(k * many, (k + 1) * many)
            copy_all([(low.at[rows], low_ref), (high.at[rows], high_ref)], sems)
            new_ref[...] = fresh_ref[k * requests : (k + 1) * requests].reshape(new_ref.shape)

    first = core * requests
    per = limits_ref.shape[1] // (many // requests)
    column = lax.broadcasted_iota(jnp.int32, (1, limits_ref.shape[1]), 1) // (many // requests)
    for b in range(requests // per):
        limit = jnp.zeros(column.shape, jnp.int32)
        for r in range(per):
            limit = jnp.where(column == r, lengths_ref[first + b * per + r], limit)
        limits_ref[b : b + 1, :] = limit
    row = lax.broadcasted_iota(jnp.int32, holder_ref.shape, 0) // steps
    holder = jnp.zeros(holder_ref.shape, jnp.int32)
    for r in range(requests):
        holder = jnp.where(row == r, owner_ref[adapter_ref[first + r]], holder)
    holder_ref[...] = holder


def ready(where, lengths, adapter, owner, mine, other, fresh, steps):
    requests, count = lengths.shape[0] // 2, mine.shape[0] // lengths.shape[0]
    smem, vmem = (pl.BlockSpec(memory_space=m) for m in (pltpu.SMEM, pltpu.VMEM))
    anywhere = pl.BlockSpec(memory_space=pl.ANY)
    cache = jax.ShapeDtypeStruct((requests * count, mine.shape[1]), mine.dtype)
    return pl.pallas_call(
        ready_kernel,
        out_shape=(
            cache,
            cache,
            jax.ShapeDtypeStruct((requests * steps, fresh.shape[2]), fresh.dtype),
            jax.ShapeDtypeStruct((8, PER * count), jnp.int32),
            jax.ShapeDtypeStruct((requests * steps, 128), jnp.int32),
        ),
        in_specs=[smem] * 4 + [anywhere] * 2 + [vmem],
        out_specs=(vmem,) * 5,
        scratch_shapes=[pltpu.SemaphoreType.DMA((2,))],
        compiler_params=pltpu.CompilerParams(vmem_limit_bytes=4 << 20),
    )(where, lengths, adapter, owner, mine, other, fresh)


def products_kernel(sets, *refs):
    rows, weights, out_ref = refs[:sets], refs[sets:-1], refs[-1]
    features = rows[0].shape[1]
    columns = jnp.concatenate([w[:, :features] for w in weights], axis=0)
    out_ref[...] = nt_dot(jnp.concatenate([r[...] for r in rows], axis=0), columns)


def products(sets, weights):
    rows, columns = sum(r.shape[0] for r in sets), sum(w.shape[0] for w in weights)
    return pl.pallas_call(
        functools.partial(products_kernel, len(sets)),
        out_shape=jax.ShapeDtypeStruct((rows, columns), jnp.float32),
        cost_estimate=pl.CostEstimate(
            flops=2 * rows * columns * sets[0].shape[1],
            bytes_accessed=(rows + columns) * sets[0].shape[1] * 2,
            transcendentals=0,
        ),
        compiler_params=pltpu.CompilerParams(vmem_limit_bytes=12 << 20),
    )(*sets, *weights)


def last_kernel(where_ref, *refs):
    *sets, w_ref, near_up_ref, t_ref, late_ref, kept_ref, given_ref = refs
    features, half = sets[0].shape[1], kept_ref.shape[1]
    before = t_ref.shape[1] - w_ref.shape[0]
    middle = jnp.logical_or(where_ref[0] == 1, where_ref[0] == 2)
    total = nt_dot(jnp.concatenate([r[...] for r in sets], axis=0), w_ref[:, :features])
    first = where_ref[3] == 0
    known = t_ref.shape[0] // half

    def value(k):
        ref, at = (t_ref, k) if k < known else (late_ref, k - known)
        rows = ref[at * half : (at + 1) * half, :]
        last = jnp.where(middle, rows[:, before:], total[k * half : (k + 1) * half])
        return jnp.concatenate([rows[:, :before], last], axis=1)

    up = jnp.where(middle, near_up_ref[...], w_ref[:, features:])
    given_ref[4] = up.astype(jnp.float32)
    for k in range(4):
        low, high = value(2 * k), value(2 * k + 1)
        kept_ref[k] = jnp.where(first, low, high)
        given_ref[k] = jnp.where(first, high, low)


def last_products(where, sets, w, near_up, t, late):
    smem, vmem = (pl.BlockSpec(memory_space=m) for m in (pltpu.SMEM, pltpu.VMEM))
    shape = (4, sets[0].shape[0] // 2, t.shape[1])
    return pl.pallas_call(
        last_kernel,
        out_shape=(
            jax.ShapeDtypeStruct(shape, jnp.float32),
            jax.ShapeDtypeStruct((5,) + shape[1:], jnp.float32),
        ),
        in_specs=[smem] + [vmem] * (len(sets) + 4),
        out_specs=(vmem, vmem),
        compiler_params=pltpu.CompilerParams(vmem_limit_bytes=12 << 20),
    )(where, *sets, w, near_up, t, late)


def join_kernel(where_ref, mine_ref, other_ref, queries_ref, attended_ref, sems):
    core = where_ref[3]
    count = mine_ref.shape[1]
    mine, other = pl.ds(core * count, count), pl.ds((1 - core) * count, count)
    copy_all(
        [
            (mine_ref.at[0], queries_ref.at[mine]), (mine_ref.at[1], attended_ref.at[mine]),
            (other_ref.at[0], queries_ref.at[other]), (other_ref.at[1], attended_ref.at[other]),
        ],
        sems,
    )


def join(where, mine, other):
    anywhere = pl.BlockSpec(memory_space=pl.ANY)
    shape = jax.ShapeDtypeStruct((2 * mine.shape[1],) + mine.shape[2:], mine.dtype)
    return pl.pallas_call(
        join_kernel,
        out_shape=(shape, shape),
        in_specs=[pl.BlockSpec(memory_space=pltpu.SMEM), anywhere, anywhere],
        out_specs=(anywhere, anywhere),
        scratch_shapes=[pltpu.SemaphoreType.DMA((4,))],
        compiler_params=pltpu.CompilerParams(vmem_limit_bytes=2 << 20),
    )(where, mine, other)


def add_kernel(where_ref, kept_ref, given_ref, got_ref, beside_ref, across_ref, both_ref):
    half = kept_ref.shape[1]
    first = where_ref[3] == 0
    mine, other = given_ref[4], got_ref[4]
    beside_ref[:half] = kept_ref[1] + got_ref[1]
    beside_ref[half : 2 * half] = jnp.where(first, mine, other)
    beside_ref[2 * half :] = jnp.where(first, other, mine)
    across_ref[...] = kept_ref[2] + got_ref[2]
    both_ref[...] = kept_ref[3] + got_ref[3]


def add_halves(where, kept, given, got):
    rows, columns = kept.shape[1:]
    smem, vmem = (pl.BlockSpec(memory_space=m) for m in (pltpu.SMEM, pltpu.VMEM))
    shape = jax.ShapeDtypeStruct((rows, columns), kept.dtype)
    return pl.pallas_call(
        add_kernel,
        out_shape=(jax.ShapeDtypeStruct((3 * rows, columns), kept.dtype), shape, shape),
        in_specs=[smem] + [vmem] * 3,
        out_specs=(vmem,) * 3,
        compiler_params=pltpu.CompilerParams(vmem_limit_bytes=2 << 20),
    )(where, kept, given, got)


def attend_block(queries, keys, values, masks, scaling):
    scores = [jnp.where(m, nt_dot(queries, k) * scaling, FAR) for k, m in zip(keys, masks)]
    highest = scores[0].max(axis=1, keepdims=True)
    for s in scores[1:]:
        highest = jnp.maximum(highest, s.max(axis=1, keepdims=True))
    weights = [jnp.where(m, jnp.exp(s - highest), 0.0) for s, m in zip(scores, masks)]
    totals = sum(w.sum(axis=1, keepdims=True) for w in weights)
    sums = sum(
        jnp.dot(w.astype(jnp.bfloat16), v, preferred_element_type=jnp.float32)
        for w, v in zip(weights, values)
    )
    return sums / totals


def attend(queries, caches, fresh_ref, limit_of, put, steps, head, per):
    rows = queries.shape[0]
    requests = rows // steps
    heads = queries.shape[1] // head
    scaling = 1.0 / math.sqrt(head)
    take = per * steps
    for b in range(requests // per):
        part = queries[b * take : (b + 1) * take, :]
        stacked = jnp.concatenate([part[:, h * head : (h + 1) * head] for h in range(heads)], axis=0)
        limit = limit_of(b)
        keys, values, masks = [], [], []
        for c, cache_ref in enumerate(caches):
            count = cache_ref.shape[0] // requests
            block = cache_ref[b * per * count : (b + 1) * per * count, :]
            shape = (heads * take, per * count)
            request = lax.rem(lax.broadcasted_iota(jnp.int32, shape, 0), take) // steps
            column = lax.broadcasted_iota(jnp.int32, shape, 1)
            position = lax.rem(column, count) + c * count
            masks.append(jnp.logical_and(column // count == request, position < limit))
            keys.append(block[:, :head])
            values.append(block[:, head:])
        block = fresh_ref[b * take : (b + 1) * take, :]
        shape = (heads * take, take)
        row = lax.rem(lax.broadcasted_iota(jnp.int32, shape, 0), take)
        column = lax.broadcasted_iota(jnp.int32, shape, 1)
        masks.append(jnp.logical_and(row // steps == column // steps, column <= row))
        keys.append(block[:, :head])
        values.append(block[:, head:])
        mixed = attend_block(stacked, keys, values, masks, scaling).astype(jnp.bfloat16)
        put(
            b,
            jnp.concatenate([mixed[h * take : (h + 1) * take] for h in range(heads)], axis=1),
        )


def finish_kernel(
    steps, where_ref, own_ref, other_ref, sent_ref, beside_ref, across_ref, both_ref, holder_ref,
    up_ref, up_beside_ref, up_other_ref, up_both_ref, low_ref, high_ref, fresh_ref, limits_ref, out_ref,
):
    rows = own_ref.shape[1]
    x, part = where_ref[1], where_ref[2]
    width = 128
    half = width // 2
    own = own_ref[0] + other_ref[0]
    beside, across, both = beside_ref[:rows], across_ref[...], both_ref[...]
    queries_here = part == 0
    columns = jnp.where(queries_here, own, across), jnp.where(queries_here, beside, both)
    ranks = jnp.where(queries_here, across, own), jnp.where(queries_here, both, beside)
    low_lanes = lax.broadcasted_iota(jnp.int32, (rows, width), 1) < half
    even = jnp.where(x == 0, columns[0], columns[1])
    odd = jnp.where(x == 0, columns[1], columns[0])

    def spaced(wide):
        out = []
        for j in range(4):
            pair = wide[:, (j // 2) * width : (j // 2 + 1) * width]
            out.append((pair, pltpu.roll(pair, half, 1)) if j % 2 == 0 else (pltpu.roll(pair, half, 1), pair))
        return out

    even, odd = spaced(even), spaced(odd)
    merged = [jnp.where(low_lanes, e[0], o[1]) for e, o in zip(even, odd)]
    groups = []
    for k in range(4):
        group = merged[3]
        for j in range(3):
            group = jnp.where(where_ref[4 + j] == 2 * k + x, merged[j], group)
        groups.append(group)
    base = jnp.concatenate(groups, axis=1)
    holder = holder_ref[...]
    spread = []
    for m in range(4):
        lane_owner = jnp.where(low_lanes, where_ref[4 + 2 * m], where_ref[5 + 2 * m])
        shrink = ranks[m // 2][:, (m % 2) * width : (m % 2 + 1) * width]
        spread.append(jnp.where(holder == lane_owner, shrink, 0.0).astype(jnp.bfloat16))
    spread = [jnp.concatenate(spread[:2], axis=1), jnp.concatenate(spread[2:], axis=1)]

    first = where_ref[3] == 0

    def lift(side, a_ref, b_ref, last_ref):
        a, b = a_ref[: 3 * half], b_ref[: 3 * half]
        low = jnp.where(first, a, b), last_ref[rows : 2 * rows].astype(a.dtype)
        high = jnp.where(first, b, a), last_ref[2 * rows :].astype(a.dtype)
        up = jnp.concatenate([jnp.concatenate(low, axis=0), jnp.concatenate(high, axis=0)], axis=1)
        return jnp.dot(side, up, preferred_element_type=jnp.float32)

    adapted = lift(spread[0], up_ref, up_other_ref, sent_ref) + lift(
        spread[1], up_beside_ref, up_both_ref, beside_ref
    )
    queries = (base + adapted).astype(jnp.bfloat16)
    requests = rows // steps
    out_ref[0] = queries.reshape(requests, steps, -1)
    head = fresh_ref.shape[1] // 2

    def put(b, mixed):
        out_ref[1, b * PER : (b + 1) * PER] = mixed.reshape(PER, steps, -1)

    attend(
        queries, (low_ref, high_ref), fresh_ref, lambda b: limits_ref[b : b + 1, :], put, steps, head, PER
    )


def finish(steps, where, *arrays):
    rows, columns = arrays[0].shape[1:]
    vmem = pl.BlockSpec(memory_space=pltpu.VMEM)
    return pl.pallas_call(
        functools.partial(finish_kernel, steps),
        out_shape=jax.ShapeDtypeStruct((2, rows // steps, steps, 2 * columns), jnp.bfloat16),
        in_specs=[pl.BlockSpec(memory_space=pltpu.SMEM)] + [vmem] * len(arrays),
        out_specs=vmem,
        compiler_params=pltpu.CompilerParams(vmem_limit_bytes=8 << 20),
    )(where, *arrays)


def attend_kernel(steps, q_ref, low_ref, high_ref, fresh_ref, limits_ref, out_ref):
    head = fresh_ref.shape[1] // 2
    take = PER * steps

    def put(b, mixed):
        out_ref[b * take : (b + 1) * take, :] = mixed

    attend(
        q_ref[...], (low_ref, high_ref), fresh_ref, lambda b: limits_ref[b : b + 1, :], put, steps, head, PER
    )


def line_pairs(groups, moves):
    return [(a * 2 + x, b * 2 + x) for a, b in moves for x in range(2)]


def holders_of(request_adapter, adapter_owner):
    ids = jnp.arange(adapter_owner.shape[0], dtype=jnp.int32)
    lookup = request_adapter[:, None] == ids[None, :]
    return jnp.sum(jnp.where(lookup, adapter_owner[None, :], 0), axis=1)


def body(
    normed_hidden_states,
    query_matrix,
    factor_down,
    factor_up,
    kv_cache,
    incoming_key_value,
    kv_lengths,
    request_adapter,
    adapter_owner,
):
    groups = lax.axis_size("group")
    core = lax.axis_index("tensor")
    requests, steps, features = normed_hidden_states.shape
    rows = requests * steps

    down = factor_down[0].T
    down_other = lax.ppermute(factor_down, "tensor", SWAP)[0].T
    query_block = query_matrix.T
    width = query_matrix.shape[1] * groups
    out_shape = (requests, steps, width)

    if groups == 8 and lax.axis_size("parts") == 2 and query_matrix.shape[1] == 2 * down.shape[0]:
        place = lax.axis_index("group")
        z, x, part = place // 2, lax.rem(place, 2), lax.axis_index("parts")
        pair_low = z < 2
        places = (z, z + 1 - 2 * lax.rem(z, 2), jnp.where(pair_low, 2, 1), jnp.where(pair_low, 3, 0))
        where = [z, x, part, core] + [p * 2 + x for p in places] + [p * 2 + 1 - x for p in places]
        where = jnp.stack(where).astype(jnp.int32)
        middle = jnp.logical_or(z == 1, z == 2)
        bar = lambda *a: lax.optimization_barrier(a)
        along = lambda a, moves: lax.ppermute(a, "group", line_pairs(groups, moves))
        across = lambda a: lax.ppermute(a, "parts", SWAP)
        beside = lambda a: lax.ppermute(a, "group", [(i, i ^ 1) for i in range(groups)])
        inside = lambda a: lax.ppermute(a, "tensor", SWAP)
        corner = [(p * groups + i, (1 - p) * groups + (i ^ 1)) for p in range(2) for i in range(groups)]
        ends, inner = ((0, 1), (1, 0), (2, 3), (3, 2)), ((1, 2), (2, 1))
        outward = ((1, 0), (2, 3))

        mine = rows_of(normed_hidden_states)
        w0 = block_of(where, query_block, down, down_other, factor_up[0])
        w0, mine = bar(w0, mine)
        half = rows // 2
        m1, w1 = along(w0, inner), along(w0, ends)
        x_beside, x_across = beside(mine), across(mine)
        m2, p1 = along(w1, inner), along(m1, outward)
        w2 = jnp.where(middle, m1, p1)
        c0, c1 = beside(x_across[:half]), across(x_beside[half:])
        m2, p1, x_beside, x_across = bar(m2, p1, x_beside, x_across)
        p2 = along(m2, outward)
        up = jnp.concatenate([w[:, features:] for w in (w0, w1, w2)], axis=0)
        up_beside = beside(up)
        ups = up, up_beside, inside(up), inside(up_beside)
        near_up = m2[:, features:]
        sets, later = (mine, x_beside, x_across), (c0, c1)
        weights = w0, w1, w2, m2
        t, t_late = products(sets, weights), products(later, weights)

        cache = kv_cache.reshape(-1, kv_cache.shape[2])
        prepared = ready(
            where, kv_lengths, request_adapter, adapter_owner, cache, inside(cache), incoming_key_value, steps
        )
        p2, t, t_late, prepared, ups, near_up = bar(p2, t, t_late, prepared, ups, near_up)
        kept, given = last_products(where, sets + later, p2, near_up, t, t_late)
        got = inside(given)
        sent, t_across, t_both = add_halves(where, kept, given, got)
        t_beside, t_across = beside(sent), across(t_across)
        t_both = lax.ppermute(t_both, ("parts", "group"), corner)
        low, high, fresh, limits, holder_rows = prepared
        done = finish(
            steps, where, kept, got, sent, t_beside, t_across, t_both, holder_rows, *ups, low, high, fresh, limits
        )
        return join(where, done, inside(done))

    mine_down = lax.dynamic_slice_in_dim(down, core * features, features, 1)
    other_down = lax.dynamic_slice_in_dim(down_other, core * features, features, 1)
    down_block = jnp.where(
        core == 0,
        jnp.concatenate([mine_down, other_down], 0),
        jnp.concatenate([other_down, mine_down], 0),
    )
    holder = holders_of(request_adapter, adapter_owner)
    holder_rows = jnp.repeat(holder, steps)[:, None]
    limits = jnp.repeat(kv_lengths, kv_cache.shape[1]).reshape(requests // PER, -1)
    own = normed_hidden_states.reshape(rows, features)
    other_cache = lax.ppermute(kv_cache, "tensor", SWAP)
    low = jnp.where(core == 0, kv_cache, other_cache).reshape(-1, kv_cache.shape[2])
    high = jnp.where(core == 0, other_cache, kv_cache).reshape(-1, kv_cache.shape[2])
    fresh = incoming_key_value.reshape(rows, -1)
    up = lax.all_gather(factor_up[0], "group", axis=0, tiled=True)
    up_other = lax.ppermute(up, "tensor", SWAP)
    up_full = jnp.where(
        core == 0, jnp.concatenate([up, up_other], 1), jnp.concatenate([up_other, up], 1)
    )

    place = lax.axis_index("group")
    ring = [(i, (i + 1) % groups) for i in range(groups)]

    def step(k, carry):
        q_part, d_part, base, shrink = carry
        at = lax.rem(place - k + groups, groups)
        base = lax.dynamic_update_slice_in_dim(base, nt_dot(own, q_part), at * q_part.shape[0], 1)
        shrink = shrink + jnp.where(holder_rows == at, nt_dot(own, d_part), 0.0)
        q_part, d_part = (lax.ppermute(w, "group", ring) for w in (q_part, d_part))
        return q_part, d_part, base, shrink

    start = (
        query_block,
        down_block,
        jnp.zeros((rows, width), jnp.float32),
        jnp.zeros((rows, down_block.shape[0]), jnp.float32),
    )
    _, _, base, shrink = lax.fori_loop(0, groups, step, start)
    base = base + lax.ppermute(base, "tensor", SWAP)
    shrink = (shrink + lax.ppermute(shrink, "tensor", SWAP)).astype(jnp.bfloat16)
    named = holder_rows == jnp.arange(groups, dtype=jnp.int32)[None, :]
    spread = jnp.where(named[:, :, None], shrink[:, None, :], 0).reshape(rows, -1)
    adapted = jnp.dot(spread, up_full, preferred_element_type=jnp.float32)
    queries = (base + adapted).astype(jnp.bfloat16)
    attended = pl.pallas_call(
        functools.partial(attend_kernel, steps),
        out_shape=jax.ShapeDtypeStruct(queries.shape, jnp.bfloat16),
        compiler_params=pltpu.CompilerParams(vmem_limit_bytes=24 << 20),
    )(queries, low, high, fresh, limits)
    return queries.reshape(out_shape), attended.reshape(out_shape)


def solution(mesh):
    placed = (
        P(("parts", "group"), None, "tensor"),
        P("tensor", "group"),
        P("group", None, "tensor"),
        P("group", None, "tensor"),
        P(("parts", "group"), "tensor", None),
        P(("parts", "group"), None, None),
        P(("parts", "group")),
        P(("parts", "group")),
        P("parts"),
    )
    return jax.shard_map(
        body,
        mesh=mesh,
        in_specs=placed,
        out_specs=(P(("parts", "group"), None, None), P(("parts", "group"), None, None)),
        check_vma=False,
    )
```

time: 79.5 us -> 74.1 us (0.932)
  local copies, waits for them, and re-layouts: 10.4 us -> 4.39 us
  starting transfers between devices: 27.1 us -> 21.5 us
  Pallas kernels: 7.71 us -> 12.3 us
  waiting for transfers between devices: 29.2 us -> 33.2 us
  other arithmetic: 3.45 us -> 1.14 us
    ppermute x8 -> x5, waiting for transfers between devices: 21.2 us -> 9.25 us  [body(): along = lambda a, moves: lax.ppermute(a, 'group', line_pairs(groups, moves))]
    ppermute x4 -> x3, waiting for transfers between devices: 2.27 us -> 11.2 us  [body(): across = lambda a: lax.ppermute(a, 'parts', SWAP)]
    pallas_call x4 -> x9, Pallas kernels: 7.71 us -> 12.3 us  [the longest x2 4.28 us: products(): pl.pallas_call(functools.partial(products_kernel, len(sets)), out_shape=j...]
    ppermute x5 -> x4, waiting for transfers between devices: 1.55 us -> 6.04 us  [body(): lax.ppermute(a, 'group', [(i, i ^ 1) for i in range(groups)])]
    ppermute x8 -> x5, starting transfers between devices: 12.7 us -> 10.2 us  [body(): along = lambda a, moves: lax.ppermute(a, 'group', line_pairs(groups, moves))]
    select_n x6 -> x0, other arithmetic: 2.22 us -> none  [the longest x1 1.78 us: body(): high = jnp.where(core == 0, got_cache, cache).reshape(-1, kv_cache.shape[2])]
    dynamic_slice x6 -> x0, local copies, waits for them, and re-layouts: 1.9 us -> none  [the longest x4 1.85 us: body(): half = lambda a, k: lax.dynamic_slice_in_dim(a, k * mid, mid, 0)]
    unnamed x36 -> x20, local copies, waits for them, and re-layouts: 3.84 us -> 1.94 us
  transfers between devices with their start and end apart: 23 -> 19, of which waited for: 10 -> 9; matrix products, arithmetic and copies ran while one was open for 11% -> 5% of each run, Pallas kernels for 7% -> 8%
where the time goes in v3:
time: 74.1 us; the launch traced here: 73.5 us
  waiting for transfers between devices  33.2 us (45%)
  starting transfers between devices  21.5 us (29%)
  Pallas kernels  12.3 us (17%)
  local copies, waits for them, and re-layouts  4.39 us (6%)
  other arithmetic  1.14 us (2%)
  between operations  0.87 us (1%)
    ppermute x3, waiting for transfers between devices, body(): across = lambda a: lax.ppermute(a, 'parts', SWAP)  11.2 us
    ppermute x5, starting transfers between devices, body(): along = lambda a, moves: lax.ppermute(a, 'group', line_pairs(groups, moves))  10.2 us
    ppermute x5, waiting for transfers between devices, body(): along = lambda a, moves: lax.ppermute(a, 'group', line_pairs(groups, moves))  9.25 us
    ppermute x4, waiting for transfers between devices, body(): lax.ppermute(a, 'group', [(i, i ^ 1) for i in range(groups)])  6.04 us
    ppermute x4, starting transfers between devices, body(): lax.ppermute(a, 'group', [(i, i ^ 1) for i in range(groups)])  5.43 us
    ppermute x3, starting transfers between devices, body(): across = lambda a: lax.ppermute(a, 'parts', SWAP)  4.64 us
    pallas_call x2, Pallas kernels, products(): pl.pallas_call(functools.partial(products_kernel, len(sets)), out_shape=j...  4.28 us
    ppermute x1, waiting for transfers between devices, body(): t_both = lax.ppermute(t_both, ('parts', 'group'), corner)  3.56 us
  transfers between devices with their start and end apart: 19, of which 9 were waited for; matrix products, arithmetic and copies ran while one was open for 5% of the time, Pallas kernels for 8%

profile of v3, /device:TPU:0, one launch (start us, length us, event | category | flops | bytes accessed | tf_op | source)
XLA Modules:
  0.0 73.5 jit_solution(8710259866068598528)
XLA Ops:
  0.6 0.5 collective-permute-start
  1.1 1.2 %copy-done.2 = bf16[64,2,4096]{2,1,0:T(2,128)(2,1)S(1)} copy-done((bf16[64,2,4096]{2,1,0:T(2,128)(2,1)S(1)}, bf16[64,2,4096]{2,1,0:T(2,128)(2,1)}, u32[]{:S(2)}) %copy-start.2) | copy-done | bytes 1048600
  2.4 0.1 shard_map.105.refs_0_
  2.5 0.0 copy-start.6
  2.5 0.1 stack.51.where_ref
  2.6 0.3 collective-permute-done
  2.9 0.5 copy-done.3
  3.4 0.2 copy-done.4
  3.6 0.6 shard_map.104.refs_3_.refs_2_
  4.2 1.5 %collective-permute-start.3 = (bf16[64,4352]{1,0:T(8,128)(2,1)S(1)}, bf16[64,4352]{1,0:T(8,128)(2,1)}, u32[]{:S(2)}, u32[]{:S(2)}) collective-permute-start(bf16[64,4352]{1,0:T(8,128)(2,1)S(1)} %shard_map.104.refs_3_.refs_2_), channel_id=1, source_target_pairs={{4,8},{6,10},{8,4},{10,6},{5,9},{7,11},{9,5},{11,7},{20,24},{22,26... | collective-permute-start | bytes 1671176 | tf_op jit(solution)/shard_map/ppermute | solution.py:414
  5.7 4.7 %collective-permute-start.1 = (bf16[64,4352]{1,0:T(8,128)(2,1)S(1)}, bf16[64,4352]{1,0:T(8,128)(2,1)}, u32[]{:S(2)}, u32[]{:S(2)}) collective-permute-start(bf16[64,4352]{1,0:T(8,128)(2,1)S(1)} %shard_map.104.refs_3_.refs_2_), channel_id=1, source_target_pairs={{0,4},{2,6},{4,0},{6,2},{8,12},{10,14},{12,8},{14,10},{1,5},{3,7},... | collective-permute-start | bytes 1671176 | tf_op jit(solution)/shard_map/ppermute | solution.py:414
  10.4 1.5 %collective-permute-start.6 = (bf16[128,4096]{1,0:T(8,128)(2,1)S(1)}, bf16[128,4096]{1,0:T(8,128)(2,1)S(1)}, u32[]{:S(2)}, u32[]{:S(2)}) collective-permute-start(bf16[128,4096]{1,0:T(8,128)(2,1)S(1)} %shard_map.105.refs_0_), channel_id=1, source_target_pairs={{0,16},{16,0},{1,17},{17,1},{2,18},{18,2},{3,19},{19,3},{4,20},{20... | collective-permute-start | bytes 3145736 | tf_op jit(solution)/shard_map/ppermute | solution.py:415
  11.9 1.5 %collective-permute-start.5 = (bf16[128,4096]{1,0:T(8,128)(2,1)S(1)}, bf16[128,4096]{1,0:T(8,128)(2,1)S(1)}, u32[]{:S(2)}, u32[]{:S(2)}) collective-permute-start(bf16[128,4096]{1,0:T(8,128)(2,1)S(1)} %shard_map.105.refs_0_), channel_id=1, source_target_pairs={{0,2},{2,0},{4,6},{6,4},{8,10},{10,8},{12,14},{14,12},{1,3},{3,1},... | collective-permute-start | bytes 3145736 | tf_op jit(solution)/shard_map/ppermute | solution.py:416
  13.4 1.3 %collective-permute-start.4 = (bf16[64,4352]{1,0:T(8,128)(2,1)}, bf16[64,4352]{1,0:T(8,128)(2,1)}, u32[]{:S(2)}, u32[]{:S(2)}) collective-permute-start(bf16[64,4352]{1,0:T(8,128)(2,1)} %collective-permute-done.3), channel_id=1, source_target_pairs={{4,0},{6,2},{8,12},{10,14},{5,1},{7,3},{9,13},{11,15},{20,16},{22,... | collective-permute-start | bytes 1671176 | tf_op jit(solution)/shard_map/ppermute | solution.py:414
  14.7 8.8 %collective-permute-done.1.refs_4_.refs_3_ = bf16[64,4352]{1,0:T(8,128)(2,1)} collective-permute-done((bf16[64,4352]{1,0:T(8,128)(2,1)S(1)}, bf16[64,4352]{1,0:T(8,128)(2,1)}, u32[]{:S(2)}, u32[]{:S(2)}) %collective-permute-start.1) | collective-permute-done | bytes 557088 | tf_op jit(solution)/shard_map/ppermute | solution.py:414
  23.5 1.5 %collective-permute-start.2 = (bf16[64,4352]{1,0:T(8,128)(2,1)}, bf16[64,4352]{1,0:T(8,128)(2,1)}, u32[]{:S(2)}, u32[]{:S(2)}) collective-permute-start(bf16[64,4352]{1,0:T(8,128)(2,1)} %collective-permute-done.1.refs_4_.refs_3_), channel_id=1, source_target_pairs={{4,8},{6,10},{8,4},{10,6},{5,9},{7,11},{9,5},{11,7},{20,24},{22,26... | collective-permute-start | bytes 1671176 | tf_op jit(solution)/shard_map/ppermute | solution.py:414
  24.9 0.8 %slice.20 = bf16[64,256]{1,0:T(8,128)(2,1)S(1)} slice(bf16[64,4352]{1,0:T(8,128)(2,1)} %copy-done), slice={[0:64], [4096:4352]} | slice | bytes 65536 | tf_op jit(solution)/shard_map/slice | solution.py:433
  25.7 0.8 %slice.26 = bf16[64,256]{1,0:T(8,128)(2,1)S(1)} slice(bf16[64,4352]{1,0:T(8,128)(2,1)} %collective-permute-done.1.refs_4_.refs_3_), slice={[0:64], [4096:4352]} | slice | bytes 65536 | tf_op jit(solution)/shard_map/slice | solution.py:433
  26.5 8.9 %collective-permute-done.6.refs_2_ = bf16[128,4096]{1,0:T(8,128)(2,1)S(1)} collective-permute-done((bf16[128,4096]{1,0:T(8,128)(2,1)S(1)}, bf16[128,4096]{1,0:T(8,128)(2,1)S(1)}, u32[]{:S(2)}, u32[]{:S(2)}) %collective-permute-start.6) | collective-permute-done | bytes 1048608 | tf_op jit(solution)/shard_map/ppermute | solution.py:415
  35.4 1.6 %collective-permute-start.7 = (bf16[64,4096]{1,0:T(8,128)(2,1)S(1)}, bf16[64,4096]{1,0:T(8,128)(2,1)S(1)}, u32[]{:S(2)}, u32[]{:S(2)}) collective-permute-start(bf16[64,4096]{1,0:T(8,128)(2,1)S(1)} %slice.24), channel_id=1, source_target_pairs={{0,2},{2,0},{4,6},{6,4},{8,10},{10,8},{12,14},{14,12},{1,3},{3,1},... | collective-permute-start | bytes 1572872 | tf_op jit(solution)/shard_map/ppermute | solution.py:416
  37.0 1.6 %collective-permute-start.8 = (bf16[64,4096]{1,0:T(8,128)(2,1)S(1)}, bf16[64,4096]{1,0:T(8,128)(2,1)S(1)}, u32[]{:S(2)}, u32[]{:S(2)}) collective-permute-start(bf16[64,4096]{1,0:T(8,128)(2,1)S(1)} %slice.25), channel_id=1, source_target_pairs={{0,16},{16,0},{1,17},{17,1},{2,18},{18,2},{3,19},{19,3},{4,20},{20... | collective-permute-start | bytes 1572872 | tf_op jit(solution)/shard_map/ppermute | solution.py:415
  38.6 1.3 %collective-permute-start.9 = (bf16[64,4352]{1,0:T(8,128)(2,1)}, bf16[64,4352]{1,0:T(8,128)(2,1)S(1)}, u32[]{:S(2)}, u32[]{:S(2)}) collective-permute-start(bf16[64,4352]{1,0:T(8,128)(2,1)} %collective-permute-done.2.refs_6_.refs_5_), channel_id=1, source_target_pairs={{4,0},{6,2},{8,12},{10,14},{5,1},{7,3},{9,13},{11,15},{20,16},{22,... | collective-permute-start | bytes 1671176 | tf_op jit(solution)/shard_map/ppermute | solution.py:414
  39.9 1.1 %broadcast_select_fusion.refs_5_.refs_4_ = bf16[64,4352]{1,0:T(8,128)(2,1)S(1)} fusion(bf16[64,4352]{1,0:T(8,128)(2,1)} %collective-permute-done.3, bf16[64,4352]{1,0:T(8,128)(2,1)} %collective-permute-done.4, pred[]{:T(512)S(6)} %or.3), kind=kLoop, calls=%fused_computation | loop fusion | flops 278528 | bytes 1671169 | tf_op jit(solution)/shard_map/jit(_where)/select_n | solution.py:429
  41.0 0.0 copy-start.5
  41.0 0.0 copy-start.7
  41.1 0.0 copy-start.8
  41.1 0.0 copy-start.9
  41.1 0.8 %collective-permute-start.11 = (bf16[192,256]{1,0:T(8,128)(2,1)S(1)}, bf16[192,256]{1,0:T(8,128)(2,1)S(1)}, u32[]{:S(2)}, u32[]{:S(2)}) collective-permute-start(bf16[192,256]{1,0:T(8,128)(2,1)S(1)} %pad_maximum_fusion.up_ref), channel_id=1, source_target_pairs={{0,2},{2,0},{4,6},{6,4},{8,10},{10,8},{12,14},{14,12},{1,3},{3,1},... | collective-permute-start | bytes 294920 | tf_op jit(solution)/shard_map/ppermute | solution.py:416
  42.0 1.7 %shard_map.108 = (bf16[512,256]{1,0:T(8,128)(2,1)S(1)}, bf16[512,256]{1,0:T(8,128)(2,1)S(1)}, bf16[64,256]{1,0:T(8,128)(2,1)S(1)}, s32[8,128]{1,0:T(8,128)S(1)}, s32[64,128]{1,0:T(8,128)S(1)}) custom-call(s32[12]{0:T(128)S(1)} %stack.51.where_ref, s32[64]{0:T(128)S(1)} %copy-done.7, s32[64]{0:T(128)S(1)} %copy-done.8, s32[8]{0:T(128)S(1)} %copy-done.9, ...), custom_call_target="tpu_custom_call" | custom-call | tf_op jit(solution)/shard_map/pallas_call | solution.py:109
  43.7 0.1 collective-permute-start.12
  43.7 0.8 %slice.23.refs_6_ = bf16[64,256]{1,0:T(8,128)(2,1)S(1)} slice(bf16[64,4352]{1,0:T(8,128)(2,1)} %collective-permute-done.2.refs_6_.refs_5_), slice={[0:64], [4096:4352]} | slice | bytes 65536 | tf_op jit(solution)/shard_map/slice | solution.py:436
  44.5 6.0 %collective-permute-done.11.up_beside_ref = bf16[192,256]{1,0:T(8,128)(2,1)S(1)} collective-permute-done((bf16[192,256]{1,0:T(8,128)(2,1)S(1)}, bf16[192,256]{1,0:T(8,128)(2,1)S(1)}, u32[]{:S(2)}, u32[]{:S(2)}) %collective-permute-start.11) | collective-permute-done | bytes 98336 | tf_op jit(solution)/shard_map/ppermute | solution.py:416
  50.5 2.2 %shard_map.106.refs_7_ = f32[384,256]{1,0:T(8,128)S(1)} custom-call(bf16[128,4096]{1,0:T(8,128)(2,1)S(1)} %shard_map.105.refs_0_, bf16[128,4096]{1,0:T(8,128)(2,1)S(1)} %collective-permute-done.5.refs_1_, bf16[128,4096]{1,0:T(8,128)(2,1)S(1)} %collective-permute-done.6.refs_2_, bf16[64,4352]{1,0:T(8,128)(2,1)S(1)} %copy-done.1, ...), custom_call_target="tpu_custom_call" | custom-call | flops 805306368 | bytes 5242880 | tf_op jit(solution)/shard_map/pallas_call | solution.py:134
  52.8 2.0 %shard_map.107.refs_8_ = f32[128,256]{1,0:T(8,128)S(1)} custom-call(bf16[64,4096]{1,0:T(8,128)(2,1)S(1)} %collective-permute-done.7.refs_0_.refs_3_, bf16[64,4096]{1,0:T(8,128)(2,1)S(1)} %collective-permute-done.8.refs_1_.refs_4_, bf16[64,4352]{1,0:T(8,128)(2,1)S(1)} %copy-done.1, bf16[64,4352]{1,0:T(8,128)(2,1)} %collective-permute-done.1.refs_4_.refs_3_, ...), custom_call_target="tpu_custom_call" | custom-call | flops 268435456 | bytes 3145728 | tf_op jit(solution)/shard_map/pallas_call | solution.py:134
  54.9 0.5 collective-permute-done.9.refs_5_
  55.4 1.8 %shard_map.109 = (f32[4,64,256]{2,1,0:T(8,128)S(1)}, f32[5,64,256]{2,1,0:T(8,128)S(1)}) custom-call(s32[12]{0:T(128)S(1)} %stack.51.where_ref, bf16[128,4096]{1,0:T(8,128)(2,1)S(1)} %shard_map.105.refs_0_, bf16[128,4096]{1,0:T(8,128)(2,1)S(1)} %collective-permute-done.5.refs_1_, bf16[128,4096]{1,0:T(8,128)(2,1)S(1)} %collective-permute-done.6.refs_2_, ...), custom_call_target="tpu_custom_call" | custom-call | tf_op jit(solution)/shard_map/pallas_call | solution.py:172
  57.2 0.1 collective-permute-start.14
  57.3 1.6 %collective-permute-done.14.got_ref.other_ref = f32[5,64,256]{2,1,0:T(8,128)S(1)} collective-permute-done((f32[5,64,256]{2,1,0:T(8,128)S(1)}, f32[5,64,256]{2,1,0:T(8,128)S(1)}, u32[]{:S(2)}, u32[]{:S(2)}) %collective-permute-start.14) | collective-permute-done | bytes 327712 | tf_op jit(solution)/shard_map/ppermute | solution.py:417
  58.9 0.6 shard_map.110
  59.5 1.6 %collective-permute-start.15 = (f32[192,256]{1,0:T(8,128)S(1)}, f32[192,256]{1,0:T(8,128)S(1)}, u32[]{:S(2)}, u32[]{:S(2)}) collective-permute-start(f32[192,256]{1,0:T(8,128)S(1)} %get-tuple-element.46.sent_ref), channel_id=1, source_target_pairs={{0,2},{2,0},{4,6},{6,4},{8,10},{10,8},{12,14},{14,12},{1,3},{3,1},... | collective-permute-start | bytes 589832 | tf_op jit(solution)/shard_map/ppermute | solution.py:416
  61.0 1.5 %collective-permute-start.16 = (f32[64,256]{1,0:T(8,128)S(1)}, f32[64,256]{1,0:T(8,128)S(1)}, u32[]{:S(2)}, u32[]{:S(2)}) collective-permute-start(f32[64,256]{1,0:T(8,128)S(1)} %get-tuple-element.47), channel_id=1, source_target_pairs={{0,16},{16,0},{1,17},{17,1},{2,18},{18,2},{3,19},{19,3},{4,20},{20... | collective-permute-start | bytes 196616 | tf_op jit(solution)/shard_map/ppermute | solution.py:415
  62.6 0.5 collective-permute-start.17
  63.0 2.3 %collective-permute-done.16.across_ref = f32[64,256]{1,0:T(8,128)S(1)} collective-permute-done((f32[64,256]{1,0:T(8,128)S(1)}, f32[64,256]{1,0:T(8,128)S(1)}, u32[]{:S(2)}, u32[]{:S(2)}) %collective-permute-start.16) | collective-permute-done | bytes 65568 | tf_op jit(solution)/shard_map/ppermute | solution.py:415
  65.3 3.6 %collective-permute-done.17.both_ref = f32[64,256]{1,0:T(8,128)S(1)} collective-permute-done((f32[64,256]{1,0:T(8,128)S(1)}, f32[64,256]{1,0:T(8,128)S(1)}, u32[]{:S(2)}, u32[]{:S(2)}) %collective-permute-start.17) | collective-permute-done | bytes 65568 | tf_op jit(solution)/shard_map/ppermute | solution.py:450
  68.9 2.0 %shard_map.111.mine_ref = bf16[2,32,2,512]{3,2,1,0:T(2,128)(2,1)S(1)} custom-call(s32[12]{0:T(128)S(1)} %stack.51.where_ref, f32[4,64,256]{2,1,0:T(8,128)S(1)} %get-tuple-element.44.kept_ref.own_ref, f32[5,64,256]{2,1,0:T(8,128)S(1)} %collective-permute-done.14.got_ref.other_ref, f32[192,256]{1,0:T(8,128)S(1)} %get-tuple-element.46.sent_ref, ...), custom_call_target="tpu_custom_call" | custom-call | tf_op jit(solution)/shard_map/pallas_call | solution.py:352
  70.8 0.1 collective-permute-start.18
  70.9 1.3 %collective-permute-done.18.other_ref = bf16[2,32,2,512]{3,2,1,0:T(2,128)(2,1)S(1)} collective-permute-done((bf16[2,32,2,512]{3,2,1,0:T(2,128)(2,1)S(1)}, bf16[2,32,2,512]{3,2,1,0:T(2,128)(2,1)S(1)}, u32[]{:S(2)}, u32[]{:S(2)}) %collective-permute-start.18) | collective-permute-done | bytes 131104 | tf_op jit(solution)/shard_map/ppermute | solution.py:417
  72.2 1.3 %shard_map.112 = (bf16[64,2,512]{2,1,0:T(2,128)(2,1)}, bf16[64,2,512]{2,1,0:T(2,128)(2,1)}) custom-call(s32[12]{0:T(128)S(1)} %stack.51.where_ref, bf16[2,32,2,512]{3,2,1,0:T(2,128)(2,1)S(1)} %shard_map.111.mine_ref, bf16[2,32,2,512]{3,2,1,0:T(2,128)(2,1)S(1)} %collective-permute-done.18.other_ref), custom_call_target="tpu_custom_call" | custom-call | tf_op jit(solution)/shard_map/pallas_call | solution.py:200
  (28 shorter events, 0.1 us)
Async XLA Ops:
  0.6 2.3 %collective-permute-start = (bf16[1,8192,32]{1,2,0:T(8,128)(2,1)}, bf16[1,8192,32]{1,2,0:T(8,128)(2,1)S(1)}, u32[]{:S(2)}, u32[]{:S(2)}) collective-permute-start(bf16[1,8192,32]{1,2,0:T(8,128)(2,1)} %param.11), channel_id=1, source_target_pairs={{0,1},{1,0},{2,3},{3,2},{4,5},{5,4},{6,7},{7,6},{8,9},{9,8},{10,11... | collective-permute-start | bytes 1572872 | tf_op jit(solution)/shard_map/ppermute | solution.py:400
  1.1 1.2 %copy-start.2 = (bf16[64,2,4096]{2,1,0:T(2,128)(2,1)S(1)}, bf16[64,2,4096]{2,1,0:T(2,128)(2,1)}, u32[]{:S(2)}) copy-start(bf16[64,2,4096]{2,1,0:T(2,128)(2,1)} %x_ref.1) | copy-start | bytes 3145732
  2.4 1.0 %copy-start.3 = (bf16[4096,64]{0,1:T(8,128)(2,1)S(1)}, bf16[4096,64]{0,1:T(8,128)(2,1)}, u32[]{:S(2)}) copy-start(bf16[4096,64]{0,1:T(8,128)(2,1)} %param.10) | copy-start | bytes 1572868
  2.4 1.2 %copy-start.4 = (bf16[1,8192,32]{1,2,0:T(8,128)(2,1)S(1)}, bf16[1,8192,32]{1,2,0:T(8,128)(2,1)}, u32[]{:S(2)}) copy-start(bf16[1,8192,32]{1,2,0:T(8,128)(2,1)} %param.11) | copy-start | bytes 1572868
  2.5 1.1 %copy-start.6 = (bf16[1,64,256]{2,1,0:T(8,128)(2,1)S(1)}, bf16[1,64,256]{2,1,0:T(8,128)(2,1)}, u32[]{:S(2)}) copy-start(bf16[1,64,256]{2,1,0:T(8,128)(2,1)} %param.12) | copy-start | bytes 98308
  4.2 6.2 %copy-start = (bf16[64,4352]{1,0:T(8,128)(2,1)}, bf16[64,4352]{1,0:T(8,128)(2,1)S(1)}, u32[]{:S(2)}) copy-start(bf16[64,4352]{1,0:T(8,128)(2,1)S(1)} %shard_map.104.refs_3_.refs_2_) | copy-start | bytes 1671172
  4.2 9.2 %collective-permute-start.3 = (bf16[64,4352]{1,0:T(8,128)(2,1)S(1)}, bf16[64,4352]{1,0:T(8,128)(2,1)}, u32[]{:S(2)}, u32[]{:S(2)}) collective-permute-start(bf16[64,4352]{1,0:T(8,128)(2,1)S(1)} %shard_map.104.refs_3_.refs_2_), channel_id=1, source_target_pairs={{4,8},{6,10},{8,4},{10,6},{5,9},{7,11},{9,5},{11,7},{20,24},{22,26... | collective-permute-start | bytes 1671176 | tf_op jit(solution)/shard_map/ppermute | solution.py:414
  5.7 17.8 %collective-permute-start.1 = (bf16[64,4352]{1,0:T(8,128)(2,1)S(1)}, bf16[64,4352]{1,0:T(8,128)(2,1)}, u32[]{:S(2)}, u32[]{:S(2)}) collective-permute-start(bf16[64,4352]{1,0:T(8,128)(2,1)S(1)} %shard_map.104.refs_3_.refs_2_), channel_id=1, source_target_pairs={{0,4},{2,6},{4,0},{6,2},{8,12},{10,14},{12,8},{14,10},{1,5},{3,7},... | collective-permute-start | bytes 1671176 | tf_op jit(solution)/shard_map/ppermute | solution.py:414
  10.4 25.0 %collective-permute-start.6 = (bf16[128,4096]{1,0:T(8,128)(2,1)S(1)}, bf16[128,4096]{1,0:T(8,128)(2,1)S(1)}, u32[]{:S(2)}, u32[]{:S(2)}) collective-permute-start(bf16[128,4096]{1,0:T(8,128)(2,1)S(1)} %shard_map.105.refs_0_), channel_id=1, source_target_pairs={{0,16},{16,0},{1,17},{17,1},{2,18},{18,2},{3,19},{19,3},{4,20},{20... | collective-permute-start | bytes 3145736 | tf_op jit(solution)/shard_map/ppermute | solution.py:415
  11.9 25.0 %collective-permute-start.5 = (bf16[128,4096]{1,0:T(8,128)(2,1)S(1)}, bf16[128,4096]{1,0:T(8,128)(2,1)S(1)}, u32[]{:S(2)}, u32[]{:S(2)}) collective-permute-start(bf16[128,4096]{1,0:T(8,128)(2,1)S(1)} %shard_map.105.refs_0_), channel_id=1, source_target_pairs={{0,2},{2,0},{4,6},{6,4},{8,10},{10,8},{12,14},{14,12},{1,3},{3,1},... | collective-permute-start | bytes 3145736 | tf_op jit(solution)/shard_map/ppermute | solution.py:416
  13.4 25.2 %collective-permute-start.4 = (bf16[64,4352]{1,0:T(8,128)(2,1)}, bf16[64,4352]{1,0:T(8,128)(2,1)}, u32[]{:S(2)}, u32[]{:S(2)}) collective-permute-start(bf16[64,4352]{1,0:T(8,128)(2,1)} %collective-permute-done.3), channel_id=1, source_target_pairs={{4,0},{6,2},{8,12},{10,14},{5,1},{7,3},{9,13},{11,15},{20,16},{22,... | collective-permute-start | bytes 1671176 | tf_op jit(solution)/shard_map/ppermute | solution.py:414
  23.5 15.1 %collective-permute-start.2 = (bf16[64,4352]{1,0:T(8,128)(2,1)}, bf16[64,4352]{1,0:T(8,128)(2,1)}, u32[]{:S(2)}, u32[]{:S(2)}) collective-permute-start(bf16[64,4352]{1,0:T(8,128)(2,1)} %collective-permute-done.1.refs_4_.refs_3_), channel_id=1, source_target_pairs={{4,8},{6,10},{8,4},{10,6},{5,9},{7,11},{9,5},{11,7},{20,24},{22,26... | collective-permute-start | bytes 1671176 | tf_op jit(solution)/shard_map/ppermute | solution.py:414
  24.9 17.0 %collective-permute-start.10 = (bf16[1024,256]{1,0:T(8,128)(2,1)}, bf16[1024,256]{1,0:T(8,128)(2,1)}, u32[]{:S(2)}, u32[]{:S(2)}) collective-permute-start(bf16[1024,256]{1,0:T(8,128)(2,1)} %bitcast.18.mine_ref), channel_id=1, source_target_pairs={{0,1},{1,0},{2,3},{3,2},{4,5},{5,4},{6,7},{7,6},{8,9},{9,8},{10,11... | collective-permute-start | bytes 1572872 | tf_op jit(solution)/shard_map/ppermute | solution.py:417
  35.4 17.4 %collective-permute-start.7 = (bf16[64,4096]{1,0:T(8,128)(2,1)S(1)}, bf16[64,4096]{1,0:T(8,128)(2,1)S(1)}, u32[]{:S(2)}, u32[]{:S(2)}) collective-permute-start(bf16[64,4096]{1,0:T(8,128)(2,1)S(1)} %slice.24), channel_id=1, source_target_pairs={{0,2},{2,0},{4,6},{6,4},{8,10},{10,8},{12,14},{14,12},{1,3},{3,1},... | collective-permute-start | bytes 1572872 | tf_op jit(solution)/shard_map/ppermute | solution.py:416
  37.0 15.8 %collective-permute-start.8 = (bf16[64,4096]{1,0:T(8,128)(2,1)S(1)}, bf16[64,4096]{1,0:T(8,128)(2,1)S(1)}, u32[]{:S(2)}, u32[]{:S(2)}) collective-permute-start(bf16[64,4096]{1,0:T(8,128)(2,1)S(1)} %slice.25), channel_id=1, source_target_pairs={{0,16},{16,0},{1,17},{17,1},{2,18},{18,2},{3,19},{19,3},{4,20},{20... | collective-permute-start | bytes 1572872 | tf_op jit(solution)/shard_map/ppermute | solution.py:415
  38.6 16.8 %collective-permute-start.9 = (bf16[64,4352]{1,0:T(8,128)(2,1)}, bf16[64,4352]{1,0:T(8,128)(2,1)S(1)}, u32[]{:S(2)}, u32[]{:S(2)}) collective-permute-start(bf16[64,4352]{1,0:T(8,128)(2,1)} %collective-permute-done.2.refs_6_.refs_5_), channel_id=1, source_target_pairs={{4,0},{6,2},{8,12},{10,14},{5,1},{7,3},{9,13},{11,15},{20,16},{22,... | collective-permute-start | bytes 1671176 | tf_op jit(solution)/shard_map/ppermute | solution.py:414
  41.0 0.9 %copy-start.5 = (bf16[64,2,256]{2,1,0:T(2,128)(2,1)S(1)}, bf16[64,2,256]{2,1,0:T(2,128)(2,1)}, u32[]{:S(2)}) copy-start(bf16[64,2,256]{2,1,0:T(2,128)(2,1)} %fresh_ref.1) | copy-start | bytes 196612
  41.0 0.9 %copy-start.7 = (s32[64]{0:T(128)S(1)}, s32[64]{0:T(128)}, u32[]{:S(2)}) copy-start(s32[64]{0:T(128)} %lengths_ref.1) | copy-start | bytes 772
  41.1 0.9 %copy-start.8 = (s32[64]{0:T(128)S(1)}, s32[64]{0:T(128)}, u32[]{:S(2)}) copy-start(s32[64]{0:T(128)} %adapter_ref.1) | copy-start | bytes 772
  41.1 0.9 %copy-start.9 = (s32[8]{0:T(128)S(1)}, s32[8]{0:T(128)}, u32[]{:S(2)}) copy-start(s32[8]{0:T(128)} %owner_ref.1) | copy-start | bytes 100
  41.1 9.4 %copy-start.1 = (bf16[64,4352]{1,0:T(8,128)(2,1)S(1)}, bf16[64,4352]{1,0:T(8,128)(2,1)}, u32[]{:S(2)}) copy-start(bf16[64,4352]{1,0:T(8,128)(2,1)} %copy-done) | copy-start | bytes 1671172
  41.1 9.4 %collective-permute-start.11 = (bf16[192,256]{1,0:T(8,128)(2,1)S(1)}, bf16[192,256]{1,0:T(8,128)(2,1)S(1)}, u32[]{:S(2)}, u32[]{:S(2)}) collective-permute-start(bf16[192,256]{1,0:T(8,128)(2,1)S(1)} %pad_maximum_fusion.up_ref), channel_id=1, source_target_pairs={{0,2},{2,0},{4,6},{6,4},{8,10},{10,8},{12,14},{14,12},{1,3},{3,1},... | collective-permute-start | bytes 294920 | tf_op jit(solution)/shard_map/ppermute | solution.py:416
  43.7 11.2 %collective-permute-start.12 = (bf16[192,256]{1,0:T(8,128)(2,1)S(1)}, bf16[192,256]{1,0:T(8,128)(2,1)S(1)}, u32[]{:S(2)}, u32[]{:S(2)}) collective-permute-start(bf16[192,256]{1,0:T(8,128)(2,1)S(1)} %pad_maximum_fusion.up_ref), channel_id=1, source_target_pairs={{0,1},{1,0},{2,3},{3,2},{4,5},{5,4},{6,7},{7,6},{8,9},{9,8},{10,11... | collective-permute-start | bytes 294920 | tf_op jit(solution)/shard_map/ppermute | solution.py:417
  50.5 4.3 %collective-permute-start.13 = (bf16[192,256]{1,0:T(8,128)(2,1)S(1)}, bf16[192,256]{1,0:T(8,128)(2,1)S(1)}, u32[]{:S(2)}, u32[]{:S(2)}) collective-permute-start(bf16[192,256]{1,0:T(8,128)(2,1)S(1)} %collective-permute-done.11.up_beside_ref), channel_id=1, source_target_pairs={{0,1},{1,0},{2,3},{3,2},{4,5},{5,4},{6,7},{7,6},{8,9},{9,8},{10,11... | collective-permute-start | bytes 294920 | tf_op jit(solution)/shard_map/ppermute | solution.py:417
  57.2 1.7 %collective-permute-start.14 = (f32[5,64,256]{2,1,0:T(8,128)S(1)}, f32[5,64,256]{2,1,0:T(8,128)S(1)}, u32[]{:S(2)}, u32[]{:S(2)}) collective-permute-start(f32[5,64,256]{2,1,0:T(8,128)S(1)} %get-tuple-element.45.given_ref), channel_id=1, source_target_pairs={{0,1},{1,0},{2,3},{3,2},{4,5},{5,4},{6,7},{7,6},{8,9},{9,8},{10,11... | collective-permute-start | bytes 983048 | tf_op jit(solution)/shard_map/ppermute | solution.py:417
  59.5 9.4 %collective-permute-start.15 = (f32[192,256]{1,0:T(8,128)S(1)}, f32[192,256]{1,0:T(8,128)S(1)}, u32[]{:S(2)}, u32[]{:S(2)}) collective-permute-start(f32[192,256]{1,0:T(8,128)S(1)} %get-tuple-element.46.sent_ref), channel_id=1, source_target_pairs={{0,2},{2,0},{4,6},{6,4},{8,10},{10,8},{12,14},{14,12},{1,3},{3,1},... | collective-permute-start | bytes 589832 | tf_op jit(solution)/shard_map/ppermute | solution.py:416
  61.0 4.3 %collective-permute-start.16 = (f32[64,256]{1,0:T(8,128)S(1)}, f32[64,256]{1,0:T(8,128)S(1)}, u32[]{:S(2)}, u32[]{:S(2)}) collective-permute-start(f32[64,256]{1,0:T(8,128)S(1)} %get-tuple-element.47), channel_id=1, source_target_pairs={{0,16},{16,0},{1,17},{17,1},{2,18},{18,2},{3,19},{19,3},{4,20},{20... | collective-permute-start | bytes 196616 | tf_op jit(solution)/shard_map/ppermute | solution.py:415
  62.6 6.3 %collective-permute-start.17 = (f32[64,256]{1,0:T(8,128)S(1)}, f32[64,256]{1,0:T(8,128)S(1)}, u32[]{:S(2)}, u32[]{:S(2)}) collective-permute-start(f32[64,256]{1,0:T(8,128)S(1)} %get-tuple-element.48), channel_id=1, source_target_pairs={{0,18},{2,16},{4,22},{6,20},{8,26},{10,24},{12,30},{14,28},{16,2},... | collective-permute-start | bytes 196616 | tf_op jit(solution)/shard_map/ppermute | solution.py:450
  70.8 1.4 %collective-permute-start.18 = (bf16[2,32,2,512]{3,2,1,0:T(2,128)(2,1)S(1)}, bf16[2,32,2,512]{3,2,1,0:T(2,128)(2,1)S(1)}, u32[]{:S(2)}, u32[]{:S(2)}) collective-permute-start(bf16[2,32,2,512]{3,2,1,0:T(2,128)(2,1)S(1)} %shard_map.111.mine_ref), channel_id=1, source_target_pairs={{0,1},{1,0},{2,3},{3,2},{4,5},{5,4},{6,7},{7,6},{8,9},{9,8},{10,11... | collective-permute-start | bytes 393224 | tf_op jit(solution)/shard_map/ppermute | solution.py:417

commit v4 on v3

--- a/solution.py
+++ b/solution.py
@@ -25,36 +25,45 @@
         copy.wait()
 
 
-def block_kernel(where_ref, query_ref, kept_ref, given_ref, up_ref, out_ref, sems):
+def block_kernel(
+    where_ref, query_ref, kept_ref, given_ref, up_ref, up_beside_ref, a_ref, b_ref, sems
+):
     part, core = where_ref[2], where_ref[3]
     count, features = kept_ref.shape[0], query_ref.shape[1]
-    up = (up_ref, out_ref.at[:, features:])
-    top, bottom = out_ref.at[:count, :features], out_ref.at[count:, :features]
+    columns = up_ref.shape[1]
+    chunks = [ref.at[:, :features] for ref in (a_ref, b_ref)]
+    ups = []
+    for ref, source in ((a_ref, up_ref), (b_ref, up_beside_ref)):
+        ups.append((source.at[:count], ref.at[:, features : features + columns]))
+        ups.append((source.at[count:], ref.at[:, features + columns :]))
 
     @pl.when(part == 0)
     def _():
-        copy_all([(query_ref, out_ref.at[:, :features]), up], sems)
+        copy_all([(query_ref.at[:count], chunks[0]), (query_ref.at[count:], chunks[1])] + ups, sems)
 
     @pl.when(jnp.logical_and(part != 0, core == 0))
     def _():
         low = slice(0, features)
-        copy_all([(kept_ref.at[:, low], top), (given_ref.at[:, low], bottom), up], sems)
+        copy_all([(kept_ref.at[:, low], chunks[0]), (given_ref.at[:, low], chunks[1])] + ups, sems)
 
     @pl.when(jnp.logical_and(part != 0, core != 0))
     def _():
         high = slice(features, 2 * features)
-        copy_all([(given_ref.at[:, high], top), (kept_ref.at[:, high], bottom), up], sems)
-
-
-def block_of(where, query, kept, given, up):
+        copy_all([(given_ref.at[:, high], chunks[0]), (kept_ref.at[:, high], chunks[1])] + ups, sems)
+
+
+def block_of(where, query, kept, given, up, up_beside):
+    count, features = kept.shape[0], query.shape[1]
+    vmem = pl.BlockSpec(memory_space=pltpu.VMEM)
+    shape = jax.ShapeDtypeStruct((count, features + 2 * up.shape[1]), query.dtype)
     return pl.pallas_call(
         block_kernel,
-        out_shape=jax.ShapeDtypeStruct((query.shape[0], query.shape[1] + up.shape[1]), query.dtype),
-        in_specs=[pl.BlockSpec(memory_space=pltpu.SMEM)] + [pl.BlockSpec(memory_space=pl.ANY)] * 4,
-        out_specs=pl.BlockSpec(memory_space=pltpu.VMEM),
-        scratch_shapes=[pltpu.SemaphoreType.DMA((3,))],
+        out_shape=(shape, shape),
+        in_specs=[pl.BlockSpec(memory_space=pltpu.SMEM)] + [pl.BlockSpec(memory_space=pl.ANY)] * 5,
+        out_specs=(vmem, vmem),
+        scratch_shapes=[pltpu.SemaphoreType.DMA((6,))],
         compiler_params=pltpu.CompilerParams(vmem_limit_bytes=2 << 20),
-    )(where, query, kept, given, up)
+    )(where, query, kept, given, up, up_beside)
 
 
 def rows_kernel(x_ref, out_ref):
@@ -143,42 +152,39 @@
     )(*sets, *weights)
 
 
-def last_kernel(where_ref, *refs):
-    *sets, w_ref, near_up_ref, t_ref, late_ref, kept_ref, given_ref = refs
-    features, half = sets[0].shape[1], kept_ref.shape[1]
-    before = t_ref.shape[1] - w_ref.shape[0]
-    middle = jnp.logical_or(where_ref[0] == 1, where_ref[0] == 2)
-    total = nt_dot(jnp.concatenate([r[...] for r in sets], axis=0), w_ref[:, :features])
+def late_kernel(where_ref, low_ref, high_ref, *refs):
+    weights, (t_ref, kept_ref, given_ref, up_ref) = refs[:-4], refs[-4:]
+    half, features = low_ref.shape
+    count, columns = weights[0].shape[0], up_ref.shape[1]
+    for k, ref in enumerate(weights):
+        at = (k % 2) * (len(weights) * count) + (k // 2) * (2 * count)
+        for part in range(2):
+            lanes = slice(features + part * columns, features + (part + 1) * columns)
+            up_ref[at + part * count : at + (part + 1) * count] = ref[:, lanes]
+    columns = jnp.concatenate([w[:, :features] for w in weights], axis=0)
+    late = nt_dot(jnp.concatenate([low_ref[...], high_ref[...]], axis=0), columns)
     first = where_ref[3] == 0
-    known = t_ref.shape[0] // half
-
-    def value(k):
-        ref, at = (t_ref, k) if k < known else (late_ref, k - known)
-        rows = ref[at * half : (at + 1) * half, :]
-        last = jnp.where(middle, rows[:, before:], total[k * half : (k + 1) * half])
-        return jnp.concatenate([rows[:, :before], last], axis=1)
-
-    up = jnp.where(middle, near_up_ref[...], w_ref[:, features:])
-    given_ref[4] = up.astype(jnp.float32)
     for k in range(4):
-        low, high = value(2 * k), value(2 * k + 1)
+        if k < 3:
+            low, high = (t_ref[at * half : (at + 1) * half] for at in (2 * k, 2 * k + 1))
+        else:
+            low, high = late[:half], late[half:]
         kept_ref[k] = jnp.where(first, low, high)
         given_ref[k] = jnp.where(first, high, low)
 
 
-def last_products(where, sets, w, near_up, t, late):
+def late_products(where, low, high, weights, t):
     smem, vmem = (pl.BlockSpec(memory_space=m) for m in (pltpu.SMEM, pltpu.VMEM))
-    shape = (4, sets[0].shape[0] // 2, t.shape[1])
-    return pl.pallas_call(
-        last_kernel,
-        out_shape=(
-            jax.ShapeDtypeStruct(shape, jnp.float32),
-            jax.ShapeDtypeStruct((5,) + shape[1:], jnp.float32),
-        ),
-        in_specs=[smem] + [vmem] * (len(sets) + 4),
-        out_specs=(vmem, vmem),
+    shape = jax.ShapeDtypeStruct((4, low.shape[0], t.shape[1]), jnp.float32)
+    count, lanes = weights[0].shape
+    up = ((2 * len(weights)) * count, (lanes - low.shape[1]) // 2)
+    return pl.pallas_call(
+        late_kernel,
+        out_shape=(shape, shape, jax.ShapeDtypeStruct(up, low.dtype)),
+        in_specs=[smem] + [vmem] * (len(weights) + 3),
+        out_specs=(vmem,) * 3,
         compiler_params=pltpu.CompilerParams(vmem_limit_bytes=12 << 20),
-    )(where, *sets, w, near_up, t, late)
+    )(where, low, high, *weights, t)
 
 
 def join_kernel(where_ref, mine_ref, other_ref, queries_ref, attended_ref, sems):
@@ -207,28 +213,18 @@
     )(where, mine, other)
 
 
-def add_kernel(where_ref, kept_ref, given_ref, got_ref, beside_ref, across_ref, both_ref):
-    half = kept_ref.shape[1]
-    first = where_ref[3] == 0
-    mine, other = given_ref[4], got_ref[4]
-    beside_ref[:half] = kept_ref[1] + got_ref[1]
-    beside_ref[half : 2 * half] = jnp.where(first, mine, other)
-    beside_ref[2 * half :] = jnp.where(first, other, mine)
-    across_ref[...] = kept_ref[2] + got_ref[2]
-    both_ref[...] = kept_ref[3] + got_ref[3]
-
-
-def add_halves(where, kept, given, got):
-    rows, columns = kept.shape[1:]
-    smem, vmem = (pl.BlockSpec(memory_space=m) for m in (pltpu.SMEM, pltpu.VMEM))
-    shape = jax.ShapeDtypeStruct((rows, columns), kept.dtype)
+def add_kernel(a_ref, b_ref, *outs):
+    for k, out in enumerate(outs):
+        out[...] = a_ref[k + 1] + b_ref[k + 1]
+
+
+def add_halves(a, b):
+    shape = jax.ShapeDtypeStruct(a.shape[1:], a.dtype)
     return pl.pallas_call(
         add_kernel,
-        out_shape=(jax.ShapeDtypeStruct((3 * rows, columns), kept.dtype), shape, shape),
-        in_specs=[smem] + [vmem] * 3,
-        out_specs=(vmem,) * 3,
+        out_shape=(shape,) * (a.shape[0] - 1),
         compiler_params=pltpu.CompilerParams(vmem_limit_bytes=2 << 20),
-    )(where, kept, given, got)
+    )(a, b)
 
 
 def attend_block(queries, keys, values, masks, scaling):
@@ -281,15 +277,15 @@
 
 
 def finish_kernel(
-    steps, where_ref, own_ref, other_ref, sent_ref, beside_ref, across_ref, both_ref, holder_ref,
-    up_ref, up_beside_ref, up_other_ref, up_both_ref, low_ref, high_ref, fresh_ref, limits_ref, out_ref,
+    steps, where_ref, own_ref, other_ref, beside_ref, across_ref, both_ref, holder_ref,
+    up_ref, up_other_ref, low_ref, high_ref, fresh_ref, limits_ref, out_ref,
 ):
     rows = own_ref.shape[1]
     x, part = where_ref[1], where_ref[2]
     width = 128
     half = width // 2
     own = own_ref[0] + other_ref[0]
-    beside, across, both = beside_ref[:rows], across_ref[...], both_ref[...]
+    beside, across, both = beside_ref[...], across_ref[...], both_ref[...]
     queries_here = part == 0
     columns = jnp.where(queries_here, own, across), jnp.where(queries_here, beside, both)
     ranks = jnp.where(queries_here, across, own), jnp.where(queries_here, both, beside)
@@ -319,20 +315,12 @@
         lane_owner = jnp.where(low_lanes, where_ref[4 + 2 * m], where_ref[5 + 2 * m])
         shrink = ranks[m // 2][:, (m % 2) * width : (m % 2 + 1) * width]
         spread.append(jnp.where(holder == lane_owner, shrink, 0.0).astype(jnp.bfloat16))
-    spread = [jnp.concatenate(spread[:2], axis=1), jnp.concatenate(spread[2:], axis=1)]
-
+    spread = jnp.concatenate(spread, axis=1)
+    mine, other = (
+        jnp.dot(spread, ref[...], preferred_element_type=jnp.float32) for ref in (up_ref, up_other_ref)
+    )
     first = where_ref[3] == 0
-
-    def lift(side, a_ref, b_ref, last_ref):
-        a, b = a_ref[: 3 * half], b_ref[: 3 * half]
-        low = jnp.where(first, a, b), last_ref[rows : 2 * rows].astype(a.dtype)
-        high = jnp.where(first, b, a), last_ref[2 * rows :].astype(a.dtype)
-        up = jnp.concatenate([jnp.concatenate(low, axis=0), jnp.concatenate(high, axis=0)], axis=1)
-        return jnp.dot(side, up, preferred_element_type=jnp.float32)
-
-    adapted = lift(spread[0], up_ref, up_other_ref, sent_ref) + lift(
-        spread[1], up_beside_ref, up_both_ref, beside_ref
-    )
+    adapted = jnp.concatenate([jnp.where(first, mine, other), jnp.where(first, other, mine)], axis=1)
     queries = (base + adapted).astype(jnp.bfloat16)
     requests = rows // steps
     out_ref[0] = queries.reshape(requests, steps, -1)
@@ -347,11 +335,11 @@
 
 
 def finish(steps, where, *arrays):
-    rows, columns = arrays[0].shape[1:]
+    rows, up = arrays[0].shape[1], arrays[6]
     vmem = pl.BlockSpec(memory_space=pltpu.VMEM)
     return pl.pallas_call(
         functools.partial(finish_kernel, steps),
-        out_shape=jax.ShapeDtypeStruct((2, rows // steps, steps, 2 * columns), jnp.bfloat16),
+        out_shape=jax.ShapeDtypeStruct((2, rows // steps, steps, 2 * up.shape[1]), jnp.bfloat16),
         in_specs=[pl.BlockSpec(memory_space=pltpu.SMEM)] + [vmem] * len(arrays),
         out_specs=vmem,
         compiler_params=pltpu.CompilerParams(vmem_limit_bytes=8 << 20),
@@ -405,52 +393,49 @@
     if groups == 8 and lax.axis_size("parts") == 2 and query_matrix.shape[1] == 2 * down.shape[0]:
         place = lax.axis_index("group")
         z, x, part = place // 2, lax.rem(place, 2), lax.axis_index("parts")
-        pair_low = z < 2
-        places = (z, z + 1 - 2 * lax.rem(z, 2), jnp.where(pair_low, 2, 1), jnp.where(pair_low, 3, 0))
+        order = z ^ (z // 2)
+        steps_back = [lax.rem(order + 4 - k, 4) for k in range(4)]
+        places = [k ^ (k // 2) for k in steps_back]
         where = [z, x, part, core] + [p * 2 + x for p in places] + [p * 2 + 1 - x for p in places]
         where = jnp.stack(where).astype(jnp.int32)
-        middle = jnp.logical_or(z == 1, z == 2)
         bar = lambda *a: lax.optimization_barrier(a)
         along = lambda a, moves: lax.ppermute(a, "group", line_pairs(groups, moves))
         across = lambda a: lax.ppermute(a, "parts", SWAP)
         beside = lambda a: lax.ppermute(a, "group", [(i, i ^ 1) for i in range(groups)])
         inside = lambda a: lax.ppermute(a, "tensor", SWAP)
         corner = [(p * groups + i, (1 - p) * groups + (i ^ 1)) for p in range(2) for i in range(groups)]
-        ends, inner = ((0, 1), (1, 0), (2, 3), (3, 2)), ((1, 2), (2, 1))
-        outward = ((1, 0), (2, 3))
-
+        ring = ((0, 1), (1, 3), (3, 2), (2, 0))
+
+        half = rows // 2
         mine = rows_of(normed_hidden_states)
-        w0 = block_of(where, query_block, down, down_other, factor_up[0])
-        w0, mine = bar(w0, mine)
-        half = rows // 2
-        m1, w1 = along(w0, inner), along(w0, ends)
+        up_beside = beside(factor_up[0])
+        a0, b0 = block_of(where, query_block, down, down_other, factor_up[0], up_beside)
+        a0, b0, mine = bar(a0, b0, mine)
+        a1, b1 = along(a0, ring), along(b0, ring)
         x_beside, x_across = beside(mine), across(mine)
-        m2, p1 = along(w1, inner), along(m1, outward)
-        w2 = jnp.where(middle, m1, p1)
-        c0, c1 = beside(x_across[:half]), across(x_beside[half:])
-        m2, p1, x_beside, x_across = bar(m2, p1, x_beside, x_across)
-        p2 = along(m2, outward)
-        up = jnp.concatenate([w[:, features:] for w in (w0, w1, w2)], axis=0)
-        up_beside = beside(up)
-        ups = up, up_beside, inside(up), inside(up_beside)
-        near_up = m2[:, features:]
-        sets, later = (mine, x_beside, x_across), (c0, c1)
-        weights = w0, w1, w2, m2
-        t, t_late = products(sets, weights), products(later, weights)
-
+        a2 = along(a1, ring)
+        b2 = along(b1, ring)
+        a3 = along(a2, ring)
+        low, high = beside(x_across[:half]), across(x_beside[half:])
         cache = kv_cache.reshape(-1, kv_cache.shape[2])
         prepared = ready(
             where, kv_lengths, request_adapter, adapter_owner, cache, inside(cache), incoming_key_value, steps
         )
-        p2, t, t_late, prepared, ups, near_up = bar(p2, t, t_late, prepared, ups, near_up)
-        kept, given = last_products(where, sets + later, p2, near_up, t, t_late)
+        b2, x_beside, x_across, prepared = bar(b2, x_beside, x_across, prepared)
+        b3 = along(b2, ring)
+        weights = a0, b0, a1, b1, a2, b2, a3, b3
+        t = products((mine, x_beside, x_across), weights)
+
+        low, high, t, prepared = bar(low, high, t, prepared)
+        kept, given, up = late_products(where, low, high, weights, t)
         got = inside(given)
-        sent, t_across, t_both = add_halves(where, kept, given, got)
-        t_beside, t_across = beside(sent), across(t_across)
+        t_beside, t_across, t_both = add_halves(kept, got)
+        t_beside, t_across = beside(t_beside), across(t_across)
         t_both = lax.ppermute(t_both, ("parts", "group"), corner)
-        low, high, fresh, limits, holder_rows = prepared
+        cache_low, cache_high, fresh, limits, holder_rows = prepared
         done = finish(
-            steps, where, kept, got, sent, t_beside, t_across, t_both, holder_rows, *ups, low, high, fresh, limits
+            steps, where, kept, got, t_beside, t_across, t_both, holder_rows, up, inside(up),
+            cache_low, cache_high, fresh, limits,
         )
         return join(where, done, inside(done))
 

time: 74.1 us -> 66.3 us (0.89)
  Pallas kernels: 12.3 us -> 7.18 us
  local copies, waits for them, and re-layouts: 4.39 us -> 1.65 us
  waiting for transfers between devices: 33.2 us -> 34.7 us
  other arithmetic: 1.14 us -> 0 us
    ppermute x5 -> x6, waiting for transfers between devices: 9.25 us -> 23.9 us  [body(): along = lambda a, moves: lax.ppermute(a, 'group', line_pairs(groups, moves))]
    ppermute x3, waiting for transfers between devices: 11.2 us -> 5.9 us  [body(): across = lambda a: lax.ppermute(a, 'parts', SWAP)]
    ppermute x4, waiting for transfers between devices: 6.04 us -> 1.74 us  [body(): lax.ppermute(a, 'group', [(i, i ^ 1) for i in range(groups)])]
    pallas_call x2 -> x1, Pallas kernels: 4.28 us -> 1.04 us  [products(): pl.pallas_call(functools.partial(products_kernel, len(sets)), out_shape=j...]
    ppermute x1, waiting for transfers between devices: 3.56 us -> 0.88 us  [body(): t_both = lax.ppermute(t_both, ('parts', 'group'), corner)]
    slice x6 -> x2, local copies, waits for them, and re-layouts: 2.36 us -> 0.07 us  [body(): low, high = (beside(x_across[:half]), across(x_beside[half:]))]
    ppermute x5 -> x6, starting transfers between devices: 10.2 us -> 8.87 us  [body(): along = lambda a, moves: lax.ppermute(a, 'group', line_pairs(groups, moves))]
    ppermute x1, starting transfers between devices: 0.46 us -> 1.63 us  [body(): t_both = lax.ppermute(t_both, ('parts', 'group'), corner)]
  transfers between devices with their start and end apart: 19 -> 19, of which waited for: 9 -> 13; matrix products, arithmetic and copies ran while one was open for 5% -> 0% of each run, Pallas kernels for 8% -> 3%
where the time goes in v4:
time: 66.3 us; the launch traced here: 66.1 us
  waiting for transfers between devices  34.7 us (52%)
  starting transfers between devices  21.8 us (33%)
  Pallas kernels  7.18 us (11%)
  local copies, waits for them, and re-layouts  1.65 us (2%)
  between operations  0.81 us (1%)
    ppermute x6, waiting for transfers between devices, body(): along = lambda a, moves: lax.ppermute(a, 'group', line_pairs(groups, moves))  23.9 us
    ppermute x6, starting transfers between devices, body(): along = lambda a, moves: lax.ppermute(a, 'group', line_pairs(groups, moves))  8.87 us
    ppermute x4, starting transfers between devices, body(): lax.ppermute(a, 'group', [(i, i ^ 1) for i in range(groups)])  6.22 us
    ppermute x3, waiting for transfers between devices, body(): across = lambda a: lax.ppermute(a, 'parts', SWAP)  5.9 us
    ppermute x3, starting transfers between devices, body(): across = lambda a: lax.ppermute(a, 'parts', SWAP)  3.88 us
    ppermute x4, waiting for transfers between devices, body(): inside = lambda a: lax.ppermute(a, 'tensor', SWAP)  2.36 us
    pallas_call x1, Pallas kernels, finish(): pl.pallas_call(functools.partial(finish_kernel, steps), out_shape=jax.Sha...  1.97 us
    ppermute x4, waiting for transfers between devices, body(): lax.ppermute(a, 'group', [(i, i ^ 1) for i in range(groups)])  1.74 us
  transfers between devices with their start and end apart: 19, of which 13 were waited for; matrix products, arithmetic and copies ran while one was open for 0% of the time, Pallas kernels for 3%

profile of v4, /device:TPU:0, one launch (start us, length us, event | category | flops | bytes accessed | tf_op | source)
XLA Modules:
  0.0 66.1 jit_solution(13886781080006335905)
XLA Ops:
  0.6 0.5 collective-permute-start
  1.1 2.6 %collective-permute-start.1 = (bf16[64,256]{1,0:T(8,128)(2,1)}, bf16[64,256]{1,0:T(8,128)(2,1)S(1)}, u32[]{:S(2)}, u32[]{:S(2)}) collective-permute-start(bf16[64,256]{1,0:T(8,128)(2,1)} %bitcast.26), channel_id=1, source_target_pairs={{0,2},{2,0},{4,6},{6,4},{8,10},{10,8},{12,14},{14,12},{1,3},{3,1},... | collective-permute-start | bytes 98312 | tf_op jit(solution)/shard_map/ppermute | solution.py:404
  3.7 1.2 %copy-done = bf16[64,2,4096]{2,1,0:T(2,128)(2,1)S(1)} copy-done((bf16[64,2,4096]{2,1,0:T(2,128)(2,1)S(1)}, bf16[64,2,4096]{2,1,0:T(2,128)(2,1)}, u32[]{:S(2)}) %copy-start) | copy-done | bytes 1048600
  4.9 0.1 shard_map.105.refs_0_
  5.1 0.0 copy-start.5
  5.1 0.1 stack.51.where_ref
  5.2 0.7 %collective-permute-done.1.up_beside_ref = bf16[64,256]{1,0:T(8,128)(2,1)S(1)} collective-permute-done((bf16[64,256]{1,0:T(8,128)(2,1)}, bf16[64,256]{1,0:T(8,128)(2,1)S(1)}, u32[]{:S(2)}, u32[]{:S(2)}) %collective-permute-start.1) | collective-permute-done | bytes 32800 | tf_op jit(solution)/shard_map/ppermute | solution.py:404
  5.9 0.1 copy-done.1
  6.0 0.2 copy-done.2
  6.1 0.7 %shard_map.104 = (bf16[32,4608]{1,0:T(8,128)(2,1)S(1)}, bf16[32,4608]{1,0:T(8,128)(2,1)S(1)}) custom-call(s32[12]{0:T(128)S(1)} %stack.51.where_ref, bf16[64,4096]{1,0:T(8,128)(2,1)S(1)} %bitcast.21, bf16[32,8192]{1,0:T(8,128)(2,1)S(1)} %bitcast.22, bf16[32,8192]{1,0:T(8,128)(2,1)S(1)} %bitcast.25, bf16[64,256]{1,0:T(8,128)(2,1)S(1)} %bitcast.27, ...), custom_call_target="tpu_custom_call" | custom-call | tf_op jit(solution)/shard_map/pallas_call | solution.py:59
  6.8 1.8 %collective-permute-start.2 = (bf16[128,4096]{1,0:T(8,128)(2,1)S(1)}, bf16[128,4096]{1,0:T(8,128)(2,1)S(1)}, u32[]{:S(2)}, u32[]{:S(2)}) collective-permute-start(bf16[128,4096]{1,0:T(8,128)(2,1)S(1)} %shard_map.105.refs_0_), channel_id=1, source_target_pairs={{0,16},{16,0},{1,17},{17,1},{2,18},{18,2},{3,19},{19,3},{4,20},{20... | collective-permute-start | bytes 3145736 | tf_op jit(solution)/shard_map/ppermute | solution.py:403
  8.7 1.5 %collective-permute-start.4 = (bf16[128,4096]{1,0:T(8,128)(2,1)S(1)}, bf16[128,4096]{1,0:T(8,128)(2,1)S(1)}, u32[]{:S(2)}, u32[]{:S(2)}) collective-permute-start(bf16[128,4096]{1,0:T(8,128)(2,1)S(1)} %shard_map.105.refs_0_), channel_id=1, source_target_pairs={{0,2},{2,0},{4,6},{6,4},{8,10},{10,8},{12,14},{14,12},{1,3},{3,1},... | collective-permute-start | bytes 3145736 | tf_op jit(solution)/shard_map/ppermute | solution.py:404
  10.1 1.6 %collective-permute-start.9 = (bf16[32,4608]{1,0:T(8,128)(2,1)S(1)}, bf16[32,4608]{1,0:T(8,128)(2,1)S(1)}, u32[]{:S(2)}, u32[]{:S(2)}) collective-permute-start(bf16[32,4608]{1,0:T(8,128)(2,1)S(1)} %get-tuple-element.45.refs_3_.refs_0_), channel_id=1, source_target_pairs={{0,4},{2,6},{4,12},{6,14},{12,8},{14,10},{8,0},{10,2},{1,5},{3,7},... | collective-permute-start | bytes 884744 | tf_op jit(solution)/shard_map/ppermute | solution.py:402
  11.7 2.6 %collective-permute-start.6 = (bf16[32,4608]{1,0:T(8,128)(2,1)S(1)}, bf16[32,4608]{1,0:T(8,128)(2,1)S(1)}, u32[]{:S(2)}, u32[]{:S(2)}) collective-permute-start(bf16[32,4608]{1,0:T(8,128)(2,1)S(1)} %get-tuple-element.37.refs_4_.refs_1_), channel_id=1, source_target_pairs={{0,4},{2,6},{4,12},{6,14},{12,8},{14,10},{8,0},{10,2},{1,5},{3,7},... | collective-permute-start | bytes 884744 | tf_op jit(solution)/shard_map/ppermute | solution.py:402
  14.3 0.0 collective-permute-start.8
  14.3 6.7 %collective-permute-done.9.refs_5_.refs_2_ = bf16[32,4608]{1,0:T(8,128)(2,1)S(1)} collective-permute-done((bf16[32,4608]{1,0:T(8,128)(2,1)S(1)}, bf16[32,4608]{1,0:T(8,128)(2,1)S(1)}, u32[]{:S(2)}, u32[]{:S(2)}) %collective-permute-start.9) | collective-permute-done | bytes 294944 | tf_op jit(solution)/shard_map/ppermute | solution.py:402
  21.0 0.8 %collective-permute-start.10 = (bf16[32,4608]{1,0:T(8,128)(2,1)S(1)}, bf16[32,4608]{1,0:T(8,128)(2,1)S(1)}, u32[]{:S(2)}, u32[]{:S(2)}) collective-permute-start(bf16[32,4608]{1,0:T(8,128)(2,1)S(1)} %collective-permute-done.9.refs_5_.refs_2_), channel_id=1, source_target_pairs={{0,4},{2,6},{4,12},{6,14},{12,8},{14,10},{8,0},{10,2},{1,5},{3,7},... | collective-permute-start | bytes 884744 | tf_op jit(solution)/shard_map/ppermute | solution.py:402
  21.8 5.5 %collective-permute-done.6.refs_6_.refs_3_ = bf16[32,4608]{1,0:T(8,128)(2,1)S(1)} collective-permute-done((bf16[32,4608]{1,0:T(8,128)(2,1)S(1)}, bf16[32,4608]{1,0:T(8,128)(2,1)S(1)}, u32[]{:S(2)}, u32[]{:S(2)}) %collective-permute-start.6) | collective-permute-done | bytes 294944 | tf_op jit(solution)/shard_map/ppermute | solution.py:402
  27.3 0.8 %collective-permute-start.7 = (bf16[32,4608]{1,0:T(8,128)(2,1)S(1)}, bf16[32,4608]{1,0:T(8,128)(2,1)S(1)}, u32[]{:S(2)}, u32[]{:S(2)}) collective-permute-start(bf16[32,4608]{1,0:T(8,128)(2,1)S(1)} %collective-permute-done.6.refs_6_.refs_3_), channel_id=1, source_target_pairs={{0,4},{2,6},{4,12},{6,14},{12,8},{14,10},{8,0},{10,2},{1,5},{3,7},... | collective-permute-start | bytes 884744 | tf_op jit(solution)/shard_map/ppermute | solution.py:402
  28.1 4.0 %collective-permute-done.2.refs_2_ = bf16[128,4096]{1,0:T(8,128)(2,1)S(1)} collective-permute-done((bf16[128,4096]{1,0:T(8,128)(2,1)S(1)}, bf16[128,4096]{1,0:T(8,128)(2,1)S(1)}, u32[]{:S(2)}, u32[]{:S(2)}) %collective-permute-start.2) | collective-permute-done | bytes 1048608 | tf_op jit(solution)/shard_map/ppermute | solution.py:403
  32.2 0.0 copy-start.4
  32.2 0.0 copy-start.6
  32.2 0.0 copy-start.7
  32.2 0.0 copy-start.8
  32.2 0.9 %collective-permute-start.3 = (bf16[64,4096]{1,0:T(8,128)(2,1)S(1)}, bf16[64,4096]{1,0:T(8,128)(2,1)S(1)}, u32[]{:S(2)}, u32[]{:S(2)}) collective-permute-start(bf16[64,4096]{1,0:T(8,128)(2,1)S(1)} %slice.8), channel_id=1, source_target_pairs={{0,2},{2,0},{4,6},{6,4},{8,10},{10,8},{12,14},{14,12},{1,3},{3,1},... | collective-permute-start | bytes 1572872 | tf_op jit(solution)/shard_map/ppermute | solution.py:404
  33.1 0.2 collective-permute-done.4.refs_1_
  33.4 1.4 %collective-permute-start.5 = (bf16[64,4096]{1,0:T(8,128)(2,1)S(1)}, bf16[64,4096]{1,0:T(8,128)(2,1)S(1)}, u32[]{:S(2)}, u32[]{:S(2)}) collective-permute-start(bf16[64,4096]{1,0:T(8,128)(2,1)S(1)} %slice.9), channel_id=1, source_target_pairs={{0,16},{16,0},{1,17},{17,1},{2,18},{18,2},{3,19},{19,3},{4,20},{20... | collective-permute-start | bytes 1572872 | tf_op jit(solution)/shard_map/ppermute | solution.py:403
  34.8 0.7 %shard_map.106 = (bf16[512,256]{1,0:T(8,128)(2,1)S(1)}, bf16[512,256]{1,0:T(8,128)(2,1)S(1)}, bf16[64,256]{1,0:T(8,128)(2,1)S(1)}, s32[8,128]{1,0:T(8,128)S(1)}, s32[64,128]{1,0:T(8,128)S(1)}) custom-call(s32[12]{0:T(128)S(1)} %stack.51.where_ref, s32[64]{0:T(128)S(1)} %copy-done.6, s32[64]{0:T(128)S(1)} %copy-done.7, s32[8]{0:T(128)S(1)} %copy-done.8, ...), custom_call_target="tpu_custom_call" | custom-call | tf_op jit(solution)/shard_map/pallas_call | solution.py:118
  35.5 1.6 %collective-permute-start.11 = (bf16[32,4608]{1,0:T(8,128)(2,1)S(1)}, bf16[32,4608]{1,0:T(8,128)(2,1)S(1)}, u32[]{:S(2)}, u32[]{:S(2)}) collective-permute-start(bf16[32,4608]{1,0:T(8,128)(2,1)S(1)} %collective-permute-done.10.refs_7_.refs_4_), channel_id=1, source_target_pairs={{0,4},{2,6},{4,12},{6,14},{12,8},{14,10},{8,0},{10,2},{1,5},{3,7},... | collective-permute-start | bytes 884744 | tf_op jit(solution)/shard_map/ppermute | solution.py:402
  37.1 1.1 %collective-permute-done.7.refs_8_.refs_5_ = bf16[32,4608]{1,0:T(8,128)(2,1)S(1)} collective-permute-done((bf16[32,4608]{1,0:T(8,128)(2,1)S(1)}, bf16[32,4608]{1,0:T(8,128)(2,1)S(1)}, u32[]{:S(2)}, u32[]{:S(2)}) %collective-permute-start.7) | collective-permute-done | bytes 294944 | tf_op jit(solution)/shard_map/ppermute | solution.py:402
  38.2 1.5 %collective-permute-start.12 = (bf16[32,4608]{1,0:T(8,128)(2,1)S(1)}, bf16[32,4608]{1,0:T(8,128)(2,1)S(1)}, u32[]{:S(2)}, u32[]{:S(2)}) collective-permute-start(bf16[32,4608]{1,0:T(8,128)(2,1)S(1)} %collective-permute-done.7.refs_8_.refs_5_), channel_id=1, source_target_pairs={{0,4},{2,6},{4,12},{6,14},{12,8},{14,10},{8,0},{10,2},{1,5},{3,7},... | collective-permute-start | bytes 884744 | tf_op jit(solution)/shard_map/ppermute | solution.py:402
  39.7 6.7 %collective-permute-done.11.refs_9_.refs_6_ = bf16[32,4608]{1,0:T(8,128)(2,1)S(1)} collective-permute-done((bf16[32,4608]{1,0:T(8,128)(2,1)S(1)}, bf16[32,4608]{1,0:T(8,128)(2,1)S(1)}, u32[]{:S(2)}, u32[]{:S(2)}) %collective-permute-start.11) | collective-permute-done | bytes 294944 | tf_op jit(solution)/shard_map/ppermute | solution.py:402
  46.4 3.9 %collective-permute-done.12.refs_10_.refs_7_ = bf16[32,4608]{1,0:T(8,128)(2,1)S(1)} collective-permute-done((bf16[32,4608]{1,0:T(8,128)(2,1)S(1)}, bf16[32,4608]{1,0:T(8,128)(2,1)S(1)}, u32[]{:S(2)}, u32[]{:S(2)}) %collective-permute-start.12) | collective-permute-done | bytes 294944 | tf_op jit(solution)/shard_map/ppermute | solution.py:402
  50.3 1.0 %shard_map.107.refs_8_ = f32[384,256]{1,0:T(8,128)S(1)} custom-call(bf16[128,4096]{1,0:T(8,128)(2,1)S(1)} %shard_map.105.refs_0_, bf16[128,4096]{1,0:T(8,128)(2,1)S(1)} %collective-permute-done.4.refs_1_, bf16[128,4096]{1,0:T(8,128)(2,1)S(1)} %collective-permute-done.2.refs_2_, bf16[32,4608]{1,0:T(8,128)(2,1)S(1)} %get-tuple-element.45.refs_3_.refs_0_, ...), custom_call_target="tpu_custom_call" | custom-call | flops 805306368 | bytes 5242880 | tf_op jit(solution)/shard_map/pallas_call | solution.py:143
  51.4 1.4 %shard_map.108 = (f32[4,64,256]{2,1,0:T(8,128)S(1)}, f32[4,64,256]{2,1,0:T(8,128)S(1)}, bf16[512,256]{1,0:T(8,128)(2,1)S(1)}) custom-call(s32[12]{0:T(128)S(1)} %stack.51.where_ref, bf16[64,4096]{1,0:T(8,128)(2,1)S(1)} %collective-permute-done.3.low_ref, bf16[64,4096]{1,0:T(8,128)(2,1)S(1)} %collective-permute-done.5.high_ref, ...), custom_call_target="tpu_custom_call" | custom-call | tf_op jit(solution)/shard_map/pallas_call | solution.py:181
  52.8 0.1 collective-permute-start.13
  52.8 0.5 collective-permute-start.17
  53.3 1.0 %collective-permute-done.13.b_ref.other_ref = f32[4,64,256]{2,1,0:T(8,128)S(1)} collective-permute-done((f32[4,64,256]{2,1,0:T(8,128)S(1)}, f32[4,64,256]{2,1,0:T(8,128)S(1)}, u32[]{:S(2)}, u32[]{:S(2)}) %collective-permute-start.13) | collective-permute-done | bytes 262176 | tf_op jit(solution)/shard_map/ppermute | solution.py:405
  54.4 1.2 %collective-permute-start.14 = (f32[64,256]{1,0:T(8,128)S(1)}, f32[64,256]{1,0:T(8,128)S(1)}, u32[]{:S(2)}, u32[]{:S(2)}) collective-permute-start(f32[64,256]{1,0:T(8,128)S(1)} %get-tuple-element.57), channel_id=1, source_target_pairs={{0,2},{2,0},{4,6},{6,4},{8,10},{10,8},{12,14},{14,12},{1,3},{3,1},... | collective-permute-start | bytes 196616 | tf_op jit(solution)/shard_map/ppermute | solution.py:404
  55.6 0.7 %collective-permute-start.15 = (f32[64,256]{1,0:T(8,128)S(1)}, f32[64,256]{1,0:T(8,128)S(1)}, u32[]{:S(2)}, u32[]{:S(2)}) collective-permute-start(f32[64,256]{1,0:T(8,128)S(1)} %get-tuple-element.58), channel_id=1, source_target_pairs={{0,16},{16,0},{1,17},{17,1},{2,18},{18,2},{3,19},{19,3},{4,20},{20... | collective-permute-start | bytes 196616 | tf_op jit(solution)/shard_map/ppermute | solution.py:403
  56.3 1.6 %collective-permute-start.16 = (f32[64,256]{1,0:T(8,128)S(1)}, f32[64,256]{1,0:T(8,128)S(1)}, u32[]{:S(2)}, u32[]{:S(2)}) collective-permute-start(f32[64,256]{1,0:T(8,128)S(1)} %get-tuple-element.59), channel_id=1, source_target_pairs={{0,18},{2,16},{4,22},{6,20},{8,26},{10,24},{12,30},{14,28},{16,2},... | collective-permute-start | bytes 196616 | tf_op jit(solution)/shard_map/ppermute | solution.py:434
  57.9 0.8 %collective-permute-done.14.beside_ref = f32[64,256]{1,0:T(8,128)S(1)} collective-permute-done((f32[64,256]{1,0:T(8,128)S(1)}, f32[64,256]{1,0:T(8,128)S(1)}, u32[]{:S(2)}, u32[]{:S(2)}) %collective-permute-start.14) | collective-permute-done | bytes 65568 | tf_op jit(solution)/shard_map/ppermute | solution.py:404
  58.7 1.9 %collective-permute-done.15.across_ref = f32[64,256]{1,0:T(8,128)S(1)} collective-permute-done((f32[64,256]{1,0:T(8,128)S(1)}, f32[64,256]{1,0:T(8,128)S(1)}, u32[]{:S(2)}, u32[]{:S(2)}) %collective-permute-start.15) | collective-permute-done | bytes 65568 | tf_op jit(solution)/shard_map/ppermute | solution.py:403
  60.6 0.9 %collective-permute-done.16.both_ref = f32[64,256]{1,0:T(8,128)S(1)} collective-permute-done((f32[64,256]{1,0:T(8,128)S(1)}, f32[64,256]{1,0:T(8,128)S(1)}, u32[]{:S(2)}, u32[]{:S(2)}) %collective-permute-start.16) | collective-permute-done | bytes 65568 | tf_op jit(solution)/shard_map/ppermute | solution.py:434
  61.5 2.0 %shard_map.110.mine_ref = bf16[2,32,2,512]{3,2,1,0:T(2,128)(2,1)S(1)} custom-call(s32[12]{0:T(128)S(1)} %stack.51.where_ref, f32[4,64,256]{2,1,0:T(8,128)S(1)} %get-tuple-element.55.a_ref.own_ref, f32[4,64,256]{2,1,0:T(8,128)S(1)} %collective-permute-done.13.b_ref.other_ref, f32[64,256]{1,0:T(8,128)S(1)} %collective-permute-done.14.beside_ref, ...), custom_call_target="tpu_custom_call" | custom-call | tf_op jit(solution)/shard_map/pallas_call | solution.py:340
  63.4 0.1 collective-permute-start.18
  63.5 1.3 %collective-permute-done.18.other_ref = bf16[2,32,2,512]{3,2,1,0:T(2,128)(2,1)S(1)} collective-permute-done((bf16[2,32,2,512]{3,2,1,0:T(2,128)(2,1)S(1)}, bf16[2,32,2,512]{3,2,1,0:T(2,128)(2,1)S(1)}, u32[]{:S(2)}, u32[]{:S(2)}) %collective-permute-start.18) | collective-permute-done | bytes 131104 | tf_op jit(solution)/shard_map/ppermute | solution.py:405
  64.9 1.3 %shard_map.111 = (bf16[64,2,512]{2,1,0:T(2,128)(2,1)}, bf16[64,2,512]{2,1,0:T(2,128)(2,1)}) custom-call(s32[12]{0:T(128)S(1)} %stack.51.where_ref, bf16[2,32,2,512]{3,2,1,0:T(2,128)(2,1)S(1)} %shard_map.110.mine_ref, bf16[2,32,2,512]{3,2,1,0:T(2,128)(2,1)S(1)} %collective-permute-done.18.other_ref), custom_call_target="tpu_custom_call" | custom-call | tf_op jit(solution)/shard_map/pallas_call | solution.py:206
  (19 shorter events, 0.1 us)
Async XLA Ops:
  0.6 5.3 %collective-permute-start = (bf16[1,8192,32]{1,2,0:T(8,128)(2,1)}, bf16[1,8192,32]{1,2,0:T(8,128)(2,1)S(1)}, u32[]{:S(2)}, u32[]{:S(2)}) collective-permute-start(bf16[1,8192,32]{1,2,0:T(8,128)(2,1)} %param.11), channel_id=1, source_target_pairs={{0,1},{1,0},{2,3},{3,2},{4,5},{5,4},{6,7},{7,6},{8,9},{9,8},{10,11... | collective-permute-start | bytes 1572872 | tf_op jit(solution)/shard_map/ppermute | solution.py:388
  1.1 4.8 %collective-permute-start.1 = (bf16[64,256]{1,0:T(8,128)(2,1)}, bf16[64,256]{1,0:T(8,128)(2,1)S(1)}, u32[]{:S(2)}, u32[]{:S(2)}) collective-permute-start(bf16[64,256]{1,0:T(8,128)(2,1)} %bitcast.26), channel_id=1, source_target_pairs={{0,2},{2,0},{4,6},{6,4},{8,10},{10,8},{12,14},{14,12},{1,3},{3,1},... | collective-permute-start | bytes 98312 | tf_op jit(solution)/shard_map/ppermute | solution.py:404
  3.7 1.2 %copy-start = (bf16[64,2,4096]{2,1,0:T(2,128)(2,1)S(1)}, bf16[64,2,4096]{2,1,0:T(2,128)(2,1)}, u32[]{:S(2)}) copy-start(bf16[64,2,4096]{2,1,0:T(2,128)(2,1)} %x_ref.1) | copy-start | bytes 3145732
  4.9 1.0 %copy-start.1 = (bf16[4096,64]{0,1:T(8,128)(2,1)S(1)}, bf16[4096,64]{0,1:T(8,128)(2,1)}, u32[]{:S(2)}) copy-start(bf16[4096,64]{0,1:T(8,128)(2,1)} %param.10) | copy-start | bytes 1572868
  4.9 1.2 %copy-start.2 = (bf16[1,8192,32]{1,2,0:T(8,128)(2,1)S(1)}, bf16[1,8192,32]{1,2,0:T(8,128)(2,1)}, u32[]{:S(2)}) copy-start(bf16[1,8192,32]{1,2,0:T(8,128)(2,1)} %param.11) | copy-start | bytes 1572868
  5.1 1.1 %copy-start.5 = (bf16[1,64,256]{2,1,0:T(8,128)(2,1)S(1)}, bf16[1,64,256]{2,1,0:T(8,128)(2,1)}, u32[]{:S(2)}) copy-start(bf16[1,64,256]{2,1,0:T(8,128)(2,1)} %param.12) | copy-start | bytes 98308
  6.1 8.2 %copy-start.3 = (bf16[64,16,256]{2,1,0:T(8,128)(2,1)S(1)}, bf16[64,16,256]{2,1,0:T(8,128)(2,1)}, u32[]{:S(2)}) copy-start(bf16[64,16,256]{2,1,0:T(8,128)(2,1)} %param.13) | copy-start | bytes 1572868
  6.8 25.3 %collective-permute-start.2 = (bf16[128,4096]{1,0:T(8,128)(2,1)S(1)}, bf16[128,4096]{1,0:T(8,128)(2,1)S(1)}, u32[]{:S(2)}, u32[]{:S(2)}) collective-permute-start(bf16[128,4096]{1,0:T(8,128)(2,1)S(1)} %shard_map.105.refs_0_), channel_id=1, source_target_pairs={{0,16},{16,0},{1,17},{17,1},{2,18},{18,2},{3,19},{19,3},{4,20},{20... | collective-permute-start | bytes 3145736 | tf_op jit(solution)/shard_map/ppermute | solution.py:403
  8.7 24.7 %collective-permute-start.4 = (bf16[128,4096]{1,0:T(8,128)(2,1)S(1)}, bf16[128,4096]{1,0:T(8,128)(2,1)S(1)}, u32[]{:S(2)}, u32[]{:S(2)}) collective-permute-start(bf16[128,4096]{1,0:T(8,128)(2,1)S(1)} %shard_map.105.refs_0_), channel_id=1, source_target_pairs={{0,2},{2,0},{4,6},{6,4},{8,10},{10,8},{12,14},{14,12},{1,3},{3,1},... | collective-permute-start | bytes 3145736 | tf_op jit(solution)/shard_map/ppermute | solution.py:404
  10.1 10.8 %collective-permute-start.9 = (bf16[32,4608]{1,0:T(8,128)(2,1)S(1)}, bf16[32,4608]{1,0:T(8,128)(2,1)S(1)}, u32[]{:S(2)}, u32[]{:S(2)}) collective-permute-start(bf16[32,4608]{1,0:T(8,128)(2,1)S(1)} %get-tuple-element.45.refs_3_.refs_0_), channel_id=1, source_target_pairs={{0,4},{2,6},{4,12},{6,14},{12,8},{14,10},{8,0},{10,2},{1,5},{3,7},... | collective-permute-start | bytes 884744 | tf_op jit(solution)/shard_map/ppermute | solution.py:402
  11.7 15.6 %collective-permute-start.6 = (bf16[32,4608]{1,0:T(8,128)(2,1)S(1)}, bf16[32,4608]{1,0:T(8,128)(2,1)S(1)}, u32[]{:S(2)}, u32[]{:S(2)}) collective-permute-start(bf16[32,4608]{1,0:T(8,128)(2,1)S(1)} %get-tuple-element.37.refs_4_.refs_1_), channel_id=1, source_target_pairs={{0,4},{2,6},{4,12},{6,14},{12,8},{14,10},{8,0},{10,2},{1,5},{3,7},... | collective-permute-start | bytes 884744 | tf_op jit(solution)/shard_map/ppermute | solution.py:402
  14.3 20.5 %collective-permute-start.8 = (bf16[1024,256]{1,0:T(8,128)(2,1)S(1)}, bf16[1024,256]{1,0:T(8,128)(2,1)S(1)}, u32[]{:S(2)}, u32[]{:S(2)}) collective-permute-start(bf16[1024,256]{1,0:T(8,128)(2,1)S(1)} %bitcast.23), channel_id=1, source_target_pairs={{0,1},{1,0},{2,3},{3,2},{4,5},{5,4},{6,7},{7,6},{8,9},{9,8},{10,11... | collective-permute-start | bytes 1572872 | tf_op jit(solution)/shard_map/ppermute | solution.py:405
  21.0 14.5 %collective-permute-start.10 = (bf16[32,4608]{1,0:T(8,128)(2,1)S(1)}, bf16[32,4608]{1,0:T(8,128)(2,1)S(1)}, u32[]{:S(2)}, u32[]{:S(2)}) collective-permute-start(bf16[32,4608]{1,0:T(8,128)(2,1)S(1)} %collective-permute-done.9.refs_5_.refs_2_), channel_id=1, source_target_pairs={{0,4},{2,6},{4,12},{6,14},{12,8},{14,10},{8,0},{10,2},{1,5},{3,7},... | collective-permute-start | bytes 884744 | tf_op jit(solution)/shard_map/ppermute | solution.py:402
  27.3 10.9 %collective-permute-start.7 = (bf16[32,4608]{1,0:T(8,128)(2,1)S(1)}, bf16[32,4608]{1,0:T(8,128)(2,1)S(1)}, u32[]{:S(2)}, u32[]{:S(2)}) collective-permute-start(bf16[32,4608]{1,0:T(8,128)(2,1)S(1)} %collective-permute-done.6.refs_6_.refs_3_), channel_id=1, source_target_pairs={{0,4},{2,6},{4,12},{6,14},{12,8},{14,10},{8,0},{10,2},{1,5},{3,7},... | collective-permute-start | bytes 884744 | tf_op jit(solution)/shard_map/ppermute | solution.py:402
  32.2 2.6 %copy-start.4 = (bf16[64,2,256]{2,1,0:T(2,128)(2,1)S(1)}, bf16[64,2,256]{2,1,0:T(2,128)(2,1)}, u32[]{:S(2)}) copy-start(bf16[64,2,256]{2,1,0:T(2,128)(2,1)} %fresh_ref.1) | copy-start | bytes 196612
  32.2 2.6 %copy-start.6 = (s32[64]{0:T(128)S(1)}, s32[64]{0:T(128)}, u32[]{:S(2)}) copy-start(s32[64]{0:T(128)} %lengths_ref.1) | copy-start | bytes 772
  32.2 2.6 %copy-start.7 = (s32[64]{0:T(128)S(1)}, s32[64]{0:T(128)}, u32[]{:S(2)}) copy-start(s32[64]{0:T(128)} %adapter_ref.1) | copy-start | bytes 772
  32.2 2.6 %copy-start.8 = (s32[8]{0:T(128)S(1)}, s32[8]{0:T(128)}, u32[]{:S(2)}) copy-start(s32[8]{0:T(128)} %owner_ref.1) | copy-start | bytes 100
  32.2 19.1 %collective-permute-start.3 = (bf16[64,4096]{1,0:T(8,128)(2,1)S(1)}, bf16[64,4096]{1,0:T(8,128)(2,1)S(1)}, u32[]{:S(2)}, u32[]{:S(2)}) collective-permute-start(bf16[64,4096]{1,0:T(8,128)(2,1)S(1)} %slice.8), channel_id=1, source_target_pairs={{0,2},{2,0},{4,6},{6,4},{8,10},{10,8},{12,14},{14,12},{1,3},{3,1},... | collective-permute-start | bytes 1572872 | tf_op jit(solution)/shard_map/ppermute | solution.py:404
  33.4 18.0 %collective-permute-start.5 = (bf16[64,4096]{1,0:T(8,128)(2,1)S(1)}, bf16[64,4096]{1,0:T(8,128)(2,1)S(1)}, u32[]{:S(2)}, u32[]{:S(2)}) collective-permute-start(bf16[64,4096]{1,0:T(8,128)(2,1)S(1)} %slice.9), channel_id=1, source_target_pairs={{0,16},{16,0},{1,17},{17,1},{2,18},{18,2},{3,19},{19,3},{4,20},{20... | collective-permute-start | bytes 1572872 | tf_op jit(solution)/shard_map/ppermute | solution.py:403
  35.5 10.9 %collective-permute-start.11 = (bf16[32,4608]{1,0:T(8,128)(2,1)S(1)}, bf16[32,4608]{1,0:T(8,128)(2,1)S(1)}, u32[]{:S(2)}, u32[]{:S(2)}) collective-permute-start(bf16[32,4608]{1,0:T(8,128)(2,1)S(1)} %collective-permute-done.10.refs_7_.refs_4_), channel_id=1, source_target_pairs={{0,4},{2,6},{4,12},{6,14},{12,8},{14,10},{8,0},{10,2},{1,5},{3,7},... | collective-permute-start | bytes 884744 | tf_op jit(solution)/shard_map/ppermute | solution.py:402
  38.2 12.1 %collective-permute-start.12 = (bf16[32,4608]{1,0:T(8,128)(2,1)S(1)}, bf16[32,4608]{1,0:T(8,128)(2,1)S(1)}, u32[]{:S(2)}, u32[]{:S(2)}) collective-permute-start(bf16[32,4608]{1,0:T(8,128)(2,1)S(1)} %collective-permute-done.7.refs_8_.refs_5_), channel_id=1, source_target_pairs={{0,4},{2,6},{4,12},{6,14},{12,8},{14,10},{8,0},{10,2},{1,5},{3,7},... | collective-permute-start | bytes 884744 | tf_op jit(solution)/shard_map/ppermute | solution.py:402
  52.8 1.6 %collective-permute-start.13 = (f32[4,64,256]{2,1,0:T(8,128)S(1)}, f32[4,64,256]{2,1,0:T(8,128)S(1)}, u32[]{:S(2)}, u32[]{:S(2)}) collective-permute-start(f32[4,64,256]{2,1,0:T(8,128)S(1)} %get-tuple-element.56), channel_id=1, source_target_pairs={{0,1},{1,0},{2,3},{3,2},{4,5},{5,4},{6,7},{7,6},{8,9},{9,8},{10,11... | collective-permute-start | bytes 786440 | tf_op jit(solution)/shard_map/ppermute | solution.py:405
  52.8 5.1 %collective-permute-start.17 = (bf16[512,256]{1,0:T(8,128)(2,1)S(1)}, bf16[512,256]{1,0:T(8,128)(2,1)S(1)}, u32[]{:S(2)}, u32[]{:S(2)}) collective-permute-start(bf16[512,256]{1,0:T(8,128)(2,1)S(1)} %get-tuple-element.61.up_ref), channel_id=1, source_target_pairs={{0,1},{1,0},{2,3},{3,2},{4,5},{5,4},{6,7},{7,6},{8,9},{9,8},{10,11... | collective-permute-start | bytes 786440 | tf_op jit(solution)/shard_map/ppermute | solution.py:405
  54.4 4.3 %collective-permute-start.14 = (f32[64,256]{1,0:T(8,128)S(1)}, f32[64,256]{1,0:T(8,128)S(1)}, u32[]{:S(2)}, u32[]{:S(2)}) collective-permute-start(f32[64,256]{1,0:T(8,128)S(1)} %get-tuple-element.57), channel_id=1, source_target_pairs={{0,2},{2,0},{4,6},{6,4},{8,10},{10,8},{12,14},{14,12},{1,3},{3,1},... | collective-permute-start | bytes 196616 | tf_op jit(solution)/shard_map/ppermute | solution.py:404
  55.6 5.0 %collective-permute-start.15 = (f32[64,256]{1,0:T(8,128)S(1)}, f32[64,256]{1,0:T(8,128)S(1)}, u32[]{:S(2)}, u32[]{:S(2)}) collective-permute-start(f32[64,256]{1,0:T(8,128)S(1)} %get-tuple-element.58), channel_id=1, source_target_pairs={{0,16},{16,0},{1,17},{17,1},{2,18},{18,2},{3,19},{19,3},{4,20},{20... | collective-permute-start | bytes 196616 | tf_op jit(solution)/shard_map/ppermute | solution.py:403
  56.3 5.2 %collective-permute-start.16 = (f32[64,256]{1,0:T(8,128)S(1)}, f32[64,256]{1,0:T(8,128)S(1)}, u32[]{:S(2)}, u32[]{:S(2)}) collective-permute-start(f32[64,256]{1,0:T(8,128)S(1)} %get-tuple-element.59), channel_id=1, source_target_pairs={{0,18},{2,16},{4,22},{6,20},{8,26},{10,24},{12,30},{14,28},{16,2},... | collective-permute-start | bytes 196616 | tf_op jit(solution)/shard_map/ppermute | solution.py:434
  63.4 1.4 %collective-permute-start.18 = (bf16[2,32,2,512]{3,2,1,0:T(2,128)(2,1)S(1)}, bf16[2,32,2,512]{3,2,1,0:T(2,128)(2,1)S(1)}, u32[]{:S(2)}, u32[]{:S(2)}) collective-permute-start(bf16[2,32,2,512]{3,2,1,0:T(2,128)(2,1)S(1)} %shard_map.110.mine_ref), channel_id=1, source_target_pairs={{0,1},{1,0},{2,3},{3,2},{4,5},{5,4},{6,7},{7,6},{8,9},{9,8},{10,11... | collective-permute-start | bytes 393224 | tf_op jit(solution)/shard_map/ppermute | solution.py:405

commit v5 on v4

--- a/solution.py
+++ b/solution.py
@@ -152,8 +152,9 @@
     )(*sets, *weights)
 
 
-def late_kernel(where_ref, low_ref, high_ref, *refs):
-    weights, (t_ref, kept_ref, given_ref, up_ref) = refs[:-4], refs[-4:]
+def late_kernel(where_ref, *refs):
+    sets, (low_ref, high_ref) = refs[:3], refs[3:5]
+    weights, (t_ref, kept_ref, given_ref, up_ref) = refs[5:-4], refs[-4:]
     half, features = low_ref.shape
     count, columns = weights[0].shape[0], up_ref.shape[1]
     for k, ref in enumerate(weights):
@@ -161,30 +162,35 @@
         for part in range(2):
             lanes = slice(features + part * columns, features + (part + 1) * columns)
             up_ref[at + part * count : at + (part + 1) * count] = ref[:, lanes]
-    columns = jnp.concatenate([w[:, :features] for w in weights], axis=0)
-    late = nt_dot(jnp.concatenate([low_ref[...], high_ref[...]], axis=0), columns)
+    all_columns = jnp.concatenate([w[:, :features] for w in weights], axis=0)
+    late = nt_dot(jnp.concatenate([low_ref[...], high_ref[...]], axis=0), all_columns)
+    last = nt_dot(jnp.concatenate([r[...] for r in sets], axis=0), weights[-1][:, :features])
     first = where_ref[3] == 0
     for k in range(4):
         if k < 3:
-            low, high = (t_ref[at * half : (at + 1) * half] for at in (2 * k, 2 * k + 1))
+            low, high = (
+                jnp.concatenate([r[at * half : (at + 1) * half] for r in (t_ref, last)], axis=1)
+                for at in (2 * k, 2 * k + 1)
+            )
         else:
             low, high = late[:half], late[half:]
         kept_ref[k] = jnp.where(first, low, high)
         given_ref[k] = jnp.where(first, high, low)
 
 
-def late_products(where, low, high, weights, t):
+def late_products(where, sets, low, high, weights, t):
     smem, vmem = (pl.BlockSpec(memory_space=m) for m in (pltpu.SMEM, pltpu.VMEM))
-    shape = jax.ShapeDtypeStruct((4, low.shape[0], t.shape[1]), jnp.float32)
     count, lanes = weights[0].shape
-    up = ((2 * len(weights)) * count, (lanes - low.shape[1]) // 2)
+    half, features = low.shape
+    shape = jax.ShapeDtypeStruct((4, half, len(weights) * count), jnp.float32)
+    up = ((2 * len(weights)) * count, (lanes - features) // 2)
     return pl.pallas_call(
         late_kernel,
         out_shape=(shape, shape, jax.ShapeDtypeStruct(up, low.dtype)),
-        in_specs=[smem] + [vmem] * (len(weights) + 3),
+        in_specs=[smem] + [vmem] * (len(sets) + len(weights) + 3),
         out_specs=(vmem,) * 3,
         compiler_params=pltpu.CompilerParams(vmem_limit_bytes=12 << 20),
-    )(where, low, high, *weights, t)
+    )(where, *sets, low, high, *weights, t)
 
 
 def join_kernel(where_ref, mine_ref, other_ref, queries_ref, attended_ref, sems):
@@ -424,10 +430,11 @@
         b2, x_beside, x_across, prepared = bar(b2, x_beside, x_across, prepared)
         b3 = along(b2, ring)
         weights = a0, b0, a1, b1, a2, b2, a3, b3
-        t = products((mine, x_beside, x_across), weights)
+        sets = mine, x_beside, x_across
+        t = products(sets, weights[:-1])
 
         low, high, t, prepared = bar(low, high, t, prepared)
-        kept, given, up = late_products(where, low, high, weights, t)
+        kept, given, up = late_products(where, sets, low, high, weights, t)
         got = inside(given)
         t_beside, t_across, t_both = add_halves(kept, got)
         t_beside, t_across = beside(t_beside), across(t_across)

time: 66.3 us -> 65.8 us (level)
  starting transfers between devices: 21.8 us -> 21 us
  Pallas kernels: 7.18 us -> 7.93 us
    ppermute x6, starting transfers between devices: 8.87 us -> 8.1 us  [body(): along = lambda a, moves: lax.ppermute(a, 'group', line_pairs(groups, moves))]
    pallas_call x1, Pallas kernels: 1.39 us -> 2.15 us  [late_products(): pl.pallas_call(late_kernel, out_shape=(shape, shape, jax.ShapeDtypeStruct...]
where the time goes in v5:
time: 65.8 us; the launch traced here: 65.6 us
  waiting for transfers between devices  34.3 us (52%)
  starting transfers between devices  21 us (32%)
  Pallas kernels  7.93 us (12%)
  local copies, waits for them, and re-layouts  1.65 us (3%)
  between operations  0.8 us (1%)
    ppermute x6, waiting for transfers between devices, body(): along = lambda a, moves: lax.ppermute(a, 'group', line_pairs(groups, moves))  23.6 us
    ppermute x6, starting transfers between devices, body(): along = lambda a, moves: lax.ppermute(a, 'group', line_pairs(groups, moves))  8.1 us
    ppermute x4, starting transfers between devices, body(): lax.ppermute(a, 'group', [(i, i ^ 1) for i in range(groups)])  6.21 us
    ppermute x3, waiting for transfers between devices, body(): across = lambda a: lax.ppermute(a, 'parts', SWAP)  5.9 us
    ppermute x3, starting transfers between devices, body(): across = lambda a: lax.ppermute(a, 'parts', SWAP)  3.69 us
    ppermute x4, waiting for transfers between devices, body(): inside = lambda a: lax.ppermute(a, 'tensor', SWAP)  2.36 us
    pallas_call x1, Pallas kernels, late_products(): pl.pallas_call(late_kernel, out_shape=(shape, shape, jax.ShapeDtypeStruct...  2.15 us
    pallas_call x1, Pallas kernels, finish(): pl.pallas_call(functools.partial(finish_kernel, steps), out_shape=jax.Sha...  1.97 us
  transfers between devices with their start and end apart: 19, of which 13 were waited for; matrix products, arithmetic and copies ran while one was open for 0% of the time, Pallas kernels for 3%

profile of v5, /device:TPU:0, one launch (start us, length us, event | category | flops | bytes accessed | tf_op | source)
XLA Modules:
  0.0 65.6 jit_solution(10838330650620526445)
XLA Ops:
  0.6 0.5 collective-permute-start
  1.1 2.6 %collective-permute-start.1 = (bf16[64,256]{1,0:T(8,128)(2,1)}, bf16[64,256]{1,0:T(8,128)(2,1)S(1)}, u32[]{:S(2)}, u32[]{:S(2)}) collective-permute-start(bf16[64,256]{1,0:T(8,128)(2,1)} %bitcast.26), channel_id=1, source_target_pairs={{0,2},{2,0},{4,6},{6,4},{8,10},{10,8},{12,14},{14,12},{1,3},{3,1},... | collective-permute-start | bytes 98312 | tf_op jit(solution)/shard_map/ppermute | solution.py:410
  3.7 1.2 %copy-done = bf16[64,2,4096]{2,1,0:T(2,128)(2,1)S(1)} copy-done((bf16[64,2,4096]{2,1,0:T(2,128)(2,1)S(1)}, bf16[64,2,4096]{2,1,0:T(2,128)(2,1)}, u32[]{:S(2)}) %copy-start) | copy-done | bytes 1048600
  4.9 0.1 shard_map.105.refs_0_
  5.1 0.0 copy-start.5
  5.1 0.1 stack.51.where_ref
  5.2 0.7 %collective-permute-done.1.up_beside_ref = bf16[64,256]{1,0:T(8,128)(2,1)S(1)} collective-permute-done((bf16[64,256]{1,0:T(8,128)(2,1)}, bf16[64,256]{1,0:T(8,128)(2,1)S(1)}, u32[]{:S(2)}, u32[]{:S(2)}) %collective-permute-start.1) | collective-permute-done | bytes 32800 | tf_op jit(solution)/shard_map/ppermute | solution.py:410
  5.9 0.0 collective-permute-done
  5.9 0.1 copy-done.1
  6.0 0.2 copy-done.2
  6.1 0.7 %shard_map.104 = (bf16[32,4608]{1,0:T(8,128)(2,1)S(1)}, bf16[32,4608]{1,0:T(8,128)(2,1)S(1)}) custom-call(s32[12]{0:T(128)S(1)} %stack.51.where_ref, bf16[64,4096]{1,0:T(8,128)(2,1)S(1)} %bitcast.21, bf16[32,8192]{1,0:T(8,128)(2,1)S(1)} %bitcast.22, bf16[32,8192]{1,0:T(8,128)(2,1)S(1)} %bitcast.25, bf16[64,256]{1,0:T(8,128)(2,1)S(1)} %bitcast.27, ...), custom_call_target="tpu_custom_call" | custom-call | tf_op jit(solution)/shard_map/pallas_call | solution.py:59
  6.8 1.8 %collective-permute-start.5 = (bf16[128,4096]{1,0:T(8,128)(2,1)S(1)}, bf16[128,4096]{1,0:T(8,128)(2,1)S(1)}, u32[]{:S(2)}, u32[]{:S(2)}) collective-permute-start(bf16[128,4096]{1,0:T(8,128)(2,1)S(1)} %shard_map.105.refs_0_), channel_id=1, source_target_pairs={{0,16},{16,0},{1,17},{17,1},{2,18},{18,2},{3,19},{19,3},{4,20},{20... | collective-permute-start | bytes 3145736 | tf_op jit(solution)/shard_map/ppermute | solution.py:409
  8.7 1.5 %collective-permute-start.4 = (bf16[128,4096]{1,0:T(8,128)(2,1)S(1)}, bf16[128,4096]{1,0:T(8,128)(2,1)S(1)}, u32[]{:S(2)}, u32[]{:S(2)}) collective-permute-start(bf16[128,4096]{1,0:T(8,128)(2,1)S(1)} %shard_map.105.refs_0_), channel_id=1, source_target_pairs={{0,2},{2,0},{4,6},{6,4},{8,10},{10,8},{12,14},{14,12},{1,3},{3,1},... | collective-permute-start | bytes 3145736 | tf_op jit(solution)/shard_map/ppermute | solution.py:410
  10.1 1.6 %collective-permute-start.9 = (bf16[32,4608]{1,0:T(8,128)(2,1)S(1)}, bf16[32,4608]{1,0:T(8,128)(2,1)S(1)}, u32[]{:S(2)}, u32[]{:S(2)}) collective-permute-start(bf16[32,4608]{1,0:T(8,128)(2,1)S(1)} %get-tuple-element.45.refs_3_.refs_5_), channel_id=1, source_target_pairs={{0,4},{2,6},{4,12},{6,14},{12,8},{14,10},{8,0},{10,2},{1,5},{3,7},... | collective-permute-start | bytes 884744 | tf_op jit(solution)/shard_map/ppermute | solution.py:408
  11.7 2.6 %collective-permute-start.2 = (bf16[32,4608]{1,0:T(8,128)(2,1)S(1)}, bf16[32,4608]{1,0:T(8,128)(2,1)S(1)}, u32[]{:S(2)}, u32[]{:S(2)}) collective-permute-start(bf16[32,4608]{1,0:T(8,128)(2,1)S(1)} %get-tuple-element.37.refs_4_.refs_6_), channel_id=1, source_target_pairs={{0,4},{2,6},{4,12},{6,14},{12,8},{14,10},{8,0},{10,2},{1,5},{3,7},... | collective-permute-start | bytes 884744 | tf_op jit(solution)/shard_map/ppermute | solution.py:408
  14.3 6.7 %collective-permute-done.9.refs_5_.refs_7_ = bf16[32,4608]{1,0:T(8,128)(2,1)S(1)} collective-permute-done((bf16[32,4608]{1,0:T(8,128)(2,1)S(1)}, bf16[32,4608]{1,0:T(8,128)(2,1)S(1)}, u32[]{:S(2)}, u32[]{:S(2)}) %collective-permute-start.9) | collective-permute-done | bytes 294944 | tf_op jit(solution)/shard_map/ppermute | solution.py:408
  21.0 0.8 %collective-permute-start.10 = (bf16[32,4608]{1,0:T(8,128)(2,1)S(1)}, bf16[32,4608]{1,0:T(8,128)(2,1)S(1)}, u32[]{:S(2)}, u32[]{:S(2)}) collective-permute-start(bf16[32,4608]{1,0:T(8,128)(2,1)S(1)} %collective-permute-done.9.refs_5_.refs_7_), channel_id=1, source_target_pairs={{0,4},{2,6},{4,12},{6,14},{12,8},{14,10},{8,0},{10,2},{1,5},{3,7},... | collective-permute-start | bytes 884744 | tf_op jit(solution)/shard_map/ppermute | solution.py:408
  21.8 5.5 %collective-permute-done.2.refs_6_.refs_8_ = bf16[32,4608]{1,0:T(8,128)(2,1)S(1)} collective-permute-done((bf16[32,4608]{1,0:T(8,128)(2,1)S(1)}, bf16[32,4608]{1,0:T(8,128)(2,1)S(1)}, u32[]{:S(2)}, u32[]{:S(2)}) %collective-permute-start.2) | collective-permute-done | bytes 294944 | tf_op jit(solution)/shard_map/ppermute | solution.py:408
  27.3 0.8 %collective-permute-start.3 = (bf16[32,4608]{1,0:T(8,128)(2,1)S(1)}, bf16[32,4608]{1,0:T(8,128)(2,1)S(1)}, u32[]{:S(2)}, u32[]{:S(2)}) collective-permute-start(bf16[32,4608]{1,0:T(8,128)(2,1)S(1)} %collective-permute-done.2.refs_6_.refs_8_), channel_id=1, source_target_pairs={{0,4},{2,6},{4,12},{6,14},{12,8},{14,10},{8,0},{10,2},{1,5},{3,7},... | collective-permute-start | bytes 884744 | tf_op jit(solution)/shard_map/ppermute | solution.py:408
  28.1 4.0 %collective-permute-done.5.refs_2_ = bf16[128,4096]{1,0:T(8,128)(2,1)S(1)} collective-permute-done((bf16[128,4096]{1,0:T(8,128)(2,1)S(1)}, bf16[128,4096]{1,0:T(8,128)(2,1)S(1)}, u32[]{:S(2)}, u32[]{:S(2)}) %collective-permute-start.5) | collective-permute-done | bytes 1048608 | tf_op jit(solution)/shard_map/ppermute | solution.py:409
  32.2 0.0 copy-start.4
  32.2 0.0 copy-start.6
  32.2 0.0 copy-start.7
  32.2 0.0 copy-start.8
  32.2 0.9 %collective-permute-start.7 = (bf16[64,4096]{1,0:T(8,128)(2,1)S(1)}, bf16[64,4096]{1,0:T(8,128)(2,1)S(1)}, u32[]{:S(2)}, u32[]{:S(2)}) collective-permute-start(bf16[64,4096]{1,0:T(8,128)(2,1)S(1)} %slice.8), channel_id=1, source_target_pairs={{0,2},{2,0},{4,6},{6,4},{8,10},{10,8},{12,14},{14,12},{1,3},{3,1},... | collective-permute-start | bytes 1572872 | tf_op jit(solution)/shard_map/ppermute | solution.py:410
  33.1 0.2 collective-permute-done.4.refs_1_
  33.4 1.4 %collective-permute-start.8 = (bf16[64,4096]{1,0:T(8,128)(2,1)S(1)}, bf16[64,4096]{1,0:T(8,128)(2,1)S(1)}, u32[]{:S(2)}, u32[]{:S(2)}) collective-permute-start(bf16[64,4096]{1,0:T(8,128)(2,1)S(1)} %slice.9), channel_id=1, source_target_pairs={{0,16},{16,0},{1,17},{17,1},{2,18},{18,2},{3,19},{19,3},{4,20},{20... | collective-permute-start | bytes 1572872 | tf_op jit(solution)/shard_map/ppermute | solution.py:409
  34.8 1.6 %collective-permute-start.11 = (bf16[32,4608]{1,0:T(8,128)(2,1)S(1)}, bf16[32,4608]{1,0:T(8,128)(2,1)S(1)}, u32[]{:S(2)}, u32[]{:S(2)}) collective-permute-start(bf16[32,4608]{1,0:T(8,128)(2,1)S(1)} %collective-permute-done.10.refs_7_.refs_9_), channel_id=1, source_target_pairs={{0,4},{2,6},{4,12},{6,14},{12,8},{14,10},{8,0},{10,2},{1,5},{3,7},... | collective-permute-start | bytes 884744 | tf_op jit(solution)/shard_map/ppermute | solution.py:408
  36.4 0.7 %shard_map.106 = (bf16[512,256]{1,0:T(8,128)(2,1)S(1)}, bf16[512,256]{1,0:T(8,128)(2,1)S(1)}, bf16[64,256]{1,0:T(8,128)(2,1)S(1)}, s32[8,128]{1,0:T(8,128)S(1)}, s32[64,128]{1,0:T(8,128)S(1)}) custom-call(s32[12]{0:T(128)S(1)} %stack.51.where_ref, s32[64]{0:T(128)S(1)} %copy-done.6, s32[64]{0:T(128)S(1)} %copy-done.7, s32[8]{0:T(128)S(1)} %copy-done.8, ...), custom_call_target="tpu_custom_call" | custom-call | tf_op jit(solution)/shard_map/pallas_call | solution.py:118
  37.1 1.9 %collective-permute-done.3.refs_8_.refs_10_ = bf16[32,4608]{1,0:T(8,128)(2,1)S(1)} collective-permute-done((bf16[32,4608]{1,0:T(8,128)(2,1)S(1)}, bf16[32,4608]{1,0:T(8,128)(2,1)S(1)}, u32[]{:S(2)}, u32[]{:S(2)}) %collective-permute-start.3) | collective-permute-done | bytes 294944 | tf_op jit(solution)/shard_map/ppermute | solution.py:408
  39.0 0.8 %collective-permute-start.12 = (bf16[32,4608]{1,0:T(8,128)(2,1)S(1)}, bf16[32,4608]{1,0:T(8,128)(2,1)S(1)}, u32[]{:S(2)}, u32[]{:S(2)}) collective-permute-start(bf16[32,4608]{1,0:T(8,128)(2,1)S(1)} %collective-permute-done.3.refs_8_.refs_10_), channel_id=1, source_target_pairs={{0,4},{2,6},{4,12},{6,14},{12,8},{14,10},{8,0},{10,2},{1,5},{3,7},... | collective-permute-start | bytes 884744 | tf_op jit(solution)/shard_map/ppermute | solution.py:408
  39.8 5.8 %collective-permute-done.11.refs_9_.refs_11_ = bf16[32,4608]{1,0:T(8,128)(2,1)S(1)} collective-permute-done((bf16[32,4608]{1,0:T(8,128)(2,1)S(1)}, bf16[32,4608]{1,0:T(8,128)(2,1)S(1)}, u32[]{:S(2)}, u32[]{:S(2)}) %collective-permute-start.11) | collective-permute-done | bytes 294944 | tf_op jit(solution)/shard_map/ppermute | solution.py:408
  45.6 1.0 %shard_map.107.refs_13_ = f32[384,224]{1,0:T(8,128)S(1)} custom-call(bf16[128,4096]{1,0:T(8,128)(2,1)S(1)} %shard_map.105.refs_0_, bf16[128,4096]{1,0:T(8,128)(2,1)S(1)} %collective-permute-done.4.refs_1_, bf16[128,4096]{1,0:T(8,128)(2,1)S(1)} %collective-permute-done.5.refs_2_, bf16[32,4608]{1,0:T(8,128)(2,1)S(1)} %get-tuple-element.45.refs_3_.refs_5_, ...), custom_call_target="tpu_custom_call" | custom-call | flops 704643072 | bytes 4980736 | tf_op jit(solution)/shard_map/pallas_call | solution.py:143
  46.7 3.6 %collective-permute-done.12.refs_12_ = bf16[32,4608]{1,0:T(8,128)(2,1)S(1)} collective-permute-done((bf16[32,4608]{1,0:T(8,128)(2,1)S(1)}, bf16[32,4608]{1,0:T(8,128)(2,1)S(1)}, u32[]{:S(2)}, u32[]{:S(2)}) %collective-permute-start.12) | collective-permute-done | bytes 294944 | tf_op jit(solution)/shard_map/ppermute | solution.py:408
  50.3 2.2 %shard_map.108 = (f32[4,64,256]{2,1,0:T(8,128)S(1)}, f32[4,64,256]{2,1,0:T(8,128)S(1)}, bf16[512,256]{1,0:T(8,128)(2,1)S(1)}) custom-call(s32[12]{0:T(128)S(1)} %stack.51.where_ref, bf16[128,4096]{1,0:T(8,128)(2,1)S(1)} %shard_map.105.refs_0_, bf16[128,4096]{1,0:T(8,128)(2,1)S(1)} %collective-permute-done.4.refs_1_, ...), custom_call_target="tpu_custom_call" | custom-call | tf_op jit(solution)/shard_map/pallas_call | solution.py:187
  52.5 0.1 collective-permute-start.13
  52.5 0.5 collective-permute-start.17
  53.0 1.0 %collective-permute-done.13.b_ref.other_ref = f32[4,64,256]{2,1,0:T(8,128)S(1)} collective-permute-done((f32[4,64,256]{2,1,0:T(8,128)S(1)}, f32[4,64,256]{2,1,0:T(8,128)S(1)}, u32[]{:S(2)}, u32[]{:S(2)}) %collective-permute-start.13) | collective-permute-done | bytes 262176 | tf_op jit(solution)/shard_map/ppermute | solution.py:411
  54.1 1.2 %collective-permute-start.14 = (f32[64,256]{1,0:T(8,128)S(1)}, f32[64,256]{1,0:T(8,128)S(1)}, u32[]{:S(2)}, u32[]{:S(2)}) collective-permute-start(f32[64,256]{1,0:T(8,128)S(1)} %get-tuple-element.57), channel_id=1, source_target_pairs={{0,2},{2,0},{4,6},{6,4},{8,10},{10,8},{12,14},{14,12},{1,3},{3,1},... | collective-permute-start | bytes 196616 | tf_op jit(solution)/shard_map/ppermute | solution.py:410
  55.3 0.5 collective-permute-start.15
  55.8 1.8 %collective-permute-start.16 = (f32[64,256]{1,0:T(8,128)S(1)}, f32[64,256]{1,0:T(8,128)S(1)}, u32[]{:S(2)}, u32[]{:S(2)}) collective-permute-start(f32[64,256]{1,0:T(8,128)S(1)} %get-tuple-element.59), channel_id=1, source_target_pairs={{0,18},{2,16},{4,22},{6,20},{8,26},{10,24},{12,30},{14,28},{16,2},... | collective-permute-start | bytes 196616 | tf_op jit(solution)/shard_map/ppermute | solution.py:441
  57.6 0.8 %collective-permute-done.14.beside_ref = f32[64,256]{1,0:T(8,128)S(1)} collective-permute-done((f32[64,256]{1,0:T(8,128)S(1)}, f32[64,256]{1,0:T(8,128)S(1)}, u32[]{:S(2)}, u32[]{:S(2)}) %collective-permute-start.14) | collective-permute-done | bytes 65568 | tf_op jit(solution)/shard_map/ppermute | solution.py:410
  58.4 1.9 %collective-permute-done.15.across_ref = f32[64,256]{1,0:T(8,128)S(1)} collective-permute-done((f32[64,256]{1,0:T(8,128)S(1)}, f32[64,256]{1,0:T(8,128)S(1)}, u32[]{:S(2)}, u32[]{:S(2)}) %collective-permute-start.15) | collective-permute-done | bytes 65568 | tf_op jit(solution)/shard_map/ppermute | solution.py:409
  60.3 0.7 %collective-permute-done.16.both_ref = f32[64,256]{1,0:T(8,128)S(1)} collective-permute-done((f32[64,256]{1,0:T(8,128)S(1)}, f32[64,256]{1,0:T(8,128)S(1)}, u32[]{:S(2)}, u32[]{:S(2)}) %collective-permute-start.16) | collective-permute-done | bytes 65568 | tf_op jit(solution)/shard_map/ppermute | solution.py:441
  61.0 2.0 %shard_map.110.mine_ref = bf16[2,32,2,512]{3,2,1,0:T(2,128)(2,1)S(1)} custom-call(s32[12]{0:T(128)S(1)} %stack.51.where_ref, f32[4,64,256]{2,1,0:T(8,128)S(1)} %get-tuple-element.55.a_ref.own_ref, f32[4,64,256]{2,1,0:T(8,128)S(1)} %collective-permute-done.13.b_ref.other_ref, f32[64,256]{1,0:T(8,128)S(1)} %collective-permute-done.14.beside_ref, ...), custom_call_target="tpu_custom_call" | custom-call | tf_op jit(solution)/shard_map/pallas_call | solution.py:346
  63.0 0.1 collective-permute-start.18
  63.0 1.3 %collective-permute-done.18.other_ref = bf16[2,32,2,512]{3,2,1,0:T(2,128)(2,1)S(1)} collective-permute-done((bf16[2,32,2,512]{3,2,1,0:T(2,128)(2,1)S(1)}, bf16[2,32,2,512]{3,2,1,0:T(2,128)(2,1)S(1)}, u32[]{:S(2)}, u32[]{:S(2)}) %collective-permute-start.18) | collective-permute-done | bytes 131104 | tf_op jit(solution)/shard_map/ppermute | solution.py:411
  64.4 1.3 %shard_map.111 = (bf16[64,2,512]{2,1,0:T(2,128)(2,1)}, bf16[64,2,512]{2,1,0:T(2,128)(2,1)}) custom-call(s32[12]{0:T(128)S(1)} %stack.51.where_ref, bf16[2,32,2,512]{3,2,1,0:T(2,128)(2,1)S(1)} %shard_map.110.mine_ref, bf16[2,32,2,512]{3,2,1,0:T(2,128)(2,1)S(1)} %collective-permute-done.18.other_ref), custom_call_target="tpu_custom_call" | custom-call | tf_op jit(solution)/shard_map/pallas_call | solution.py:212
  (19 shorter events, 0.1 us)
Async XLA Ops:
  0.6 5.3 %collective-permute-start = (bf16[1,8192,32]{1,2,0:T(8,128)(2,1)}, bf16[1,8192,32]{1,2,0:T(8,128)(2,1)S(1)}, u32[]{:S(2)}, u32[]{:S(2)}) collective-permute-start(bf16[1,8192,32]{1,2,0:T(8,128)(2,1)} %param.11), channel_id=1, source_target_pairs={{0,1},{1,0},{2,3},{3,2},{4,5},{5,4},{6,7},{7,6},{8,9},{9,8},{10,11... | collective-permute-start | bytes 1572872 | tf_op jit(solution)/shard_map/ppermute | solution.py:394
  1.1 4.8 %collective-permute-start.1 = (bf16[64,256]{1,0:T(8,128)(2,1)}, bf16[64,256]{1,0:T(8,128)(2,1)S(1)}, u32[]{:S(2)}, u32[]{:S(2)}) collective-permute-start(bf16[64,256]{1,0:T(8,128)(2,1)} %bitcast.26), channel_id=1, source_target_pairs={{0,2},{2,0},{4,6},{6,4},{8,10},{10,8},{12,14},{14,12},{1,3},{3,1},... | collective-permute-start | bytes 98312 | tf_op jit(solution)/shard_map/ppermute | solution.py:410
  3.7 1.2 %copy-start = (bf16[64,2,4096]{2,1,0:T(2,128)(2,1)S(1)}, bf16[64,2,4096]{2,1,0:T(2,128)(2,1)}, u32[]{:S(2)}) copy-start(bf16[64,2,4096]{2,1,0:T(2,128)(2,1)} %x_ref.1) | copy-start | bytes 3145732
  4.9 1.0 %copy-start.1 = (bf16[4096,64]{0,1:T(8,128)(2,1)S(1)}, bf16[4096,64]{0,1:T(8,128)(2,1)}, u32[]{:S(2)}) copy-start(bf16[4096,64]{0,1:T(8,128)(2,1)} %param.10) | copy-start | bytes 1572868
  4.9 1.2 %copy-start.2 = (bf16[1,8192,32]{1,2,0:T(8,128)(2,1)S(1)}, bf16[1,8192,32]{1,2,0:T(8,128)(2,1)}, u32[]{:S(2)}) copy-start(bf16[1,8192,32]{1,2,0:T(8,128)(2,1)} %param.11) | copy-start | bytes 1572868
  5.1 1.1 %copy-start.5 = (bf16[1,64,256]{2,1,0:T(8,128)(2,1)S(1)}, bf16[1,64,256]{2,1,0:T(8,128)(2,1)}, u32[]{:S(2)}) copy-start(bf16[1,64,256]{2,1,0:T(8,128)(2,1)} %param.12) | copy-start | bytes 98308
  6.1 8.2 %copy-start.3 = (bf16[64,16,256]{2,1,0:T(8,128)(2,1)S(1)}, bf16[64,16,256]{2,1,0:T(8,128)(2,1)}, u32[]{:S(2)}) copy-start(bf16[64,16,256]{2,1,0:T(8,128)(2,1)} %param.13) | copy-start | bytes 1572868
  6.8 25.3 %collective-permute-start.5 = (bf16[128,4096]{1,0:T(8,128)(2,1)S(1)}, bf16[128,4096]{1,0:T(8,128)(2,1)S(1)}, u32[]{:S(2)}, u32[]{:S(2)}) collective-permute-start(bf16[128,4096]{1,0:T(8,128)(2,1)S(1)} %shard_map.105.refs_0_), channel_id=1, source_target_pairs={{0,16},{16,0},{1,17},{17,1},{2,18},{18,2},{3,19},{19,3},{4,20},{20... | collective-permute-start | bytes 3145736 | tf_op jit(solution)/shard_map/ppermute | solution.py:409
  8.7 24.7 %collective-permute-start.4 = (bf16[128,4096]{1,0:T(8,128)(2,1)S(1)}, bf16[128,4096]{1,0:T(8,128)(2,1)S(1)}, u32[]{:S(2)}, u32[]{:S(2)}) collective-permute-start(bf16[128,4096]{1,0:T(8,128)(2,1)S(1)} %shard_map.105.refs_0_), channel_id=1, source_target_pairs={{0,2},{2,0},{4,6},{6,4},{8,10},{10,8},{12,14},{14,12},{1,3},{3,1},... | collective-permute-start | bytes 3145736 | tf_op jit(solution)/shard_map/ppermute | solution.py:410
  10.1 10.8 %collective-permute-start.9 = (bf16[32,4608]{1,0:T(8,128)(2,1)S(1)}, bf16[32,4608]{1,0:T(8,128)(2,1)S(1)}, u32[]{:S(2)}, u32[]{:S(2)}) collective-permute-start(bf16[32,4608]{1,0:T(8,128)(2,1)S(1)} %get-tuple-element.45.refs_3_.refs_5_), channel_id=1, source_target_pairs={{0,4},{2,6},{4,12},{6,14},{12,8},{14,10},{8,0},{10,2},{1,5},{3,7},... | collective-permute-start | bytes 884744 | tf_op jit(solution)/shard_map/ppermute | solution.py:408
  11.7 15.6 %collective-permute-start.2 = (bf16[32,4608]{1,0:T(8,128)(2,1)S(1)}, bf16[32,4608]{1,0:T(8,128)(2,1)S(1)}, u32[]{:S(2)}, u32[]{:S(2)}) collective-permute-start(bf16[32,4608]{1,0:T(8,128)(2,1)S(1)} %get-tuple-element.37.refs_4_.refs_6_), channel_id=1, source_target_pairs={{0,4},{2,6},{4,12},{6,14},{12,8},{14,10},{8,0},{10,2},{1,5},{3,7},... | collective-permute-start | bytes 884744 | tf_op jit(solution)/shard_map/ppermute | solution.py:408
  14.3 22.0 %collective-permute-start.6 = (bf16[1024,256]{1,0:T(8,128)(2,1)S(1)}, bf16[1024,256]{1,0:T(8,128)(2,1)S(1)}, u32[]{:S(2)}, u32[]{:S(2)}) collective-permute-start(bf16[1024,256]{1,0:T(8,128)(2,1)S(1)} %bitcast.23), channel_id=1, source_target_pairs={{0,1},{1,0},{2,3},{3,2},{4,5},{5,4},{6,7},{7,6},{8,9},{9,8},{10,11... | collective-permute-start | bytes 1572872 | tf_op jit(solution)/shard_map/ppermute | solution.py:411
  21.0 13.8 %collective-permute-start.10 = (bf16[32,4608]{1,0:T(8,128)(2,1)S(1)}, bf16[32,4608]{1,0:T(8,128)(2,1)S(1)}, u32[]{:S(2)}, u32[]{:S(2)}) collective-permute-start(bf16[32,4608]{1,0:T(8,128)(2,1)S(1)} %collective-permute-done.9.refs_5_.refs_7_), channel_id=1, source_target_pairs={{0,4},{2,6},{4,12},{6,14},{12,8},{14,10},{8,0},{10,2},{1,5},{3,7},... | collective-permute-start | bytes 884744 | tf_op jit(solution)/shard_map/ppermute | solution.py:408
  27.3 11.7 %collective-permute-start.3 = (bf16[32,4608]{1,0:T(8,128)(2,1)S(1)}, bf16[32,4608]{1,0:T(8,128)(2,1)S(1)}, u32[]{:S(2)}, u32[]{:S(2)}) collective-permute-start(bf16[32,4608]{1,0:T(8,128)(2,1)S(1)} %collective-permute-done.2.refs_6_.refs_8_), channel_id=1, source_target_pairs={{0,4},{2,6},{4,12},{6,14},{12,8},{14,10},{8,0},{10,2},{1,5},{3,7},... | collective-permute-start | bytes 884744 | tf_op jit(solution)/shard_map/ppermute | solution.py:408
  32.2 4.2 %copy-start.4 = (bf16[64,2,256]{2,1,0:T(2,128)(2,1)S(1)}, bf16[64,2,256]{2,1,0:T(2,128)(2,1)}, u32[]{:S(2)}) copy-start(bf16[64,2,256]{2,1,0:T(2,128)(2,1)} %fresh_ref.1) | copy-start | bytes 196612
  32.2 4.2 %copy-start.6 = (s32[64]{0:T(128)S(1)}, s32[64]{0:T(128)}, u32[]{:S(2)}) copy-start(s32[64]{0:T(128)} %lengths_ref.1) | copy-start | bytes 772
  32.2 4.2 %copy-start.7 = (s32[64]{0:T(128)S(1)}, s32[64]{0:T(128)}, u32[]{:S(2)}) copy-start(s32[64]{0:T(128)} %adapter_ref.1) | copy-start | bytes 772
  32.2 4.2 %copy-start.8 = (s32[8]{0:T(128)S(1)}, s32[8]{0:T(128)}, u32[]{:S(2)}) copy-start(s32[8]{0:T(128)} %owner_ref.1) | copy-start | bytes 100
  32.2 14.4 %collective-permute-start.7 = (bf16[64,4096]{1,0:T(8,128)(2,1)S(1)}, bf16[64,4096]{1,0:T(8,128)(2,1)S(1)}, u32[]{:S(2)}, u32[]{:S(2)}) collective-permute-start(bf16[64,4096]{1,0:T(8,128)(2,1)S(1)} %slice.8), channel_id=1, source_target_pairs={{0,2},{2,0},{4,6},{6,4},{8,10},{10,8},{12,14},{14,12},{1,3},{3,1},... | collective-permute-start | bytes 1572872 | tf_op jit(solution)/shard_map/ppermute | solution.py:410
  33.4 13.3 %collective-permute-start.8 = (bf16[64,4096]{1,0:T(8,128)(2,1)S(1)}, bf16[64,4096]{1,0:T(8,128)(2,1)S(1)}, u32[]{:S(2)}, u32[]{:S(2)}) collective-permute-start(bf16[64,4096]{1,0:T(8,128)(2,1)S(1)} %slice.9), channel_id=1, source_target_pairs={{0,16},{16,0},{1,17},{17,1},{2,18},{18,2},{3,19},{19,3},{4,20},{20... | collective-permute-start | bytes 1572872 | tf_op jit(solution)/shard_map/ppermute | solution.py:409
  34.8 10.8 %collective-permute-start.11 = (bf16[32,4608]{1,0:T(8,128)(2,1)S(1)}, bf16[32,4608]{1,0:T(8,128)(2,1)S(1)}, u32[]{:S(2)}, u32[]{:S(2)}) collective-permute-start(bf16[32,4608]{1,0:T(8,128)(2,1)S(1)} %collective-permute-done.10.refs_7_.refs_9_), channel_id=1, source_target_pairs={{0,4},{2,6},{4,12},{6,14},{12,8},{14,10},{8,0},{10,2},{1,5},{3,7},... | collective-permute-start | bytes 884744 | tf_op jit(solution)/shard_map/ppermute | solution.py:408
  39.0 11.3 %collective-permute-start.12 = (bf16[32,4608]{1,0:T(8,128)(2,1)S(1)}, bf16[32,4608]{1,0:T(8,128)(2,1)S(1)}, u32[]{:S(2)}, u32[]{:S(2)}) collective-permute-start(bf16[32,4608]{1,0:T(8,128)(2,1)S(1)} %collective-permute-done.3.refs_8_.refs_10_), channel_id=1, source_target_pairs={{0,4},{2,6},{4,12},{6,14},{12,8},{14,10},{8,0},{10,2},{1,5},{3,7},... | collective-permute-start | bytes 884744 | tf_op jit(solution)/shard_map/ppermute | solution.py:408
  52.5 1.6 %collective-permute-start.13 = (f32[4,64,256]{2,1,0:T(8,128)S(1)}, f32[4,64,256]{2,1,0:T(8,128)S(1)}, u32[]{:S(2)}, u32[]{:S(2)}) collective-permute-start(f32[4,64,256]{2,1,0:T(8,128)S(1)} %get-tuple-element.56), channel_id=1, source_target_pairs={{0,1},{1,0},{2,3},{3,2},{4,5},{5,4},{6,7},{7,6},{8,9},{9,8},{10,11... | collective-permute-start | bytes 786440 | tf_op jit(solution)/shard_map/ppermute | solution.py:411
  52.5 5.1 %collective-permute-start.17 = (bf16[512,256]{1,0:T(8,128)(2,1)S(1)}, bf16[512,256]{1,0:T(8,128)(2,1)S(1)}, u32[]{:S(2)}, u32[]{:S(2)}) collective-permute-start(bf16[512,256]{1,0:T(8,128)(2,1)S(1)} %get-tuple-element.61.up_ref), channel_id=1, source_target_pairs={{0,1},{1,0},{2,3},{3,2},{4,5},{5,4},{6,7},{7,6},{8,9},{9,8},{10,11... | collective-permute-start | bytes 786440 | tf_op jit(solution)/shard_map/ppermute | solution.py:411
  54.1 4.3 %collective-permute-start.14 = (f32[64,256]{1,0:T(8,128)S(1)}, f32[64,256]{1,0:T(8,128)S(1)}, u32[]{:S(2)}, u32[]{:S(2)}) collective-permute-start(f32[64,256]{1,0:T(8,128)S(1)} %get-tuple-element.57), channel_id=1, source_target_pairs={{0,2},{2,0},{4,6},{6,4},{8,10},{10,8},{12,14},{14,12},{1,3},{3,1},... | collective-permute-start | bytes 196616 | tf_op jit(solution)/shard_map/ppermute | solution.py:410
  55.3 5.0 %collective-permute-start.15 = (f32[64,256]{1,0:T(8,128)S(1)}, f32[64,256]{1,0:T(8,128)S(1)}, u32[]{:S(2)}, u32[]{:S(2)}) collective-permute-start(f32[64,256]{1,0:T(8,128)S(1)} %get-tuple-element.58), channel_id=1, source_target_pairs={{0,16},{16,0},{1,17},{17,1},{2,18},{18,2},{3,19},{19,3},{4,20},{20... | collective-permute-start | bytes 196616 | tf_op jit(solution)/shard_map/ppermute | solution.py:409
  55.8 5.2 %collective-permute-start.16 = (f32[64,256]{1,0:T(8,128)S(1)}, f32[64,256]{1,0:T(8,128)S(1)}, u32[]{:S(2)}, u32[]{:S(2)}) collective-permute-start(f32[64,256]{1,0:T(8,128)S(1)} %get-tuple-element.59), channel_id=1, source_target_pairs={{0,18},{2,16},{4,22},{6,20},{8,26},{10,24},{12,30},{14,28},{16,2},... | collective-permute-start | bytes 196616 | tf_op jit(solution)/shard_map/ppermute | solution.py:441
  63.0 1.4 %collective-permute-start.18 = (bf16[2,32,2,512]{3,2,1,0:T(2,128)(2,1)S(1)}, bf16[2,32,2,512]{3,2,1,0:T(2,128)(2,1)S(1)}, u32[]{:S(2)}, u32[]{:S(2)}) collective-permute-start(bf16[2,32,2,512]{3,2,1,0:T(2,128)(2,1)S(1)} %shard_map.110.mine_ref), channel_id=1, source_target_pairs={{0,1},{1,0},{2,3},{3,2},{4,5},{5,4},{6,7},{7,6},{8,9},{9,8},{10,11... | collective-permute-start | bytes 393224 | tf_op jit(solution)/shard_map/ppermute | solution.py:411

commit v6 on v5

--- a/solution.py
+++ b/solution.py
@@ -10,7 +10,7 @@
 
 SWAP = [(0, 1), (1, 0)]
 FAR = -1e30
-PER = 8
+PER = 16
 
 
 def nt_dot(a, b):
@@ -153,44 +153,43 @@
 
 
 def late_kernel(where_ref, *refs):
-    sets, (low_ref, high_ref) = refs[:3], refs[3:5]
-    weights, (t_ref, kept_ref, given_ref, up_ref) = refs[5:-4], refs[-4:]
-    half, features = low_ref.shape
+    sets, weights = refs[:5], refs[5:-5]
+    t_ref, corner_ref, kept_ref, given_ref, up_ref = refs[-5:]
+    half, features = sets[-1].shape
     count, columns = weights[0].shape[0], up_ref.shape[1]
     for k, ref in enumerate(weights):
         at = (k % 2) * (len(weights) * count) + (k // 2) * (2 * count)
         for part in range(2):
             lanes = slice(features + part * columns, features + (part + 1) * columns)
             up_ref[at + part * count : at + (part + 1) * count] = ref[:, lanes]
-    all_columns = jnp.concatenate([w[:, :features] for w in weights], axis=0)
-    late = nt_dot(jnp.concatenate([low_ref[...], high_ref[...]], axis=0), all_columns)
     last = nt_dot(jnp.concatenate([r[...] for r in sets], axis=0), weights[-1][:, :features])
     first = where_ref[3] == 0
     for k in range(4):
-        if k < 3:
-            low, high = (
-                jnp.concatenate([r[at * half : (at + 1) * half] for r in (t_ref, last)], axis=1)
-                for at in (2 * k, 2 * k + 1)
+        ref, base = (t_ref, 2 * k * half) if k < 3 else (corner_ref, 0)
+        low, high = (
+            jnp.concatenate(
+                [ref[base + p * half : base + (p + 1) * half], last[(2 * k + p) * half : (2 * k + p + 1) * half]],
+                axis=1,
             )
-        else:
-            low, high = late[:half], late[half:]
+            for p in range(2)
+        )
         kept_ref[k] = jnp.where(first, low, high)
         given_ref[k] = jnp.where(first, high, low)
 
 
-def late_products(where, sets, low, high, weights, t):
+def late_products(where, sets, weights, t, corner):
     smem, vmem = (pl.BlockSpec(memory_space=m) for m in (pltpu.SMEM, pltpu.VMEM))
     count, lanes = weights[0].shape
-    half, features = low.shape
+    half, features = sets[-1].shape
     shape = jax.ShapeDtypeStruct((4, half, len(weights) * count), jnp.float32)
     up = ((2 * len(weights)) * count, (lanes - features) // 2)
     return pl.pallas_call(
         late_kernel,
-        out_shape=(shape, shape, jax.ShapeDtypeStruct(up, low.dtype)),
-        in_specs=[smem] + [vmem] * (len(sets) + len(weights) + 3),
+        out_shape=(shape, shape, jax.ShapeDtypeStruct(up, sets[0].dtype)),
+        in_specs=[smem] + [vmem] * (len(sets) + len(weights) + 2),
         out_specs=(vmem,) * 3,
         compiler_params=pltpu.CompilerParams(vmem_limit_bytes=12 << 20),
-    )(where, *sets, low, high, *weights, t)
+    )(where, *sets, *weights, t, corner)
 
 
 def join_kernel(where_ref, mine_ref, other_ref, queries_ref, attended_ref, sems):
@@ -233,17 +232,12 @@
     )(a, b)
 
 
-def attend_block(queries, keys, values, masks, scaling):
-    scores = [jnp.where(m, nt_dot(queries, k) * scaling, FAR) for k, m in zip(keys, masks)]
-    highest = scores[0].max(axis=1, keepdims=True)
-    for s in scores[1:]:
-        highest = jnp.maximum(highest, s.max(axis=1, keepdims=True))
-    weights = [jnp.where(m, jnp.exp(s - highest), 0.0) for s, m in zip(scores, masks)]
-    totals = sum(w.sum(axis=1, keepdims=True) for w in weights)
-    sums = sum(
-        jnp.dot(w.astype(jnp.bfloat16), v, preferred_element_type=jnp.float32)
-        for w, v in zip(weights, values)
-    )
+def attend_block(queries, keys, values, mask, scaling):
+    scores = jnp.where(mask, nt_dot(queries, keys) * scaling, FAR)
+    highest = scores.max(axis=1, keepdims=True)
+    weights = jnp.where(mask, jnp.exp(scores - highest), 0.0)
+    totals = weights.sum(axis=1, keepdims=True)
+    sums = jnp.dot(weights.astype(jnp.bfloat16), values, preferred_element_type=jnp.float32)
     return sums / totals
 
 
@@ -275,7 +269,10 @@
         masks.append(jnp.logical_and(row // steps == column // steps, column <= row))
         keys.append(block[:, :head])
         values.append(block[:, head:])
-        mixed = attend_block(stacked, keys, values, masks, scaling).astype(jnp.bfloat16)
+        mixed = attend_block(
+            stacked, *(jnp.concatenate(a, axis=0) for a in (keys, values)),
+            jnp.concatenate(masks, axis=1), scaling,
+        ).astype(jnp.bfloat16)
         put(
             b,
             jnp.concatenate([mixed[h * take : (h + 1) * take] for h in range(heads)], axis=1),
@@ -431,10 +428,10 @@
         b3 = along(b2, ring)
         weights = a0, b0, a1, b1, a2, b2, a3, b3
         sets = mine, x_beside, x_across
-        t = products(sets, weights[:-1])
-
-        low, high, t, prepared = bar(low, high, t, prepared)
-        kept, given, up = late_products(where, sets, low, high, weights, t)
+        t, corner_t = products(sets, weights[:-1]), products((low, high), weights[:-1])
+
+        t, corner_t, prepared = bar(t, corner_t, prepared)
+        kept, given, up = late_products(where, sets + (low, high), weights, t, corner_t)
         got = inside(given)
         t_beside, t_across, t_both = add_halves(kept, got)
         t_beside, t_across = beside(t_beside), across(t_across)

time: 65.8 us -> 65.1 us (0.989)
  waiting for transfers between devices: 34.3 us -> 33.5 us
    ppermute x6, waiting for transfers between devices: 23.6 us -> 22.8 us  [body(): along = lambda a, moves: lax.ppermute(a, 'group', line_pairs(groups, moves))]
    pallas_call x1 -> x2, Pallas kernels: 1.03 us -> 1.77 us  [products(): pl.pallas_call(functools.partial(products_kernel, len(sets)), out_shape=j...]
  transfers between devices with their start and end apart: 19 -> 19, of which waited for: 13 -> 13; matrix products, arithmetic and copies ran while one was open for 0% -> 0% of each run, Pallas kernels for 3% -> 4%
where the time goes in v6:
time: 65.1 us; the launch traced here: 64.9 us
  waiting for transfers between devices  33.5 us (51%)
  starting transfers between devices  21 us (32%)
  Pallas kernels  7.95 us (12%)
  local copies, waits for them, and re-layouts  1.65 us (3%)
  between operations  0.8 us (1%)
    ppermute x6, waiting for transfers between devices, body(): along = lambda a, moves: lax.ppermute(a, 'group', line_pairs(groups, moves))  22.8 us
    ppermute x6, starting transfers between devices, body(): along = lambda a, moves: lax.ppermute(a, 'group', line_pairs(groups, moves))  8.1 us
    ppermute x4, starting transfers between devices, body(): lax.ppermute(a, 'group', [(i, i ^ 1) for i in range(groups)])  6.21 us
    ppermute x3, waiting for transfers between devices, body(): across = lambda a: lax.ppermute(a, 'parts', SWAP)  5.9 us
    ppermute x3, starting transfers between devices, body(): across = lambda a: lax.ppermute(a, 'parts', SWAP)  3.69 us
    ppermute x4, waiting for transfers between devices, body(): inside = lambda a: lax.ppermute(a, 'tensor', SWAP)  2.36 us
    pallas_call x1, Pallas kernels, late_products(): pl.pallas_call(late_kernel, out_shape=(shape, shape, jax.ShapeDtypeStruct...  1.85 us
    ppermute x1, starting transfers between devices, body(): t_both = lax.ppermute(t_both, ('parts', 'group'), corner)  1.82 us
  transfers between devices with their start and end apart: 19, of which 13 were waited for; matrix products, arithmetic and copies ran while one was open for 0% of the time, Pallas kernels for 4%

profile of v6, /device:TPU:0, one launch (start us, length us, event | category | flops | bytes accessed | tf_op | source)
XLA Modules:
  0.0 64.9 jit_solution(5774564332674964560)
XLA Ops:
  0.6 0.5 collective-permute-start
  1.1 2.6 %collective-permute-start.1 = (bf16[64,256]{1,0:T(8,128)(2,1)}, bf16[64,256]{1,0:T(8,128)(2,1)S(1)}, u32[]{:S(2)}, u32[]{:S(2)}) collective-permute-start(bf16[64,256]{1,0:T(8,128)(2,1)} %bitcast.26), channel_id=1, source_target_pairs={{0,2},{2,0},{4,6},{6,4},{8,10},{10,8},{12,14},{14,12},{1,3},{3,1},... | collective-permute-start | bytes 98312 | tf_op jit(solution)/shard_map/ppermute | solution.py:407
  3.7 1.2 %copy-done = bf16[64,2,4096]{2,1,0:T(2,128)(2,1)S(1)} copy-done((bf16[64,2,4096]{2,1,0:T(2,128)(2,1)S(1)}, bf16[64,2,4096]{2,1,0:T(2,128)(2,1)}, u32[]{:S(2)}) %copy-start) | copy-done | bytes 1048600
  4.9 0.1 shard_map.105.refs_0_
  5.1 0.0 copy-start.5
  5.1 0.1 stack.51.where_ref
  5.2 0.7 %collective-permute-done.1.up_beside_ref = bf16[64,256]{1,0:T(8,128)(2,1)S(1)} collective-permute-done((bf16[64,256]{1,0:T(8,128)(2,1)}, bf16[64,256]{1,0:T(8,128)(2,1)S(1)}, u32[]{:S(2)}, u32[]{:S(2)}) %collective-permute-start.1) | collective-permute-done | bytes 32800 | tf_op jit(solution)/shard_map/ppermute | solution.py:407
  5.9 0.1 copy-done.1
  6.0 0.2 copy-done.2
  6.1 0.7 %shard_map.104 = (bf16[32,4608]{1,0:T(8,128)(2,1)S(1)}, bf16[32,4608]{1,0:T(8,128)(2,1)S(1)}) custom-call(s32[12]{0:T(128)S(1)} %stack.51.where_ref, bf16[64,4096]{1,0:T(8,128)(2,1)S(1)} %bitcast.21, bf16[32,8192]{1,0:T(8,128)(2,1)S(1)} %bitcast.22, bf16[32,8192]{1,0:T(8,128)(2,1)S(1)} %bitcast.25, bf16[64,256]{1,0:T(8,128)(2,1)S(1)} %bitcast.27, ...), custom_call_target="tpu_custom_call" | custom-call | tf_op jit(solution)/shard_map/pallas_call | solution.py:59
  6.8 1.8 %collective-permute-start.5 = (bf16[128,4096]{1,0:T(8,128)(2,1)S(1)}, bf16[128,4096]{1,0:T(8,128)(2,1)S(1)}, u32[]{:S(2)}, u32[]{:S(2)}) collective-permute-start(bf16[128,4096]{1,0:T(8,128)(2,1)S(1)} %shard_map.105.refs_0_), channel_id=1, source_target_pairs={{0,16},{16,0},{1,17},{17,1},{2,18},{18,2},{3,19},{19,3},{4,20},{20... | collective-permute-start | bytes 3145736 | tf_op jit(solution)/shard_map/ppermute | solution.py:406
  8.7 1.5 %collective-permute-start.4 = (bf16[128,4096]{1,0:T(8,128)(2,1)S(1)}, bf16[128,4096]{1,0:T(8,128)(2,1)S(1)}, u32[]{:S(2)}, u32[]{:S(2)}) collective-permute-start(bf16[128,4096]{1,0:T(8,128)(2,1)S(1)} %shard_map.105.refs_0_), channel_id=1, source_target_pairs={{0,2},{2,0},{4,6},{6,4},{8,10},{10,8},{12,14},{14,12},{1,3},{3,1},... | collective-permute-start | bytes 3145736 | tf_op jit(solution)/shard_map/ppermute | solution.py:407
  10.1 1.6 %collective-permute-start.9 = (bf16[32,4608]{1,0:T(8,128)(2,1)S(1)}, bf16[32,4608]{1,0:T(8,128)(2,1)S(1)}, u32[]{:S(2)}, u32[]{:S(2)}) collective-permute-start(bf16[32,4608]{1,0:T(8,128)(2,1)S(1)} %get-tuple-element.44.refs_3_.refs_2_.refs_5_), channel_id=1, source_target_pairs={{0,4},{2,6},{4,12},{6,14},{12,8},{14,10},{8,0},{10,2},{1,5},{3,7},... | collective-permute-start | bytes 884744 | tf_op jit(solution)/shard_map/ppermute | solution.py:405
  11.7 2.6 %collective-permute-start.2 = (bf16[32,4608]{1,0:T(8,128)(2,1)S(1)}, bf16[32,4608]{1,0:T(8,128)(2,1)S(1)}, u32[]{:S(2)}, u32[]{:S(2)}) collective-permute-start(bf16[32,4608]{1,0:T(8,128)(2,1)S(1)} %get-tuple-element.36.refs_4_.refs_3_.refs_6_), channel_id=1, source_target_pairs={{0,4},{2,6},{4,12},{6,14},{12,8},{14,10},{8,0},{10,2},{1,5},{3,7},... | collective-permute-start | bytes 884744 | tf_op jit(solution)/shard_map/ppermute | solution.py:405
  14.3 6.7 %collective-permute-done.9.refs_5_.refs_4_.refs_7_ = bf16[32,4608]{1,0:T(8,128)(2,1)S(1)} collective-permute-done((bf16[32,4608]{1,0:T(8,128)(2,1)S(1)}, bf16[32,4608]{1,0:T(8,128)(2,1)S(1)}, u32[]{:S(2)}, u32[]{:S(2)}) %collective-permute-start.9) | collective-permute-done | bytes 294944 | tf_op jit(solution)/shard_map/ppermute | solution.py:405
  21.0 0.8 %collective-permute-start.10 = (bf16[32,4608]{1,0:T(8,128)(2,1)S(1)}, bf16[32,4608]{1,0:T(8,128)(2,1)S(1)}, u32[]{:S(2)}, u32[]{:S(2)}) collective-permute-start(bf16[32,4608]{1,0:T(8,128)(2,1)S(1)} %collective-permute-done.9.refs_5_.refs_4_.refs_7_), channel_id=1, source_target_pairs={{0,4},{2,6},{4,12},{6,14},{12,8},{14,10},{8,0},{10,2},{1,5},{3,7},... | collective-permute-start | bytes 884744 | tf_op jit(solution)/shard_map/ppermute | solution.py:405
  21.8 5.5 %collective-permute-done.2.refs_6_.refs_5_.refs_8_ = bf16[32,4608]{1,0:T(8,128)(2,1)S(1)} collective-permute-done((bf16[32,4608]{1,0:T(8,128)(2,1)S(1)}, bf16[32,4608]{1,0:T(8,128)(2,1)S(1)}, u32[]{:S(2)}, u32[]{:S(2)}) %collective-permute-start.2) | collective-permute-done | bytes 294944 | tf_op jit(solution)/shard_map/ppermute | solution.py:405
  27.3 0.8 %collective-permute-start.3 = (bf16[32,4608]{1,0:T(8,128)(2,1)S(1)}, bf16[32,4608]{1,0:T(8,128)(2,1)S(1)}, u32[]{:S(2)}, u32[]{:S(2)}) collective-permute-start(bf16[32,4608]{1,0:T(8,128)(2,1)S(1)} %collective-permute-done.2.refs_6_.refs_5_.refs_8_), channel_id=1, source_target_pairs={{0,4},{2,6},{4,12},{6,14},{12,8},{14,10},{8,0},{10,2},{1,5},{3,7},... | collective-permute-start | bytes 884744 | tf_op jit(solution)/shard_map/ppermute | solution.py:405
  28.1 4.0 %collective-permute-done.5.refs_2_ = bf16[128,4096]{1,0:T(8,128)(2,1)S(1)} collective-permute-done((bf16[128,4096]{1,0:T(8,128)(2,1)S(1)}, bf16[128,4096]{1,0:T(8,128)(2,1)S(1)}, u32[]{:S(2)}, u32[]{:S(2)}) %collective-permute-start.5) | collective-permute-done | bytes 1048608 | tf_op jit(solution)/shard_map/ppermute | solution.py:406
  32.2 0.0 copy-start.4
  32.2 0.0 copy-start.6
  32.2 0.0 copy-start.7
  32.2 0.0 copy-start.8
  32.2 0.9 %collective-permute-start.7 = (bf16[64,4096]{1,0:T(8,128)(2,1)S(1)}, bf16[64,4096]{1,0:T(8,128)(2,1)S(1)}, u32[]{:S(2)}, u32[]{:S(2)}) collective-permute-start(bf16[64,4096]{1,0:T(8,128)(2,1)S(1)} %slice.8), channel_id=1, source_target_pairs={{0,2},{2,0},{4,6},{6,4},{8,10},{10,8},{12,14},{14,12},{1,3},{3,1},... | collective-permute-start | bytes 1572872 | tf_op jit(solution)/shard_map/ppermute | solution.py:407
  33.1 0.2 collective-permute-done.4.refs_1_
  33.4 1.4 %collective-permute-start.8 = (bf16[64,4096]{1,0:T(8,128)(2,1)S(1)}, bf16[64,4096]{1,0:T(8,128)(2,1)S(1)}, u32[]{:S(2)}, u32[]{:S(2)}) collective-permute-start(bf16[64,4096]{1,0:T(8,128)(2,1)S(1)} %slice.9), channel_id=1, source_target_pairs={{0,16},{16,0},{1,17},{17,1},{2,18},{18,2},{3,19},{19,3},{4,20},{20... | collective-permute-start | bytes 1572872 | tf_op jit(solution)/shard_map/ppermute | solution.py:406
  34.8 1.6 %collective-permute-start.11 = (bf16[32,4608]{1,0:T(8,128)(2,1)S(1)}, bf16[32,4608]{1,0:T(8,128)(2,1)S(1)}, u32[]{:S(2)}, u32[]{:S(2)}) collective-permute-start(bf16[32,4608]{1,0:T(8,128)(2,1)S(1)} %collective-permute-done.10.refs_7_.refs_6_.refs_9_), channel_id=1, source_target_pairs={{0,4},{2,6},{4,12},{6,14},{12,8},{14,10},{8,0},{10,2},{1,5},{3,7},... | collective-permute-start | bytes 884744 | tf_op jit(solution)/shard_map/ppermute | solution.py:405
  36.4 0.7 %shard_map.106 = (bf16[512,256]{1,0:T(8,128)(2,1)S(1)}, bf16[512,256]{1,0:T(8,128)(2,1)S(1)}, bf16[64,256]{1,0:T(8,128)(2,1)S(1)}, s32[8,256]{1,0:T(8,128)S(1)}, s32[64,128]{1,0:T(8,128)S(1)}) custom-call(s32[12]{0:T(128)S(1)} %stack.51.where_ref, s32[64]{0:T(128)S(1)} %copy-done.6, s32[64]{0:T(128)S(1)} %copy-done.7, s32[8]{0:T(128)S(1)} %copy-done.8, ...), custom_call_target="tpu_custom_call" | custom-call | tf_op jit(solution)/shard_map/pallas_call | solution.py:118
  37.1 1.9 %collective-permute-done.3.refs_8_.refs_7_.refs_10_ = bf16[32,4608]{1,0:T(8,128)(2,1)S(1)} collective-permute-done((bf16[32,4608]{1,0:T(8,128)(2,1)S(1)}, bf16[32,4608]{1,0:T(8,128)(2,1)S(1)}, u32[]{:S(2)}, u32[]{:S(2)}) %collective-permute-start.3) | collective-permute-done | bytes 294944 | tf_op jit(solution)/shard_map/ppermute | solution.py:405
  39.0 0.8 %collective-permute-start.12 = (bf16[32,4608]{1,0:T(8,128)(2,1)S(1)}, bf16[32,4608]{1,0:T(8,128)(2,1)S(1)}, u32[]{:S(2)}, u32[]{:S(2)}) collective-permute-start(bf16[32,4608]{1,0:T(8,128)(2,1)S(1)} %collective-permute-done.3.refs_8_.refs_7_.refs_10_), channel_id=1, source_target_pairs={{0,4},{2,6},{4,12},{6,14},{12,8},{14,10},{8,0},{10,2},{1,5},{3,7},... | collective-permute-start | bytes 884744 | tf_op jit(solution)/shard_map/ppermute | solution.py:405
  39.8 5.8 %collective-permute-done.11.refs_9_.refs_8_.refs_11_ = bf16[32,4608]{1,0:T(8,128)(2,1)S(1)} collective-permute-done((bf16[32,4608]{1,0:T(8,128)(2,1)S(1)}, bf16[32,4608]{1,0:T(8,128)(2,1)S(1)}, u32[]{:S(2)}, u32[]{:S(2)}) %collective-permute-start.11) | collective-permute-done | bytes 294944 | tf_op jit(solution)/shard_map/ppermute | solution.py:405
  45.6 1.0 %shard_map.107.refs_13_ = f32[384,224]{1,0:T(8,128)S(1)} custom-call(bf16[128,4096]{1,0:T(8,128)(2,1)S(1)} %shard_map.105.refs_0_, bf16[128,4096]{1,0:T(8,128)(2,1)S(1)} %collective-permute-done.4.refs_1_, bf16[128,4096]{1,0:T(8,128)(2,1)S(1)} %collective-permute-done.5.refs_2_, bf16[32,4608]{1,0:T(8,128)(2,1)S(1)} %get-tuple-element.44.refs_3_.refs_2_.refs_5_, ...), custom_call_target="tpu_custom_call" | custom-call | flops 704643072 | bytes 4980736 | tf_op jit(solution)/shard_map/pallas_call | solution.py:143
  46.7 0.7 %shard_map.108.refs_14_ = f32[128,224]{1,0:T(8,128)S(1)} custom-call(bf16[64,4096]{1,0:T(8,128)(2,1)S(1)} %collective-permute-done.7.refs_0_.refs_3_, bf16[64,4096]{1,0:T(8,128)(2,1)S(1)} %collective-permute-done.8.refs_1_.refs_4_, bf16[32,4608]{1,0:T(8,128)(2,1)S(1)} %get-tuple-element.44.refs_3_.refs_2_.refs_5_, ...), custom_call_target="tpu_custom_call" | custom-call | flops 234881024 | bytes 2883584 | tf_op jit(solution)/shard_map/pallas_call | solution.py:143
  47.4 2.9 %collective-permute-done.12.refs_12_ = bf16[32,4608]{1,0:T(8,128)(2,1)S(1)} collective-permute-done((bf16[32,4608]{1,0:T(8,128)(2,1)S(1)}, bf16[32,4608]{1,0:T(8,128)(2,1)S(1)}, u32[]{:S(2)}, u32[]{:S(2)}) %collective-permute-start.12) | collective-permute-done | bytes 294944 | tf_op jit(solution)/shard_map/ppermute | solution.py:405
  50.3 1.8 %shard_map.109 = (f32[4,64,256]{2,1,0:T(8,128)S(1)}, f32[4,64,256]{2,1,0:T(8,128)S(1)}, bf16[512,256]{1,0:T(8,128)(2,1)S(1)}) custom-call(s32[12]{0:T(128)S(1)} %stack.51.where_ref, bf16[128,4096]{1,0:T(8,128)(2,1)S(1)} %shard_map.105.refs_0_, bf16[128,4096]{1,0:T(8,128)(2,1)S(1)} %collective-permute-done.4.refs_1_, ...), custom_call_target="tpu_custom_call" | custom-call | tf_op jit(solution)/shard_map/pallas_call | solution.py:186
  52.1 0.1 collective-permute-start.13
  52.2 0.5 collective-permute-start.17
  52.7 1.0 %collective-permute-done.13.b_ref.other_ref = f32[4,64,256]{2,1,0:T(8,128)S(1)} collective-permute-done((f32[4,64,256]{2,1,0:T(8,128)S(1)}, f32[4,64,256]{2,1,0:T(8,128)S(1)}, u32[]{:S(2)}, u32[]{:S(2)}) %collective-permute-start.13) | collective-permute-done | bytes 262176 | tf_op jit(solution)/shard_map/ppermute | solution.py:408
  53.8 1.2 %collective-permute-start.14 = (f32[64,256]{1,0:T(8,128)S(1)}, f32[64,256]{1,0:T(8,128)S(1)}, u32[]{:S(2)}, u32[]{:S(2)}) collective-permute-start(f32[64,256]{1,0:T(8,128)S(1)} %get-tuple-element.55), channel_id=1, source_target_pairs={{0,2},{2,0},{4,6},{6,4},{8,10},{10,8},{12,14},{14,12},{1,3},{3,1},... | collective-permute-start | bytes 196616 | tf_op jit(solution)/shard_map/ppermute | solution.py:407
  55.0 0.5 collective-permute-start.15
  55.5 1.8 %collective-permute-start.16 = (f32[64,256]{1,0:T(8,128)S(1)}, f32[64,256]{1,0:T(8,128)S(1)}, u32[]{:S(2)}, u32[]{:S(2)}) collective-permute-start(f32[64,256]{1,0:T(8,128)S(1)} %get-tuple-element.57), channel_id=1, source_target_pairs={{0,18},{2,16},{4,22},{6,20},{8,26},{10,24},{12,30},{14,28},{16,2},... | collective-permute-start | bytes 196616 | tf_op jit(solution)/shard_map/ppermute | solution.py:438
  57.3 0.8 %collective-permute-done.14.beside_ref = f32[64,256]{1,0:T(8,128)S(1)} collective-permute-done((f32[64,256]{1,0:T(8,128)S(1)}, f32[64,256]{1,0:T(8,128)S(1)}, u32[]{:S(2)}, u32[]{:S(2)}) %collective-permute-start.14) | collective-permute-done | bytes 65568 | tf_op jit(solution)/shard_map/ppermute | solution.py:407
  58.1 1.9 %collective-permute-done.15.across_ref = f32[64,256]{1,0:T(8,128)S(1)} collective-permute-done((f32[64,256]{1,0:T(8,128)S(1)}, f32[64,256]{1,0:T(8,128)S(1)}, u32[]{:S(2)}, u32[]{:S(2)}) %collective-permute-start.15) | collective-permute-done | bytes 65568 | tf_op jit(solution)/shard_map/ppermute | solution.py:406
  60.0 0.7 %collective-permute-done.16.both_ref = f32[64,256]{1,0:T(8,128)S(1)} collective-permute-done((f32[64,256]{1,0:T(8,128)S(1)}, f32[64,256]{1,0:T(8,128)S(1)}, u32[]{:S(2)}, u32[]{:S(2)}) %collective-permute-start.16) | collective-permute-done | bytes 65568 | tf_op jit(solution)/shard_map/ppermute | solution.py:438
  60.7 1.5 %shard_map.111.mine_ref = bf16[2,32,2,512]{3,2,1,0:T(2,128)(2,1)S(1)} custom-call(s32[12]{0:T(128)S(1)} %stack.51.where_ref, f32[4,64,256]{2,1,0:T(8,128)S(1)} %get-tuple-element.53.a_ref.own_ref, f32[4,64,256]{2,1,0:T(8,128)S(1)} %collective-permute-done.13.b_ref.other_ref, f32[64,256]{1,0:T(8,128)S(1)} %collective-permute-done.14.beside_ref, ...), custom_call_target="tpu_custom_call" | custom-call | tf_op jit(solution)/shard_map/pallas_call | solution.py:343
  62.2 0.1 collective-permute-start.18
  62.3 1.3 %collective-permute-done.18.other_ref = bf16[2,32,2,512]{3,2,1,0:T(2,128)(2,1)S(1)} collective-permute-done((bf16[2,32,2,512]{3,2,1,0:T(2,128)(2,1)S(1)}, bf16[2,32,2,512]{3,2,1,0:T(2,128)(2,1)S(1)}, u32[]{:S(2)}, u32[]{:S(2)}) %collective-permute-start.18) | collective-permute-done | bytes 131104 | tf_op jit(solution)/shard_map/ppermute | solution.py:408
  63.6 1.3 %shard_map.112 = (bf16[64,2,512]{2,1,0:T(2,128)(2,1)}, bf16[64,2,512]{2,1,0:T(2,128)(2,1)}) custom-call(s32[12]{0:T(128)S(1)} %stack.51.where_ref, bf16[2,32,2,512]{3,2,1,0:T(2,128)(2,1)S(1)} %shard_map.111.mine_ref, bf16[2,32,2,512]{3,2,1,0:T(2,128)(2,1)S(1)} %collective-permute-done.18.other_ref), custom_call_target="tpu_custom_call" | custom-call | tf_op jit(solution)/shard_map/pallas_call | solution.py:211
  (20 shorter events, 0.1 us)
Async XLA Ops:
  0.6 5.3 %collective-permute-start = (bf16[1,8192,32]{1,2,0:T(8,128)(2,1)}, bf16[1,8192,32]{1,2,0:T(8,128)(2,1)S(1)}, u32[]{:S(2)}, u32[]{:S(2)}) collective-permute-start(bf16[1,8192,32]{1,2,0:T(8,128)(2,1)} %param.11), channel_id=1, source_target_pairs={{0,1},{1,0},{2,3},{3,2},{4,5},{5,4},{6,7},{7,6},{8,9},{9,8},{10,11... | collective-permute-start | bytes 1572872 | tf_op jit(solution)/shard_map/ppermute | solution.py:391
  1.1 4.8 %collective-permute-start.1 = (bf16[64,256]{1,0:T(8,128)(2,1)}, bf16[64,256]{1,0:T(8,128)(2,1)S(1)}, u32[]{:S(2)}, u32[]{:S(2)}) collective-permute-start(bf16[64,256]{1,0:T(8,128)(2,1)} %bitcast.26), channel_id=1, source_target_pairs={{0,2},{2,0},{4,6},{6,4},{8,10},{10,8},{12,14},{14,12},{1,3},{3,1},... | collective-permute-start | bytes 98312 | tf_op jit(solution)/shard_map/ppermute | solution.py:407
  3.7 1.2 %copy-start = (bf16[64,2,4096]{2,1,0:T(2,128)(2,1)S(1)}, bf16[64,2,4096]{2,1,0:T(2,128)(2,1)}, u32[]{:S(2)}) copy-start(bf16[64,2,4096]{2,1,0:T(2,128)(2,1)} %x_ref.1) | copy-start | bytes 3145732
  4.9 1.0 %copy-start.1 = (bf16[4096,64]{0,1:T(8,128)(2,1)S(1)}, bf16[4096,64]{0,1:T(8,128)(2,1)}, u32[]{:S(2)}) copy-start(bf16[4096,64]{0,1:T(8,128)(2,1)} %param.10) | copy-start | bytes 1572868
  4.9 1.2 %copy-start.2 = (bf16[1,8192,32]{1,2,0:T(8,128)(2,1)S(1)}, bf16[1,8192,32]{1,2,0:T(8,128)(2,1)}, u32[]{:S(2)}) copy-start(bf16[1,8192,32]{1,2,0:T(8,128)(2,1)} %param.11) | copy-start | bytes 1572868
  5.1 1.1 %copy-start.5 = (bf16[1,64,256]{2,1,0:T(8,128)(2,1)S(1)}, bf16[1,64,256]{2,1,0:T(8,128)(2,1)}, u32[]{:S(2)}) copy-start(bf16[1,64,256]{2,1,0:T(8,128)(2,1)} %param.12) | copy-start | bytes 98308
  6.1 8.2 %copy-start.3 = (bf16[64,16,256]{2,1,0:T(8,128)(2,1)S(1)}, bf16[64,16,256]{2,1,0:T(8,128)(2,1)}, u32[]{:S(2)}) copy-start(bf16[64,16,256]{2,1,0:T(8,128)(2,1)} %param.13) | copy-start | bytes 1572868
  6.8 25.3 %collective-permute-start.5 = (bf16[128,4096]{1,0:T(8,128)(2,1)S(1)}, bf16[128,4096]{1,0:T(8,128)(2,1)S(1)}, u32[]{:S(2)}, u32[]{:S(2)}) collective-permute-start(bf16[128,4096]{1,0:T(8,128)(2,1)S(1)} %shard_map.105.refs_0_), channel_id=1, source_target_pairs={{0,16},{16,0},{1,17},{17,1},{2,18},{18,2},{3,19},{19,3},{4,20},{20... | collective-permute-start | bytes 3145736 | tf_op jit(solution)/shard_map/ppermute | solution.py:406
  8.7 24.7 %collective-permute-start.4 = (bf16[128,4096]{1,0:T(8,128)(2,1)S(1)}, bf16[128,4096]{1,0:T(8,128)(2,1)S(1)}, u32[]{:S(2)}, u32[]{:S(2)}) collective-permute-start(bf16[128,4096]{1,0:T(8,128)(2,1)S(1)} %shard_map.105.refs_0_), channel_id=1, source_target_pairs={{0,2},{2,0},{4,6},{6,4},{8,10},{10,8},{12,14},{14,12},{1,3},{3,1},... | collective-permute-start | bytes 3145736 | tf_op jit(solution)/shard_map/ppermute | solution.py:407
  10.1 10.8 %collective-permute-start.9 = (bf16[32,4608]{1,0:T(8,128)(2,1)S(1)}, bf16[32,4608]{1,0:T(8,128)(2,1)S(1)}, u32[]{:S(2)}, u32[]{:S(2)}) collective-permute-start(bf16[32,4608]{1,0:T(8,128)(2,1)S(1)} %get-tuple-element.44.refs_3_.refs_2_.refs_5_), channel_id=1, source_target_pairs={{0,4},{2,6},{4,12},{6,14},{12,8},{14,10},{8,0},{10,2},{1,5},{3,7},... | collective-permute-start | bytes 884744 | tf_op jit(solution)/shard_map/ppermute | solution.py:405
  11.7 15.6 %collective-permute-start.2 = (bf16[32,4608]{1,0:T(8,128)(2,1)S(1)}, bf16[32,4608]{1,0:T(8,128)(2,1)S(1)}, u32[]{:S(2)}, u32[]{:S(2)}) collective-permute-start(bf16[32,4608]{1,0:T(8,128)(2,1)S(1)} %get-tuple-element.36.refs_4_.refs_3_.refs_6_), channel_id=1, source_target_pairs={{0,4},{2,6},{4,12},{6,14},{12,8},{14,10},{8,0},{10,2},{1,5},{3,7},... | collective-permute-start | bytes 884744 | tf_op jit(solution)/shard_map/ppermute | solution.py:405
  14.3 22.0 %collective-permute-start.6 = (bf16[1024,256]{1,0:T(8,128)(2,1)S(1)}, bf16[1024,256]{1,0:T(8,128)(2,1)S(1)}, u32[]{:S(2)}, u32[]{:S(2)}) collective-permute-start(bf16[1024,256]{1,0:T(8,128)(2,1)S(1)} %bitcast.23), channel_id=1, source_target_pairs={{0,1},{1,0},{2,3},{3,2},{4,5},{5,4},{6,7},{7,6},{8,9},{9,8},{10,11... | collective-permute-start | bytes 1572872 | tf_op jit(solution)/shard_map/ppermute | solution.py:408
  21.0 13.8 %collective-permute-start.10 = (bf16[32,4608]{1,0:T(8,128)(2,1)S(1)}, bf16[32,4608]{1,0:T(8,128)(2,1)S(1)}, u32[]{:S(2)}, u32[]{:S(2)}) collective-permute-start(bf16[32,4608]{1,0:T(8,128)(2,1)S(1)} %collective-permute-done.9.refs_5_.refs_4_.refs_7_), channel_id=1, source_target_pairs={{0,4},{2,6},{4,12},{6,14},{12,8},{14,10},{8,0},{10,2},{1,5},{3,7},... | collective-permute-start | bytes 884744 | tf_op jit(solution)/shard_map/ppermute | solution.py:405
  27.3 11.7 %collective-permute-start.3 = (bf16[32,4608]{1,0:T(8,128)(2,1)S(1)}, bf16[32,4608]{1,0:T(8,128)(2,1)S(1)}, u32[]{:S(2)}, u32[]{:S(2)}) collective-permute-start(bf16[32,4608]{1,0:T(8,128)(2,1)S(1)} %collective-permute-done.2.refs_6_.refs_5_.refs_8_), channel_id=1, source_target_pairs={{0,4},{2,6},{4,12},{6,14},{12,8},{14,10},{8,0},{10,2},{1,5},{3,7},... | collective-permute-start | bytes 884744 | tf_op jit(solution)/shard_map/ppermute | solution.py:405
  32.2 4.2 %copy-start.4 = (bf16[64,2,256]{2,1,0:T(2,128)(2,1)S(1)}, bf16[64,2,256]{2,1,0:T(2,128)(2,1)}, u32[]{:S(2)}) copy-start(bf16[64,2,256]{2,1,0:T(2,128)(2,1)} %fresh_ref.1) | copy-start | bytes 196612
  32.2 4.2 %copy-start.6 = (s32[64]{0:T(128)S(1)}, s32[64]{0:T(128)}, u32[]{:S(2)}) copy-start(s32[64]{0:T(128)} %lengths_ref.1) | copy-start | bytes 772
  32.2 4.2 %copy-start.7 = (s32[64]{0:T(128)S(1)}, s32[64]{0:T(128)}, u32[]{:S(2)}) copy-start(s32[64]{0:T(128)} %adapter_ref.1) | copy-start | bytes 772
  32.2 4.2 %copy-start.8 = (s32[8]{0:T(128)S(1)}, s32[8]{0:T(128)}, u32[]{:S(2)}) copy-start(s32[8]{0:T(128)} %owner_ref.1) | copy-start | bytes 100
  32.2 14.4 %collective-permute-start.7 = (bf16[64,4096]{1,0:T(8,128)(2,1)S(1)}, bf16[64,4096]{1,0:T(8,128)(2,1)S(1)}, u32[]{:S(2)}, u32[]{:S(2)}) collective-permute-start(bf16[64,4096]{1,0:T(8,128)(2,1)S(1)} %slice.8), channel_id=1, source_target_pairs={{0,2},{2,0},{4,6},{6,4},{8,10},{10,8},{12,14},{14,12},{1,3},{3,1},... | collective-permute-start | bytes 1572872 | tf_op jit(solution)/shard_map/ppermute | solution.py:407
  33.4 13.3 %collective-permute-start.8 = (bf16[64,4096]{1,0:T(8,128)(2,1)S(1)}, bf16[64,4096]{1,0:T(8,128)(2,1)S(1)}, u32[]{:S(2)}, u32[]{:S(2)}) collective-permute-start(bf16[64,4096]{1,0:T(8,128)(2,1)S(1)} %slice.9), channel_id=1, source_target_pairs={{0,16},{16,0},{1,17},{17,1},{2,18},{18,2},{3,19},{19,3},{4,20},{20... | collective-permute-start | bytes 1572872 | tf_op jit(solution)/shard_map/ppermute | solution.py:406
  34.8 10.8 %collective-permute-start.11 = (bf16[32,4608]{1,0:T(8,128)(2,1)S(1)}, bf16[32,4608]{1,0:T(8,128)(2,1)S(1)}, u32[]{:S(2)}, u32[]{:S(2)}) collective-permute-start(bf16[32,4608]{1,0:T(8,128)(2,1)S(1)} %collective-permute-done.10.refs_7_.refs_6_.refs_9_), channel_id=1, source_target_pairs={{0,4},{2,6},{4,12},{6,14},{12,8},{14,10},{8,0},{10,2},{1,5},{3,7},... | collective-permute-start | bytes 884744 | tf_op jit(solution)/shard_map/ppermute | solution.py:405
  39.0 11.3 %collective-permute-start.12 = (bf16[32,4608]{1,0:T(8,128)(2,1)S(1)}, bf16[32,4608]{1,0:T(8,128)(2,1)S(1)}, u32[]{:S(2)}, u32[]{:S(2)}) collective-permute-start(bf16[32,4608]{1,0:T(8,128)(2,1)S(1)} %collective-permute-done.3.refs_8_.refs_7_.refs_10_), channel_id=1, source_target_pairs={{0,4},{2,6},{4,12},{6,14},{12,8},{14,10},{8,0},{10,2},{1,5},{3,7},... | collective-permute-start | bytes 884744 | tf_op jit(solution)/shard_map/ppermute | solution.py:405
  52.1 1.6 %collective-permute-start.13 = (f32[4,64,256]{2,1,0:T(8,128)S(1)}, f32[4,64,256]{2,1,0:T(8,128)S(1)}, u32[]{:S(2)}, u32[]{:S(2)}) collective-permute-start(f32[4,64,256]{2,1,0:T(8,128)S(1)} %get-tuple-element.54), channel_id=1, source_target_pairs={{0,1},{1,0},{2,3},{3,2},{4,5},{5,4},{6,7},{7,6},{8,9},{9,8},{10,11... | collective-permute-start | bytes 786440 | tf_op jit(solution)/shard_map/ppermute | solution.py:408
  52.2 5.1 %collective-permute-start.17 = (bf16[512,256]{1,0:T(8,128)(2,1)S(1)}, bf16[512,256]{1,0:T(8,128)(2,1)S(1)}, u32[]{:S(2)}, u32[]{:S(2)}) collective-permute-start(bf16[512,256]{1,0:T(8,128)(2,1)S(1)} %get-tuple-element.59.up_ref), channel_id=1, source_target_pairs={{0,1},{1,0},{2,3},{3,2},{4,5},{5,4},{6,7},{7,6},{8,9},{9,8},{10,11... | collective-permute-start | bytes 786440 | tf_op jit(solution)/shard_map/ppermute | solution.py:408
  53.8 4.3 %collective-permute-start.14 = (f32[64,256]{1,0:T(8,128)S(1)}, f32[64,256]{1,0:T(8,128)S(1)}, u32[]{:S(2)}, u32[]{:S(2)}) collective-permute-start(f32[64,256]{1,0:T(8,128)S(1)} %get-tuple-element.55), channel_id=1, source_target_pairs={{0,2},{2,0},{4,6},{6,4},{8,10},{10,8},{12,14},{14,12},{1,3},{3,1},... | collective-permute-start | bytes 196616 | tf_op jit(solution)/shard_map/ppermute | solution.py:407
  55.0 5.0 %collective-permute-start.15 = (f32[64,256]{1,0:T(8,128)S(1)}, f32[64,256]{1,0:T(8,128)S(1)}, u32[]{:S(2)}, u32[]{:S(2)}) collective-permute-start(f32[64,256]{1,0:T(8,128)S(1)} %get-tuple-element.56), channel_id=1, source_target_pairs={{0,16},{16,0},{1,17},{17,1},{2,18},{18,2},{3,19},{19,3},{4,20},{20... | collective-permute-start | bytes 196616 | tf_op jit(solution)/shard_map/ppermute | solution.py:406
  55.5 5.2 %collective-permute-start.16 = (f32[64,256]{1,0:T(8,128)S(1)}, f32[64,256]{1,0:T(8,128)S(1)}, u32[]{:S(2)}, u32[]{:S(2)}) collective-permute-start(f32[64,256]{1,0:T(8,128)S(1)} %get-tuple-element.57), channel_id=1, source_target_pairs={{0,18},{2,16},{4,22},{6,20},{8,26},{10,24},{12,30},{14,28},{16,2},... | collective-permute-start | bytes 196616 | tf_op jit(solution)/shard_map/ppermute | solution.py:438
  62.2 1.4 %collective-permute-start.18 = (bf16[2,32,2,512]{3,2,1,0:T(2,128)(2,1)S(1)}, bf16[2,32,2,512]{3,2,1,0:T(2,128)(2,1)S(1)}, u32[]{:S(2)}, u32[]{:S(2)}) collective-permute-start(bf16[2,32,2,512]{3,2,1,0:T(2,128)(2,1)S(1)} %shard_map.111.mine_ref), channel_id=1, source_target_pairs={{0,1},{1,0},{2,3},{3,2},{4,5},{5,4},{6,7},{7,6},{8,9},{9,8},{10,11... | collective-permute-start | bytes 393224 | tf_op jit(solution)/shard_map/ppermute | solution.py:408

commit v7 on v6

--- a/solution.py
+++ b/solution.py
@@ -397,7 +397,7 @@
         place = lax.axis_index("group")
         z, x, part = place // 2, lax.rem(place, 2), lax.axis_index("parts")
         order = z ^ (z // 2)
-        steps_back = [lax.rem(order + 4 - k, 4) for k in range(4)]
+        steps_back = [lax.rem(order + k, 4) for k in range(4)]
         places = [k ^ (k // 2) for k in steps_back]
         where = [z, x, part, core] + [p * 2 + x for p in places] + [p * 2 + 1 - x for p in places]
         where = jnp.stack(where).astype(jnp.int32)
@@ -407,7 +407,7 @@
         beside = lambda a: lax.ppermute(a, "group", [(i, i ^ 1) for i in range(groups)])
         inside = lambda a: lax.ppermute(a, "tensor", SWAP)
         corner = [(p * groups + i, (1 - p) * groups + (i ^ 1)) for p in range(2) for i in range(groups)]
-        ring = ((0, 1), (1, 3), (3, 2), (2, 0))
+        ring = ((1, 0), (3, 1), (2, 3), (0, 2))
 
         half = rows // 2
         mine = rows_of(normed_hidden_states)
@@ -424,7 +424,7 @@
         prepared = ready(
             where, kv_lengths, request_adapter, adapter_owner, cache, inside(cache), incoming_key_value, steps
         )
-        b2, x_beside, x_across, prepared = bar(b2, x_beside, x_across, prepared)
+        b2, x_across, prepared = bar(b2, x_across, prepared)
         b3 = along(b2, ring)
         weights = a0, b0, a1, b1, a2, b2, a3, b3
         sets = mine, x_beside, x_across

time: 65.1 us -> 64.3 us (0.988)
  waiting for transfers between devices: 33.5 us -> 24 us
  starting transfers between devices: 21 us -> 29.8 us
    ppermute x6, starting transfers between devices: 8.1 us -> 16.9 us  [body(): along = lambda a, moves: lax.ppermute(a, 'group', line_pairs(groups, moves))]
    ppermute x6, waiting for transfers between devices: 22.8 us -> 14.9 us  [body(): along = lambda a, moves: lax.ppermute(a, 'group', line_pairs(groups, moves))]
    ppermute x3, waiting for transfers between devices: 5.9 us -> 4.27 us  [body(): across = lambda a: lax.ppermute(a, 'parts', SWAP)]
  transfers between devices with their start and end apart: 19 -> 19, of which waited for: 13 -> 14; matrix products, arithmetic and copies ran while one was open for 0% -> 0% of each run, Pallas kernels for 4% -> 4%
where the time goes in v7:
time: 64.3 us; the launch traced here: 64.1 us
  starting transfers between devices  29.8 us (46%)
  waiting for transfers between devices  24 us (37%)
  Pallas kernels  7.94 us (12%)
  local copies, waits for them, and re-layouts  1.65 us (3%)
  between operations  0.8 us (1%)
    ppermute x6, starting transfers between devices, body(): along = lambda a, moves: lax.ppermute(a, 'group', line_pairs(groups, moves))  16.9 us
    ppermute x6, waiting for transfers between devices, body(): along = lambda a, moves: lax.ppermute(a, 'group', line_pairs(groups, moves))  14.9 us
    ppermute x4, starting transfers between devices, body(): lax.ppermute(a, 'group', [(i, i ^ 1) for i in range(groups)])  6.21 us
    ppermute x3, waiting for transfers between devices, body(): across = lambda a: lax.ppermute(a, 'parts', SWAP)  4.27 us
    ppermute x3, starting transfers between devices, body(): across = lambda a: lax.ppermute(a, 'parts', SWAP)  3.69 us
    ppermute x4, waiting for transfers between devices, body(): inside = lambda a: lax.ppermute(a, 'tensor', SWAP)  2.36 us
    pallas_call x1, Pallas kernels, late_products(): pl.pallas_call(late_kernel, out_shape=(shape, shape, jax.ShapeDtypeStruct...  1.85 us
    ppermute x1, starting transfers between devices, body(): t_both = lax.ppermute(t_both, ('parts', 'group'), corner)  1.82 us
  transfers between devices with their start and end apart: 19, of which 14 were waited for; matrix products, arithmetic and copies ran while one was open for 0% of the time, Pallas kernels for 4%

profile of v7, /device:TPU:0, one launch (start us, length us, event | category | flops | bytes accessed | tf_op | source)
XLA Modules:
  0.0 64.1 jit_solution(12982567240860773172)
XLA Ops:
  0.6 0.5 collective-permute-start
  1.1 2.6 %collective-permute-start.1 = (bf16[64,256]{1,0:T(8,128)(2,1)}, bf16[64,256]{1,0:T(8,128)(2,1)S(1)}, u32[]{:S(2)}, u32[]{:S(2)}) collective-permute-start(bf16[64,256]{1,0:T(8,128)(2,1)} %bitcast.26), channel_id=1, source_target_pairs={{0,2},{2,0},{4,6},{6,4},{8,10},{10,8},{12,14},{14,12},{1,3},{3,1},... | collective-permute-start | bytes 98312 | tf_op jit(solution)/shard_map/ppermute | solution.py:407
  3.7 1.2 %copy-done = bf16[64,2,4096]{2,1,0:T(2,128)(2,1)S(1)} copy-done((bf16[64,2,4096]{2,1,0:T(2,128)(2,1)S(1)}, bf16[64,2,4096]{2,1,0:T(2,128)(2,1)}, u32[]{:S(2)}) %copy-start) | copy-done | bytes 1048600
  4.9 0.1 shard_map.105.refs_0_
  5.1 0.0 copy-start.5
  5.1 0.1 stack.51.where_ref
  5.2 0.7 %collective-permute-done.1.up_beside_ref = bf16[64,256]{1,0:T(8,128)(2,1)S(1)} collective-permute-done((bf16[64,256]{1,0:T(8,128)(2,1)}, bf16[64,256]{1,0:T(8,128)(2,1)S(1)}, u32[]{:S(2)}, u32[]{:S(2)}) %collective-permute-start.1) | collective-permute-done | bytes 32800 | tf_op jit(solution)/shard_map/ppermute | solution.py:407
  5.9 0.1 copy-done.1
  6.0 0.2 copy-done.2
  6.1 0.7 %shard_map.104 = (bf16[32,4608]{1,0:T(8,128)(2,1)S(1)}, bf16[32,4608]{1,0:T(8,128)(2,1)S(1)}) custom-call(s32[12]{0:T(128)S(1)} %stack.51.where_ref, bf16[64,4096]{1,0:T(8,128)(2,1)S(1)} %bitcast.21, bf16[32,8192]{1,0:T(8,128)(2,1)S(1)} %bitcast.22, bf16[32,8192]{1,0:T(8,128)(2,1)S(1)} %bitcast.25, bf16[64,256]{1,0:T(8,128)(2,1)S(1)} %bitcast.27, ...), custom_call_target="tpu_custom_call" | custom-call | tf_op jit(solution)/shard_map/pallas_call | solution.py:59
  6.8 1.8 %collective-permute-start.5 = (bf16[128,4096]{1,0:T(8,128)(2,1)S(1)}, bf16[128,4096]{1,0:T(8,128)(2,1)S(1)}, u32[]{:S(2)}, u32[]{:S(2)}) collective-permute-start(bf16[128,4096]{1,0:T(8,128)(2,1)S(1)} %shard_map.105.refs_0_), channel_id=1, source_target_pairs={{0,16},{16,0},{1,17},{17,1},{2,18},{18,2},{3,19},{19,3},{4,20},{20... | collective-permute-start | bytes 3145736 | tf_op jit(solution)/shard_map/ppermute | solution.py:406
  8.7 1.5 %collective-permute-start.2 = (bf16[128,4096]{1,0:T(8,128)(2,1)S(1)}, bf16[128,4096]{1,0:T(8,128)(2,1)S(1)}, u32[]{:S(2)}, u32[]{:S(2)}) collective-permute-start(bf16[128,4096]{1,0:T(8,128)(2,1)S(1)} %shard_map.105.refs_0_), channel_id=1, source_target_pairs={{0,2},{2,0},{4,6},{6,4},{8,10},{10,8},{12,14},{14,12},{1,3},{3,1},... | collective-permute-start | bytes 3145736 | tf_op jit(solution)/shard_map/ppermute | solution.py:407
  10.1 2.6 %collective-permute-start.9 = (bf16[32,4608]{1,0:T(8,128)(2,1)S(1)}, bf16[32,4608]{1,0:T(8,128)(2,1)S(1)}, u32[]{:S(2)}, u32[]{:S(2)}) collective-permute-start(bf16[32,4608]{1,0:T(8,128)(2,1)S(1)} %get-tuple-element.42.refs_3_.refs_2_.refs_5_), channel_id=1, source_target_pairs={{4,0},{6,2},{12,4},{14,6},{8,12},{10,14},{0,8},{2,10},{5,1},{7,3},... | collective-permute-start | bytes 884744 | tf_op jit(solution)/shard_map/ppermute | solution.py:405
  12.7 1.6 %collective-permute-start.3 = (bf16[32,4608]{1,0:T(8,128)(2,1)S(1)}, bf16[32,4608]{1,0:T(8,128)(2,1)S(1)}, u32[]{:S(2)}, u32[]{:S(2)}) collective-permute-start(bf16[32,4608]{1,0:T(8,128)(2,1)S(1)} %get-tuple-element.35.refs_4_.refs_3_.refs_6_), channel_id=1, source_target_pairs={{4,0},{6,2},{12,4},{14,6},{8,12},{10,14},{0,8},{2,10},{5,1},{7,3},... | collective-permute-start | bytes 884744 | tf_op jit(solution)/shard_map/ppermute | solution.py:405
  14.3 5.9 %collective-permute-done.9.refs_5_.refs_4_.refs_7_ = bf16[32,4608]{1,0:T(8,128)(2,1)S(1)} collective-permute-done((bf16[32,4608]{1,0:T(8,128)(2,1)S(1)}, bf16[32,4608]{1,0:T(8,128)(2,1)S(1)}, u32[]{:S(2)}, u32[]{:S(2)}) %collective-permute-start.9) | collective-permute-done | bytes 294944 | tf_op jit(solution)/shard_map/ppermute | solution.py:405
  20.2 3.4 %collective-permute-start.10 = (bf16[32,4608]{1,0:T(8,128)(2,1)S(1)}, bf16[32,4608]{1,0:T(8,128)(2,1)S(1)}, u32[]{:S(2)}, u32[]{:S(2)}) collective-permute-start(bf16[32,4608]{1,0:T(8,128)(2,1)S(1)} %collective-permute-done.9.refs_5_.refs_4_.refs_7_), channel_id=1, source_target_pairs={{4,0},{6,2},{12,4},{14,6},{8,12},{10,14},{0,8},{2,10},{5,1},{7,3},... | collective-permute-start | bytes 884744 | tf_op jit(solution)/shard_map/ppermute | solution.py:405
  23.6 2.9 %collective-permute-done.3.refs_6_.refs_5_.refs_8_ = bf16[32,4608]{1,0:T(8,128)(2,1)S(1)} collective-permute-done((bf16[32,4608]{1,0:T(8,128)(2,1)S(1)}, bf16[32,4608]{1,0:T(8,128)(2,1)S(1)}, u32[]{:S(2)}, u32[]{:S(2)}) %collective-permute-start.3) | collective-permute-done | bytes 294944 | tf_op jit(solution)/shard_map/ppermute | solution.py:405
  26.5 3.4 %collective-permute-start.4 = (bf16[32,4608]{1,0:T(8,128)(2,1)S(1)}, bf16[32,4608]{1,0:T(8,128)(2,1)S(1)}, u32[]{:S(2)}, u32[]{:S(2)}) collective-permute-start(bf16[32,4608]{1,0:T(8,128)(2,1)S(1)} %collective-permute-done.3.refs_6_.refs_5_.refs_8_), channel_id=1, source_target_pairs={{4,0},{6,2},{12,4},{14,6},{8,12},{10,14},{0,8},{2,10},{5,1},{7,3},... | collective-permute-start | bytes 884744 | tf_op jit(solution)/shard_map/ppermute | solution.py:405
  29.9 2.2 %collective-permute-done.5.refs_2_ = bf16[128,4096]{1,0:T(8,128)(2,1)S(1)} collective-permute-done((bf16[128,4096]{1,0:T(8,128)(2,1)S(1)}, bf16[128,4096]{1,0:T(8,128)(2,1)S(1)}, u32[]{:S(2)}, u32[]{:S(2)}) %collective-permute-start.5) | collective-permute-done | bytes 1048608 | tf_op jit(solution)/shard_map/ppermute | solution.py:406
  32.2 0.0 copy-start.4
  32.2 0.0 copy-start.6
  32.2 0.0 copy-start.7
  32.2 0.9 %collective-permute-start.7 = (bf16[64,4096]{1,0:T(8,128)(2,1)S(1)}, bf16[64,4096]{1,0:T(8,128)(2,1)S(1)}, u32[]{:S(2)}, u32[]{:S(2)}) collective-permute-start(bf16[64,4096]{1,0:T(8,128)(2,1)S(1)} %slice.8), channel_id=1, source_target_pairs={{0,2},{2,0},{4,6},{6,4},{8,10},{10,8},{12,14},{14,12},{1,3},{3,1},... | collective-permute-start | bytes 1572872 | tf_op jit(solution)/shard_map/ppermute | solution.py:407
  33.1 0.2 collective-permute-done.2.refs_1_
  33.4 1.4 %collective-permute-start.8 = (bf16[64,4096]{1,0:T(8,128)(2,1)S(1)}, bf16[64,4096]{1,0:T(8,128)(2,1)S(1)}, u32[]{:S(2)}, u32[]{:S(2)}) collective-permute-start(bf16[64,4096]{1,0:T(8,128)(2,1)S(1)} %slice.9), channel_id=1, source_target_pairs={{0,16},{16,0},{1,17},{17,1},{2,18},{18,2},{3,19},{19,3},{4,20},{20... | collective-permute-start | bytes 1572872 | tf_op jit(solution)/shard_map/ppermute | solution.py:406
  34.8 2.6 %collective-permute-start.11 = (bf16[32,4608]{1,0:T(8,128)(2,1)S(1)}, bf16[32,4608]{1,0:T(8,128)(2,1)S(1)}, u32[]{:S(2)}, u32[]{:S(2)}) collective-permute-start(bf16[32,4608]{1,0:T(8,128)(2,1)S(1)} %collective-permute-done.10.refs_7_.refs_6_.refs_9_), channel_id=1, source_target_pairs={{4,0},{6,2},{12,4},{14,6},{8,12},{10,14},{0,8},{2,10},{5,1},{7,3},... | collective-permute-start | bytes 884744 | tf_op jit(solution)/shard_map/ppermute | solution.py:405
  37.4 0.7 %shard_map.106 = (bf16[512,256]{1,0:T(8,128)(2,1)S(1)}, bf16[512,256]{1,0:T(8,128)(2,1)S(1)}, bf16[64,256]{1,0:T(8,128)(2,1)S(1)}, s32[8,256]{1,0:T(8,128)S(1)}, s32[64,128]{1,0:T(8,128)S(1)}) custom-call(s32[12]{0:T(128)S(1)} %stack.51.where_ref, s32[64]{0:T(128)S(1)} %copy-done.6, s32[64]{0:T(128)S(1)} %copy-done.7, s32[8]{0:T(128)S(1)} %copy-done.8, ...), custom_call_target="tpu_custom_call" | custom-call | tf_op jit(solution)/shard_map/pallas_call | solution.py:118
  38.1 0.1 collective-permute-done.4.refs_8_.refs_7_.refs_10_
  38.2 3.4 %collective-permute-start.12 = (bf16[32,4608]{1,0:T(8,128)(2,1)S(1)}, bf16[32,4608]{1,0:T(8,128)(2,1)S(1)}, u32[]{:S(2)}, u32[]{:S(2)}) collective-permute-start(bf16[32,4608]{1,0:T(8,128)(2,1)S(1)} %collective-permute-done.4.refs_8_.refs_7_.refs_10_), channel_id=1, source_target_pairs={{4,0},{6,2},{12,4},{14,6},{8,12},{10,14},{0,8},{2,10},{5,1},{7,3},... | collective-permute-start | bytes 884744 | tf_op jit(solution)/shard_map/ppermute | solution.py:405
  41.6 3.2 %collective-permute-done.11.refs_9_.refs_8_.refs_11_ = bf16[32,4608]{1,0:T(8,128)(2,1)S(1)} collective-permute-done((bf16[32,4608]{1,0:T(8,128)(2,1)S(1)}, bf16[32,4608]{1,0:T(8,128)(2,1)S(1)}, u32[]{:S(2)}, u32[]{:S(2)}) %collective-permute-start.11) | collective-permute-done | bytes 294944 | tf_op jit(solution)/shard_map/ppermute | solution.py:405
  44.8 1.0 %shard_map.107.refs_13_ = f32[384,224]{1,0:T(8,128)S(1)} custom-call(bf16[128,4096]{1,0:T(8,128)(2,1)S(1)} %shard_map.105.refs_0_, bf16[128,4096]{1,0:T(8,128)(2,1)S(1)} %collective-permute-done.2.refs_1_, bf16[128,4096]{1,0:T(8,128)(2,1)S(1)} %collective-permute-done.5.refs_2_, bf16[32,4608]{1,0:T(8,128)(2,1)S(1)} %get-tuple-element.42.refs_3_.refs_2_.refs_5_, ...), custom_call_target="tpu_custom_call" | custom-call | flops 704643072 | bytes 4980736 | tf_op jit(solution)/shard_map/pallas_call | solution.py:143
  45.9 0.2 collective-permute-done.8.refs_1_.refs_4_
  46.0 0.7 %shard_map.108.refs_14_ = f32[128,224]{1,0:T(8,128)S(1)} custom-call(bf16[64,4096]{1,0:T(8,128)(2,1)S(1)} %collective-permute-done.7.refs_0_.refs_3_, bf16[64,4096]{1,0:T(8,128)(2,1)S(1)} %collective-permute-done.8.refs_1_.refs_4_, bf16[32,4608]{1,0:T(8,128)(2,1)S(1)} %get-tuple-element.42.refs_3_.refs_2_.refs_5_, ...), custom_call_target="tpu_custom_call" | custom-call | flops 234881024 | bytes 2883584 | tf_op jit(solution)/shard_map/pallas_call | solution.py:143
  46.8 2.7 %collective-permute-done.12.refs_12_ = bf16[32,4608]{1,0:T(8,128)(2,1)S(1)} collective-permute-done((bf16[32,4608]{1,0:T(8,128)(2,1)S(1)}, bf16[32,4608]{1,0:T(8,128)(2,1)S(1)}, u32[]{:S(2)}, u32[]{:S(2)}) %collective-permute-start.12) | collective-permute-done | bytes 294944 | tf_op jit(solution)/shard_map/ppermute | solution.py:405
  49.5 1.8 %shard_map.109 = (f32[4,64,256]{2,1,0:T(8,128)S(1)}, f32[4,64,256]{2,1,0:T(8,128)S(1)}, bf16[512,256]{1,0:T(8,128)(2,1)S(1)}) custom-call(s32[12]{0:T(128)S(1)} %stack.51.where_ref, bf16[128,4096]{1,0:T(8,128)(2,1)S(1)} %shard_map.105.refs_0_, bf16[128,4096]{1,0:T(8,128)(2,1)S(1)} %collective-permute-done.2.refs_1_, ...), custom_call_target="tpu_custom_call" | custom-call | tf_op jit(solution)/shard_map/pallas_call | solution.py:186
  51.4 0.1 collective-permute-start.13
  51.4 0.5 collective-permute-start.17
  51.9 1.0 %collective-permute-done.13.b_ref.other_ref = f32[4,64,256]{2,1,0:T(8,128)S(1)} collective-permute-done((f32[4,64,256]{2,1,0:T(8,128)S(1)}, f32[4,64,256]{2,1,0:T(8,128)S(1)}, u32[]{:S(2)}, u32[]{:S(2)}) %collective-permute-start.13) | collective-permute-done | bytes 262176 | tf_op jit(solution)/shard_map/ppermute | solution.py:408
  53.0 1.2 %collective-permute-start.14 = (f32[64,256]{1,0:T(8,128)S(1)}, f32[64,256]{1,0:T(8,128)S(1)}, u32[]{:S(2)}, u32[]{:S(2)}) collective-permute-start(f32[64,256]{1,0:T(8,128)S(1)} %get-tuple-element.53), channel_id=1, source_target_pairs={{0,2},{2,0},{4,6},{6,4},{8,10},{10,8},{12,14},{14,12},{1,3},{3,1},... | collective-permute-start | bytes 196616 | tf_op jit(solution)/shard_map/ppermute | solution.py:407
  54.2 0.5 collective-permute-start.15
  54.7 1.8 %collective-permute-start.16 = (f32[64,256]{1,0:T(8,128)S(1)}, f32[64,256]{1,0:T(8,128)S(1)}, u32[]{:S(2)}, u32[]{:S(2)}) collective-permute-start(f32[64,256]{1,0:T(8,128)S(1)} %get-tuple-element.55), channel_id=1, source_target_pairs={{0,18},{2,16},{4,22},{6,20},{8,26},{10,24},{12,30},{14,28},{16,2},... | collective-permute-start | bytes 196616 | tf_op jit(solution)/shard_map/ppermute | solution.py:438
  56.5 0.8 %collective-permute-done.14.beside_ref = f32[64,256]{1,0:T(8,128)S(1)} collective-permute-done((f32[64,256]{1,0:T(8,128)S(1)}, f32[64,256]{1,0:T(8,128)S(1)}, u32[]{:S(2)}, u32[]{:S(2)}) %collective-permute-start.14) | collective-permute-done | bytes 65568 | tf_op jit(solution)/shard_map/ppermute | solution.py:407
  57.3 1.9 %collective-permute-done.15.across_ref = f32[64,256]{1,0:T(8,128)S(1)} collective-permute-done((f32[64,256]{1,0:T(8,128)S(1)}, f32[64,256]{1,0:T(8,128)S(1)}, u32[]{:S(2)}, u32[]{:S(2)}) %collective-permute-start.15) | collective-permute-done | bytes 65568 | tf_op jit(solution)/shard_map/ppermute | solution.py:406
  59.2 0.7 %collective-permute-done.16.both_ref = f32[64,256]{1,0:T(8,128)S(1)} collective-permute-done((f32[64,256]{1,0:T(8,128)S(1)}, f32[64,256]{1,0:T(8,128)S(1)}, u32[]{:S(2)}, u32[]{:S(2)}) %collective-permute-start.16) | collective-permute-done | bytes 65568 | tf_op jit(solution)/shard_map/ppermute | solution.py:438
  59.9 1.5 %shard_map.111.mine_ref = bf16[2,32,2,512]{3,2,1,0:T(2,128)(2,1)S(1)} custom-call(s32[12]{0:T(128)S(1)} %stack.51.where_ref, f32[4,64,256]{2,1,0:T(8,128)S(1)} %get-tuple-element.51.a_ref.own_ref, f32[4,64,256]{2,1,0:T(8,128)S(1)} %collective-permute-done.13.b_ref.other_ref, f32[64,256]{1,0:T(8,128)S(1)} %collective-permute-done.14.beside_ref, ...), custom_call_target="tpu_custom_call" | custom-call | tf_op jit(solution)/shard_map/pallas_call | solution.py:343
  61.4 0.1 collective-permute-start.18
  61.5 1.3 %collective-permute-done.18.other_ref = bf16[2,32,2,512]{3,2,1,0:T(2,128)(2,1)S(1)} collective-permute-done((bf16[2,32,2,512]{3,2,1,0:T(2,128)(2,1)S(1)}, bf16[2,32,2,512]{3,2,1,0:T(2,128)(2,1)S(1)}, u32[]{:S(2)}, u32[]{:S(2)}) %collective-permute-start.18) | collective-permute-done | bytes 131104 | tf_op jit(solution)/shard_map/ppermute | solution.py:408
  62.9 1.3 %shard_map.112 = (bf16[64,2,512]{2,1,0:T(2,128)(2,1)}, bf16[64,2,512]{2,1,0:T(2,128)(2,1)}) custom-call(s32[12]{0:T(128)S(1)} %stack.51.where_ref, bf16[2,32,2,512]{3,2,1,0:T(2,128)(2,1)S(1)} %shard_map.111.mine_ref, bf16[2,32,2,512]{3,2,1,0:T(2,128)(2,1)S(1)} %collective-permute-done.18.other_ref), custom_call_target="tpu_custom_call" | custom-call | tf_op jit(solution)/shard_map/pallas_call | solution.py:211
  (20 shorter events, 0.1 us)
Async XLA Ops:
  0.6 5.3 %collective-permute-start = (bf16[1,8192,32]{1,2,0:T(8,128)(2,1)}, bf16[1,8192,32]{1,2,0:T(8,128)(2,1)S(1)}, u32[]{:S(2)}, u32[]{:S(2)}) collective-permute-start(bf16[1,8192,32]{1,2,0:T(8,128)(2,1)} %param.11), channel_id=1, source_target_pairs={{0,1},{1,0},{2,3},{3,2},{4,5},{5,4},{6,7},{7,6},{8,9},{9,8},{10,11... | collective-permute-start | bytes 1572872 | tf_op jit(solution)/shard_map/ppermute | solution.py:391
  1.1 4.8 %collective-permute-start.1 = (bf16[64,256]{1,0:T(8,128)(2,1)}, bf16[64,256]{1,0:T(8,128)(2,1)S(1)}, u32[]{:S(2)}, u32[]{:S(2)}) collective-permute-start(bf16[64,256]{1,0:T(8,128)(2,1)} %bitcast.26), channel_id=1, source_target_pairs={{0,2},{2,0},{4,6},{6,4},{8,10},{10,8},{12,14},{14,12},{1,3},{3,1},... | collective-permute-start | bytes 98312 | tf_op jit(solution)/shard_map/ppermute | solution.py:407
  3.7 1.2 %copy-start = (bf16[64,2,4096]{2,1,0:T(2,128)(2,1)S(1)}, bf16[64,2,4096]{2,1,0:T(2,128)(2,1)}, u32[]{:S(2)}) copy-start(bf16[64,2,4096]{2,1,0:T(2,128)(2,1)} %x_ref.1) | copy-start | bytes 3145732
  4.9 1.0 %copy-start.1 = (bf16[4096,64]{0,1:T(8,128)(2,1)S(1)}, bf16[4096,64]{0,1:T(8,128)(2,1)}, u32[]{:S(2)}) copy-start(bf16[4096,64]{0,1:T(8,128)(2,1)} %param.10) | copy-start | bytes 1572868
  4.9 1.2 %copy-start.2 = (bf16[1,8192,32]{1,2,0:T(8,128)(2,1)S(1)}, bf16[1,8192,32]{1,2,0:T(8,128)(2,1)}, u32[]{:S(2)}) copy-start(bf16[1,8192,32]{1,2,0:T(8,128)(2,1)} %param.11) | copy-start | bytes 1572868
  5.1 1.1 %copy-start.5 = (bf16[1,64,256]{2,1,0:T(8,128)(2,1)S(1)}, bf16[1,64,256]{2,1,0:T(8,128)(2,1)}, u32[]{:S(2)}) copy-start(bf16[1,64,256]{2,1,0:T(8,128)(2,1)} %param.12) | copy-start | bytes 98308
  6.1 8.2 %copy-start.3 = (bf16[64,16,256]{2,1,0:T(8,128)(2,1)S(1)}, bf16[64,16,256]{2,1,0:T(8,128)(2,1)}, u32[]{:S(2)}) copy-start(bf16[64,16,256]{2,1,0:T(8,128)(2,1)} %param.13) | copy-start | bytes 1572868
  6.8 25.3 %collective-permute-start.5 = (bf16[128,4096]{1,0:T(8,128)(2,1)S(1)}, bf16[128,4096]{1,0:T(8,128)(2,1)S(1)}, u32[]{:S(2)}, u32[]{:S(2)}) collective-permute-start(bf16[128,4096]{1,0:T(8,128)(2,1)S(1)} %shard_map.105.refs_0_), channel_id=1, source_target_pairs={{0,16},{16,0},{1,17},{17,1},{2,18},{18,2},{3,19},{19,3},{4,20},{20... | collective-permute-start | bytes 3145736 | tf_op jit(solution)/shard_map/ppermute | solution.py:406
  8.7 24.7 %collective-permute-start.2 = (bf16[128,4096]{1,0:T(8,128)(2,1)S(1)}, bf16[128,4096]{1,0:T(8,128)(2,1)S(1)}, u32[]{:S(2)}, u32[]{:S(2)}) collective-permute-start(bf16[128,4096]{1,0:T(8,128)(2,1)S(1)} %shard_map.105.refs_0_), channel_id=1, source_target_pairs={{0,2},{2,0},{4,6},{6,4},{8,10},{10,8},{12,14},{14,12},{1,3},{3,1},... | collective-permute-start | bytes 3145736 | tf_op jit(solution)/shard_map/ppermute | solution.py:407
  10.1 10.1 %collective-permute-start.9 = (bf16[32,4608]{1,0:T(8,128)(2,1)S(1)}, bf16[32,4608]{1,0:T(8,128)(2,1)S(1)}, u32[]{:S(2)}, u32[]{:S(2)}) collective-permute-start(bf16[32,4608]{1,0:T(8,128)(2,1)S(1)} %get-tuple-element.42.refs_3_.refs_2_.refs_5_), channel_id=1, source_target_pairs={{4,0},{6,2},{12,4},{14,6},{8,12},{10,14},{0,8},{2,10},{5,1},{7,3},... | collective-permute-start | bytes 884744 | tf_op jit(solution)/shard_map/ppermute | solution.py:405
  12.7 13.8 %collective-permute-start.3 = (bf16[32,4608]{1,0:T(8,128)(2,1)S(1)}, bf16[32,4608]{1,0:T(8,128)(2,1)S(1)}, u32[]{:S(2)}, u32[]{:S(2)}) collective-permute-start(bf16[32,4608]{1,0:T(8,128)(2,1)S(1)} %get-tuple-element.35.refs_4_.refs_3_.refs_6_), channel_id=1, source_target_pairs={{4,0},{6,2},{12,4},{14,6},{8,12},{10,14},{0,8},{2,10},{5,1},{7,3},... | collective-permute-start | bytes 884744 | tf_op jit(solution)/shard_map/ppermute | solution.py:405
  14.3 23.1 %collective-permute-start.6 = (bf16[1024,256]{1,0:T(8,128)(2,1)S(1)}, bf16[1024,256]{1,0:T(8,128)(2,1)S(1)}, u32[]{:S(2)}, u32[]{:S(2)}) collective-permute-start(bf16[1024,256]{1,0:T(8,128)(2,1)S(1)} %bitcast.23), channel_id=1, source_target_pairs={{0,1},{1,0},{2,3},{3,2},{4,5},{5,4},{6,7},{7,6},{8,9},{9,8},{10,11... | collective-permute-start | bytes 1572872 | tf_op jit(solution)/shard_map/ppermute | solution.py:408
  20.2 14.6 %collective-permute-start.10 = (bf16[32,4608]{1,0:T(8,128)(2,1)S(1)}, bf16[32,4608]{1,0:T(8,128)(2,1)S(1)}, u32[]{:S(2)}, u32[]{:S(2)}) collective-permute-start(bf16[32,4608]{1,0:T(8,128)(2,1)S(1)} %collective-permute-done.9.refs_5_.refs_4_.refs_7_), channel_id=1, source_target_pairs={{4,0},{6,2},{12,4},{14,6},{8,12},{10,14},{0,8},{2,10},{5,1},{7,3},... | collective-permute-start | bytes 884744 | tf_op jit(solution)/shard_map/ppermute | solution.py:405
  26.5 11.7 %collective-permute-start.4 = (bf16[32,4608]{1,0:T(8,128)(2,1)S(1)}, bf16[32,4608]{1,0:T(8,128)(2,1)S(1)}, u32[]{:S(2)}, u32[]{:S(2)}) collective-permute-start(bf16[32,4608]{1,0:T(8,128)(2,1)S(1)} %collective-permute-done.3.refs_6_.refs_5_.refs_8_), channel_id=1, source_target_pairs={{4,0},{6,2},{12,4},{14,6},{8,12},{10,14},{0,8},{2,10},{5,1},{7,3},... | collective-permute-start | bytes 884744 | tf_op jit(solution)/shard_map/ppermute | solution.py:405
  32.2 5.2 %copy-start.4 = (bf16[64,2,256]{2,1,0:T(2,128)(2,1)S(1)}, bf16[64,2,256]{2,1,0:T(2,128)(2,1)}, u32[]{:S(2)}) copy-start(bf16[64,2,256]{2,1,0:T(2,128)(2,1)} %fresh_ref.1) | copy-start | bytes 196612
  32.2 5.2 %copy-start.6 = (s32[64]{0:T(128)S(1)}, s32[64]{0:T(128)}, u32[]{:S(2)}) copy-start(s32[64]{0:T(128)} %lengths_ref.1) | copy-start | bytes 772
  32.2 5.2 %copy-start.7 = (s32[64]{0:T(128)S(1)}, s32[64]{0:T(128)}, u32[]{:S(2)}) copy-start(s32[64]{0:T(128)} %adapter_ref.1) | copy-start | bytes 772
  32.2 5.2 %copy-start.8 = (s32[8]{0:T(128)S(1)}, s32[8]{0:T(128)}, u32[]{:S(2)}) copy-start(s32[8]{0:T(128)} %owner_ref.1) | copy-start | bytes 100
  32.2 13.6 %collective-permute-start.7 = (bf16[64,4096]{1,0:T(8,128)(2,1)S(1)}, bf16[64,4096]{1,0:T(8,128)(2,1)S(1)}, u32[]{:S(2)}, u32[]{:S(2)}) collective-permute-start(bf16[64,4096]{1,0:T(8,128)(2,1)S(1)} %slice.8), channel_id=1, source_target_pairs={{0,2},{2,0},{4,6},{6,4},{8,10},{10,8},{12,14},{14,12},{1,3},{3,1},... | collective-permute-start | bytes 1572872 | tf_op jit(solution)/shard_map/ppermute | solution.py:407
  33.4 12.6 %collective-permute-start.8 = (bf16[64,4096]{1,0:T(8,128)(2,1)S(1)}, bf16[64,4096]{1,0:T(8,128)(2,1)S(1)}, u32[]{:S(2)}, u32[]{:S(2)}) collective-permute-start(bf16[64,4096]{1,0:T(8,128)(2,1)S(1)} %slice.9), channel_id=1, source_target_pairs={{0,16},{16,0},{1,17},{17,1},{2,18},{18,2},{3,19},{19,3},{4,20},{20... | collective-permute-start | bytes 1572872 | tf_op jit(solution)/shard_map/ppermute | solution.py:406
  34.8 10.1 %collective-permute-start.11 = (bf16[32,4608]{1,0:T(8,128)(2,1)S(1)}, bf16[32,4608]{1,0:T(8,128)(2,1)S(1)}, u32[]{:S(2)}, u32[]{:S(2)}) collective-permute-start(bf16[32,4608]{1,0:T(8,128)(2,1)S(1)} %collective-permute-done.10.refs_7_.refs_6_.refs_9_), channel_id=1, source_target_pairs={{4,0},{6,2},{12,4},{14,6},{8,12},{10,14},{0,8},{2,10},{5,1},{7,3},... | collective-permute-start | bytes 884744 | tf_op jit(solution)/shard_map/ppermute | solution.py:405
  38.2 11.3 %collective-permute-start.12 = (bf16[32,4608]{1,0:T(8,128)(2,1)S(1)}, bf16[32,4608]{1,0:T(8,128)(2,1)S(1)}, u32[]{:S(2)}, u32[]{:S(2)}) collective-permute-start(bf16[32,4608]{1,0:T(8,128)(2,1)S(1)} %collective-permute-done.4.refs_8_.refs_7_.refs_10_), channel_id=1, source_target_pairs={{4,0},{6,2},{12,4},{14,6},{8,12},{10,14},{0,8},{2,10},{5,1},{7,3},... | collective-permute-start | bytes 884744 | tf_op jit(solution)/shard_map/ppermute | solution.py:405
  51.4 1.6 %collective-permute-start.13 = (f32[4,64,256]{2,1,0:T(8,128)S(1)}, f32[4,64,256]{2,1,0:T(8,128)S(1)}, u32[]{:S(2)}, u32[]{:S(2)}) collective-permute-start(f32[4,64,256]{2,1,0:T(8,128)S(1)} %get-tuple-element.52), channel_id=1, source_target_pairs={{0,1},{1,0},{2,3},{3,2},{4,5},{5,4},{6,7},{7,6},{8,9},{9,8},{10,11... | collective-permute-start | bytes 786440 | tf_op jit(solution)/shard_map/ppermute | solution.py:408
  51.4 5.1 %collective-permute-start.17 = (bf16[512,256]{1,0:T(8,128)(2,1)S(1)}, bf16[512,256]{1,0:T(8,128)(2,1)S(1)}, u32[]{:S(2)}, u32[]{:S(2)}) collective-permute-start(bf16[512,256]{1,0:T(8,128)(2,1)S(1)} %get-tuple-element.57.up_ref), channel_id=1, source_target_pairs={{0,1},{1,0},{2,3},{3,2},{4,5},{5,4},{6,7},{7,6},{8,9},{9,8},{10,11... | collective-permute-start | bytes 786440 | tf_op jit(solution)/shard_map/ppermute | solution.py:408
  53.0 4.3 %collective-permute-start.14 = (f32[64,256]{1,0:T(8,128)S(1)}, f32[64,256]{1,0:T(8,128)S(1)}, u32[]{:S(2)}, u32[]{:S(2)}) collective-permute-start(f32[64,256]{1,0:T(8,128)S(1)} %get-tuple-element.53), channel_id=1, source_target_pairs={{0,2},{2,0},{4,6},{6,4},{8,10},{10,8},{12,14},{14,12},{1,3},{3,1},... | collective-permute-start | bytes 196616 | tf_op jit(solution)/shard_map/ppermute | solution.py:407
  54.2 5.0 %collective-permute-start.15 = (f32[64,256]{1,0:T(8,128)S(1)}, f32[64,256]{1,0:T(8,128)S(1)}, u32[]{:S(2)}, u32[]{:S(2)}) collective-permute-start(f32[64,256]{1,0:T(8,128)S(1)} %get-tuple-element.54), channel_id=1, source_target_pairs={{0,16},{16,0},{1,17},{17,1},{2,18},{18,2},{3,19},{19,3},{4,20},{20... | collective-permute-start | bytes 196616 | tf_op jit(solution)/shard_map/ppermute | solution.py:406
  54.7 5.2 %collective-permute-start.16 = (f32[64,256]{1,0:T(8,128)S(1)}, f32[64,256]{1,0:T(8,128)S(1)}, u32[]{:S(2)}, u32[]{:S(2)}) collective-permute-start(f32[64,256]{1,0:T(8,128)S(1)} %get-tuple-element.55), channel_id=1, source_target_pairs={{0,18},{2,16},{4,22},{6,20},{8,26},{10,24},{12,30},{14,28},{16,2},... | collective-permute-start | bytes 196616 | tf_op jit(solution)/shard_map/ppermute | solution.py:438
  61.4 1.4 %collective-permute-start.18 = (bf16[2,32,2,512]{3,2,1,0:T(2,128)(2,1)S(1)}, bf16[2,32,2,512]{3,2,1,0:T(2,128)(2,1)S(1)}, u32[]{:S(2)}, u32[]{:S(2)}) collective-permute-start(bf16[2,32,2,512]{3,2,1,0:T(2,128)(2,1)S(1)} %shard_map.111.mine_ref), channel_id=1, source_target_pairs={{0,1},{1,0},{2,3},{3,2},{4,5},{5,4},{6,7},{7,6},{8,9},{9,8},{10,11... | collective-permute-start | bytes 393224 | tf_op jit(solution)/shard_map/ppermute | solution.py:408

commit v8 on v7

--- a/solution.py
+++ b/solution.py
@@ -29,33 +29,31 @@
     where_ref, query_ref, kept_ref, given_ref, up_ref, up_beside_ref, a_ref, b_ref, sems
 ):
     part, core = where_ref[2], where_ref[3]
-    count, features = kept_ref.shape[0], query_ref.shape[1]
-    columns = up_ref.shape[1]
-    chunks = [ref.at[:, :features] for ref in (a_ref, b_ref)]
-    ups = []
-    for ref, source in ((a_ref, up_ref), (b_ref, up_beside_ref)):
-        ups.append((source.at[:count], ref.at[:, features : features + columns]))
-        ups.append((source.at[count:], ref.at[:, features + columns :]))
+    count, width = kept_ref.shape[0], query_ref.shape[1] // 2
+    chunks = [ref.at[:, :width] for ref in (a_ref, b_ref)]
+    ups = [(up_ref, a_ref.at[:, width:]), (up_beside_ref, b_ref.at[:, width:])]
 
     @pl.when(part == 0)
     def _():
-        copy_all([(query_ref.at[:count], chunks[0]), (query_ref.at[count:], chunks[1])] + ups, sems)
-
-    @pl.when(jnp.logical_and(part != 0, core == 0))
-    def _():
-        low = slice(0, features)
-        copy_all([(kept_ref.at[:, low], chunks[0]), (given_ref.at[:, low], chunks[1])] + ups, sems)
-
-    @pl.when(jnp.logical_and(part != 0, core != 0))
-    def _():
-        high = slice(features, 2 * features)
-        copy_all([(given_ref.at[:, high], chunks[0]), (kept_ref.at[:, high], chunks[1])] + ups, sems)
+        copy_all([(query_ref.at[:, k * width : (k + 1) * width], chunks[k]) for k in range(2)] + ups, sems)
+
+    for own in range(2):
+
+        @pl.when(jnp.logical_and(part != 0, core == own))
+        def _():
+            copies = []
+            for k in range(2):
+                features = slice((2 * own + k) * width, (2 * own + k + 1) * width)
+                for owner in range(2):
+                    source = kept_ref if owner == own else given_ref
+                    target = (a_ref, b_ref)[k].at[owner * count : (owner + 1) * count, :width]
+                    copies.append((source.at[:, features], target))
+            copy_all(copies + ups, sems)
 
 
 def block_of(where, query, kept, given, up, up_beside):
-    count, features = kept.shape[0], query.shape[1]
     vmem = pl.BlockSpec(memory_space=pltpu.VMEM)
-    shape = jax.ShapeDtypeStruct((count, features + 2 * up.shape[1]), query.dtype)
+    shape = jax.ShapeDtypeStruct((query.shape[0], query.shape[1] // 2 + up.shape[1]), query.dtype)
     return pl.pallas_call(
         block_kernel,
         out_shape=(shape, shape),
@@ -133,13 +131,19 @@
 
 def products_kernel(sets, *refs):
     rows, weights, out_ref = refs[:sets], refs[sets:-1], refs[-1]
-    features = rows[0].shape[1]
-    columns = jnp.concatenate([w[:, :features] for w in weights], axis=0)
-    out_ref[...] = nt_dot(jnp.concatenate([r[...] for r in rows], axis=0), columns)
+    width = rows[0].shape[1] // 2
+    firsts, seconds = (
+        jnp.concatenate([w[:, :width] for w in weights[k::2]], axis=0) for k in range(2)
+    )
+    known = seconds.shape[0]
+    total = nt_dot(jnp.concatenate([r[:, :width] for r in rows], axis=0), firsts)
+    more = nt_dot(jnp.concatenate([r[:, width:] for r in rows], axis=0), seconds)
+    out_ref[:, :known] = total[:, :known] + more
+    out_ref[:, known:] = total[:, known:]
 
 
 def products(sets, weights):
-    rows, columns = sum(r.shape[0] for r in sets), sum(w.shape[0] for w in weights)
+    rows, columns = sum(r.shape[0] for r in sets), (len(weights) + 1) // 2 * weights[0].shape[0]
     return pl.pallas_call(
         functools.partial(products_kernel, len(sets)),
         out_shape=jax.ShapeDtypeStruct((rows, columns), jnp.float32),
@@ -155,20 +159,23 @@
 def late_kernel(where_ref, *refs):
     sets, weights = refs[:5], refs[5:-5]
     t_ref, corner_ref, kept_ref, given_ref, up_ref = refs[-5:]
-    half, features = sets[-1].shape
-    count, columns = weights[0].shape[0], up_ref.shape[1]
+    half, width = sets[-1].shape[0], sets[-1].shape[1] // 2
+    count = weights[0].shape[0]
     for k, ref in enumerate(weights):
-        at = (k % 2) * (len(weights) * count) + (k // 2) * (2 * count)
-        for part in range(2):
-            lanes = slice(features + part * columns, features + (part + 1) * columns)
-            up_ref[at + part * count : at + (part + 1) * count] = ref[:, lanes]
-    last = nt_dot(jnp.concatenate([r[...] for r in sets], axis=0), weights[-1][:, :features])
+        at = (k % 2) * (len(weights) // 2 * count) + (k // 2) * count
+        up_ref[at : at + count] = ref[:, width:]
+    last = nt_dot(jnp.concatenate([r[:, width:] for r in sets], axis=0), weights[-1][:, :width])
     first = where_ref[3] == 0
+    known = t_ref.shape[1] - count
     for k in range(4):
         ref, base = (t_ref, 2 * k * half) if k < 3 else (corner_ref, 0)
         low, high = (
             jnp.concatenate(
-                [ref[base + p * half : base + (p + 1) * half], last[(2 * k + p) * half : (2 * k + p + 1) * half]],
+                [
+                    ref[base + p * half : base + (p + 1) * half, :known],
+                    ref[base + p * half : base + (p + 1) * half, known:]
+                    + last[(2 * k + p) * half : (2 * k + p + 1) * half],
+                ],
                 axis=1,
             )
             for p in range(2)
@@ -181,8 +188,8 @@
     smem, vmem = (pl.BlockSpec(memory_space=m) for m in (pltpu.SMEM, pltpu.VMEM))
     count, lanes = weights[0].shape
     half, features = sets[-1].shape
-    shape = jax.ShapeDtypeStruct((4, half, len(weights) * count), jnp.float32)
-    up = ((2 * len(weights)) * count, (lanes - features) // 2)
+    shape = jax.ShapeDtypeStruct((4, half, len(weights) // 2 * count), jnp.float32)
+    up = (len(weights) * count, lanes - features // 2)
     return pl.pallas_call(
         late_kernel,
         out_shape=(shape, shape, jax.ShapeDtypeStruct(up, sets[0].dtype)),

time: 64.3 us -> 63.8 us (level)
  no operation moved by 1% of the time
where the time goes in v8:
time: 63.8 us; the launch traced here: 63.6 us
  starting transfers between devices  29.9 us (47%)
  waiting for transfers between devices  23.9 us (37%)
  Pallas kernels  7.32 us (11%)
  local copies, waits for them, and re-layouts  1.65 us (3%)
  between operations  0.8 us (1%)
    ppermute x6, starting transfers between devices, body(): along = lambda a, moves: lax.ppermute(a, 'group', line_pairs(groups, moves))  16.9 us
    ppermute x6, waiting for transfers between devices, body(): along = lambda a, moves: lax.ppermute(a, 'group', line_pairs(groups, moves))  14.9 us
    ppermute x4, starting transfers between devices, body(): lax.ppermute(a, 'group', [(i, i ^ 1) for i in range(groups)])  6.21 us
    ppermute x3, waiting for transfers between devices, body(): across = lambda a: lax.ppermute(a, 'parts', SWAP)  4.04 us
    ppermute x3, starting transfers between devices, body(): across = lambda a: lax.ppermute(a, 'parts', SWAP)  3.69 us
    ppermute x4, waiting for transfers between devices, body(): inside = lambda a: lax.ppermute(a, 'tensor', SWAP)  2.36 us
    ppermute x1, starting transfers between devices, body(): t_both = lax.ppermute(t_both, ('parts', 'group'), corner)  1.95 us
    ppermute x4, waiting for transfers between devices, body(): lax.ppermute(a, 'group', [(i, i ^ 1) for i in range(groups)])  1.87 us
  transfers between devices with their start and end apart: 19, of which 14 were waited for; matrix products, arithmetic and copies ran while one was open for 0% of the time, Pallas kernels for 4%

profile of v8, /device:TPU:0, one launch (start us, length us, event | category | flops | bytes accessed | tf_op | source)
XLA Modules:
  0.0 63.6 jit_solution(15093557242614598244)
XLA Ops:
  0.6 0.5 collective-permute-start
  1.1 2.6 %collective-permute-start.1 = (bf16[64,256]{1,0:T(8,128)(2,1)}, bf16[64,256]{1,0:T(8,128)(2,1)S(1)}, u32[]{:S(2)}, u32[]{:S(2)}) collective-permute-start(bf16[64,256]{1,0:T(8,128)(2,1)} %bitcast.26), channel_id=1, source_target_pairs={{0,2},{2,0},{4,6},{6,4},{8,10},{10,8},{12,14},{14,12},{1,3},{3,1},... | collective-permute-start | bytes 98312 | tf_op jit(solution)/shard_map/ppermute | solution.py:414
  3.7 1.2 %copy-done = bf16[64,2,4096]{2,1,0:T(2,128)(2,1)S(1)} copy-done((bf16[64,2,4096]{2,1,0:T(2,128)(2,1)S(1)}, bf16[64,2,4096]{2,1,0:T(2,128)(2,1)}, u32[]{:S(2)}) %copy-start) | copy-done | bytes 1048600
  4.9 0.1 shard_map.105.refs_0_
  5.1 0.0 copy-start.5
  5.1 0.1 stack.51.where_ref
  5.2 0.7 %collective-permute-done.1.up_beside_ref = bf16[64,256]{1,0:T(8,128)(2,1)S(1)} collective-permute-done((bf16[64,256]{1,0:T(8,128)(2,1)}, bf16[64,256]{1,0:T(8,128)(2,1)S(1)}, u32[]{:S(2)}, u32[]{:S(2)}) %collective-permute-start.1) | collective-permute-done | bytes 32800 | tf_op jit(solution)/shard_map/ppermute | solution.py:414
  5.9 0.1 copy-done.1
  6.0 0.2 copy-done.2
  6.1 0.7 %shard_map.104 = (bf16[64,2304]{1,0:T(8,128)(2,1)S(1)}, bf16[64,2304]{1,0:T(8,128)(2,1)S(1)}) custom-call(s32[12]{0:T(128)S(1)} %stack.51.where_ref, bf16[64,4096]{1,0:T(8,128)(2,1)S(1)} %bitcast.21, bf16[32,8192]{1,0:T(8,128)(2,1)S(1)} %bitcast.22, bf16[32,8192]{1,0:T(8,128)(2,1)S(1)} %bitcast.25, bf16[64,256]{1,0:T(8,128)(2,1)S(1)} %bitcast.27, ...), custom_call_target="tpu_custom_call" | custom-call | tf_op jit(solution)/shard_map/pallas_call | solution.py:57
  6.8 2.0 %collective-permute-start.5 = (bf16[128,4096]{1,0:T(8,128)(2,1)S(1)}, bf16[128,4096]{1,0:T(8,128)(2,1)S(1)}, u32[]{:S(2)}, u32[]{:S(2)}) collective-permute-start(bf16[128,4096]{1,0:T(8,128)(2,1)S(1)} %shard_map.105.refs_0_), channel_id=1, source_target_pairs={{0,16},{16,0},{1,17},{17,1},{2,18},{18,2},{3,19},{19,3},{4,20},{20... | collective-permute-start | bytes 3145736 | tf_op jit(solution)/shard_map/ppermute | solution.py:413
  8.8 1.5 %collective-permute-start.2 = (bf16[128,4096]{1,0:T(8,128)(2,1)S(1)}, bf16[128,4096]{1,0:T(8,128)(2,1)S(1)}, u32[]{:S(2)}, u32[]{:S(2)}) collective-permute-start(bf16[128,4096]{1,0:T(8,128)(2,1)S(1)} %shard_map.105.refs_0_), channel_id=1, source_target_pairs={{0,2},{2,0},{4,6},{6,4},{8,10},{10,8},{12,14},{14,12},{1,3},{3,1},... | collective-permute-start | bytes 3145736 | tf_op jit(solution)/shard_map/ppermute | solution.py:414
  10.3 2.6 %collective-permute-start.9 = (bf16[64,2304]{1,0:T(8,128)(2,1)S(1)}, bf16[64,2304]{1,0:T(8,128)(2,1)S(1)}, u32[]{:S(2)}, u32[]{:S(2)}) collective-permute-start(bf16[64,2304]{1,0:T(8,128)(2,1)S(1)} %get-tuple-element.42.refs_3_.refs_2_.refs_5_), channel_id=1, source_target_pairs={{4,0},{6,2},{12,4},{14,6},{8,12},{10,14},{0,8},{2,10},{5,1},{7,3},... | collective-permute-start | bytes 884744 | tf_op jit(solution)/shard_map/ppermute | solution.py:412
  12.9 1.6 %collective-permute-start.3 = (bf16[64,2304]{1,0:T(8,128)(2,1)S(1)}, bf16[64,2304]{1,0:T(8,128)(2,1)S(1)}, u32[]{:S(2)}, u32[]{:S(2)}) collective-permute-start(bf16[64,2304]{1,0:T(8,128)(2,1)S(1)} %get-tuple-element.35.refs_4_.refs_3_.refs_6_), channel_id=1, source_target_pairs={{4,0},{6,2},{12,4},{14,6},{8,12},{10,14},{0,8},{2,10},{5,1},{7,3},... | collective-permute-start | bytes 884744 | tf_op jit(solution)/shard_map/ppermute | solution.py:412
  14.4 5.9 %collective-permute-done.9.refs_5_.refs_4_.refs_7_ = bf16[64,2304]{1,0:T(8,128)(2,1)S(1)} collective-permute-done((bf16[64,2304]{1,0:T(8,128)(2,1)S(1)}, bf16[64,2304]{1,0:T(8,128)(2,1)S(1)}, u32[]{:S(2)}, u32[]{:S(2)}) %collective-permute-start.9) | collective-permute-done | bytes 294944 | tf_op jit(solution)/shard_map/ppermute | solution.py:412
  20.3 3.4 %collective-permute-start.10 = (bf16[64,2304]{1,0:T(8,128)(2,1)S(1)}, bf16[64,2304]{1,0:T(8,128)(2,1)S(1)}, u32[]{:S(2)}, u32[]{:S(2)}) collective-permute-start(bf16[64,2304]{1,0:T(8,128)(2,1)S(1)} %collective-permute-done.9.refs_5_.refs_4_.refs_7_), channel_id=1, source_target_pairs={{4,0},{6,2},{12,4},{14,6},{8,12},{10,14},{0,8},{2,10},{5,1},{7,3},... | collective-permute-start | bytes 884744 | tf_op jit(solution)/shard_map/ppermute | solution.py:412
  23.7 2.9 %collective-permute-done.3.refs_6_.refs_5_.refs_8_ = bf16[64,2304]{1,0:T(8,128)(2,1)S(1)} collective-permute-done((bf16[64,2304]{1,0:T(8,128)(2,1)S(1)}, bf16[64,2304]{1,0:T(8,128)(2,1)S(1)}, u32[]{:S(2)}, u32[]{:S(2)}) %collective-permute-start.3) | collective-permute-done | bytes 294944 | tf_op jit(solution)/shard_map/ppermute | solution.py:412
  26.6 3.4 %collective-permute-start.4 = (bf16[64,2304]{1,0:T(8,128)(2,1)S(1)}, bf16[64,2304]{1,0:T(8,128)(2,1)S(1)}, u32[]{:S(2)}, u32[]{:S(2)}) collective-permute-start(bf16[64,2304]{1,0:T(8,128)(2,1)S(1)} %collective-permute-done.3.refs_6_.refs_5_.refs_8_), channel_id=1, source_target_pairs={{4,0},{6,2},{12,4},{14,6},{8,12},{10,14},{0,8},{2,10},{5,1},{7,3},... | collective-permute-start | bytes 884744 | tf_op jit(solution)/shard_map/ppermute | solution.py:412
  30.0 2.1 %collective-permute-done.5.refs_2_ = bf16[128,4096]{1,0:T(8,128)(2,1)S(1)} collective-permute-done((bf16[128,4096]{1,0:T(8,128)(2,1)S(1)}, bf16[128,4096]{1,0:T(8,128)(2,1)S(1)}, u32[]{:S(2)}, u32[]{:S(2)}) %collective-permute-start.5) | collective-permute-done | bytes 1048608 | tf_op jit(solution)/shard_map/ppermute | solution.py:413
  32.1 0.0 copy-start.4
  32.2 0.0 copy-start.6
  32.2 0.0 copy-start.8
  32.2 0.9 %collective-permute-start.7 = (bf16[64,4096]{1,0:T(8,128)(2,1)S(1)}, bf16[64,4096]{1,0:T(8,128)(2,1)S(1)}, u32[]{:S(2)}, u32[]{:S(2)}) collective-permute-start(bf16[64,4096]{1,0:T(8,128)(2,1)S(1)} %slice.8), channel_id=1, source_target_pairs={{0,2},{2,0},{4,6},{6,4},{8,10},{10,8},{12,14},{14,12},{1,3},{3,1},... | collective-permute-start | bytes 1572872 | tf_op jit(solution)/shard_map/ppermute | solution.py:414
  33.1 0.4 collective-permute-done.2.refs_1_
  33.5 1.4 %collective-permute-start.8 = (bf16[64,4096]{1,0:T(8,128)(2,1)S(1)}, bf16[64,4096]{1,0:T(8,128)(2,1)S(1)}, u32[]{:S(2)}, u32[]{:S(2)}) collective-permute-start(bf16[64,4096]{1,0:T(8,128)(2,1)S(1)} %slice.9), channel_id=1, source_target_pairs={{0,16},{16,0},{1,17},{17,1},{2,18},{18,2},{3,19},{19,3},{4,20},{20... | collective-permute-start | bytes 1572872 | tf_op jit(solution)/shard_map/ppermute | solution.py:413
  34.9 2.6 %collective-permute-start.11 = (bf16[64,2304]{1,0:T(8,128)(2,1)S(1)}, bf16[64,2304]{1,0:T(8,128)(2,1)S(1)}, u32[]{:S(2)}, u32[]{:S(2)}) collective-permute-start(bf16[64,2304]{1,0:T(8,128)(2,1)S(1)} %collective-permute-done.10.refs_7_.refs_6_.refs_9_), channel_id=1, source_target_pairs={{4,0},{6,2},{12,4},{14,6},{8,12},{10,14},{0,8},{2,10},{5,1},{7,3},... | collective-permute-start | bytes 884744 | tf_op jit(solution)/shard_map/ppermute | solution.py:412
  37.5 0.7 %shard_map.106 = (bf16[512,256]{1,0:T(8,128)(2,1)S(1)}, bf16[512,256]{1,0:T(8,128)(2,1)S(1)}, bf16[64,256]{1,0:T(8,128)(2,1)S(1)}, s32[8,256]{1,0:T(8,128)S(1)}, s32[64,128]{1,0:T(8,128)S(1)}) custom-call(s32[12]{0:T(128)S(1)} %stack.51.where_ref, s32[64]{0:T(128)S(1)} %copy-done.6, s32[64]{0:T(128)S(1)} %copy-done.7, s32[8]{0:T(128)S(1)} %copy-done.8, ...), custom_call_target="tpu_custom_call" | custom-call | tf_op jit(solution)/shard_map/pallas_call | solution.py:116
  38.2 0.1 collective-permute-done.4.refs_8_.refs_7_.refs_10_
  38.4 3.4 %collective-permute-start.12 = (bf16[64,2304]{1,0:T(8,128)(2,1)S(1)}, bf16[64,2304]{1,0:T(8,128)(2,1)S(1)}, u32[]{:S(2)}, u32[]{:S(2)}) collective-permute-start(bf16[64,2304]{1,0:T(8,128)(2,1)S(1)} %collective-permute-done.4.refs_8_.refs_7_.refs_10_), channel_id=1, source_target_pairs={{4,0},{6,2},{12,4},{14,6},{8,12},{10,14},{0,8},{2,10},{5,1},{7,3},... | collective-permute-start | bytes 884744 | tf_op jit(solution)/shard_map/ppermute | solution.py:412
  41.7 3.2 %collective-permute-done.11.refs_9_.refs_8_.refs_11_ = bf16[64,2304]{1,0:T(8,128)(2,1)S(1)} collective-permute-done((bf16[64,2304]{1,0:T(8,128)(2,1)S(1)}, bf16[64,2304]{1,0:T(8,128)(2,1)S(1)}, u32[]{:S(2)}, u32[]{:S(2)}) %collective-permute-start.11) | collective-permute-done | bytes 294944 | tf_op jit(solution)/shard_map/ppermute | solution.py:412
  44.9 1.0 %shard_map.107.refs_13_ = f32[384,256]{1,0:T(8,128)S(1)} custom-call(bf16[128,4096]{1,0:T(8,128)(2,1)S(1)} %shard_map.105.refs_0_, bf16[128,4096]{1,0:T(8,128)(2,1)S(1)} %collective-permute-done.2.refs_1_, bf16[128,4096]{1,0:T(8,128)(2,1)S(1)} %collective-permute-done.5.refs_2_, bf16[64,2304]{1,0:T(8,128)(2,1)S(1)} %get-tuple-element.42.refs_3_.refs_2_.refs_5_, ...), custom_call_target="tpu_custom_call" | custom-call | flops 805306368 | bytes 5242880 | tf_op jit(solution)/shard_map/pallas_call | solution.py:147
  46.0 0.2 collective-permute-done.8.refs_1_.refs_4_
  46.2 0.7 %shard_map.108.refs_14_ = f32[128,256]{1,0:T(8,128)S(1)} custom-call(bf16[64,4096]{1,0:T(8,128)(2,1)S(1)} %collective-permute-done.7.refs_0_.refs_3_, bf16[64,4096]{1,0:T(8,128)(2,1)S(1)} %collective-permute-done.8.refs_1_.refs_4_, bf16[64,2304]{1,0:T(8,128)(2,1)S(1)} %get-tuple-element.42.refs_3_.refs_2_.refs_5_, ...), custom_call_target="tpu_custom_call" | custom-call | flops 268435456 | bytes 3145728 | tf_op jit(solution)/shard_map/pallas_call | solution.py:147
  46.9 2.8 %collective-permute-done.12.refs_12_ = bf16[64,2304]{1,0:T(8,128)(2,1)S(1)} collective-permute-done((bf16[64,2304]{1,0:T(8,128)(2,1)S(1)}, bf16[64,2304]{1,0:T(8,128)(2,1)S(1)}, u32[]{:S(2)}, u32[]{:S(2)}) %collective-permute-start.12) | collective-permute-done | bytes 294944 | tf_op jit(solution)/shard_map/ppermute | solution.py:412
  49.6 1.3 %shard_map.109 = (f32[4,64,256]{2,1,0:T(8,128)S(1)}, f32[4,64,256]{2,1,0:T(8,128)S(1)}, bf16[512,256]{1,0:T(8,128)(2,1)S(1)}) custom-call(s32[12]{0:T(128)S(1)} %stack.51.where_ref, bf16[128,4096]{1,0:T(8,128)(2,1)S(1)} %shard_map.105.refs_0_, bf16[128,4096]{1,0:T(8,128)(2,1)S(1)} %collective-permute-done.2.refs_1_, ...), custom_call_target="tpu_custom_call" | custom-call | tf_op jit(solution)/shard_map/pallas_call | solution.py:193
  50.9 0.1 collective-permute-start.13
  51.0 0.5 collective-permute-start.17
  51.5 1.0 %collective-permute-done.13.b_ref.other_ref = f32[4,64,256]{2,1,0:T(8,128)S(1)} collective-permute-done((f32[4,64,256]{2,1,0:T(8,128)S(1)}, f32[4,64,256]{2,1,0:T(8,128)S(1)}, u32[]{:S(2)}, u32[]{:S(2)}) %collective-permute-start.13) | collective-permute-done | bytes 262176 | tf_op jit(solution)/shard_map/ppermute | solution.py:415
  52.6 1.2 %collective-permute-start.14 = (f32[64,256]{1,0:T(8,128)S(1)}, f32[64,256]{1,0:T(8,128)S(1)}, u32[]{:S(2)}, u32[]{:S(2)}) collective-permute-start(f32[64,256]{1,0:T(8,128)S(1)} %get-tuple-element.53), channel_id=1, source_target_pairs={{0,2},{2,0},{4,6},{6,4},{8,10},{10,8},{12,14},{14,12},{1,3},{3,1},... | collective-permute-start | bytes 196616 | tf_op jit(solution)/shard_map/ppermute | solution.py:414
  53.8 0.4 collective-permute-start.15
  54.2 2.0 %collective-permute-start.16 = (f32[64,256]{1,0:T(8,128)S(1)}, f32[64,256]{1,0:T(8,128)S(1)}, u32[]{:S(2)}, u32[]{:S(2)}) collective-permute-start(f32[64,256]{1,0:T(8,128)S(1)} %get-tuple-element.55), channel_id=1, source_target_pairs={{0,18},{2,16},{4,22},{6,20},{8,26},{10,24},{12,30},{14,28},{16,2},... | collective-permute-start | bytes 196616 | tf_op jit(solution)/shard_map/ppermute | solution.py:445
  56.1 0.8 %collective-permute-done.14.beside_ref = f32[64,256]{1,0:T(8,128)S(1)} collective-permute-done((f32[64,256]{1,0:T(8,128)S(1)}, f32[64,256]{1,0:T(8,128)S(1)}, u32[]{:S(2)}, u32[]{:S(2)}) %collective-permute-start.14) | collective-permute-done | bytes 65568 | tf_op jit(solution)/shard_map/ppermute | solution.py:414
  56.9 1.8 %collective-permute-done.15.across_ref = f32[64,256]{1,0:T(8,128)S(1)} collective-permute-done((f32[64,256]{1,0:T(8,128)S(1)}, f32[64,256]{1,0:T(8,128)S(1)}, u32[]{:S(2)}, u32[]{:S(2)}) %collective-permute-start.15) | collective-permute-done | bytes 65568 | tf_op jit(solution)/shard_map/ppermute | solution.py:413
  58.7 0.7 %collective-permute-done.16.both_ref = f32[64,256]{1,0:T(8,128)S(1)} collective-permute-done((f32[64,256]{1,0:T(8,128)S(1)}, f32[64,256]{1,0:T(8,128)S(1)}, u32[]{:S(2)}, u32[]{:S(2)}) %collective-permute-start.16) | collective-permute-done | bytes 65568 | tf_op jit(solution)/shard_map/ppermute | solution.py:445
  59.3 1.5 %shard_map.111.mine_ref = bf16[2,32,2,512]{3,2,1,0:T(2,128)(2,1)S(1)} custom-call(s32[12]{0:T(128)S(1)} %stack.51.where_ref, f32[4,64,256]{2,1,0:T(8,128)S(1)} %get-tuple-element.51.a_ref.own_ref, f32[4,64,256]{2,1,0:T(8,128)S(1)} %collective-permute-done.13.b_ref.other_ref, f32[64,256]{1,0:T(8,128)S(1)} %collective-permute-done.14.beside_ref, ...), custom_call_target="tpu_custom_call" | custom-call | tf_op jit(solution)/shard_map/pallas_call | solution.py:350
  60.9 0.1 collective-permute-start.18
  61.0 1.3 %collective-permute-done.18.other_ref = bf16[2,32,2,512]{3,2,1,0:T(2,128)(2,1)S(1)} collective-permute-done((bf16[2,32,2,512]{3,2,1,0:T(2,128)(2,1)S(1)}, bf16[2,32,2,512]{3,2,1,0:T(2,128)(2,1)S(1)}, u32[]{:S(2)}, u32[]{:S(2)}) %collective-permute-start.18) | collective-permute-done | bytes 131104 | tf_op jit(solution)/shard_map/ppermute | solution.py:415
  62.3 1.3 %shard_map.112 = (bf16[64,2,512]{2,1,0:T(2,128)(2,1)}, bf16[64,2,512]{2,1,0:T(2,128)(2,1)}) custom-call(s32[12]{0:T(128)S(1)} %stack.51.where_ref, bf16[2,32,2,512]{3,2,1,0:T(2,128)(2,1)S(1)} %shard_map.111.mine_ref, bf16[2,32,2,512]{3,2,1,0:T(2,128)(2,1)S(1)} %collective-permute-done.18.other_ref), custom_call_target="tpu_custom_call" | custom-call | tf_op jit(solution)/shard_map/pallas_call | solution.py:218
  (20 shorter events, 0.1 us)
Async XLA Ops:
  0.6 5.3 %collective-permute-start = (bf16[1,8192,32]{1,2,0:T(8,128)(2,1)}, bf16[1,8192,32]{1,2,0:T(8,128)(2,1)S(1)}, u32[]{:S(2)}, u32[]{:S(2)}) collective-permute-start(bf16[1,8192,32]{1,2,0:T(8,128)(2,1)} %param.11), channel_id=1, source_target_pairs={{0,1},{1,0},{2,3},{3,2},{4,5},{5,4},{6,7},{7,6},{8,9},{9,8},{10,11... | collective-permute-start | bytes 1572872 | tf_op jit(solution)/shard_map/ppermute | solution.py:398
  1.1 4.8 %collective-permute-start.1 = (bf16[64,256]{1,0:T(8,128)(2,1)}, bf16[64,256]{1,0:T(8,128)(2,1)S(1)}, u32[]{:S(2)}, u32[]{:S(2)}) collective-permute-start(bf16[64,256]{1,0:T(8,128)(2,1)} %bitcast.26), channel_id=1, source_target_pairs={{0,2},{2,0},{4,6},{6,4},{8,10},{10,8},{12,14},{14,12},{1,3},{3,1},... | collective-permute-start | bytes 98312 | tf_op jit(solution)/shard_map/ppermute | solution.py:414
  3.7 1.2 %copy-start = (bf16[64,2,4096]{2,1,0:T(2,128)(2,1)S(1)}, bf16[64,2,4096]{2,1,0:T(2,128)(2,1)}, u32[]{:S(2)}) copy-start(bf16[64,2,4096]{2,1,0:T(2,128)(2,1)} %x_ref.1) | copy-start | bytes 3145732
  4.9 1.0 %copy-start.1 = (bf16[4096,64]{0,1:T(8,128)(2,1)S(1)}, bf16[4096,64]{0,1:T(8,128)(2,1)}, u32[]{:S(2)}) copy-start(bf16[4096,64]{0,1:T(8,128)(2,1)} %param.10) | copy-start | bytes 1572868
  4.9 1.2 %copy-start.2 = (bf16[1,8192,32]{1,2,0:T(8,128)(2,1)S(1)}, bf16[1,8192,32]{1,2,0:T(8,128)(2,1)}, u32[]{:S(2)}) copy-start(bf16[1,8192,32]{1,2,0:T(8,128)(2,1)} %param.11) | copy-start | bytes 1572868
  5.1 1.1 %copy-start.5 = (bf16[1,64,256]{2,1,0:T(8,128)(2,1)S(1)}, bf16[1,64,256]{2,1,0:T(8,128)(2,1)}, u32[]{:S(2)}) copy-start(bf16[1,64,256]{2,1,0:T(8,128)(2,1)} %param.12) | copy-start | bytes 98308
  6.1 8.3 %copy-start.3 = (bf16[64,16,256]{2,1,0:T(8,128)(2,1)S(1)}, bf16[64,16,256]{2,1,0:T(8,128)(2,1)}, u32[]{:S(2)}) copy-start(bf16[64,16,256]{2,1,0:T(8,128)(2,1)} %param.13) | copy-start | bytes 1572868
  6.8 25.3 %collective-permute-start.5 = (bf16[128,4096]{1,0:T(8,128)(2,1)S(1)}, bf16[128,4096]{1,0:T(8,128)(2,1)S(1)}, u32[]{:S(2)}, u32[]{:S(2)}) collective-permute-start(bf16[128,4096]{1,0:T(8,128)(2,1)S(1)} %shard_map.105.refs_0_), channel_id=1, source_target_pairs={{0,16},{16,0},{1,17},{17,1},{2,18},{18,2},{3,19},{19,3},{4,20},{20... | collective-permute-start | bytes 3145736 | tf_op jit(solution)/shard_map/ppermute | solution.py:413
  8.8 24.7 %collective-permute-start.2 = (bf16[128,4096]{1,0:T(8,128)(2,1)S(1)}, bf16[128,4096]{1,0:T(8,128)(2,1)S(1)}, u32[]{:S(2)}, u32[]{:S(2)}) collective-permute-start(bf16[128,4096]{1,0:T(8,128)(2,1)S(1)} %shard_map.105.refs_0_), channel_id=1, source_target_pairs={{0,2},{2,0},{4,6},{6,4},{8,10},{10,8},{12,14},{14,12},{1,3},{3,1},... | collective-permute-start | bytes 3145736 | tf_op jit(solution)/shard_map/ppermute | solution.py:414
  10.3 10.1 %collective-permute-start.9 = (bf16[64,2304]{1,0:T(8,128)(2,1)S(1)}, bf16[64,2304]{1,0:T(8,128)(2,1)S(1)}, u32[]{:S(2)}, u32[]{:S(2)}) collective-permute-start(bf16[64,2304]{1,0:T(8,128)(2,1)S(1)} %get-tuple-element.42.refs_3_.refs_2_.refs_5_), channel_id=1, source_target_pairs={{4,0},{6,2},{12,4},{14,6},{8,12},{10,14},{0,8},{2,10},{5,1},{7,3},... | collective-permute-start | bytes 884744 | tf_op jit(solution)/shard_map/ppermute | solution.py:412
  12.9 13.8 %collective-permute-start.3 = (bf16[64,2304]{1,0:T(8,128)(2,1)S(1)}, bf16[64,2304]{1,0:T(8,128)(2,1)S(1)}, u32[]{:S(2)}, u32[]{:S(2)}) collective-permute-start(bf16[64,2304]{1,0:T(8,128)(2,1)S(1)} %get-tuple-element.35.refs_4_.refs_3_.refs_6_), channel_id=1, source_target_pairs={{4,0},{6,2},{12,4},{14,6},{8,12},{10,14},{0,8},{2,10},{5,1},{7,3},... | collective-permute-start | bytes 884744 | tf_op jit(solution)/shard_map/ppermute | solution.py:412
  14.4 23.1 %collective-permute-start.6 = (bf16[1024,256]{1,0:T(8,128)(2,1)S(1)}, bf16[1024,256]{1,0:T(8,128)(2,1)S(1)}, u32[]{:S(2)}, u32[]{:S(2)}) collective-permute-start(bf16[1024,256]{1,0:T(8,128)(2,1)S(1)} %bitcast.23), channel_id=1, source_target_pairs={{0,1},{1,0},{2,3},{3,2},{4,5},{5,4},{6,7},{7,6},{8,9},{9,8},{10,11... | collective-permute-start | bytes 1572872 | tf_op jit(solution)/shard_map/ppermute | solution.py:415
  20.3 14.6 %collective-permute-start.10 = (bf16[64,2304]{1,0:T(8,128)(2,1)S(1)}, bf16[64,2304]{1,0:T(8,128)(2,1)S(1)}, u32[]{:S(2)}, u32[]{:S(2)}) collective-permute-start(bf16[64,2304]{1,0:T(8,128)(2,1)S(1)} %collective-permute-done.9.refs_5_.refs_4_.refs_7_), channel_id=1, source_target_pairs={{4,0},{6,2},{12,4},{14,6},{8,12},{10,14},{0,8},{2,10},{5,1},{7,3},... | collective-permute-start | bytes 884744 | tf_op jit(solution)/shard_map/ppermute | solution.py:412
  26.6 11.7 %collective-permute-start.4 = (bf16[64,2304]{1,0:T(8,128)(2,1)S(1)}, bf16[64,2304]{1,0:T(8,128)(2,1)S(1)}, u32[]{:S(2)}, u32[]{:S(2)}) collective-permute-start(bf16[64,2304]{1,0:T(8,128)(2,1)S(1)} %collective-permute-done.3.refs_6_.refs_5_.refs_8_), channel_id=1, source_target_pairs={{4,0},{6,2},{12,4},{14,6},{8,12},{10,14},{0,8},{2,10},{5,1},{7,3},... | collective-permute-start | bytes 884744 | tf_op jit(solution)/shard_map/ppermute | solution.py:412
  32.1 5.3 %copy-start.4 = (bf16[64,2,256]{2,1,0:T(2,128)(2,1)S(1)}, bf16[64,2,256]{2,1,0:T(2,128)(2,1)}, u32[]{:S(2)}) copy-start(bf16[64,2,256]{2,1,0:T(2,128)(2,1)} %fresh_ref.1) | copy-start | bytes 196612
  32.2 5.3 %copy-start.6 = (s32[64]{0:T(128)S(1)}, s32[64]{0:T(128)}, u32[]{:S(2)}) copy-start(s32[64]{0:T(128)} %lengths_ref.1) | copy-start | bytes 772
  32.2 5.3 %copy-start.7 = (s32[64]{0:T(128)S(1)}, s32[64]{0:T(128)}, u32[]{:S(2)}) copy-start(s32[64]{0:T(128)} %adapter_ref.1) | copy-start | bytes 772
  32.2 5.3 %copy-start.8 = (s32[8]{0:T(128)S(1)}, s32[8]{0:T(128)}, u32[]{:S(2)}) copy-start(s32[8]{0:T(128)} %owner_ref.1) | copy-start | bytes 100
  32.2 13.8 %collective-permute-start.7 = (bf16[64,4096]{1,0:T(8,128)(2,1)S(1)}, bf16[64,4096]{1,0:T(8,128)(2,1)S(1)}, u32[]{:S(2)}, u32[]{:S(2)}) collective-permute-start(bf16[64,4096]{1,0:T(8,128)(2,1)S(1)} %slice.8), channel_id=1, source_target_pairs={{0,2},{2,0},{4,6},{6,4},{8,10},{10,8},{12,14},{14,12},{1,3},{3,1},... | collective-permute-start | bytes 1572872 | tf_op jit(solution)/shard_map/ppermute | solution.py:414
  33.5 12.6 %collective-permute-start.8 = (bf16[64,4096]{1,0:T(8,128)(2,1)S(1)}, bf16[64,4096]{1,0:T(8,128)(2,1)S(1)}, u32[]{:S(2)}, u32[]{:S(2)}) collective-permute-start(bf16[64,4096]{1,0:T(8,128)(2,1)S(1)} %slice.9), channel_id=1, source_target_pairs={{0,16},{16,0},{1,17},{17,1},{2,18},{18,2},{3,19},{19,3},{4,20},{20... | collective-permute-start | bytes 1572872 | tf_op jit(solution)/shard_map/ppermute | solution.py:413
  34.9 10.1 %collective-permute-start.11 = (bf16[64,2304]{1,0:T(8,128)(2,1)S(1)}, bf16[64,2304]{1,0:T(8,128)(2,1)S(1)}, u32[]{:S(2)}, u32[]{:S(2)}) collective-permute-start(bf16[64,2304]{1,0:T(8,128)(2,1)S(1)} %collective-permute-done.10.refs_7_.refs_6_.refs_9_), channel_id=1, source_target_pairs={{4,0},{6,2},{12,4},{14,6},{8,12},{10,14},{0,8},{2,10},{5,1},{7,3},... | collective-permute-start | bytes 884744 | tf_op jit(solution)/shard_map/ppermute | solution.py:412
  38.4 11.3 %collective-permute-start.12 = (bf16[64,2304]{1,0:T(8,128)(2,1)S(1)}, bf16[64,2304]{1,0:T(8,128)(2,1)S(1)}, u32[]{:S(2)}, u32[]{:S(2)}) collective-permute-start(bf16[64,2304]{1,0:T(8,128)(2,1)S(1)} %collective-permute-done.4.refs_8_.refs_7_.refs_10_), channel_id=1, source_target_pairs={{4,0},{6,2},{12,4},{14,6},{8,12},{10,14},{0,8},{2,10},{5,1},{7,3},... | collective-permute-start | bytes 884744 | tf_op jit(solution)/shard_map/ppermute | solution.py:412
  50.9 1.6 %collective-permute-start.13 = (f32[4,64,256]{2,1,0:T(8,128)S(1)}, f32[4,64,256]{2,1,0:T(8,128)S(1)}, u32[]{:S(2)}, u32[]{:S(2)}) collective-permute-start(f32[4,64,256]{2,1,0:T(8,128)S(1)} %get-tuple-element.52), channel_id=1, source_target_pairs={{0,1},{1,0},{2,3},{3,2},{4,5},{5,4},{6,7},{7,6},{8,9},{9,8},{10,11... | collective-permute-start | bytes 786440 | tf_op jit(solution)/shard_map/ppermute | solution.py:415
  51.0 5.1 %collective-permute-start.17 = (bf16[512,256]{1,0:T(8,128)(2,1)S(1)}, bf16[512,256]{1,0:T(8,128)(2,1)S(1)}, u32[]{:S(2)}, u32[]{:S(2)}) collective-permute-start(bf16[512,256]{1,0:T(8,128)(2,1)S(1)} %get-tuple-element.57.up_ref), channel_id=1, source_target_pairs={{0,1},{1,0},{2,3},{3,2},{4,5},{5,4},{6,7},{7,6},{8,9},{9,8},{10,11... | collective-permute-start | bytes 786440 | tf_op jit(solution)/shard_map/ppermute | solution.py:415
  52.6 4.3 %collective-permute-start.14 = (f32[64,256]{1,0:T(8,128)S(1)}, f32[64,256]{1,0:T(8,128)S(1)}, u32[]{:S(2)}, u32[]{:S(2)}) collective-permute-start(f32[64,256]{1,0:T(8,128)S(1)} %get-tuple-element.53), channel_id=1, source_target_pairs={{0,2},{2,0},{4,6},{6,4},{8,10},{10,8},{12,14},{14,12},{1,3},{3,1},... | collective-permute-start | bytes 196616 | tf_op jit(solution)/shard_map/ppermute | solution.py:414
  53.8 4.9 %collective-permute-start.15 = (f32[64,256]{1,0:T(8,128)S(1)}, f32[64,256]{1,0:T(8,128)S(1)}, u32[]{:S(2)}, u32[]{:S(2)}) collective-permute-start(f32[64,256]{1,0:T(8,128)S(1)} %get-tuple-element.54), channel_id=1, source_target_pairs={{0,16},{16,0},{1,17},{17,1},{2,18},{18,2},{3,19},{19,3},{4,20},{20... | collective-permute-start | bytes 196616 | tf_op jit(solution)/shard_map/ppermute | solution.py:413
  54.2 5.2 %collective-permute-start.16 = (f32[64,256]{1,0:T(8,128)S(1)}, f32[64,256]{1,0:T(8,128)S(1)}, u32[]{:S(2)}, u32[]{:S(2)}) collective-permute-start(f32[64,256]{1,0:T(8,128)S(1)} %get-tuple-element.55), channel_id=1, source_target_pairs={{0,18},{2,16},{4,22},{6,20},{8,26},{10,24},{12,30},{14,28},{16,2},... | collective-permute-start | bytes 196616 | tf_op jit(solution)/shard_map/ppermute | solution.py:445
  60.9 1.4 %collective-permute-start.18 = (bf16[2,32,2,512]{3,2,1,0:T(2,128)(2,1)S(1)}, bf16[2,32,2,512]{3,2,1,0:T(2,128)(2,1)S(1)}, u32[]{:S(2)}, u32[]{:S(2)}) collective-permute-start(bf16[2,32,2,512]{3,2,1,0:T(2,128)(2,1)S(1)} %shard_map.111.mine_ref), channel_id=1, source_target_pairs={{0,1},{1,0},{2,3},{3,2},{4,5},{5,4},{6,7},{7,6},{8,9},{9,8},{10,11... | collective-permute-start | bytes 393224 | tf_op jit(solution)/shard_map/ppermute | solution.py:415

commit v9 on v8

--- a/solution.py
+++ b/solution.py
@@ -242,7 +242,7 @@
 def attend_block(queries, keys, values, mask, scaling):
     scores = jnp.where(mask, nt_dot(queries, keys) * scaling, FAR)
     highest = scores.max(axis=1, keepdims=True)
-    weights = jnp.where(mask, jnp.exp(scores - highest), 0.0)
+    weights = jnp.exp(scores - highest)
     totals = weights.sum(axis=1, keepdims=True)
     sums = jnp.dot(weights.astype(jnp.bfloat16), values, preferred_element_type=jnp.float32)
     return sums / totals

time: 63.8 us -> 63.7 us (level)
  no operation moved by 1% of the time
where the time goes in v9:
time: 63.7 us; the launch traced here: 63.5 us
  starting transfers between devices  29.9 us (47%)
  waiting for transfers between devices  23.9 us (38%)
  Pallas kernels  7.29 us (11%)
  local copies, waits for them, and re-layouts  1.65 us (3%)
  between operations  0.8 us (1%)
    ppermute x6, starting transfers between devices, body(): along = lambda a, moves: lax.ppermute(a, 'group', line_pairs(groups, moves))  16.9 us
    ppermute x6, waiting for transfers between devices, body(): along = lambda a, moves: lax.ppermute(a, 'group', line_pairs(groups, moves))  14.9 us
    ppermute x4, starting transfers between devices, body(): lax.ppermute(a, 'group', [(i, i ^ 1) for i in range(groups)])  6.21 us
    ppermute x3, waiting for transfers between devices, body(): across = lambda a: lax.ppermute(a, 'parts', SWAP)  4.04 us
    ppermute x3, starting transfers between devices, body(): across = lambda a: lax.ppermute(a, 'parts', SWAP)  3.69 us
    ppermute x4, waiting for transfers between devices, body(): inside = lambda a: lax.ppermute(a, 'tensor', SWAP)  2.36 us
    ppermute x1, starting transfers between devices, body(): t_both = lax.ppermute(t_both, ('parts', 'group'), corner)  1.95 us
    ppermute x4, waiting for transfers between devices, body(): lax.ppermute(a, 'group', [(i, i ^ 1) for i in range(groups)])  1.87 us
  transfers between devices with their start and end apart: 19, of which 14 were waited for; matrix products, arithmetic and copies ran while one was open for 0% of the time, Pallas kernels for 4%

profile of v9, /device:TPU:0, one launch (start us, length us, event | category | flops | bytes accessed | tf_op | source)
XLA Modules:
  0.0 63.5 jit_solution(8769312011769821226)
XLA Ops:
  0.6 0.5 collective-permute-start
  1.1 2.6 %collective-permute-start.1 = (bf16[64,256]{1,0:T(8,128)(2,1)}, bf16[64,256]{1,0:T(8,128)(2,1)S(1)}, u32[]{:S(2)}, u32[]{:S(2)}) collective-permute-start(bf16[64,256]{1,0:T(8,128)(2,1)} %bitcast.26), channel_id=1, source_target_pairs={{0,2},{2,0},{4,6},{6,4},{8,10},{10,8},{12,14},{14,12},{1,3},{3,1},... | collective-permute-start | bytes 98312 | tf_op jit(solution)/shard_map/ppermute | solution.py:414
  3.7 1.2 %copy-done = bf16[64,2,4096]{2,1,0:T(2,128)(2,1)S(1)} copy-done((bf16[64,2,4096]{2,1,0:T(2,128)(2,1)S(1)}, bf16[64,2,4096]{2,1,0:T(2,128)(2,1)}, u32[]{:S(2)}) %copy-start) | copy-done | bytes 1048600
  4.9 0.1 shard_map.105.refs_0_
  5.1 0.0 copy-start.5
  5.1 0.1 stack.51.where_ref
  5.2 0.7 %collective-permute-done.1.up_beside_ref = bf16[64,256]{1,0:T(8,128)(2,1)S(1)} collective-permute-done((bf16[64,256]{1,0:T(8,128)(2,1)}, bf16[64,256]{1,0:T(8,128)(2,1)S(1)}, u32[]{:S(2)}, u32[]{:S(2)}) %collective-permute-start.1) | collective-permute-done | bytes 32800 | tf_op jit(solution)/shard_map/ppermute | solution.py:414
  5.9 0.1 copy-done.1
  6.0 0.2 copy-done.2
  6.1 0.7 %shard_map.104 = (bf16[64,2304]{1,0:T(8,128)(2,1)S(1)}, bf16[64,2304]{1,0:T(8,128)(2,1)S(1)}) custom-call(s32[12]{0:T(128)S(1)} %stack.51.where_ref, bf16[64,4096]{1,0:T(8,128)(2,1)S(1)} %bitcast.21, bf16[32,8192]{1,0:T(8,128)(2,1)S(1)} %bitcast.22, bf16[32,8192]{1,0:T(8,128)(2,1)S(1)} %bitcast.25, bf16[64,256]{1,0:T(8,128)(2,1)S(1)} %bitcast.27, ...), custom_call_target="tpu_custom_call" | custom-call | tf_op jit(solution)/shard_map/pallas_call | solution.py:57
  6.8 2.0 %collective-permute-start.5 = (bf16[128,4096]{1,0:T(8,128)(2,1)S(1)}, bf16[128,4096]{1,0:T(8,128)(2,1)S(1)}, u32[]{:S(2)}, u32[]{:S(2)}) collective-permute-start(bf16[128,4096]{1,0:T(8,128)(2,1)S(1)} %shard_map.105.refs_0_), channel_id=1, source_target_pairs={{0,16},{16,0},{1,17},{17,1},{2,18},{18,2},{3,19},{19,3},{4,20},{20... | collective-permute-start | bytes 3145736 | tf_op jit(solution)/shard_map/ppermute | solution.py:413
  8.8 1.5 %collective-permute-start.2 = (bf16[128,4096]{1,0:T(8,128)(2,1)S(1)}, bf16[128,4096]{1,0:T(8,128)(2,1)S(1)}, u32[]{:S(2)}, u32[]{:S(2)}) collective-permute-start(bf16[128,4096]{1,0:T(8,128)(2,1)S(1)} %shard_map.105.refs_0_), channel_id=1, source_target_pairs={{0,2},{2,0},{4,6},{6,4},{8,10},{10,8},{12,14},{14,12},{1,3},{3,1},... | collective-permute-start | bytes 3145736 | tf_op jit(solution)/shard_map/ppermute | solution.py:414
  10.3 2.6 %collective-permute-start.9 = (bf16[64,2304]{1,0:T(8,128)(2,1)S(1)}, bf16[64,2304]{1,0:T(8,128)(2,1)S(1)}, u32[]{:S(2)}, u32[]{:S(2)}) collective-permute-start(bf16[64,2304]{1,0:T(8,128)(2,1)S(1)} %get-tuple-element.42.refs_3_.refs_2_.refs_5_), channel_id=1, source_target_pairs={{4,0},{6,2},{12,4},{14,6},{8,12},{10,14},{0,8},{2,10},{5,1},{7,3},... | collective-permute-start | bytes 884744 | tf_op jit(solution)/shard_map/ppermute | solution.py:412
  12.9 1.6 %collective-permute-start.3 = (bf16[64,2304]{1,0:T(8,128)(2,1)S(1)}, bf16[64,2304]{1,0:T(8,128)(2,1)S(1)}, u32[]{:S(2)}, u32[]{:S(2)}) collective-permute-start(bf16[64,2304]{1,0:T(8,128)(2,1)S(1)} %get-tuple-element.35.refs_4_.refs_3_.refs_6_), channel_id=1, source_target_pairs={{4,0},{6,2},{12,4},{14,6},{8,12},{10,14},{0,8},{2,10},{5,1},{7,3},... | collective-permute-start | bytes 884744 | tf_op jit(solution)/shard_map/ppermute | solution.py:412
  14.4 5.9 %collective-permute-done.9.refs_5_.refs_4_.refs_7_ = bf16[64,2304]{1,0:T(8,128)(2,1)S(1)} collective-permute-done((bf16[64,2304]{1,0:T(8,128)(2,1)S(1)}, bf16[64,2304]{1,0:T(8,128)(2,1)S(1)}, u32[]{:S(2)}, u32[]{:S(2)}) %collective-permute-start.9) | collective-permute-done | bytes 294944 | tf_op jit(solution)/shard_map/ppermute | solution.py:412
  20.3 3.4 %collective-permute-start.10 = (bf16[64,2304]{1,0:T(8,128)(2,1)S(1)}, bf16[64,2304]{1,0:T(8,128)(2,1)S(1)}, u32[]{:S(2)}, u32[]{:S(2)}) collective-permute-start(bf16[64,2304]{1,0:T(8,128)(2,1)S(1)} %collective-permute-done.9.refs_5_.refs_4_.refs_7_), channel_id=1, source_target_pairs={{4,0},{6,2},{12,4},{14,6},{8,12},{10,14},{0,8},{2,10},{5,1},{7,3},... | collective-permute-start | bytes 884744 | tf_op jit(solution)/shard_map/ppermute | solution.py:412
  23.7 2.9 %collective-permute-done.3.refs_6_.refs_5_.refs_8_ = bf16[64,2304]{1,0:T(8,128)(2,1)S(1)} collective-permute-done((bf16[64,2304]{1,0:T(8,128)(2,1)S(1)}, bf16[64,2304]{1,0:T(8,128)(2,1)S(1)}, u32[]{:S(2)}, u32[]{:S(2)}) %collective-permute-start.3) | collective-permute-done | bytes 294944 | tf_op jit(solution)/shard_map/ppermute | solution.py:412
  26.6 3.4 %collective-permute-start.4 = (bf16[64,2304]{1,0:T(8,128)(2,1)S(1)}, bf16[64,2304]{1,0:T(8,128)(2,1)S(1)}, u32[]{:S(2)}, u32[]{:S(2)}) collective-permute-start(bf16[64,2304]{1,0:T(8,128)(2,1)S(1)} %collective-permute-done.3.refs_6_.refs_5_.refs_8_), channel_id=1, source_target_pairs={{4,0},{6,2},{12,4},{14,6},{8,12},{10,14},{0,8},{2,10},{5,1},{7,3},... | collective-permute-start | bytes 884744 | tf_op jit(solution)/shard_map/ppermute | solution.py:412
  30.0 2.1 %collective-permute-done.5.refs_2_ = bf16[128,4096]{1,0:T(8,128)(2,1)S(1)} collective-permute-done((bf16[128,4096]{1,0:T(8,128)(2,1)S(1)}, bf16[128,4096]{1,0:T(8,128)(2,1)S(1)}, u32[]{:S(2)}, u32[]{:S(2)}) %collective-permute-start.5) | collective-permute-done | bytes 1048608 | tf_op jit(solution)/shard_map/ppermute | solution.py:413
  32.1 0.0 copy-start.4
  32.2 0.0 copy-start.7
  32.2 0.0 copy-start.8
  32.2 0.9 %collective-permute-start.7 = (bf16[64,4096]{1,0:T(8,128)(2,1)S(1)}, bf16[64,4096]{1,0:T(8,128)(2,1)S(1)}, u32[]{:S(2)}, u32[]{:S(2)}) collective-permute-start(bf16[64,4096]{1,0:T(8,128)(2,1)S(1)} %slice.8), channel_id=1, source_target_pairs={{0,2},{2,0},{4,6},{6,4},{8,10},{10,8},{12,14},{14,12},{1,3},{3,1},... | collective-permute-start | bytes 1572872 | tf_op jit(solution)/shard_map/ppermute | solution.py:414
  33.1 0.4 collective-permute-done.2.refs_1_
  33.5 1.4 %collective-permute-start.8 = (bf16[64,4096]{1,0:T(8,128)(2,1)S(1)}, bf16[64,4096]{1,0:T(8,128)(2,1)S(1)}, u32[]{:S(2)}, u32[]{:S(2)}) collective-permute-start(bf16[64,4096]{1,0:T(8,128)(2,1)S(1)} %slice.9), channel_id=1, source_target_pairs={{0,16},{16,0},{1,17},{17,1},{2,18},{18,2},{3,19},{19,3},{4,20},{20... | collective-permute-start | bytes 1572872 | tf_op jit(solution)/shard_map/ppermute | solution.py:413
  34.9 2.6 %collective-permute-start.11 = (bf16[64,2304]{1,0:T(8,128)(2,1)S(1)}, bf16[64,2304]{1,0:T(8,128)(2,1)S(1)}, u32[]{:S(2)}, u32[]{:S(2)}) collective-permute-start(bf16[64,2304]{1,0:T(8,128)(2,1)S(1)} %collective-permute-done.10.refs_7_.refs_6_.refs_9_), channel_id=1, source_target_pairs={{4,0},{6,2},{12,4},{14,6},{8,12},{10,14},{0,8},{2,10},{5,1},{7,3},... | collective-permute-start | bytes 884744 | tf_op jit(solution)/shard_map/ppermute | solution.py:412
  37.5 0.7 %shard_map.106 = (bf16[512,256]{1,0:T(8,128)(2,1)S(1)}, bf16[512,256]{1,0:T(8,128)(2,1)S(1)}, bf16[64,256]{1,0:T(8,128)(2,1)S(1)}, s32[8,256]{1,0:T(8,128)S(1)}, s32[64,128]{1,0:T(8,128)S(1)}) custom-call(s32[12]{0:T(128)S(1)} %stack.51.where_ref, s32[64]{0:T(128)S(1)} %copy-done.6, s32[64]{0:T(128)S(1)} %copy-done.7, s32[8]{0:T(128)S(1)} %copy-done.8, ...), custom_call_target="tpu_custom_call" | custom-call | tf_op jit(solution)/shard_map/pallas_call | solution.py:116
  38.2 0.1 collective-permute-done.4.refs_8_.refs_7_.refs_10_
  38.4 3.4 %collective-permute-start.12 = (bf16[64,2304]{1,0:T(8,128)(2,1)S(1)}, bf16[64,2304]{1,0:T(8,128)(2,1)S(1)}, u32[]{:S(2)}, u32[]{:S(2)}) collective-permute-start(bf16[64,2304]{1,0:T(8,128)(2,1)S(1)} %collective-permute-done.4.refs_8_.refs_7_.refs_10_), channel_id=1, source_target_pairs={{4,0},{6,2},{12,4},{14,6},{8,12},{10,14},{0,8},{2,10},{5,1},{7,3},... | collective-permute-start | bytes 884744 | tf_op jit(solution)/shard_map/ppermute | solution.py:412
  41.7 3.2 %collective-permute-done.11.refs_9_.refs_8_.refs_11_ = bf16[64,2304]{1,0:T(8,128)(2,1)S(1)} collective-permute-done((bf16[64,2304]{1,0:T(8,128)(2,1)S(1)}, bf16[64,2304]{1,0:T(8,128)(2,1)S(1)}, u32[]{:S(2)}, u32[]{:S(2)}) %collective-permute-start.11) | collective-permute-done | bytes 294944 | tf_op jit(solution)/shard_map/ppermute | solution.py:412
  44.9 1.0 %shard_map.107.refs_13_ = f32[384,256]{1,0:T(8,128)S(1)} custom-call(bf16[128,4096]{1,0:T(8,128)(2,1)S(1)} %shard_map.105.refs_0_, bf16[128,4096]{1,0:T(8,128)(2,1)S(1)} %collective-permute-done.2.refs_1_, bf16[128,4096]{1,0:T(8,128)(2,1)S(1)} %collective-permute-done.5.refs_2_, bf16[64,2304]{1,0:T(8,128)(2,1)S(1)} %get-tuple-element.42.refs_3_.refs_2_.refs_5_, ...), custom_call_target="tpu_custom_call" | custom-call | flops 805306368 | bytes 5242880 | tf_op jit(solution)/shard_map/pallas_call | solution.py:147
  46.0 0.2 collective-permute-done.8.refs_1_.refs_4_
  46.2 0.7 %shard_map.108.refs_14_ = f32[128,256]{1,0:T(8,128)S(1)} custom-call(bf16[64,4096]{1,0:T(8,128)(2,1)S(1)} %collective-permute-done.7.refs_0_.refs_3_, bf16[64,4096]{1,0:T(8,128)(2,1)S(1)} %collective-permute-done.8.refs_1_.refs_4_, bf16[64,2304]{1,0:T(8,128)(2,1)S(1)} %get-tuple-element.42.refs_3_.refs_2_.refs_5_, ...), custom_call_target="tpu_custom_call" | custom-call | flops 268435456 | bytes 3145728 | tf_op jit(solution)/shard_map/pallas_call | solution.py:147
  46.9 2.8 %collective-permute-done.12.refs_12_ = bf16[64,2304]{1,0:T(8,128)(2,1)S(1)} collective-permute-done((bf16[64,2304]{1,0:T(8,128)(2,1)S(1)}, bf16[64,2304]{1,0:T(8,128)(2,1)S(1)}, u32[]{:S(2)}, u32[]{:S(2)}) %collective-permute-start.12) | collective-permute-done | bytes 294944 | tf_op jit(solution)/shard_map/ppermute | solution.py:412
  49.6 1.3 %shard_map.109 = (f32[4,64,256]{2,1,0:T(8,128)S(1)}, f32[4,64,256]{2,1,0:T(8,128)S(1)}, bf16[512,256]{1,0:T(8,128)(2,1)S(1)}) custom-call(s32[12]{0:T(128)S(1)} %stack.51.where_ref, bf16[128,4096]{1,0:T(8,128)(2,1)S(1)} %shard_map.105.refs_0_, bf16[128,4096]{1,0:T(8,128)(2,1)S(1)} %collective-permute-done.2.refs_1_, ...), custom_call_target="tpu_custom_call" | custom-call | tf_op jit(solution)/shard_map/pallas_call | solution.py:193
  50.9 0.1 collective-permute-start.13
  51.0 0.5 collective-permute-start.17
  51.5 1.0 %collective-permute-done.13.b_ref.other_ref = f32[4,64,256]{2,1,0:T(8,128)S(1)} collective-permute-done((f32[4,64,256]{2,1,0:T(8,128)S(1)}, f32[4,64,256]{2,1,0:T(8,128)S(1)}, u32[]{:S(2)}, u32[]{:S(2)}) %collective-permute-start.13) | collective-permute-done | bytes 262176 | tf_op jit(solution)/shard_map/ppermute | solution.py:415
  52.6 1.2 %collective-permute-start.14 = (f32[64,256]{1,0:T(8,128)S(1)}, f32[64,256]{1,0:T(8,128)S(1)}, u32[]{:S(2)}, u32[]{:S(2)}) collective-permute-start(f32[64,256]{1,0:T(8,128)S(1)} %get-tuple-element.53), channel_id=1, source_target_pairs={{0,2},{2,0},{4,6},{6,4},{8,10},{10,8},{12,14},{14,12},{1,3},{3,1},... | collective-permute-start | bytes 196616 | tf_op jit(solution)/shard_map/ppermute | solution.py:414
  53.8 0.4 collective-permute-start.15
  54.2 2.0 %collective-permute-start.16 = (f32[64,256]{1,0:T(8,128)S(1)}, f32[64,256]{1,0:T(8,128)S(1)}, u32[]{:S(2)}, u32[]{:S(2)}) collective-permute-start(f32[64,256]{1,0:T(8,128)S(1)} %get-tuple-element.55), channel_id=1, source_target_pairs={{0,18},{2,16},{4,22},{6,20},{8,26},{10,24},{12,30},{14,28},{16,2},... | collective-permute-start | bytes 196616 | tf_op jit(solution)/shard_map/ppermute | solution.py:445
  56.1 0.8 %collective-permute-done.14.beside_ref = f32[64,256]{1,0:T(8,128)S(1)} collective-permute-done((f32[64,256]{1,0:T(8,128)S(1)}, f32[64,256]{1,0:T(8,128)S(1)}, u32[]{:S(2)}, u32[]{:S(2)}) %collective-permute-start.14) | collective-permute-done | bytes 65568 | tf_op jit(solution)/shard_map/ppermute | solution.py:414
  56.9 1.8 %collective-permute-done.15.across_ref = f32[64,256]{1,0:T(8,128)S(1)} collective-permute-done((f32[64,256]{1,0:T(8,128)S(1)}, f32[64,256]{1,0:T(8,128)S(1)}, u32[]{:S(2)}, u32[]{:S(2)}) %collective-permute-start.15) | collective-permute-done | bytes 65568 | tf_op jit(solution)/shard_map/ppermute | solution.py:413
  58.7 0.7 %collective-permute-done.16.both_ref = f32[64,256]{1,0:T(8,128)S(1)} collective-permute-done((f32[64,256]{1,0:T(8,128)S(1)}, f32[64,256]{1,0:T(8,128)S(1)}, u32[]{:S(2)}, u32[]{:S(2)}) %collective-permute-start.16) | collective-permute-done | bytes 65568 | tf_op jit(solution)/shard_map/ppermute | solution.py:445
  59.3 1.5 %shard_map.111.mine_ref = bf16[2,32,2,512]{3,2,1,0:T(2,128)(2,1)S(1)} custom-call(s32[12]{0:T(128)S(1)} %stack.51.where_ref, f32[4,64,256]{2,1,0:T(8,128)S(1)} %get-tuple-element.51.a_ref.own_ref, f32[4,64,256]{2,1,0:T(8,128)S(1)} %collective-permute-done.13.b_ref.other_ref, f32[64,256]{1,0:T(8,128)S(1)} %collective-permute-done.14.beside_ref, ...), custom_call_target="tpu_custom_call" | custom-call | tf_op jit(solution)/shard_map/pallas_call | solution.py:350
  60.9 0.1 collective-permute-start.18
  60.9 1.3 %collective-permute-done.18.other_ref = bf16[2,32,2,512]{3,2,1,0:T(2,128)(2,1)S(1)} collective-permute-done((bf16[2,32,2,512]{3,2,1,0:T(2,128)(2,1)S(1)}, bf16[2,32,2,512]{3,2,1,0:T(2,128)(2,1)S(1)}, u32[]{:S(2)}, u32[]{:S(2)}) %collective-permute-start.18) | collective-permute-done | bytes 131104 | tf_op jit(solution)/shard_map/ppermute | solution.py:415
  62.3 1.3 %shard_map.112 = (bf16[64,2,512]{2,1,0:T(2,128)(2,1)}, bf16[64,2,512]{2,1,0:T(2,128)(2,1)}) custom-call(s32[12]{0:T(128)S(1)} %stack.51.where_ref, bf16[2,32,2,512]{3,2,1,0:T(2,128)(2,1)S(1)} %shard_map.111.mine_ref, bf16[2,32,2,512]{3,2,1,0:T(2,128)(2,1)S(1)} %collective-permute-done.18.other_ref), custom_call_target="tpu_custom_call" | custom-call | tf_op jit(solution)/shard_map/pallas_call | solution.py:218
  (20 shorter events, 0.1 us)
Async XLA Ops:
  0.6 5.3 %collective-permute-start = (bf16[1,8192,32]{1,2,0:T(8,128)(2,1)}, bf16[1,8192,32]{1,2,0:T(8,128)(2,1)S(1)}, u32[]{:S(2)}, u32[]{:S(2)}) collective-permute-start(bf16[1,8192,32]{1,2,0:T(8,128)(2,1)} %param.11), channel_id=1, source_target_pairs={{0,1},{1,0},{2,3},{3,2},{4,5},{5,4},{6,7},{7,6},{8,9},{9,8},{10,11... | collective-permute-start | bytes 1572872 | tf_op jit(solution)/shard_map/ppermute | solution.py:398
  1.1 4.8 %collective-permute-start.1 = (bf16[64,256]{1,0:T(8,128)(2,1)}, bf16[64,256]{1,0:T(8,128)(2,1)S(1)}, u32[]{:S(2)}, u32[]{:S(2)}) collective-permute-start(bf16[64,256]{1,0:T(8,128)(2,1)} %bitcast.26), channel_id=1, source_target_pairs={{0,2},{2,0},{4,6},{6,4},{8,10},{10,8},{12,14},{14,12},{1,3},{3,1},... | collective-permute-start | bytes 98312 | tf_op jit(solution)/shard_map/ppermute | solution.py:414
  3.7 1.2 %copy-start = (bf16[64,2,4096]{2,1,0:T(2,128)(2,1)S(1)}, bf16[64,2,4096]{2,1,0:T(2,128)(2,1)}, u32[]{:S(2)}) copy-start(bf16[64,2,4096]{2,1,0:T(2,128)(2,1)} %x_ref.1) | copy-start | bytes 3145732
  4.9 1.0 %copy-start.1 = (bf16[4096,64]{0,1:T(8,128)(2,1)S(1)}, bf16[4096,64]{0,1:T(8,128)(2,1)}, u32[]{:S(2)}) copy-start(bf16[4096,64]{0,1:T(8,128)(2,1)} %param.10) | copy-start | bytes 1572868
  4.9 1.2 %copy-start.2 = (bf16[1,8192,32]{1,2,0:T(8,128)(2,1)S(1)}, bf16[1,8192,32]{1,2,0:T(8,128)(2,1)}, u32[]{:S(2)}) copy-start(bf16[1,8192,32]{1,2,0:T(8,128)(2,1)} %param.11) | copy-start | bytes 1572868
  5.1 1.1 %copy-start.5 = (bf16[1,64,256]{2,1,0:T(8,128)(2,1)S(1)}, bf16[1,64,256]{2,1,0:T(8,128)(2,1)}, u32[]{:S(2)}) copy-start(bf16[1,64,256]{2,1,0:T(8,128)(2,1)} %param.12) | copy-start | bytes 98308
  6.1 8.3 %copy-start.3 = (bf16[64,16,256]{2,1,0:T(8,128)(2,1)S(1)}, bf16[64,16,256]{2,1,0:T(8,128)(2,1)}, u32[]{:S(2)}) copy-start(bf16[64,16,256]{2,1,0:T(8,128)(2,1)} %param.13) | copy-start | bytes 1572868
  6.8 25.3 %collective-permute-start.5 = (bf16[128,4096]{1,0:T(8,128)(2,1)S(1)}, bf16[128,4096]{1,0:T(8,128)(2,1)S(1)}, u32[]{:S(2)}, u32[]{:S(2)}) collective-permute-start(bf16[128,4096]{1,0:T(8,128)(2,1)S(1)} %shard_map.105.refs_0_), channel_id=1, source_target_pairs={{0,16},{16,0},{1,17},{17,1},{2,18},{18,2},{3,19},{19,3},{4,20},{20... | collective-permute-start | bytes 3145736 | tf_op jit(solution)/shard_map/ppermute | solution.py:413
  8.8 24.7 %collective-permute-start.2 = (bf16[128,4096]{1,0:T(8,128)(2,1)S(1)}, bf16[128,4096]{1,0:T(8,128)(2,1)S(1)}, u32[]{:S(2)}, u32[]{:S(2)}) collective-permute-start(bf16[128,4096]{1,0:T(8,128)(2,1)S(1)} %shard_map.105.refs_0_), channel_id=1, source_target_pairs={{0,2},{2,0},{4,6},{6,4},{8,10},{10,8},{12,14},{14,12},{1,3},{3,1},... | collective-permute-start | bytes 3145736 | tf_op jit(solution)/shard_map/ppermute | solution.py:414
  10.3 10.1 %collective-permute-start.9 = (bf16[64,2304]{1,0:T(8,128)(2,1)S(1)}, bf16[64,2304]{1,0:T(8,128)(2,1)S(1)}, u32[]{:S(2)}, u32[]{:S(2)}) collective-permute-start(bf16[64,2304]{1,0:T(8,128)(2,1)S(1)} %get-tuple-element.42.refs_3_.refs_2_.refs_5_), channel_id=1, source_target_pairs={{4,0},{6,2},{12,4},{14,6},{8,12},{10,14},{0,8},{2,10},{5,1},{7,3},... | collective-permute-start | bytes 884744 | tf_op jit(solution)/shard_map/ppermute | solution.py:412
  12.9 13.8 %collective-permute-start.3 = (bf16[64,2304]{1,0:T(8,128)(2,1)S(1)}, bf16[64,2304]{1,0:T(8,128)(2,1)S(1)}, u32[]{:S(2)}, u32[]{:S(2)}) collective-permute-start(bf16[64,2304]{1,0:T(8,128)(2,1)S(1)} %get-tuple-element.35.refs_4_.refs_3_.refs_6_), channel_id=1, source_target_pairs={{4,0},{6,2},{12,4},{14,6},{8,12},{10,14},{0,8},{2,10},{5,1},{7,3},... | collective-permute-start | bytes 884744 | tf_op jit(solution)/shard_map/ppermute | solution.py:412
  14.4 23.1 %collective-permute-start.6 = (bf16[1024,256]{1,0:T(8,128)(2,1)S(1)}, bf16[1024,256]{1,0:T(8,128)(2,1)S(1)}, u32[]{:S(2)}, u32[]{:S(2)}) collective-permute-start(bf16[1024,256]{1,0:T(8,128)(2,1)S(1)} %bitcast.23), channel_id=1, source_target_pairs={{0,1},{1,0},{2,3},{3,2},{4,5},{5,4},{6,7},{7,6},{8,9},{9,8},{10,11... | collective-permute-start | bytes 1572872 | tf_op jit(solution)/shard_map/ppermute | solution.py:415
  20.3 14.6 %collective-permute-start.10 = (bf16[64,2304]{1,0:T(8,128)(2,1)S(1)}, bf16[64,2304]{1,0:T(8,128)(2,1)S(1)}, u32[]{:S(2)}, u32[]{:S(2)}) collective-permute-start(bf16[64,2304]{1,0:T(8,128)(2,1)S(1)} %collective-permute-done.9.refs_5_.refs_4_.refs_7_), channel_id=1, source_target_pairs={{4,0},{6,2},{12,4},{14,6},{8,12},{10,14},{0,8},{2,10},{5,1},{7,3},... | collective-permute-start | bytes 884744 | tf_op jit(solution)/shard_map/ppermute | solution.py:412
  26.6 11.7 %collective-permute-start.4 = (bf16[64,2304]{1,0:T(8,128)(2,1)S(1)}, bf16[64,2304]{1,0:T(8,128)(2,1)S(1)}, u32[]{:S(2)}, u32[]{:S(2)}) collective-permute-start(bf16[64,2304]{1,0:T(8,128)(2,1)S(1)} %collective-permute-done.3.refs_6_.refs_5_.refs_8_), channel_id=1, source_target_pairs={{4,0},{6,2},{12,4},{14,6},{8,12},{10,14},{0,8},{2,10},{5,1},{7,3},... | collective-permute-start | bytes 884744 | tf_op jit(solution)/shard_map/ppermute | solution.py:412
  32.1 5.3 %copy-start.4 = (bf16[64,2,256]{2,1,0:T(2,128)(2,1)S(1)}, bf16[64,2,256]{2,1,0:T(2,128)(2,1)}, u32[]{:S(2)}) copy-start(bf16[64,2,256]{2,1,0:T(2,128)(2,1)} %fresh_ref.1) | copy-start | bytes 196612
  32.2 5.3 %copy-start.6 = (s32[64]{0:T(128)S(1)}, s32[64]{0:T(128)}, u32[]{:S(2)}) copy-start(s32[64]{0:T(128)} %lengths_ref.1) | copy-start | bytes 772
  32.2 5.3 %copy-start.7 = (s32[64]{0:T(128)S(1)}, s32[64]{0:T(128)}, u32[]{:S(2)}) copy-start(s32[64]{0:T(128)} %adapter_ref.1) | copy-start | bytes 772
  32.2 5.3 %copy-start.8 = (s32[8]{0:T(128)S(1)}, s32[8]{0:T(128)}, u32[]{:S(2)}) copy-start(s32[8]{0:T(128)} %owner_ref.1) | copy-start | bytes 100
  32.2 13.8 %collective-permute-start.7 = (bf16[64,4096]{1,0:T(8,128)(2,1)S(1)}, bf16[64,4096]{1,0:T(8,128)(2,1)S(1)}, u32[]{:S(2)}, u32[]{:S(2)}) collective-permute-start(bf16[64,4096]{1,0:T(8,128)(2,1)S(1)} %slice.8), channel_id=1, source_target_pairs={{0,2},{2,0},{4,6},{6,4},{8,10},{10,8},{12,14},{14,12},{1,3},{3,1},... | collective-permute-start | bytes 1572872 | tf_op jit(solution)/shard_map/ppermute | solution.py:414
  33.5 12.6 %collective-permute-start.8 = (bf16[64,4096]{1,0:T(8,128)(2,1)S(1)}, bf16[64,4096]{1,0:T(8,128)(2,1)S(1)}, u32[]{:S(2)}, u32[]{:S(2)}) collective-permute-start(bf16[64,4096]{1,0:T(8,128)(2,1)S(1)} %slice.9), channel_id=1, source_target_pairs={{0,16},{16,0},{1,17},{17,1},{2,18},{18,2},{3,19},{19,3},{4,20},{20... | collective-permute-start | bytes 1572872 | tf_op jit(solution)/shard_map/ppermute | solution.py:413
  34.9 10.1 %collective-permute-start.11 = (bf16[64,2304]{1,0:T(8,128)(2,1)S(1)}, bf16[64,2304]{1,0:T(8,128)(2,1)S(1)}, u32[]{:S(2)}, u32[]{:S(2)}) collective-permute-start(bf16[64,2304]{1,0:T(8,128)(2,1)S(1)} %collective-permute-done.10.refs_7_.refs_6_.refs_9_), channel_id=1, source_target_pairs={{4,0},{6,2},{12,4},{14,6},{8,12},{10,14},{0,8},{2,10},{5,1},{7,3},... | collective-permute-start | bytes 884744 | tf_op jit(solution)/shard_map/ppermute | solution.py:412
  38.4 11.3 %collective-permute-start.12 = (bf16[64,2304]{1,0:T(8,128)(2,1)S(1)}, bf16[64,2304]{1,0:T(8,128)(2,1)S(1)}, u32[]{:S(2)}, u32[]{:S(2)}) collective-permute-start(bf16[64,2304]{1,0:T(8,128)(2,1)S(1)} %collective-permute-done.4.refs_8_.refs_7_.refs_10_), channel_id=1, source_target_pairs={{4,0},{6,2},{12,4},{14,6},{8,12},{10,14},{0,8},{2,10},{5,1},{7,3},... | collective-permute-start | bytes 884744 | tf_op jit(solution)/shard_map/ppermute | solution.py:412
  50.9 1.6 %collective-permute-start.13 = (f32[4,64,256]{2,1,0:T(8,128)S(1)}, f32[4,64,256]{2,1,0:T(8,128)S(1)}, u32[]{:S(2)}, u32[]{:S(2)}) collective-permute-start(f32[4,64,256]{2,1,0:T(8,128)S(1)} %get-tuple-element.52), channel_id=1, source_target_pairs={{0,1},{1,0},{2,3},{3,2},{4,5},{5,4},{6,7},{7,6},{8,9},{9,8},{10,11... | collective-permute-start | bytes 786440 | tf_op jit(solution)/shard_map/ppermute | solution.py:415
  51.0 5.1 %collective-permute-start.17 = (bf16[512,256]{1,0:T(8,128)(2,1)S(1)}, bf16[512,256]{1,0:T(8,128)(2,1)S(1)}, u32[]{:S(2)}, u32[]{:S(2)}) collective-permute-start(bf16[512,256]{1,0:T(8,128)(2,1)S(1)} %get-tuple-element.57.up_ref), channel_id=1, source_target_pairs={{0,1},{1,0},{2,3},{3,2},{4,5},{5,4},{6,7},{7,6},{8,9},{9,8},{10,11... | collective-permute-start | bytes 786440 | tf_op jit(solution)/shard_map/ppermute | solution.py:415
  52.6 4.3 %collective-permute-start.14 = (f32[64,256]{1,0:T(8,128)S(1)}, f32[64,256]{1,0:T(8,128)S(1)}, u32[]{:S(2)}, u32[]{:S(2)}) collective-permute-start(f32[64,256]{1,0:T(8,128)S(1)} %get-tuple-element.53), channel_id=1, source_target_pairs={{0,2},{2,0},{4,6},{6,4},{8,10},{10,8},{12,14},{14,12},{1,3},{3,1},... | collective-permute-start | bytes 196616 | tf_op jit(solution)/shard_map/ppermute | solution.py:414
  53.8 4.9 %collective-permute-start.15 = (f32[64,256]{1,0:T(8,128)S(1)}, f32[64,256]{1,0:T(8,128)S(1)}, u32[]{:S(2)}, u32[]{:S(2)}) collective-permute-start(f32[64,256]{1,0:T(8,128)S(1)} %get-tuple-element.54), channel_id=1, source_target_pairs={{0,16},{16,0},{1,17},{17,1},{2,18},{18,2},{3,19},{19,3},{4,20},{20... | collective-permute-start | bytes 196616 | tf_op jit(solution)/shard_map/ppermute | solution.py:413
  54.2 5.2 %collective-permute-start.16 = (f32[64,256]{1,0:T(8,128)S(1)}, f32[64,256]{1,0:T(8,128)S(1)}, u32[]{:S(2)}, u32[]{:S(2)}) collective-permute-start(f32[64,256]{1,0:T(8,128)S(1)} %get-tuple-element.55), channel_id=1, source_target_pairs={{0,18},{2,16},{4,22},{6,20},{8,26},{10,24},{12,30},{14,28},{16,2},... | collective-permute-start | bytes 196616 | tf_op jit(solution)/shard_map/ppermute | solution.py:445
  60.9 1.4 %collective-permute-start.18 = (bf16[2,32,2,512]{3,2,1,0:T(2,128)(2,1)S(1)}, bf16[2,32,2,512]{3,2,1,0:T(2,128)(2,1)S(1)}, u32[]{:S(2)}, u32[]{:S(2)}) collective-permute-start(bf16[2,32,2,512]{3,2,1,0:T(2,128)(2,1)S(1)} %shard_map.111.mine_ref), channel_id=1, source_target_pairs={{0,1},{1,0},{2,3},{3,2},{4,5},{5,4},{6,7},{7,6},{8,9},{9,8},{10,11... | collective-permute-start | bytes 393224 | tf_op jit(solution)/shard_map/ppermute | solution.py:415
